TPU v7x, 32 devices: a whole 2x2x4 slice. The times are simulated.
32 devices in a mesh: section: 2 (over core), dp: 4 (over z), ctx: 4 (over y, x).
Axes of the slice: x: 2, y: 2, z: 4, core: 2. Of those that a mesh axis runs over, the one named last changes fastest.
Arguments:
- token_ids: int32 [2, 4, 1024], P(None, None, 'ctx'), may hold values from 0 to 49151
- doc_lengths: int32 [2, 4, 4], P(None, 'dp'), may hold values from 1 to 896, 1024 in all within a row
- picks: int32 [2, 4, 64], P(None, 'dp', 'ctx'), may hold values from -1 to 255, as said below
- targets: int32 [2, 4, 64], P(None, None, 'ctx'), may hold values from -1 to 49151, as said below
- table: float32 [49152, 768], P('dp')
- table_rows: float32 [49152], P('dp'), may hold values from 0.0020833334 to 0.008333334
- table_cols: float32 [768], replicated, may hold values from 0.0020833334 to 0.008333334
- attention_in: float32 [2, 768, 896], P('section', ('dp', 'ctx')), may hold values from -0.21875 to 0.21875
- attention_in_rows: float32 [2, 768], P('section', ('dp', 'ctx')), may hold values from 0.01536 to 0.06144
- attention_in_cols: float32 [2, 896], P('section'), may hold values from 0.01536 to 0.06144
- attention_out: float32 [2, 768, 768], P('section', ('dp', 'ctx')), may hold values from -0.875 to 0.875
- attention_out_rows: float32 [2, 768], P('section', ('dp', 'ctx')), may hold values from 0.01536 to 0.06144
- attention_out_cols: float32 [2, 768], P('section'), may hold values from 0.01536 to 0.06144
- hidden_in: float32 [2, 768, 3072], P('section', ('dp', 'ctx')), may hold values from -0.21875 to 0.21875
- hidden_in_rows: float32 [2, 768], P('section', ('dp', 'ctx')), may hold values from 0.01536 to 0.06144
- hidden_in_cols: float32 [2, 3072], P('section'), may hold values from 0.01536 to 0.06144
- hidden_out: float32 [2, 3072, 768], P('section', ('dp', 'ctx')), may hold values from -0.109375 to 0.109375
- hidden_out_rows: float32 [2, 3072], P('section', ('dp', 'ctx')), may hold values from 0.01536 to 0.06144
- hidden_out_cols: float32 [2, 768], P('section'), may hold values from 0.01536 to 0.06144
- gains: float32 [2, 4, 768], P('section', None, ('dp', 'ctx'))
- gains_stat: float32 [2, 4, 768], P('section', None, ('dp', 'ctx')), may hold values from 0.2048 to 0.8192
Outputs:
- loss_sum: float32 [], replicated
- loss_count: float32 [], replicated
- table_grad: float32 [49152, 768], P('dp')
- table_rows_new: float32 [49152], P('dp')
- table_cols_new: float32 [768], replicated
- table_new: float32 [49152, 768], P('dp')
- attention_in_grad: float32 [2, 768, 896], P('section', ('dp', 'ctx'))
- attention_in_rows_new: float32 [2, 768], P('section', ('dp', 'ctx'))
- attention_in_cols_new: float32 [2, 896], P('section')
- attention_in_new: float32 [2, 768, 896], P('section', ('dp', 'ctx'))
- attention_out_grad: float32 [2, 768, 768], P('section', ('dp', 'ctx'))
- attention_out_rows_new: float32 [2, 768], P('section', ('dp', 'ctx'))
- attention_out_cols_new: float32 [2, 768], P('section')
- attention_out_new: float32 [2, 768, 768], P('section', ('dp', 'ctx'))
- hidden_in_grad: float32 [2, 768, 3072], P('section', ('dp', 'ctx'))
- hidden_in_rows_new: float32 [2, 768], P('section', ('dp', 'ctx'))
- hidden_in_cols_new: float32 [2, 3072], P('section')
- hidden_in_new: float32 [2, 768, 3072], P('section', ('dp', 'ctx'))
- hidden_out_grad: float32 [2, 3072, 768], P('section', ('dp', 'ctx'))
- hidden_out_rows_new: float32 [2, 3072], P('section', ('dp', 'ctx'))
- hidden_out_cols_new: float32 [2, 768], P('section')
- hidden_out_new: float32 [2, 3072, 768], P('section', ('dp', 'ctx'))
- gains_grad: float32 [2, 4, 768], P('section', None, ('dp', 'ctx'))
- gains_stat_new: float32 [2, 4, 768], P('section', None, ('dp', 'ctx'))
- gains_new: float32 [2, 4, 768], P('section', None, ('dp', 'ctx'))
Inputs may be any that keep to these rules, and one draw needn't show every extreme that they name: `picks`: within each block of 16 slots (one sequence's positions on one device) the live slots come first, there is at least one, and their positions are distinct positions of that block; in every micro-batch the block of the last sequence on the last ctx device is full. `targets`: -1 exactly where picks is -1.
All inputs are finite; a program needn't handle non-finite values.
Results may differ from a plain program's by a relative error of at most 0.017.
The roundings to bfloat16 on the way count: a program that leaves them out, or rounds other values in their place, can miss the bound.
Values may be sent and summed in bfloat16 or wider, within the bound.
No kernel may reach another device: no remote copies, remote signals or barrier semaphores. Data moves between devices by JAX's collectives and lax.ppermute only.
A program may use at most 384 MiB of HBM per device.

v0:
```python
import jax
import jax.numpy as jnp
from jax import lax
from jax.sharding import PartitionSpec as P

D = 768
HD = 64
FF = 3072
VOCAB = 49152
WINDOW = 512
STEP = 10


NORM_EPS = 1e-05
SQUARE_EPS = 1e-30
SCALE_FLOOR = 0.001
RELATIVE_RATE = 0.5
MASKED = -1e30


def passed_along(block, axis, distance):
    devices = range(lax.axis_size(axis))
    route = [(i - distance, i) for i in devices if i - distance in devices]
    return lax.ppermute(block, axis, route)


def combined_all(value, axis, join):
    pieces = jax.tree.map(lambda part: lax.all_gather(part, axis), value)
    head = jax.tree.map(lambda part: part[0], pieces)
    tail = jax.tree.map(lambda part: part[1:], pieces)
    total, _ = lax.scan(lambda total, share: (join(total, share), None), head, tail)
    return total


def bfloat(values):
    return values.astype(jnp.bfloat16)


def matmul(left, right):
    return jnp.dot(left, right, preferred_element_type=jnp.float32)


def matmul_left(left, right):
    return lax.dot_general(
        left, right, (((0,), (0,)), ((), ())), preferred_element_type=jnp.float32
    )


def matmul_right(left, right):
    return lax.dot_general(
        left, right, (((1,), (1,)), ((), ())), preferred_element_type=jnp.float32
    )


def layer_norm(values, gain, shift):
    center = values - jnp.mean(values, -1, keepdims=True)
    spread = jnp.mean(center * center, -1, keepdims=True)
    return center * lax.rsqrt(spread + NORM_EPS) * gain + shift


def gelu_tanh(values):
    return jax.nn.gelu(values, approximate=True)


def doc_numbers(lengths, seq_len):
    bounds = jnp.cumsum(lengths)
    places = jnp.arange(seq_len, dtype=jnp.int32)
    return jnp.sum((places[:, None] >= bounds[None, :]).astype(jnp.int32), -1)


def hand_over(values, direction):
    return passed_along(values, "section", direction)


def sequence_rows(values):
    return lax.all_gather(values, "ctx", axis=0, tiled=True)


def reduce_grads(grads):
    return (
        lax.psum_scatter(grads[0], ("dp", "ctx"), scatter_dimension=0, tiled=True),
        lax.psum_scatter(grads[1], ("dp", "ctx"), scatter_dimension=0, tiled=True),
        lax.psum_scatter(grads[2], ("dp", "ctx"), scatter_dimension=0, tiled=True),
        lax.psum_scatter(grads[3], ("dp", "ctx"), scatter_dimension=0, tiled=True),
        lax.psum_scatter(grads[4], ("dp", "ctx"), scatter_dimension=1, tiled=True),
    )


def masked_scores(query_rows, key_rows, doc_ids, offset, block_len):
    seq_len = key_rows.shape[0]
    spots = offset + jnp.arange(block_len, dtype=jnp.int32)
    places = jnp.arange(seq_len, dtype=jnp.int32)
    owners = lax.dynamic_slice_in_dim(doc_ids, offset, block_len)
    allowed = (
        (places[None, :] <= spots[:, None])
        & (places[None, :] > spots[:, None] - WINDOW)
        & (doc_ids[None, :] == owners[:, None])
    )
    scores = jnp.einsum("hbd,kd->hbk", query_rows, key_rows, preferred_element_type=jnp.float32)
    return jnp.where(allowed[None], scores, MASKED)


def attend_forward(query, keyval, doc_ids):
    seq_len, columns = query.shape
    block_len = min(512, seq_len)
    stacked = query.reshape(seq_len, columns // HD, HD).transpose(1, 0, 2)
    key_rows, value_rows = (keyval[:, :HD], keyval[:, HD:])

    def one_block(offset):
        query_rows = lax.dynamic_slice_in_dim(stacked, offset, block_len, 1)
        scores = masked_scores(query_rows, key_rows, doc_ids, offset, block_len)
        highest = jnp.max(scores, -1, keepdims=True)
        exponents = jnp.exp(scores - highest)
        totals = jnp.sum(exponents, -1, keepdims=True)
        outputs = jnp.einsum(
            "hbk,kd->hbd",
            bfloat(exponents / totals),
            value_rows,
            preferred_element_type=jnp.float32,
        )
        return (bfloat(outputs), (highest + jnp.log(totals))[..., 0])

    offsets = jnp.arange(seq_len // block_len, dtype=jnp.int32) * block_len
    outputs, logsum = lax.map(one_block, offsets)
    return (outputs.transpose(0, 2, 1, 3).reshape(seq_len, columns), logsum)


def attend_backward(query, keyval, doc_ids, logsum, grad_out):
    seq_len, columns = query.shape
    block_len = min(512, seq_len)
    stacked = query.reshape(seq_len, columns // HD, HD).transpose(1, 0, 2)
    grad_stack = bfloat(grad_out).reshape(seq_len, columns // HD, HD).transpose(1, 0, 2)
    key_rows, value_rows = (keyval[:, :HD], keyval[:, HD:])

    def one_block(carry, inputs):
        offset, block_logsum = inputs
        query_rows = lax.dynamic_slice_in_dim(stacked, offset, block_len, 1)
        grad_rows = lax.dynamic_slice_in_dim(grad_stack, offset, block_len, 1)
        scores = masked_scores(query_rows, key_rows, doc_ids, offset, block_len)
        probs = jnp.exp(scores - block_logsum[..., None])
        grad_probs = jnp.einsum(
            "hbd,kd->hbk", grad_rows, value_rows, preferred_element_type=jnp.float32
        )
        grad_scores = bfloat(probs * (grad_probs - jnp.sum(probs * grad_probs, -1, keepdims=True)))
        grad_query = jnp.einsum(
            "hbk,kd->hbd", grad_scores, key_rows, preferred_element_type=jnp.float32
        )
        grad_keys = jnp.einsum(
            "hbk,hbd->kd", grad_scores, query_rows, preferred_element_type=jnp.float32
        )
        grad_values = jnp.einsum(
            "hbk,hbd->kd", bfloat(probs), grad_rows, preferred_element_type=jnp.float32
        )
        return (carry + jnp.concatenate([grad_keys, grad_values], 1), grad_query)

    offsets = jnp.arange(seq_len // block_len, dtype=jnp.int32) * block_len
    grad_keyval, grad_query = lax.scan(
        one_block, jnp.zeros((seq_len, 2 * HD), jnp.float32), (offsets, logsum)
    )
    return (grad_query.transpose(0, 2, 1, 3).reshape(seq_len, columns), grad_keyval)


def layer_forward(inputs, weights, doc_ids):
    attention_in, attention_out, hidden_in, hidden_out, gains = weights
    gain_values = gains.astype(jnp.float32)
    model = attention_out.shape[0]
    share = model // lax.axis_size("ctx")
    position = lax.axis_index("ctx")
    normed = bfloat(layer_norm(inputs, gain_values[0], gain_values[1]))
    whole = sequence_rows(normed)
    query_weight = lax.dynamic_slice_in_dim(attention_in, position * share, share, 1)
    query = bfloat(matmul(whole, query_weight) * HD ** (-0.5))
    keyval = bfloat(matmul(whole, attention_in[:, model:]))
    attended, logsum = attend_forward(query, keyval, doc_ids)
    out_weight = lax.dynamic_slice_in_dim(attention_out, position * share, share, 0)
    mixed = inputs + lax.psum_scatter(
        matmul(attended, out_weight).astype(jnp.bfloat16), "ctx", scatter_dimension=0, tiled=True
    ).astype(jnp.float32)
    normed_two = bfloat(layer_norm(mixed, gain_values[2], gain_values[3]))
    upper = matmul(normed_two, hidden_in)
    active = bfloat(gelu_tanh(upper))
    result = mixed + matmul(active, hidden_out)
    return (
        result,
        (inputs, normed, whole, query, keyval, logsum, attended, mixed, normed_two, upper, active),
    )


def layer_backward(grad_result, kept, weights, doc_ids):
    inputs, normed, whole, query, keyval, logsum, attended, mixed, normed_two, upper, active = kept
    attention_in, attention_out, hidden_in, hidden_out, gains = weights
    gain_values = gains.astype(jnp.float32)
    model = attention_out.shape[0]
    share = model // lax.axis_size("ctx")
    position = lax.axis_index("ctx")
    grad_low = bfloat(grad_result)
    grad_down = matmul_left(active, grad_low)
    _, gelu_pull = jax.vjp(gelu_tanh, upper)
    grad_upper = bfloat(gelu_pull(matmul_right(grad_low, hidden_out))[0])
    grad_up = matmul_left(normed_two, grad_upper)
    _, second_pull = jax.vjp(layer_norm, mixed, gain_values[2], gain_values[3])
    grad_mixed, grad_gain_two, grad_shift_two = second_pull(matmul_right(grad_upper, hidden_in))
    grad_mixed = grad_mixed + grad_result
    grad_whole = sequence_rows(bfloat(grad_mixed))
    out_weight = lax.dynamic_slice_in_dim(attention_out, position * share, share, 0)
    grad_out_rows = matmul_left(attended, grad_whole)
    grad_attended = matmul_right(grad_whole, out_weight)
    grad_query, grad_keyval = attend_backward(query, keyval, doc_ids, logsum, grad_attended)
    grad_query = bfloat(bfloat(grad_query).astype(jnp.float32) * HD ** (-0.5))
    query_weight = lax.dynamic_slice_in_dim(attention_in, position * share, share, 1)
    grad_query_weight = matmul_left(whole, grad_query)
    grad_normed, grad_keyval = (
        lax.psum_scatter(
            matmul_right(grad_query, query_weight).astype(jnp.bfloat16),
            "ctx",
            scatter_dimension=0,
            tiled=True,
        ).astype(jnp.float32),
        lax.psum_scatter(
            grad_keyval.astype(jnp.bfloat16), "ctx", scatter_dimension=0, tiled=True
        ).astype(jnp.float32),
    )
    grad_keyval = bfloat(grad_keyval)
    grad_kv_weight = matmul_left(normed, grad_keyval)
    grad_normed = grad_normed + matmul_right(grad_keyval, attention_in[:, model:])
    _, first_pull = jax.vjp(layer_norm, inputs, gain_values[0], gain_values[1])
    grad_inputs, grad_gain_one, grad_shift_one = first_pull(grad_normed)
    grad_in = jnp.zeros(attention_in.shape, jnp.float32)
    grad_in = lax.dynamic_update_slice_in_dim(grad_in, grad_query_weight, position * share, 1)
    grad_in = lax.dynamic_update_slice_in_dim(grad_in, grad_kv_weight, model, 1)
    grad_out = lax.dynamic_update_slice_in_dim(
        jnp.zeros(attention_out.shape, jnp.float32), grad_out_rows, position * share, 0
    )
    grad_gains = jnp.stack([grad_gain_one, grad_shift_one, grad_gain_two, grad_shift_two])
    return (grad_inputs + grad_mixed, (grad_in, grad_out, grad_up, grad_down, grad_gains))


def combine_stats(earlier, later):
    highest = jnp.maximum(earlier[0], later[0])
    totals = earlier[1] * jnp.exp(earlier[0] - highest) + later[1] * jnp.exp(later[0] - highest)
    return (highest, totals, earlier[2] + later[2])


def head_step(result, pick_row, target_rows, table_low, vocab_base):
    local_len = result.shape[0]
    onehot = pick_row[:, None] == jnp.arange(local_len, dtype=jnp.int32)[None, :]
    chosen = bfloat(matmul(onehot.astype(jnp.bfloat16), bfloat(result)))
    gathered = lax.all_gather(chosen, "dp", axis=0, tiled=True)
    logits = matmul_right(gathered, table_low)
    local_target = target_rows - vocab_base
    matches = local_target[:, None] == jnp.arange(table_low.shape[0], dtype=jnp.int32)[None, :]
    target_logit = jnp.sum(jnp.where(matches, logits, 0.0), -1)
    highest = jnp.max(logits, -1)
    totals = jnp.sum(jnp.exp(logits - highest[:, None]), -1)
    highest_all, totals_all, target_all = combined_all(
        (highest, totals, target_logit), "dp", combine_stats
    )
    logsum = highest_all + jnp.log(totals_all)
    live = target_rows >= 0
    losses = jnp.sum(jnp.where(live, logsum - target_all, 0.0))
    probs = jnp.exp(logits - logsum[:, None])
    grad_logits = bfloat(jnp.where(live[:, None], probs - matches.astype(jnp.float32), 0.0))
    grad_table = matmul_left(grad_logits, gathered)
    grad_chosen = lax.psum_scatter(
        matmul(grad_logits, table_low).astype(jnp.bfloat16), "dp", scatter_dimension=0, tiled=True
    ).astype(jnp.float32)
    grad_result = jnp.dot(
        onehot.astype(jnp.float32).T,
        grad_chosen,
        precision=lax.Precision.HIGHEST,
        preferred_element_type=jnp.float32,
    )
    return (losses, jnp.sum(live.astype(jnp.float32)), grad_table, grad_result)


def body(
    token_ids,
    doc_lengths,
    picks,
    targets,
    table,
    table_rows,
    table_cols,
    attention_in,
    attention_in_rows,
    attention_in_cols,
    attention_out,
    attention_out_rows,
    attention_out_cols,
    hidden_in,
    hidden_in_rows,
    hidden_in_cols,
    hidden_out,
    hidden_out_rows,
    hidden_out_cols,
    gains,
    gains_stat,
):
    section = lax.axis_index("section")
    sections = lax.axis_size("section")
    micro = token_ids.shape[0]
    local_len = token_ids.shape[2]
    is_first = section == 0
    is_last = section == sections - 1
    weights = (
        lax.all_gather(bfloat(attention_in[0]), ("dp", "ctx"), axis=0, tiled=True),
        lax.all_gather(bfloat(attention_out[0]), ("dp", "ctx"), axis=0, tiled=True),
        lax.all_gather(bfloat(hidden_in[0]), ("dp", "ctx"), axis=0, tiled=True),
        lax.all_gather(bfloat(hidden_out[0]), ("dp", "ctx"), axis=0, tiled=True),
        lax.all_gather(bfloat(gains[0]), ("dp", "ctx"), axis=1, tiled=True),
    )
    model = table.shape[1]
    table_low = bfloat(table)
    vocab_here = table.shape[0]
    me = lax.axis_index("dp")
    vocab_base = me * vocab_here
    local_ids = token_ids - vocab_base
    inside = (local_ids >= 0) & (local_ids < vocab_here)
    looked = jnp.take(table_low, jnp.clip(local_ids, 0, vocab_here - 1), axis=0) * inside[
        ..., None
    ].astype(jnp.bfloat16)
    start_rows = lax.psum_scatter(looked, "dp", scatter_dimension=1, tiled=True).astype(
        jnp.float32
    )[:, 0]
    seq_len = local_len * lax.axis_size("ctx")
    doc_ids = jnp.stack([doc_numbers(doc_lengths[index, 0], seq_len) for index in range(micro)])
    ticks = micro + sections - 1
    incoming = jnp.zeros(start_rows.shape[1:], jnp.bfloat16)
    kept_all = []
    head_grads = []
    loss_total = jnp.zeros((), jnp.float32)
    count_total = jnp.zeros((), jnp.float32)
    grad_table = jnp.zeros(table.shape, jnp.float32)
    for tick_index in range(ticks):
        micro_index = tick_index - section
        valid = (micro_index >= 0) & (micro_index < micro)
        clipped = jnp.clip(micro_index, 0, micro - 1)
        inputs = jnp.where(is_first, start_rows[clipped], incoming.astype(jnp.float32))
        result, kept = layer_forward(inputs, weights, doc_ids[clipped])
        kept_all.append(kept)
        incoming = hand_over(bfloat(result), 1)
        live = (valid & is_last).astype(jnp.float32)
        losses, counted, head_table, head_result = head_step(
            result, picks[clipped, 0], targets[clipped].reshape(-1), table_low, vocab_base
        )
        loss_total = loss_total + live * losses
        count_total = count_total + live * counted
        grad_table = grad_table + live * head_table
        head_grads.append(live * head_result)
    lookup_grads = jnp.zeros(start_rows.shape, jnp.float32)
    incoming_back = jnp.zeros(start_rows.shape[1:], jnp.bfloat16)
    summed = None
    shards = None
    for back_index in range(ticks):
        forward_index = ticks - 1 - back_index
        micro_index = forward_index - section
        valid = (micro_index >= 0) & (micro_index < micro)
        clipped = jnp.clip(micro_index, 0, micro - 1)
        grad_result = jnp.where(
            is_last, head_grads[forward_index], incoming_back.astype(jnp.float32)
        )
        grad_inputs, grads = layer_backward(
            grad_result, kept_all[forward_index], weights, doc_ids[clipped]
        )
        rounded_inputs = bfloat(grad_inputs)
        incoming_back = hand_over(rounded_inputs, -1)
        factor = valid.astype(jnp.float32)
        grads = tuple((factor * item for item in grads))
        lookup_grads = lookup_grads.at[clipped].add(
            jnp.where(valid & is_first, rounded_inputs.astype(jnp.float32), 0.0)
        )
        summed = (
            grads if summed is None else tuple((left + right for left, right in zip(summed, grads)))
        )
    shards = reduce_grads(summed)
    lookup_all = lax.all_gather(bfloat(lookup_grads)[:, None], "dp", axis=1, tiled=True)
    segment_ids = jnp.where(inside, local_ids, vocab_here).reshape(-1)
    grad_table = grad_table + jax.ops.segment_sum(
        lookup_all.reshape(-1, model).astype(jnp.float32), segment_ids, num_segments=vocab_here
    )
    grad_table, loss_sum, loss_count = (
        lax.psum(grad_table.astype(jnp.bfloat16), ("section", "ctx")).astype(jnp.float32),
        lax.psum(loss_total.astype(jnp.bfloat16), ("section", "ctx")).astype(jnp.float32),
        lax.psum(count_total.astype(jnp.bfloat16), ("section", "ctx")).astype(jnp.float32),
    )
    decay = 1.0 - STEP ** (-0.8)
    copies = lax.axis_size("ctx")
    entries = [
        (table, grad_table, table_rows, table_cols, VOCAB, copies),
        (attention_in[0], shards[0], attention_in_rows[0], attention_in_cols[0], D, 1),
        (attention_out[0], shards[1], attention_out_rows[0], attention_out_cols[0], D, 1),
        (hidden_in[0], shards[2], hidden_in_rows[0], hidden_in_cols[0], D, 1),
        (hidden_out[0], shards[3], hidden_out_rows[0], hidden_out_cols[0], FF, 1),
    ]
    rows_new_all = []
    column_parts = []
    scalar_parts = []
    for weight, gradient, row_stat, col_stat, row_count, copies_here in entries:
        square = gradient * gradient + SQUARE_EPS
        rows_new = decay * row_stat + (1.0 - decay) * jnp.mean(square, -1)
        rows_new_all.append(rows_new)
        column_parts.append(jnp.sum(square, 0) / copies_here)
        scalar_parts.append(jnp.sum(rows_new) / copies_here)
        scalar_parts.append(jnp.sum(weight * weight) / copies_here)
    gain_weight = gains[0]
    gain_grad = shards[4]
    gain_stat_new = decay * gains_stat[0] + (1.0 - decay) * (gain_grad * gain_grad + SQUARE_EPS)
    column_sums, scalar_sums, gain_squares = lax.psum(
        (
            jnp.concatenate(column_parts),
            jnp.stack(scalar_parts),
            jnp.sum(gain_weight * gain_weight, -1),
        ),
        ("dp", "ctx"),
    )
    updates = []
    cols_new_all = []
    update_parts = []
    place = 0
    for index, (weight, gradient, row_stat, col_stat, row_count, copies_here) in enumerate(entries):
        columns = col_stat.shape[0]
        cols_new = (
            decay * col_stat + (1.0 - decay) * column_sums[place : place + columns] / row_count
        )
        place = place + columns
        mean_rows = scalar_sums[2 * index] / row_count
        update = gradient * lax.rsqrt(rows_new_all[index][:, None] * cols_new[None, :] / mean_rows)
        updates.append(update)
        cols_new_all.append(cols_new)
        update_parts.append(jnp.sum(update * update) / copies_here)
    gain_update = gain_grad * lax.rsqrt(gain_stat_new)
    update_sums, gain_update_sums = lax.psum(
        (jnp.stack(update_parts), jnp.sum(gain_update * gain_update, -1)), ("dp", "ctx")
    )
    news = []
    for index, (weight, gradient, row_stat, col_stat, row_count, copies_here) in enumerate(entries):
        entry_count = row_count * col_stat.shape[0]
        clipping = jnp.maximum(1.0, jnp.sqrt(update_sums[index] / entry_count))
        size = jnp.maximum(SCALE_FLOOR, jnp.sqrt(scalar_sums[2 * index + 1] / entry_count))
        news.append(weight - RELATIVE_RATE * size * (updates[index] / clipping))
    gain_clipping = jnp.maximum(1.0, jnp.sqrt(gain_update_sums / D))
    gain_size = jnp.maximum(SCALE_FLOOR, jnp.sqrt(gain_squares / D))
    gain_new = gain_weight - RELATIVE_RATE * gain_size[:, None] * (
        gain_update / gain_clipping[:, None]
    )
    return (
        loss_sum,
        loss_count,
        grad_table,
        rows_new_all[0],
        cols_new_all[0],
        news[0],
        shards[0][None],
        rows_new_all[1][None],
        cols_new_all[1][None],
        news[1][None],
        shards[1][None],
        rows_new_all[2][None],
        cols_new_all[2][None],
        news[2][None],
        shards[2][None],
        rows_new_all[3][None],
        cols_new_all[3][None],
        news[3][None],
        shards[3][None],
        rows_new_all[4][None],
        cols_new_all[4][None],
        news[4][None],
        gain_grad[None],
        gain_stat_new[None],
        gain_new[None],
    )


def solution(mesh):
    placed = (
        P(None, None, "ctx"),
        P(None, "dp", None),
        P(None, "dp", "ctx"),
        P(None, None, "ctx"),
        P("dp", None),
        P("dp"),
        P(),
        P("section", ("dp", "ctx"), None),
        P("section", ("dp", "ctx")),
        P("section", None),
        P("section", ("dp", "ctx"), None),
        P("section", ("dp", "ctx")),
        P("section", None),
        P("section", ("dp", "ctx"), None),
        P("section", ("dp", "ctx")),
        P("section", None),
        P("section", ("dp", "ctx"), None),
        P("section", ("dp", "ctx")),
        P("section", None),
        P("section", None, ("dp", "ctx")),
        P("section", None, ("dp", "ctx")),
    )
    return jax.shard_map(
        body,
        mesh=mesh,
        in_specs=placed,
        out_specs=(
            P(),
            P(),
            P("dp", None),
            P("dp"),
            P(),
            P("dp", None),
            P("section", ("dp", "ctx"), None),
            P("section", ("dp", "ctx")),
            P("section", None),
            P("section", ("dp", "ctx"), None),
            P("section", ("dp", "ctx"), None),
            P("section", ("dp", "ctx")),
            P("section", None),
            P("section", ("dp", "ctx"), None),
            P("section", ("dp", "ctx"), None),
            P("section", ("dp", "ctx")),
            P("section", None),
            P("section", ("dp", "ctx"), None),
            P("section", ("dp", "ctx"), None),
            P("section", ("dp", "ctx")),
            P("section", None),
            P("section", ("dp", "ctx"), None),
            P("section", None, ("dp", "ctx")),
            P("section", None, ("dp", "ctx")),
            P("section", None, ("dp", "ctx")),
        ),
        check_vma=False,
    )
```

profile of v0, /device:TPU:0, one launch (start us, length us, event | category | flops | bytes accessed | tf_op | source)
XLA Modules:
  0.0 2426.0 jit_solution(10343772671136535521)
XLA Ops:
  10.1 31.9 %multiply_reduce_fusion.4 = (f32[]{:T(128)}, bf16[12288,768]{1,0:T(8,128)(2,1)}) fusion(f32[12288,768]{1,0:T(8,128)} %param.49), kind=kLoop, calls=%fused_computation.194 | loop fusion | flops 28311552 | bytes 56623108 | tf_op jit(solution)/shard_map/reduce_sum | solution.py:404
  42.0 17.3 gather_fusion
  62.9 43.6 %all-gather.10 = bf16[16,48,4]{1,2,0:T(4,128)(2,1)S(1)} all-gather(bf16[1,48,4]{1,2,0:T(4,128)(2,1)S(1)} %fusion.252), channel_id=1, replica_groups=mesh['section'=2,'dp'=4,'ctx'=4] {'dp','ctx'}, dimensions={0}, use_global_device_ids=true | all-gather | bytes 6528 | tf_op jit(solution)/shard_map/all_gather | solution.py:310
  107.3 82.1 %all-reduce.19.cloned.1.call-done = bf16[2,4,256,768]{3,2,1,0:T(8,128)(2,1)} async-done(((bf16[2,4,256,768]{3,2,1,0:T(8,128)(2,1)}), bf16[2,4,256,768]{3,2,1,0:T(8,128)(2,1)}) %all-reduce.19.cloned.1.call-update) | async-done | bytes 3145744
  198.6 32.7 %all-gather.23.cloned.1.call-done = bf16[1024,768]{1,0:T(8,128)(2,1)} async-done(((bf16[256,768]{1,0:T(8,128)(2,1)}), bf16[1024,768]{1,0:T(8,128)(2,1)}) %all-gather.23.cloned.1.call-update) | async-done | bytes 1572880 | tf_op jit(solution)/shard_map/all_gather | solution.py:76
  237.1 23.2 while.132
  261.4 29.3 %all-gather.27.cloned.1.call-done = bf16[768,768]{1,0:T(8,128)(2,1)} async-done(((bf16[48,768]{1,0:T(8,128)(2,1)}), bf16[768,768]{1,0:T(8,128)(2,1)}) %all-gather.27.cloned.1.call-update) | async-done | bytes 1179664 | tf_op jit(solution)/shard_map/all_gather | solution.py:307
  295.4 28.5 %reduce-scatter.23.cloned.1.call-done = bf16[256,768]{1,0:T(8,128)(2,1)} async-done(((bf16[1024,768]{1,0:T(8,128)(2,1)}), bf16[256,768]{1,0:T(8,128)(2,1)}) %reduce-scatter.23.cloned.1.call-update) | async-done | bytes 393232 | tf_op jit(solution)/shard_map/reduce_scatter | solution.py:176
  325.4 81.8 %all-gather.29.cloned.1.call-done = bf16[768,3072]{1,0:T(8,128)(2,1)} async-done(((bf16[48,3072]{1,0:T(8,128)(2,1)}), bf16[768,3072]{1,0:T(8,128)(2,1)}) %all-gather.29.cloned.1.call-update) | async-done | bytes 4718608 | tf_op jit(solution)/shard_map/all_gather | solution.py:308
  407.3 5.5 fusion.268
  412.8 76.5 %all-gather.31.cloned.1.call-done = bf16[3072,768]{1,0:T(8,128)(2,1)} async-done(((bf16[192,768]{1,0:T(8,128)(2,1)}), bf16[3072,768]{1,0:T(8,128)(2,1)}) %all-gather.31.cloned.1.call-update) | async-done | bytes 4718608 | tf_op jit(solution)/shard_map/all_gather | solution.py:309
  498.6 29.9 %all-gather.33.cloned.1.call-done = bf16[1024,768]{1,0:T(8,128)(2,1)} async-done(((bf16[256,768]{1,0:T(8,128)(2,1)}), bf16[1024,768]{1,0:T(8,128)(2,1)}) %all-gather.33.cloned.1.call-update) | async-done | bytes 1572880 | tf_op jit(solution)/shard_map/all_gather | solution.py:76
  534.4 23.2 while.134
  562.0 30.5 %reduce-scatter.25.cloned.1.call-done = bf16[256,768]{1,0:T(8,128)(2,1)} async-done(((bf16[1024,768]{1,0:T(8,128)(2,1)}), bf16[256,768]{1,0:T(8,128)(2,1)}) %reduce-scatter.25.cloned.1.call-update) | async-done | bytes 393232 | tf_op jit(solution)/shard_map/reduce_scatter | solution.py:176
  609.5 13.3 all_gather.105
  622.8 13.5 all-gather.35.cloned.1.call-done
  641.5 21.4 while.136
  667.2 9.7 fusion.305
  680.4 13.4 all_gather.113
  693.8 14.0 fusion.306
  713.5 5.5 fusion.272
  719.0 5.3 fusion.165
  724.4 13.7 all_gather.121
  738.0 9.7 fusion.307
  749.7 12.5 all-reduce.12
  763.4 10.3 convolution_convert_fusion.14
  773.8 16.5 reduce-scatter.29.cloned.1.call-done
  791.4 6.9 fusion.156
  806.2 28.6 %all-gather.37.cloned.1.call-done = bf16[1024,768]{1,0:T(8,128)(2,1)} async-done(((bf16[256,768]{1,0:T(8,128)(2,1)}), bf16[1024,768]{1,0:T(8,128)(2,1)}) %all-gather.37.cloned.1.call-update) | async-done | bytes 1572880 | tf_op jit(solution)/shard_map/all_gather | solution.py:76
  838.4 41.3 %while.138 = (s32[]{:T(128)}, f32[1024,128]{0,1:T(8,128)}, bf16[2,3,512,64]{2,3,1,0:T(8,128)(2,1)}, s32[2]{0:T(128)}, s32[1,1024]{1,0:T(1,128)S(1)}, /*index=5*/...) while((s32[]{:T(128)}, f32[1024,128]{0,1:T(8,128)}, ...), condition=%wide.region_61.62_spmd.clone, body=%wide.region_59.61_spmd.clone.sunk | while | flops 1028521472 | bytes 54162244 | solution.py:157
  889.8 16.1 reduce-scatter.33.cloned.1.call-done
  905.9 33.7 %reduce-scatter.31.cloned.1.call-done = bf16[256,768]{1,0:T(8,128)(2,1)} async-done(((bf16[1024,768]{1,0:T(8,128)(2,1)}), bf16[256,768]{1,0:T(8,128)(2,1)}) %reduce-scatter.31.cloned.1.call-update) | async-done | bytes 393232 | tf_op jit(solution)/shard_map/reduce_scatter | solution.py:213
  947.3 10.5 convolution_convert_fusion.13
  957.8 20.0 reduce-scatter.35.cloned.1.call-done
  979.0 5.5 fusion.149
  993.2 28.8 %all-gather.39.cloned.1.call-done = bf16[1024,768]{1,0:T(8,128)(2,1)} async-done(((bf16[256,768]{1,0:T(8,128)(2,1)}), bf16[1024,768]{1,0:T(8,128)(2,1)}) %all-gather.39.cloned.1.call-update) | async-done | bytes 1572880 | tf_op jit(solution)/shard_map/all_gather | solution.py:76
  1025.7 42.7 %while.139 = (s32[]{:T(128)}, f32[1024,128]{0,1:T(8,128)}, bf16[2,3,512,64]{2,3,1,0:T(8,128)(2,1)}, s32[2]{0:T(128)}, s32[1,1024]{1,0:T(1,128)S(1)}, /*index=5*/...) while((s32[]{:T(128)}, f32[1024,128]{0,1:T(8,128)}, ...), condition=%wide.region_72.73_spmd.clone, body=%wide.region_70.72_spmd.clone.sunk | while | flops 1028521472 | bytes 53015252 | solution.py:157
  1077.6 16.9 reduce-scatter.39.cloned.1.call-done
  1094.5 34.2 %reduce-scatter.37.cloned.1.call-done = bf16[256,768]{1,0:T(8,128)(2,1)} async-done(((bf16[1024,768]{1,0:T(8,128)(2,1)}), bf16[256,768]{1,0:T(8,128)(2,1)}) %reduce-scatter.37.cloned.1.call-update) | async-done | bytes 393232 | tf_op jit(solution)/shard_map/reduce_scatter | solution.py:213
  1136.5 10.5 convolution_convert_fusion.12
  1147.0 20.0 reduce-scatter.41.cloned.1.call-done
  1168.2 5.5 fusion.142
  1181.4 28.9 %all-gather.41.cloned.1.call-done = bf16[1024,768]{1,0:T(8,128)(2,1)} async-done(((bf16[256,768]{1,0:T(8,128)(2,1)}), bf16[1024,768]{1,0:T(8,128)(2,1)}) %all-gather.41.cloned.1.call-update) | async-done | bytes 1572880 | tf_op jit(solution)/shard_map/all_gather | solution.py:76
  1213.9 42.7 %while.140 = (s32[]{:T(128)}, f32[1024,128]{0,1:T(8,128)}, bf16[2,3,512,64]{2,3,1,0:T(8,128)(2,1)}, s32[2]{0:T(128)}, s32[1,1024]{1,0:T(1,128)S(1)}, /*index=5*/...) while((s32[]{:T(128)}, f32[1024,128]{0,1:T(8,128)}, ...), condition=%wide.region_83.84_spmd.clone, body=%wide.region_81.83_spmd.clone.sunk | while | flops 1028521472 | bytes 53015252 | solution.py:157
  1263.9 18.7 reduce-scatter.45.cloned.1.call-done
  1282.6 34.3 %reduce-scatter.43.cloned.1.call-done = bf16[256,768]{1,0:T(8,128)(2,1)} async-done(((bf16[1024,768]{1,0:T(8,128)(2,1)}), bf16[256,768]{1,0:T(8,128)(2,1)}) %reduce-scatter.43.cloned.1.call-update) | async-done | bytes 393232 | tf_op jit(solution)/shard_map/reduce_scatter | solution.py:213
  1333.1 5.7 multiply_add_fusion.5
  1356.9 6.7 dynamic_update_slice.88
  1376.3 5.5 multiply_add_fusion.2
  1393.9 15.9 fusion.274
  1409.9 15.9 fusion.275
  1425.8 38.9 %multiply_add_fusion.1 = f32[12288,768]{1,0:T(8,128)} fusion(f32[12288,768]{1,0:T(8,128)} %fusion.275, f32[12288,768]{1,0:T(8,128)} %fusion.274, bf16[64,768]{1,0:T(8,128)(2,1)S(1)} %copy-done.97, f32[]{:T(128)S(6)} %convert_element_type.484, f32[]{:T(128)S(6)} %convert_element_type.481, f32[]{:T(128)S(6)} %convert_element_type.478, ...), kind=kOutput, calls=%fused_computation.196 | convolution fusion | flops 1259864064 | bytes 116490832 | tf_op jit(solution)/shard_map/dot_general | solution.py:44
  1464.6 39.5 %scatter_custom_fusion = f32[12288,768]{1,0:T(8,128)} fusion(f32[12288,768]{1,0:T(8,128)} %multiply_add_fusion.1, s32[2048]{0:T(1024)S(1)} %bitcast.650, bf16[2048,768]{1,0:T(8,128)(2,1)} %bitcast.617), kind=kCustom, calls=%fused_computation.201 | custom fusion | flops 3145728 | bytes 40894464 | tf_op jit(solution)/shard_map/scatter-add | solution.py:378
  1504.1 20.5 convert_element_type.531
  1532.4 17.4 all-reduce.13
  1552.1 111.7 %reduce-scatter.49.cloned.1.call-done = f32[48,768]{1,0:T(8,128)} async-done(((f32[768,768]{1,0:T(8,128)}), f32[48,768]{1,0:T(8,128)}) %reduce-scatter.49.cloned.1.call-update) | async-done | bytes 147472 | tf_op jit(solution)/shard_map/reduce_scatter | solution.py:82
  1665.4 172.6 %reduce-scatter.47.cloned.1.call-done = f32[48,896]{1,0:T(8,128)} async-done(((f32[768,896]{1,0:T(8,128)}), f32[48,896]{1,0:T(8,128)}) %reduce-scatter.47.cloned.1.call-update) | async-done | bytes 172048 | tf_op jit(solution)/shard_map/reduce_scatter | solution.py:81
  1840.2 173.8 %reduce-scatter.53.cloned.1.call-done = f32[192,768]{1,0:T(8,128)} async-done(((f32[3072,768]{1,0:T(8,128)}), f32[192,768]{1,0:T(8,128)}) %reduce-scatter.53.cloned.1.call-update) | async-done | bytes 589840 | tf_op jit(solution)/shard_map/reduce_scatter | solution.py:84
  2015.3 175.9 %reduce-scatter.51.cloned.1.call-done = f32[48,3072]{1,0:T(8,128)} async-done(((f32[768,3072]{1,0:T(8,128)}), f32[48,3072]{1,0:T(8,128)}) %reduce-scatter.51.cloned.1.call-update) | async-done | bytes 589840 | tf_op jit(solution)/shard_map/reduce_scatter | solution.py:83
  2194.7 21.0 fusion.132
  2222.3 75.0 %all-reduce.11 = (f32[6272]{0:T(1024)S(1)}, f32[10]{0:T(128)S(1)}) all-reduce(f32[6272]{0:T(1024)S(1)} %constant_dynamic-update-slice_fusion, f32[10]{0:T(128)S(1)} %stack.94), channel_id=1, replica_groups=mesh['section'=2,'dp'=4,'ctx'=4] {'dp','ctx'}, use_global_device_ids=true, to_apply=%region_100.101 | all-reduce | flops 6282 | bytes 50256 | tf_op jit(solution)/shard_map/psum | solution.py:408
  2300.7 20.2 multiply_reduce_fusion.3
  2329.9 36.5 %all-reduce.10 = (f32[5]{0:T(128)S(1)}, f32[4]{0:T(128)S(1)}, f32[4]{0:T(128)S(1)}) all-reduce(f32[5]{0:T(128)S(1)} %stack.100, f32[4]{0:T(128)S(1)} %multiply_reduce_fusion.30, f32[4]{0:T(128)S(1)} %fusion.244), channel_id=1, replica_groups=mesh['section'=2,'dp'=4,'ctx'=4] {'dp','ctx'}, use_global_device_ids=true, to_apply=%region_121.122 | all-reduce | flops 13 | bytes 104 | tf_op jit(solution)/shard_map/psum | solution.py:432
  2374.6 37.9 %multiply_subtract_fusion = f32[12288,768]{1,0:T(8,128)} fusion(f32[12288,768]{1,0:T(8,128)} %param.49, f32[]{:T(128)} %bitcast.106, f32[]{:T(128)} %bitcast.94, f32[12288,768]{1,0:T(8,128)} %get-tuple-element.1297, f32[]{:T(128)} %bitcast.95, f32[768]{0:T(1024)S(1)} %get-tuple-element.1373, f32[12288]{0:T(1024)S(1)} %get-tuple-element.1296), kind=kLoop, calls=%fused_computation.191 | loop fusion | flops 56623104 | bytes 113298448 | tf_op jit(solution)/shard_map/sub | solution.py:440
  (986 shorter events, 426.2 us)
Async XLA Ops:
  8.0 181.4 %all-reduce.19.cloned.1.call-start = ((), (), s32[]{:S(2)}) async-start(), calls=%async_computation.46 | async-start | bytes 6291456
  61.3 131.5 %copy-start.93 = (f32[1,48,768]{2,1,0:T(8,128)S(1)}, f32[1,48,768]{2,1,0:T(8,128)}, u32[]{:S(2)}) copy-start(f32[1,48,768]{2,1,0:T(8,128)} %param.55) | copy-start | bytes 442372
  61.3 132.7 %copy-start.227 = (s32[2,1,4]{2,1,0:T(1,128)S(1)}, s32[2,1,4]{2,1,0:T(1,128)}, u32[]{:S(2)}) copy-start(s32[2,1,4]{2,1,0:T(1,128)} %param.46) | copy-start | bytes 100
  61.3 137.3 %all-gather.25.cloned.1.call-start = ((), (), s32[]{:S(2)}) async-start(), calls=%async_computation.18 | async-start | bytes 1462272 | tf_op jit(solution)/shard_map/all_gather | solution.py:306
  62.9 168.4 %all-gather.23.cloned.1.call-start = ((), (), s32[]{:S(2)}) async-start(), calls=%async_computation.17 | async-start | bytes 1966080 | tf_op jit(solution)/shard_map/all_gather | solution.py:76
  107.3 496.4 %copy-start.113 = (f32[768]{0:T(1024)}, f32[768]{0:T(1024)S(1)}, u32[]{:S(2)}) copy-start(f32[768]{0:T(1024)S(1)} %get-tuple-element.1100) | copy-start | bytes 9220
  107.3 606.1 %copy-start.108 = (f32[768]{0:T(1024)}, f32[768]{0:T(1024)S(1)}, u32[]{:S(2)}) copy-start(f32[768]{0:T(1024)S(1)} %get-tuple-element.1098) | copy-start | bytes 9220
  191.3 412.0 %copy-start.11 = (f32[2,1,256,768]{3,2,1,0:T(8,128)}, f32[2,1,256,768]{3,2,1,0:T(8,128)S(1)}, u32[]{:S(2)}) copy-start(f32[2,1,256,768]{3,2,1,0:T(8,128)S(1)} %dynamic-slice_convert_fusion) | copy-start | bytes 4718596
  192.7 98.1 %all-gather.27.cloned.1.call-start = ((), (), s32[]{:S(2)}) async-start(), calls=%async_computation.19 | async-start | bytes 1253376 | tf_op jit(solution)/shard_map/all_gather | solution.py:307
  193.4 130.5 %reduce-scatter.23.cloned.1.call-start = ((), (), s32[]{:S(2)}) async-start(), calls=%async_computation.20 | async-start | bytes 1966080 | tf_op jit(solution)/shard_map/reduce_scatter | solution.py:176
  261.4 63.7 %copy-start.59 = (bf16[24,8,2,512]{3,1,2,0:T(8,128)(2,1)}, bf16[24,8,2,512]{3,1,2,0:T(8,128)(2,1)S(1)}, u32[]{:S(2)}) copy-start(bf16[24,8,2,512]{3,1,2,0:T(8,128)(2,1)S(1)} %copy.97) | copy-start | bytes 1179652
  293.5 113.8 %all-gather.29.cloned.1.call-start = ((), (), s32[]{:S(2)}) async-start(), calls=%async_computation.21 | async-start | bytes 5013504 | tf_op jit(solution)/shard_map/all_gather | solution.py:308
  294.3 194.9 %all-gather.31.cloned.1.call-start = ((), (), s32[]{:S(2)}) async-start(), calls=%async_computation.22 | async-start | bytes 5013504 | tf_op jit(solution)/shard_map/all_gather | solution.py:309
  295.4 233.1 %all-gather.33.cloned.1.call-start = ((), (), s32[]{:S(2)}) async-start(), calls=%async_computation.23 | async-start | bytes 1966080 | tf_op jit(solution)/shard_map/all_gather | solution.py:76
  325.2 164.1 %copy-start.24 = (f32[256,768]{1,0:T(8,128)}, f32[256,768]{1,0:T(8,128)S(1)}, u32[]{:S(2)}) copy-start(f32[256,768]{1,0:T(8,128)S(1)} %get-tuple-element.1335) | copy-start | bytes 2359300
  325.2 87.6 %copy-start.146 = (f32[256]{0:T(256)}, f32[256]{0:T(256)S(1)}, u32[]{:S(2)}) copy-start(f32[256]{0:T(256)S(1)} %broadcast_multiply_fusion.7) | copy-start | bytes 3076
  325.4 87.3 %copy-start.181 = (f32[256]{0:T(256)}, f32[256]{0:T(256)S(1)}, u32[]{:S(2)}) copy-start(f32[256]{0:T(256)S(1)} %multiply_reduce_fusion.21) | copy-start | bytes 3076
  325.4 87.3 %copy-start.176 = (f32[256]{0:T(256)}, f32[256]{0:T(256)S(1)}, u32[]{:S(2)}) copy-start(f32[256]{0:T(256)S(1)} %fusion.255) | copy-start | bytes 3076
  494.5 2.6 collective-permute-start
  497.3 95.2 %copy-start.13 = (f32[256,768]{1,0:T(8,128)}, f32[256,768]{1,0:T(8,128)S(1)}, u32[]{:S(2)}) copy-start(f32[256,768]{1,0:T(8,128)S(1)} %get-tuple-element.1333) | copy-start | bytes 2359300
  498.6 94.0 %reduce-scatter.25.cloned.1.call-start = ((), (), s32[]{:S(2)}) async-start(), calls=%async_computation.24 | async-start | bytes 1966080 | tf_op jit(solution)/shard_map/reduce_scatter | solution.py:176
  561.6 74.7 %all-gather.35.cloned.1.call-start = ((), (), s32[]{:S(2)}) async-start(), calls=%async_computation.25 | async-start | bytes 1966080 | tf_op jit(solution)/shard_map/all_gather | solution.py:76
  600.1 3.1 collective-permute-start.1
  605.3 106.7 %reduce-scatter.27.cloned.1.call-start = ((), (), s32[]{:S(2)}) async-start(), calls=%async_computation.26 | async-start | bytes 1966080 | tf_op jit(solution)/shard_map/reduce_scatter | solution.py:176
  606.1 341.1 %copy-start.139 = (s32[64]{0:T(128)}, s32[64]{0:T(128)S(1)}, u32[]{:S(2)}) copy-start(s32[64]{0:T(128)S(1)} %sub.416) | copy-start | bytes 772
  606.2 70.9 %copy-start.141 = (s32[64]{0:T(128)}, s32[64]{0:T(128)S(1)}, u32[]{:S(2)}) copy-start(s32[64]{0:T(128)S(1)} %sub.406) | copy-start | bytes 772
  666.9 123.3 %reduce-scatter.29.cloned.1.call-start = ((), (), s32[]{:S(2)}) async-start(), calls=%async_computation.27 | async-start | bytes 122880 | tf_op jit(solution)/shard_map/reduce_scatter | solution.py:264
  713.2 90.3 %copy-start.134 = (f32[256]{0:T(256)}, f32[256]{0:T(256)S(1)}, u32[]{:S(2)}) copy-start(f32[256]{0:T(256)S(1)} %broadcast_multiply_fusion.3) | copy-start | bytes 3076
  713.5 90.0 %copy-start.161 = (f32[256]{0:T(256)}, f32[256]{0:T(256)S(1)}, u32[]{:S(2)}) copy-start(f32[256]{0:T(256)S(1)} %fusion.259) | copy-start | bytes 3076
  773.7 61.1 %all-gather.37.cloned.1.call-start = ((), (), s32[]{:S(2)}) async-start(), calls=%async_computation.28 | async-start | bytes 1966080 | tf_op jit(solution)/shard_map/all_gather | solution.py:76
  805.7 100.2 %reduce-scatter.33.cloned.1.call-start = ((), (), s32[]{:S(2)}) async-start(), calls=%async_computation.30 | async-start | bytes 327680 | tf_op jit(solution)/shard_map/reduce_scatter | solution.py:219
  881.6 58.1 %reduce-scatter.31.cloned.1.call-start = ((), (), s32[]{:S(2)}) async-start(), calls=%async_computation.29 | async-start | bytes 1966080 | tf_op jit(solution)/shard_map/reduce_scatter | solution.py:213
  887.1 90.7 %reduce-scatter.35.cloned.1.call-start = ((), (), s32[]{:S(2)}) async-start(), calls=%async_computation.31 | async-start | bytes 122880 | tf_op jit(solution)/shard_map/reduce_scatter | solution.py:264
  887.3 59.9 %copy-start.163 = (pred[64]{0:T(512)(128)(4,1)}, pred[64]{0:T(512)(128)(4,1)S(1)}, u32[]{:S(2)}) copy-start(pred[64]{0:T(512)(128)(4,1)S(1)} %ge.95) | copy-start | bytes 196
  945.7 32.1 %collective-permute-start.2 = (bf16[256,768]{1,0:T(8,128)(2,1)}, bf16[256,768]{1,0:T(8,128)(2,1)S(1)}, u32[]{:S(2)}, u32[]{:S(2)}) collective-permute-start(bf16[256,768]{1,0:T(8,128)(2,1)} %get-tuple-element.1309), channel_id=1, source_target_pairs={{16,0},{17,1},{18,2},{19,3},{20,4},{21,5},{22,6},{23,7},{24,8},{25... | collective-permute-start | bytes 1179656 | tf_op jit(solution)/shard_map/ppermute | solution.py:24
  957.8 64.3 %all-gather.39.cloned.1.call-start = ((), (), s32[]{:S(2)}) async-start(), calls=%async_computation.32 | async-start | bytes 1966080 | tf_op jit(solution)/shard_map/all_gather | solution.py:76
  993.0 101.5 %reduce-scatter.39.cloned.1.call-start = ((), (), s32[]{:S(2)}) async-start(), calls=%async_computation.34 | async-start | bytes 327680 | tf_op jit(solution)/shard_map/reduce_scatter | solution.py:219
  1070.2 58.4 %reduce-scatter.37.cloned.1.call-start = ((), (), s32[]{:S(2)}) async-start(), calls=%async_computation.33 | async-start | bytes 1966080 | tf_op jit(solution)/shard_map/reduce_scatter | solution.py:213
  1070.3 58.3 %copy-start.14 = (f32[256,768]{1,0:T(8,128)S(1)}, f32[256,768]{1,0:T(8,128)}, u32[]{:S(2)}) copy-start(f32[256,768]{1,0:T(8,128)} %copy-done.13) | copy-start | bytes 2359300
  1070.3 58.3 %copy-start.128 = (f32[256]{0:T(256)S(1)}, f32[256]{0:T(256)}, u32[]{:S(2)}) copy-start(f32[256]{0:T(256)} %copy-done.127) | copy-start | bytes 3076
  1075.7 91.3 %reduce-scatter.41.cloned.1.call-start = ((), (), s32[]{:S(2)}) async-start(), calls=%async_computation.35 | async-start | bytes 122880 | tf_op jit(solution)/shard_map/reduce_scatter | solution.py:264
  1075.9 60.5 %copy-start.167 = (pred[64]{0:T(512)(128)(4,1)}, pred[64]{0:T(512)(128)(4,1)S(1)}, u32[]{:S(2)}) copy-start(pred[64]{0:T(512)(128)(4,1)S(1)} %ge.84) | copy-start | bytes 196
  1134.7 32.3 %collective-permute-start.3 = (bf16[256,768]{1,0:T(8,128)(2,1)}, bf16[256,768]{1,0:T(8,128)(2,1)S(1)}, u32[]{:S(2)}, u32[]{:S(2)}) collective-permute-start(bf16[256,768]{1,0:T(8,128)(2,1)} %get-tuple-element.1303), channel_id=1, source_target_pairs={{16,0},{17,1},{18,2},{19,3},{20,4},{21,5},{22,6},{23,7},{24,8},{25... | collective-permute-start | bytes 1179656 | tf_op jit(solution)/shard_map/ppermute | solution.py:24
  1147.0 63.2 %all-gather.41.cloned.1.call-start = ((), (), s32[]{:S(2)}) async-start(), calls=%async_computation.36 | async-start | bytes 1966080 | tf_op jit(solution)/shard_map/all_gather | solution.py:76
  1181.1 101.5 %reduce-scatter.45.cloned.1.call-start = ((), (), s32[]{:S(2)}) async-start(), calls=%async_computation.38 | async-start | bytes 327680 | tf_op jit(solution)/shard_map/reduce_scatter | solution.py:219
  1258.4 58.6 %reduce-scatter.43.cloned.1.call-start = ((), (), s32[]{:S(2)}) async-start(), calls=%async_computation.37 | async-start | bytes 1966080 | tf_op jit(solution)/shard_map/reduce_scatter | solution.py:213
  1258.4 58.5 %copy-start.12 = (f32[2,1,256,768]{3,2,1,0:T(8,128)S(1)}, f32[2,1,256,768]{3,2,1,0:T(8,128)}, u32[]{:S(2)}) copy-start(f32[2,1,256,768]{3,2,1,0:T(8,128)} %copy-done.11) | copy-start | bytes 4718596
  1258.4 58.5 %copy-start.157 = (f32[256]{0:T(256)S(1)}, f32[256]{0:T(256)}, u32[]{:S(2)}) copy-start(f32[256]{0:T(256)} %copy-done.156) | copy-start | bytes 3076
  1263.9 200.8 %all-gather.43.cloned.1.call-start = ((), (), s32[]{:S(2)}) async-start(), calls=%async_computation.44 | async-start | bytes 3932160 | tf_op jit(solution)/shard_map/all_gather | solution.py:376
  1326.5 224.6 %reduce-scatter.55.cloned.1.call-start = ((), (), s32[]{:S(2)}) async-start(), calls=%async_computation.45 | async-start | bytes 417792
  1332.7 331.1 %reduce-scatter.49.cloned.1.call-start = ((), (), s32[]{:S(2)}) async-start(), calls=%async_computation.41 | async-start | bytes 2506752 | tf_op jit(solution)/shard_map/reduce_scatter | solution.py:82
  1338.9 499.1 %reduce-scatter.47.cloned.1.call-start = ((), (), s32[]{:S(2)}) async-start(), calls=%async_computation.40 | async-start | bytes 2924544 | tf_op jit(solution)/shard_map/reduce_scatter | solution.py:81
  1368.6 645.4 %reduce-scatter.53.cloned.1.call-start = ((), (), s32[]{:S(2)}) async-start(), calls=%async_computation.43 | async-start | bytes 10027008 | tf_op jit(solution)/shard_map/reduce_scatter | solution.py:84
  1381.8 809.3 %reduce-scatter.51.cloned.1.call-start = ((), (), s32[]{:S(2)}) async-start(), calls=%async_computation.42 | async-start | bytes 10027008 | tf_op jit(solution)/shard_map/reduce_scatter | solution.py:83
  1392.0 802.7 %all-reduce.17.cloned.1.call-start = ((), (), s32[]{:S(2)}) async-start(), calls=%async_computation.39 | async-start | bytes 37748736 | tf_op jit(solution)/shard_map/psum | solution.py:382
  1524.7 140.2 %copy-start.237 = (f32[1,48]{1,0:T(1,128)S(1)}, f32[1,48]{1,0:T(1,128)}, u32[]{:S(2)}) copy-start(f32[1,48]{1,0:T(1,128)} %param.56) | copy-start | bytes 580
  1524.7 314.4 %copy-start.235 = (f32[1,48]{1,0:T(1,128)S(1)}, f32[1,48]{1,0:T(1,128)}, u32[]{:S(2)}) copy-start(f32[1,48]{1,0:T(1,128)} %param.53) | copy-start | bytes 580
  1524.7 667.7 %copy-start.236 = (f32[1,48]{1,0:T(1,128)S(1)}, f32[1,48]{1,0:T(1,128)}, u32[]{:S(2)}) copy-start(f32[1,48]{1,0:T(1,128)} %param.59) | copy-start | bytes 580
  1524.7 668.8 %copy-start.234 = (f32[1,192]{1,0:T(1,128)S(1)}, f32[1,192]{1,0:T(1,128)}, u32[]{:S(2)}) copy-start(f32[1,192]{1,0:T(1,128)} %param.62) | copy-start | bytes 2308
  1551.9 822.0 %copy-start.138 = (f32[4,48]{1,0:T(4,128)}, f32[4,48]{1,0:T(4,128)S(1)}, u32[]{:S(2)}) copy-start(f32[4,48]{1,0:T(4,128)S(1)} %copy.95) | copy-start | bytes 2308
  2194.7 105.9 %copy-start.199 = (f32[768]{0:T(1024)S(1)}, f32[768]{0:T(1024)}, u32[]{:S(2)}) copy-start(f32[768]{0:T(1024)} %param.51) | copy-start | bytes 9220
  2216.3 158.3 %copy-start.107 = (f32[12288]{0:T(1024)}, f32[12288]{0:T(1024)S(1)}, u32[]{:S(2)}) copy-start(f32[12288]{0:T(1024)S(1)} %get-tuple-element.1296) | copy-start | bytes 147460
  2299.3 114.2 %copy-start.121 = (f32[3072]{0:T(1024)}, f32[3072]{0:T(1024)S(1)}, u32[]{:S(2)}) copy-start(f32[3072]{0:T(1024)S(1)} %fusion.215) | copy-start | bytes 36868
  2300.6 74.0 %copy-start.124 = (f32[768]{0:T(1024)}, f32[768]{0:T(1024)S(1)}, u32[]{:S(2)}) copy-start(f32[768]{0:T(1024)S(1)} %get-tuple-element.1373) | copy-start | bytes 9220
  (217 other events, 3021.1 us)
Sparse Core Ops, SparseCore 0:
  61.4 127.9 all-reduce.18
  773.8 16.3 reduce-scatter.28
  957.9 19.9 reduce-scatter.34
  1147.1 19.8 reduce-scatter.40
  1326.6 63.8 all-gather.42
  1524.9 257.1 all-reduce.16
Sparse Core Ops, SparseCore 1:
  65.2 133.3 all-gather.24
  200.9 30.4 all-gather.22
  234.5 56.2 all-gather.26
  294.3 29.6 reduce-scatter.22
  327.4 79.8 all-gather.28
  410.7 78.5 all-gather.30
  498.6 29.8 all-gather.32
  561.7 30.8 reduce-scatter.24
  605.4 30.8 all-gather.34
  667.0 30.8 reduce-scatter.26
  805.8 28.9 all-gather.36
  881.6 24.2 reduce-scatter.32
  908.8 30.8 reduce-scatter.30
  993.0 28.9 all-gather.38
  1070.3 24.1 reduce-scatter.38
  1097.8 30.8 reduce-scatter.36
  1181.2 29.0 all-gather.40
  1258.4 24.1 reduce-scatter.44
  1286.0 30.8 reduce-scatter.42
  1333.2 160.1 reduce-scatter.54
  1498.7 165.0 reduce-scatter.48
  1670.0 167.9 reduce-scatter.46
  1844.1 169.8 reduce-scatter.52
  2021.2 169.8 reduce-scatter.50
where the time goes:
time: 2440 us; the launch traced here: 2430 us
  waiting for transfers between devices  1340 us (55%)
  matrix products  380 us (16%)
  other arithmetic  306 us (13%)
  blocking collectives  225 us (9%)
  local copies, waits for them, and re-layouts  99.3 us (4%)
  between operations  39.8 us (2%)
    reduce_scatter x1, waiting for transfers between devices, reduce_grads(): lax.psum_scatter(grads[2], ('dp', 'ctx'), scatter_dimension=0, tiled=True)  176 us
    reduce_scatter x1, waiting for transfers between devices, reduce_grads(): lax.psum_scatter(grads[3], ('dp', 'ctx'), scatter_dimension=0, tiled=True)  174 us
    reduce_scatter x1, waiting for transfers between devices, reduce_grads(): lax.psum_scatter(grads[0], ('dp', 'ctx'), scatter_dimension=0, tiled=True)  173 us
    all_gather x6, waiting for transfers between devices, sequence_rows(): return lax.all_gather(values, 'ctx', axis=0, tiled=True)  162 us
    reduce_scatter x1, waiting for transfers between devices, reduce_grads(): lax.psum_scatter(grads[1], ('dp', 'ctx'), scatter_dimension=0, tiled=True)  112 us
    reduce_scatter x3, waiting for transfers between devices, layer_backward(): lax.psum_scatter(matmul_right(grad_query, query_weight).astype(jnp.bfloat...  102 us
    dot_general x18, matrix products, matmul_left(): lax.dot_general(left, right, (((0,), (0,)), ((), ())), preferred_element_...  98.4 us
    dot_general x18, matrix products, matmul_right(): lax.dot_general(left, right, (((1,), (1,)), ((), ())), preferred_element_...  91.2 us
  transfers between devices with their start and end apart: 34, of which 28 were waited for; matrix products, arithmetic and copies ran while one was open for 13% of the time, Pallas kernels for 0%

commit v1 on v0

v1 whole, which is shorter than its diff:
```python
import jax
import jax.numpy as jnp
from jax import lax
from jax.sharding import PartitionSpec as P

HD = 64
WINDOW = 512
STEP = 10
NORM_EPS = 1e-05
SQUARE_EPS = 1e-30
SCALE_FLOOR = 0.001
RELATIVE_RATE = 0.5
MASKED = -1e30
DECAY = 1.0 - STEP ** (-0.8)
BLOCKS = ("dp", "ctx")


def bfloat(values):
    return values.astype(jnp.bfloat16)


def single(values):
    return values.astype(jnp.float32)


def matmul(left, right):
    return jnp.dot(left, right, preferred_element_type=jnp.float32)


def matmul_left(left, right):
    return lax.dot_general(
        left, right, (((0,), (0,)), ((), ())), preferred_element_type=jnp.float32
    )


def matmul_right(left, right):
    return lax.dot_general(
        left, right, (((1,), (1,)), ((), ())), preferred_element_type=jnp.float32
    )


def layer_norm(values, gain, shift):
    center = values - jnp.mean(values, -1, keepdims=True)
    spread = jnp.mean(center * center, -1, keepdims=True)
    return center * lax.rsqrt(spread + NORM_EPS) * gain + shift


def gelu_tanh(values):
    return jax.nn.gelu(values, approximate=True)


def at(values, index, axis):
    return lax.dynamic_index_in_dim(values, index, axis, keepdims=False)


def swap(values):
    return lax.ppermute(values, "section", [(0, 1), (1, 0)])


def cross(values, axis, bits):
    return lax.ppermute(values, axis, [(i, i ^ bits) for i in range(lax.axis_size(axis))])


def shifted(values, axis, distance):
    devices = range(lax.axis_size(axis))
    return lax.ppermute(
        values, axis, [(i, i + distance) for i in devices if i + distance in devices]
    )


def by_fours():
    return lax.axis_size("dp") == 4 and lax.axis_size("ctx") == 4


def mine_first(mine, theirs):
    first = lax.axis_index("section") == 0
    return jnp.where(first, mine, theirs), jnp.where(first, theirs, mine)


def gather_blocks(part):
    if not by_fours():
        return lax.all_gather(part, BLOCKS, axis=0)
    z, c = lax.axis_index("dp"), lax.axis_index("ctx")
    pieces = [part] + [cross(part, "dp", k) for k in (1, 2, 3)]
    column = jnp.stack(
        [lax.select_n(z, *[pieces[place ^ k] for k in range(4)]) for place in range(4)]
    )
    beside = cross(column, "ctx", 1)
    above = cross(column, "ctx", 2)
    far = jnp.concatenate([cross(above[:2], "ctx", 1), cross(beside[2:], "ctx", 2)])
    whole = jnp.zeros((4, 4) + part.shape, part.dtype)
    for k, piece in enumerate((column, beside, above, far)):
        whole = lax.dynamic_update_slice_in_dim(whole, piece[:, None], c ^ k, 1)
    return whole.reshape((16,) + part.shape)


def scatter_blocks(parts):
    if not by_fours():
        total = lax.psum_scatter(bfloat(parts), BLOCKS, scatter_dimension=0)
        return single(total)
    z, c = lax.axis_index("dp"), lax.axis_index("ctx")
    x, y = c & 1, c >> 1
    grid = parts.reshape((4, 2, 2) + parts.shape[1:])

    def halve(values, axis, bits, index):
        sent = cross(bfloat(at(values, 1 - index, axis)), "ctx", bits)
        return single(at(values, index, axis)) + single(sent)

    near, far = grid[:2], grid[2:]
    near, far = halve(near, 2, 1, x), halve(far, 1, 2, y)
    near, far = halve(near, 1, 2, y), halve(far, 1, 1, x)
    column = jnp.concatenate([near, far])
    low = bfloat(column)
    total = at(column, z, 0)
    for k in (1, 2, 3):
        total = total + single(cross(at(low, z ^ k, 0), "dp", k))
    return total


def scatter_rows(parts):
    if not by_fours():
        return single(lax.psum_scatter(bfloat(parts), "dp", scatter_dimension=0))
    z = lax.axis_index("dp")
    low = bfloat(parts)
    total = single(at(parts, z, 0))
    for k in (1, 2, 3):
        total = total + single(cross(at(low, z ^ k, 0), "dp", k))
    return total


def summed(values, axes):
    if not by_fours():
        return lax.psum(values, axes)
    for axis in axes:
        one, two, three = (cross(values, axis, k) for k in (1, 2, 3))
        values = (values + one) + (two + three)
    return values


def doc_numbers(lengths, places):
    bounds = jnp.cumsum(lengths)
    return jnp.sum((places[:, None] >= bounds[None, :]).astype(jnp.int32), -1)


def allowed_pairs(lengths, query_places, key_places):
    query_docs = doc_numbers(lengths, query_places)
    key_docs = doc_numbers(lengths, key_places)
    return (
        (key_places[None, :] <= query_places[:, None])
        & (key_places[None, :] > query_places[:, None] - WINDOW)
        & (key_places[None, :] >= 0)
        & (key_docs[None, :] == query_docs[:, None])
    )


def earlier_count(local_len):
    return min(lax.axis_size("ctx") - 1, -(-(WINDOW - 1) // local_len))


def key_rows(keyval):
    reach = earlier_count(keyval.shape[0])
    return jnp.concatenate(
        [shifted(keyval, "ctx", k) for k in range(reach, 0, -1)] + [keyval]
    )


def key_rows_back(grads, local_len):
    reach = earlier_count(local_len)
    total = grads[reach * local_len :]
    for k in range(1, reach + 1):
        start = (reach - k) * local_len
        total = total + shifted(grads[start : start + local_len], "ctx", -k)
    return total


def attend(query, keyval, allowed):
    rows, columns = query.shape
    heads = query.reshape(rows, columns // HD, HD)
    keys, values = keyval[:, :HD], keyval[:, HD:]
    scores = jnp.einsum("qhd,kd->hqk", heads, keys, preferred_element_type=jnp.float32)
    scores = jnp.where(allowed[None], scores, MASKED)
    highest = jnp.max(scores, -1, keepdims=True)
    exponents = jnp.exp(scores - highest)
    totals = jnp.sum(exponents, -1, keepdims=True)
    output = jnp.einsum(
        "hqk,kd->qhd", bfloat(exponents / totals), values, preferred_element_type=jnp.float32
    )
    return bfloat(output).reshape(rows, columns), highest + jnp.log(totals)


def attend_back(query, keyval, allowed, logsum, grad_out):
    rows, columns = query.shape
    heads = query.reshape(rows, columns // HD, HD)
    grads = bfloat(grad_out).reshape(rows, columns // HD, HD)
    keys, values = keyval[:, :HD], keyval[:, HD:]
    scores = jnp.einsum("qhd,kd->hqk", heads, keys, preferred_element_type=jnp.float32)
    probs = jnp.exp(jnp.where(allowed[None], scores, MASKED) - logsum)
    grad_probs = jnp.einsum("qhd,kd->hqk", grads, values, preferred_element_type=jnp.float32)
    grad_scores = bfloat(probs * (grad_probs - jnp.sum(probs * grad_probs, -1, keepdims=True)))
    grad_query = jnp.einsum("hqk,kd->qhd", grad_scores, keys, preferred_element_type=jnp.float32)
    grad_keys = jnp.einsum("hqk,qhd->kd", grad_scores, heads, preferred_element_type=jnp.float32)
    grad_values = jnp.einsum(
        "hqk,qhd->kd", bfloat(probs), grads, preferred_element_type=jnp.float32
    )
    grad_query = bfloat(single(bfloat(grad_query.reshape(rows, columns))) * HD ** (-0.5))
    return grad_query, jnp.concatenate([grad_keys, grad_values], 1)


def feed_forward(mixed, weights):
    gains, hidden_in, hidden_out = weights
    rows = mixed.shape[0]
    normed = bfloat(layer_norm(mixed, gains[2], gains[3]))
    both = jnp.concatenate([normed, swap(normed)])
    upper = matmul(both, hidden_in)
    active = bfloat(gelu_tanh(upper))
    partial = matmul(active, hidden_out)
    result = mixed + (partial[:rows] + swap(partial[rows:]))
    return result, (both, upper, active)


def feed_forward_back(grad_result, mixed, kept, weights):
    gains, hidden_in, hidden_out = weights
    both, upper, active = kept
    rows = mixed.shape[0]
    low = bfloat(grad_result)
    grad_both = jnp.concatenate([low, swap(low)])
    grad_hidden_out = matmul_left(active, grad_both)
    _, pull = jax.vjp(gelu_tanh, upper)
    grad_upper = bfloat(pull(matmul_right(grad_both, hidden_out))[0])
    grad_hidden_in = matmul_left(both, grad_upper)
    partial = matmul_right(grad_upper, hidden_in)
    _, pull = jax.vjp(layer_norm, mixed, gains[2], gains[3])
    grad_mixed, grad_gain, grad_shift = pull(partial[:rows] + swap(partial[rows:]))
    return grad_mixed + grad_result, grad_hidden_in, grad_hidden_out, grad_gain, grad_shift


def factored_sums(weight, gradient, row_stat):
    square = gradient * gradient + SQUARE_EPS
    rows_new = DECAY * row_stat + (1.0 - DECAY) * jnp.mean(square, -1)
    columns = jnp.sum(square, 0)
    scaled = jnp.sum(gradient * gradient / rows_new[:, None], 0)
    return rows_new, columns, scaled, jnp.sum(rows_new), jnp.sum(weight * weight)


def factored_new(weight, gradient, rows_new, col_stat, sums, row_count):
    columns, scaled, rows_sum, weight_sum = sums
    entries = row_count * weight.shape[1]
    cols_new = DECAY * col_stat + (1.0 - DECAY) * columns / row_count
    mean_rows = rows_sum / row_count
    update_sum = mean_rows * jnp.sum(scaled / cols_new)
    clipping = jnp.maximum(1.0, jnp.sqrt(update_sum / entries))
    size = jnp.maximum(SCALE_FLOOR, jnp.sqrt(weight_sum / entries))
    update = gradient * lax.rsqrt(rows_new[:, None] * cols_new[None, :] / mean_rows)
    return cols_new, weight - RELATIVE_RATE * size * (update / clipping)


def body(
    token_ids,
    doc_lengths,
    picks,
    targets,
    table,
    table_rows,
    table_cols,
    attention_in,
    attention_in_rows,
    attention_in_cols,
    attention_out,
    attention_out_rows,
    attention_out_cols,
    hidden_in,
    hidden_in_rows,
    hidden_in_cols,
    hidden_out,
    hidden_out_rows,
    hidden_out_cols,
    gains,
    gains_stat,
):
    section = lax.axis_index("section")
    first = section == 0
    z, c = lax.axis_index("dp"), lax.axis_index("ctx")
    z_count, c_count = lax.axis_size("dp"), lax.axis_size("ctx")
    blocks = z_count * c_count
    model = table.shape[1]
    part = attention_in.shape[1]
    units = hidden_in.shape[2]
    half = units // (2 * blocks)
    wide = attention_in.shape[2]
    local_len = token_ids.shape[2]
    slots = picks.shape[2]
    vocab_here = table.shape[0]
    vocab_base = z * vocab_here

    low_in = bfloat(attention_in[0])
    low_out = jnp.concatenate(
        [bfloat(attention_out[0]), bfloat(gains[0]).T, jnp.zeros((part, wide - model - 4), jnp.bfloat16)], 1
    )
    attention_parts = mine_first(
        jnp.where(first, low_in, low_out), swap(jnp.where(first, low_out, low_in))
    )
    low_up = bfloat(hidden_in[0]).reshape(part, blocks, 2, half)
    low_down = bfloat(hidden_out[0])

    def unit_half(index):
        up = at(low_up, index, 2).reshape(part, -1, model)
        down = lax.dynamic_slice_in_dim(low_down, index * half, half, 0)
        return jnp.concatenate([up[:, k] for k in range(up.shape[1])] + [down])

    hidden_parts = mine_first(unit_half(section), swap(unit_half(1 - section)))

    def layer_weights(layer):
        mine = gather_blocks(attention_parts[layer]).reshape(model, wide)
        weight_in, weight_out = mine_first(mine, swap(mine))
        gain_rows = single(weight_out[:, model : model + 4]).T
        hidden = gather_blocks(hidden_parts[layer])
        ups = units // 2 // model
        up = jnp.concatenate(
            [hidden[:, k * part : (k + 1) * part].reshape(model, model) for k in range(ups)], 1
        )
        down = hidden[:, ups * part :].reshape(units // 2, model)
        return weight_in, weight_out[:, :model], gain_rows, up, down

    my_ids = at(token_ids, section, 0) - vocab_base
    inside = (my_ids >= 0) & (my_ids < vocab_here)
    looked = jnp.take(table, jnp.clip(my_ids, 0, vocab_here - 1), axis=0)
    start = scatter_rows(jnp.where(inside[..., None], bfloat(looked), 0))

    all_targets = lax.all_gather(targets, "ctx").transpose(1, 2, 0, 3).reshape(-1)
    all_ids = lax.all_gather(token_ids, "ctx").transpose(1, 2, 0, 3).reshape(-1)
    lengths = at(doc_lengths, section, 0)[0]
    my_picks = at(picks, section, 0)[0]

    places = c * local_len + jnp.arange(local_len, dtype=jnp.int32)
    reach = earlier_count(local_len)
    key_places = (c - reach) * local_len + jnp.arange((reach + 1) * local_len, dtype=jnp.int32)
    allowed = allowed_pairs(lengths, places, key_places)
    pick_allowed = allowed_pairs(lengths, c * local_len + jnp.maximum(my_picks, 0), key_places)
    onehot = (my_picks[:, None] == jnp.arange(local_len, dtype=jnp.int32)[None, :]).astype(
        jnp.bfloat16
    )

    in0, out0, gains0, up0, down0 = layer_weights(0)
    normed0 = bfloat(layer_norm(start, gains0[0], gains0[1]))
    mixed_in = matmul(normed0, in0)
    query0 = bfloat(mixed_in[:, :model] * HD ** (-0.5))
    keyval0 = key_rows(bfloat(mixed_in[:, model:]))
    attended0, logsum0 = attend(query0, keyval0, allowed)
    mixed0 = start + matmul(attended0, out0)
    result0, hidden0 = feed_forward(mixed0, (gains0, up0, down0))

    in1, out1, gains1, up1, down1 = layer_weights(1)
    inputs1_low = bfloat(result0)
    inputs1 = single(inputs1_low)
    normed1 = bfloat(layer_norm(inputs1, gains1[0], gains1[1]))
    keyval1 = key_rows(bfloat(matmul(normed1, in1[:, model:])))
    picked_normed = bfloat(matmul(onehot, normed1))
    picked = matmul(onehot, inputs1_low)
    query1 = bfloat(matmul(picked_normed, in1[:, :model]) * HD ** (-0.5))
    attended1, logsum1 = attend(query1, keyval1, pick_allowed)
    mixed1 = picked + matmul(attended1, out1)
    result1, hidden1 = feed_forward(mixed1, (gains1, up1, down1))

    chosen_mine = gather_blocks(bfloat(result1)).reshape(-1, model)
    chosen = jnp.concatenate(mine_first(chosen_mine, swap(chosen_mine)))
    table_low = bfloat(table)
    logits = matmul_right(chosen, table_low)
    local_target = all_targets - vocab_base
    matches = local_target[:, None] == jnp.arange(vocab_here, dtype=jnp.int32)[None, :]
    highest = jnp.max(logits, -1)
    totals = jnp.sum(jnp.exp(logits - highest[:, None]), -1)
    target_logit = jnp.sum(jnp.where(matches, logits, 0.0), -1)
    stats = jnp.stack([highest, totals, target_logit])

    def combine(one, two):
        top = jnp.maximum(one[0], two[0])
        both = one[1] * jnp.exp(one[0] - top) + two[1] * jnp.exp(two[0] - top)
        return jnp.stack([top, both, one[2] + two[2]])

    if by_fours():
        one, two, three = (cross(stats, "dp", k) for k in (1, 2, 3))
        stats = combine(combine(stats, one), combine(two, three))
    else:
        stats = lax.scan(
            lambda total, share: (combine(total, share), None),
            jnp.stack([jnp.full_like(highest, MASKED), 0 * highest, 0 * highest]),
            lax.all_gather(stats, "dp"),
        )[0]
    logsum = stats[0] + jnp.log(stats[1])
    live = all_targets >= 0
    loss_sum = jnp.sum(jnp.where(live, logsum - stats[2], 0.0))
    loss_count = jnp.sum(single(live))
    grad_logits = bfloat(
        jnp.where(live[:, None], jnp.exp(logits - logsum[:, None]) - single(matches), 0.0)
    )
    grad_head = matmul_left(grad_logits, chosen)
    mine_logits = at(
        at(grad_logits.reshape(2, z_count, c_count, slots, vocab_here), section, 0), c, 1
    )
    grad_chosen = matmul(mine_logits.reshape(-1, vocab_here), table_low)
    grad_result1 = scatter_rows(grad_chosen.reshape(z_count, slots, model))

    grad_mixed1, grad_up1, grad_down1, grad_gain2, grad_shift2 = feed_forward_back(
        grad_result1, mixed1, hidden1, (gains1, up1, down1)
    )
    grad_low = bfloat(grad_mixed1)
    grad_out1 = matmul_left(attended1, grad_low)
    grad_query, grad_keyval = attend_back(
        query1, keyval1, pick_allowed, logsum1, matmul_right(grad_low, out1)
    )
    grad_keyval = bfloat(key_rows_back(grad_keyval, local_len))
    grad_in1 = jnp.concatenate(
        [matmul_left(picked_normed, grad_query), matmul_left(normed1, grad_keyval)], 1
    )
    spread = jnp.dot(
        single(onehot).T,
        jnp.concatenate([matmul_right(grad_query, in1[:, :model]), grad_mixed1], 1),
        precision=lax.Precision.HIGHEST,
    )
    grad_normed = matmul_right(grad_keyval, in1[:, model:]) + spread[:, :model]
    _, pull = jax.vjp(layer_norm, inputs1, gains1[0], gains1[1])
    grad_inputs1, grad_gain1, grad_shift1 = pull(grad_normed)
    grad_result0 = single(bfloat(grad_inputs1 + spread[:, model:]))
    grad_gains1 = jnp.stack([grad_gain1, grad_shift1, grad_gain2, grad_shift2])

    grad_mixed0, grad_up0, grad_down0, grad_gain2, grad_shift2 = feed_forward_back(
        grad_result0, mixed0, hidden0, (gains0, up0, down0)
    )
    grad_low = bfloat(grad_mixed0)
    grad_out0 = matmul_left(attended0, grad_low)
    grad_query, grad_keyval = attend_back(
        query0, keyval0, allowed, logsum0, matmul_right(grad_low, out0)
    )
    grad_keyval = bfloat(key_rows_back(grad_keyval, local_len))
    grad_mixed_in = jnp.concatenate([grad_query, grad_keyval], 1)
    grad_in0 = matmul_left(normed0, grad_mixed_in)
    _, pull = jax.vjp(layer_norm, start, gains0[0], gains0[1])
    grad_start, grad_gain1, grad_shift1 = pull(matmul_right(grad_mixed_in, in0))
    grad_start = bfloat(grad_start + grad_mixed0)
    grad_gains0 = jnp.stack([grad_gain1, grad_shift1, grad_gain2, grad_shift2])

    if 2 * blocks * local_len <= 2 * vocab_here:
        mine = gather_blocks(grad_start).reshape(-1, model)
        looked_grads = jnp.concatenate(mine_first(mine, swap(mine)))
        local = all_ids - vocab_base
        local = jnp.where((local >= 0) & (local < vocab_here), local, vocab_here)
        lookup_grad = jax.ops.segment_sum(single(looked_grads), local, num_segments=vocab_here)
    else:
        column = lax.all_gather(grad_start, "dp").reshape(-1, model)
        local = jnp.where(inside, my_ids, vocab_here).reshape(-1)
        lookup_grad = jax.ops.segment_sum(single(column), local, num_segments=vocab_here)
        lookup_grad = single(lax.psum(bfloat(lookup_grad), ("section", "ctx")))
    grad_table = grad_head + lookup_grad

    def weight_grads(grad_in, grad_out, grad_gains, grad_up, grad_down):
        grad_out = jnp.concatenate(
            [grad_out, grad_gains.T, jnp.zeros((model, wide - model - 4), jnp.float32)], 1
        )
        kept = jnp.where(first, grad_in, grad_out)
        sent = swap(bfloat(jnp.where(first, grad_out, grad_in)))
        attention = scatter_blocks((kept + single(sent)).reshape(blocks, part, wide))
        ups = grad_up.shape[1] // model
        packed = jnp.concatenate(
            [grad_up[:, k * model : (k + 1) * model].reshape(blocks, part, model) for k in range(ups)]
            + [grad_down.reshape(blocks, half, model)],
            1,
        )
        return attention, scatter_blocks(packed)

    grads1 = weight_grads(grad_in1, grad_out1, grad_gains1, grad_up1, grad_down1)
    grads0 = weight_grads(grad_in0, grad_out0, grad_gains0, grad_up0, grad_down0)
    owned, other = [], []
    for one, two in zip(grads0, grads1):
        owned.append(jnp.where(first, one, two))
        other.append(swap(jnp.where(first, two, one)))
    shard_in, shard_out = mine_first(owned[0], other[0])
    shard_gains = shard_out[:, model : model + 4].T
    shard_out = shard_out[:, :model]
    halves = jnp.stack(mine_first(owned[1], other[1]))
    ups = units // 2 // model
    shard_up = halves[:, : ups * part].reshape(2, ups, part, model).transpose(2, 0, 1, 3)
    shard_up = shard_up.reshape(part, 2, blocks, half).transpose(0, 2, 1, 3).reshape(part, units)
    shard_down = halves[:, ups * part :].reshape(2 * half, model)

    entries = [
        (table, grad_table, table_rows, table_cols, vocab_here * z_count),
        (attention_in[0], shard_in, attention_in_rows[0], attention_in_cols[0], model),
        (attention_out[0], shard_out, attention_out_rows[0], attention_out_cols[0], model),
        (hidden_in[0], shard_up, hidden_in_rows[0], hidden_in_cols[0], model),
        (hidden_out[0], shard_down, hidden_out_rows[0], hidden_out_cols[0], units),
    ]
    sums = [factored_sums(*entry[:3]) for entry in entries]
    gain_weight = gains[0]
    gain_stat_new = DECAY * gains_stat[0] + (1.0 - DECAY) * (shard_gains * shard_gains + SQUARE_EPS)
    gain_update = shard_gains * lax.rsqrt(gain_stat_new)

    def packed(group):
        flat = [item.reshape(-1) for item in group]
        return jnp.concatenate(flat), [item.shape for item in group]

    def unpacked(flat, shapes):
        items, start = [], 0
        for shape in shapes:
            size = 1
            for length in shape:
                size *= length
            items.append(flat[start : start + size].reshape(shape))
            start += size
        return items

    table_group, table_shapes = packed(sums[0][1:])
    layer_group, layer_shapes = packed(
        [item for entry in sums[1:] for item in entry[1:]]
        + [jnp.sum(gain_weight * gain_weight, -1), jnp.sum(gain_update * gain_update, -1)]
    )
    everything = summed(jnp.concatenate([table_group, layer_group]), ("dp",))
    table_sums = unpacked(everything[: table_group.shape[0]], table_shapes)
    layer_sums = unpacked(summed(everything[table_group.shape[0] :], ("ctx",)), layer_shapes)
    groups = [table_sums] + [layer_sums[4 * k : 4 * k + 4] for k in range(4)]
    gain_squares, gain_update_sums = layer_sums[16:]
    outs = []
    for (weight, gradient, _, col_stat, row_count), own, group in zip(entries, sums, groups):
        cols_new, new = factored_new(weight, gradient, own[0], col_stat, group, row_count)
        outs.append((gradient, own[0], cols_new, new))
    gain_clipping = jnp.maximum(1.0, jnp.sqrt(gain_update_sums / model))
    gain_size = jnp.maximum(SCALE_FLOOR, jnp.sqrt(gain_squares / model))
    gain_new = gain_weight - RELATIVE_RATE * gain_size[:, None] * (
        gain_update / gain_clipping[:, None]
    )
    layered = [item[None] for out in outs[1:] for item in out]
    return (
        loss_sum,
        loss_count,
        *outs[0],
        *layered,
        shard_gains[None],
        gain_stat_new[None],
        gain_new[None],
    )


def solution(mesh):
    rows = P("section", BLOCKS, None)
    row = P("section", BLOCKS)
    shared = P("section", None)
    side = P("section", None, BLOCKS)
    matrix_in = (rows, row, shared)
    matrix_out = (rows, row, shared, rows)
    placed = (
        P(None, None, "ctx"),
        P(None, "dp", None),
        P(None, "dp", "ctx"),
        P(None, None, "ctx"),
        P("dp", None),
        P("dp"),
        P(),
        *(matrix_in * 4),
        side,
        side,
    )
    return jax.shard_map(
        body,
        mesh=mesh,
        in_specs=placed,
        out_specs=(
            P(),
            P(),
            P("dp", None),
            P("dp"),
            P(),
            P("dp", None),
            *(matrix_out * 4),
            side,
            side,
            side,
        ),
        check_vma=False,
    )
```

time: 2440 us -> 1010 us (0.41)
  waiting for transfers between devices: 1340 us -> 225 us
  matrix products: 380 us -> 135 us
  blocking collectives: 225 us -> 17 us
  starting transfers between devices: 9.73 us -> 161 us
  local copies, waits for them, and re-layouts: 99.3 us -> 135 us
  between operations: 39.8 us -> 14.7 us
    reduce_scatter x16 -> x0, waiting for transfers between devices: 903 us -> none  [the longest x1 176 us: reduce_grads(): lax.psum_scatter(grads[2], ('dp', 'ctx'), scatter_dimension=0, tiled=True)]
    all_gather x11 -> x0, waiting for transfers between devices: 353 us -> none  [the longest x6 162 us: sequence_rows(): return lax.all_gather(values, 'ctx', axis=0, tiled=True)]
    ppermute x4 -> x111, waiting for transfers between devices: 2.62 us -> 225 us  [the longest x85 208 us: cross(): lax.ppermute(values, axis, [(i, i ^ bits) for i in range(lax.axis_size(ax...]
    ppermute x4 -> x111, starting transfers between devices: 6.27 us -> 161 us  [the longest x85 140 us: cross(): lax.ppermute(values, axis, [(i, i ^ bits) for i in range(lax.axis_size(ax...]
    psum x3 -> x0, blocking collectives: 129 us -> none  [the longest x1 75 us: body(): lax.psum((jnp.concatenate(column_parts), jnp.stack(scalar_parts), jnp.sum...]
    unnamed x32 -> x0, waiting for transfers between devices: 82.6 us -> none
    dot_general x45 -> x13, matrix products: 107 us -> 28.1 us  [the longest x2 8.39 us: attend_back(): jnp.einsum('qhd,kd->hqk', grads, values, preferred_element_type=jnp.float32)]
    all_gather x4 -> x2, blocking collectives: 84 us -> 17 us  [the longest x1 8.65 us: body(): lax.all_gather(targets, 'ctx').transpose(1, 2, 0, 3).reshape(-1)]
  transfers between devices with their start and end apart: 34 -> 111, of which waited for: 28 -> 38; matrix products, arithmetic and copies ran while one was open for 13% -> 34% of each run, Pallas kernels for 0% -> 0%
where the time goes in v1:
time: 1010 us; the launch traced here: 998 us
  other arithmetic  311 us (31%)
  waiting for transfers between devices  225 us (22%)
  starting transfers between devices  161 us (16%)
  local copies, waits for them, and re-layouts  135 us (13%)
  matrix products  135 us (13%)
  blocking collectives  17 us (2%)
  between operations  14.7 us (1%)
    ppermute x85, waiting for transfers between devices, cross(): lax.ppermute(values, axis, [(i, i ^ bits) for i in range(lax.axis_size(ax...  208 us
    ppermute x85, starting transfers between devices, cross(): lax.ppermute(values, axis, [(i, i ^ bits) for i in range(lax.axis_size(ax...  140 us
    scatter-add x1, other arithmetic, body(): jax.ops.segment_sum(single(looked_grads), local, num_segments=vocab_here)  82.8 us
    dot_general x10, matrix products, matmul_right(): lax.dot_general(left, right, (((1,), (1,)), ((), ())), preferred_element_...  41.9 us
    dot_general x10, matrix products, matmul_left(): lax.dot_general(left, right, (((0,), (0,)), ((), ())), preferred_element_...  41.3 us
    sub x3, other arithmetic, factored_new(): return (cols_new, weight - RELATIVE_RATE * size * (update / clipping))  40 us
    convert_element_type x19, other arithmetic, bfloat(): return values.astype(jnp.bfloat16)  35.1 us
    unnamed x410, local copies, waits for them, and re-layouts  25.3 us
  transfers between devices with their start and end apart: 111, of which 38 were waited for; matrix products, arithmetic and copies ran while one was open for 34% of the time, Pallas kernels for 0%

profile of v1, /device:TPU:0, one launch (start us, length us, event | category | flops | bytes accessed | tf_op | source)
XLA Modules:
  0.0 998.1 jit_solution(11355434718900468496)
XLA Ops:
  12.5 16.2 %gather_fusion = bf16[1024,768]{1,0:T(8,128)(2,1)S(1)} fusion(f32[12288,768]{1,0:T(8,128)} %param.25, s32[1024]{0:T(1024)S(1)} %broadcast_clamp_fusion), kind=kCustom, calls=%fused_computation | custom fusion | bytes 3149824 | tf_op jit(solution)/shard_map/jit(_take)/gather | solution.py:326
  30.3 3.0 collective-permute-start
  33.4 17.4 %multiply_reduce_fusion = f32[]{:T(128)} fusion(f32[12288,768]{1,0:T(8,128)} %param.25), kind=kLoop, calls=%fused_computation.3 | loop fusion | flops 18874368 | bytes 37748740 | tf_op jit(solution)/shard_map/reduce_sum | solution.py:242
  50.8 8.3 all-gather.1
  60.7 8.7 all-gather
  85.8 3.2 collective-permute-start.24
  91.3 12.8 %collective-permute-done.25 = bf16[48,896]{1,0:T(8,128)(2,1)S(1)} collective-permute-done((bf16[48,896]{1,0:T(8,128)(2,1)S(1)}, bf16[48,896]{1,0:T(8,128)(2,1)S(1)}, u32[]{:S(2)}, u32[]{:S(2)}) %collective-permute-start.25) | collective-permute-done | bytes 86048 | tf_op jit(solution)/shard_map/ppermute | solution.py:61
  111.8 19.5 %collective-permute-done.1 = bf16[256,768]{1,0:T(8,128)(2,1)S(1)} collective-permute-done((bf16[256,768]{1,0:T(8,128)(2,1)}, bf16[256,768]{1,0:T(8,128)(2,1)S(1)}, u32[]{:S(2)}, u32[]{:S(2)}) %collective-permute-start.1) | collective-permute-done | bytes 393248 | tf_op jit(solution)/shard_map/ppermute | solution.py:61
  131.3 4.2 collective-permute-start.37
  137.8 3.9 collective-permute-start.18
  143.4 16.0 %collective-permute-start.16 = (bf16[192,768]{1,0:T(8,128)(2,1)S(1)}, bf16[192,768]{1,0:T(8,128)(2,1)S(1)}, u32[]{:S(2)}, u32[]{:S(2)}) collective-permute-start(bf16[192,768]{1,0:T(8,128)(2,1)S(1)} %get-tuple-element.292), channel_id=1, source_target_pairs={{0,4},{4,0},{8,12},{12,8},{1,5},{5,1},{9,13},{13,9},{2,6},{6,2},{1... | collective-permute-start | bytes 884744 | tf_op jit(solution)/shard_map/ppermute | solution.py:61
  159.5 5.9 collective-permute-done.36
  168.3 5.6 collective-permute-done.17
  177.7 34.2 %collective-permute-done.9 = bf16[2,48,896]{2,1,0:T(8,128)(2,1)S(1)} collective-permute-done((bf16[2,48,896]{2,1,0:T(8,128)(2,1)S(1)}, bf16[2,48,896]{2,1,0:T(8,128)(2,1)S(1)}, u32[]{:S(2)}, u32[]{:S(2)}) %collective-permute-start.9) | collective-permute-done | bytes 172064 | tf_op jit(solution)/shard_map/ppermute | solution.py:61
  220.4 2.7 collective-permute-done.29
  236.7 3.9 collective-permute-start.13
  243.1 3.7 collective-permute-start.22
  250.4 3.0 copy-done.3
  272.6 2.9 collective-permute-start.33
  275.5 3.7 collective-permute-start.32
  285.8 2.7 slice.516
  290.9 2.6 collective-permute-start.45
  293.5 3.2 collective-permute-start.44
  323.4 25.7 %fusion.288 = (f32[512]{0:T(512)S(1)}, f32[512,12288]{1,0:T(8,128)}) fusion(f32[12288,768]{1,0:T(8,128)} %param.25, bf16[256,768]{1,0:T(8,128)(2,1)} %get-tuple-element.286, bf16[256,768]{1,0:T(8,128)(2,1)} %get-tuple-element.285), kind=kOutput, calls=%fused_computation.683 | convolution fusion | flops 9680977920 | bytes 63703040 | tf_op jit(solution)/shard_map/dot_general | solution.py:37
  349.1 12.1 %exponential_reduce_fusion = (f32[512]{0:T(512)S(1)}, f32[512]{0:T(512)S(1)}) fusion(f32[512,12288]{1,0:T(8,128)} %get-tuple-element.363, f32[512]{0:T(512)S(1)} %get-tuple-element.362, s32[512]{0:T(512)} %sub.316), kind=kLoop, calls=%fused_computation.12 | loop fusion | flops 31456256 | bytes 25174016 | tf_op jit(solution)/shard_map/reduce_sum | solution.py:371
  375.1 17.3 %select_convert_fusion = bf16[512,12288]{1,0:T(8,128)(2,1)} fusion(f32[512,12288]{1,0:T(8,128)} %get-tuple-element.363, f32[512]{0:T(512)S(1)} %log_add_fusion.2, s32[512]{0:T(512)} %sub.316, pred[512]{0:T(512)(128)(4,1)} %ge.129), kind=kLoop, calls=%fused_computation.9 | loop fusion | flops 37748736 | bytes 37753344 | tf_op jit(solution)/shard_map/convert_element_type | solution.py:19
  392.3 16.3 %fusion.289 = (bf16[4,16,768]{2,1,0:T(8,128)(2,1)}, f32[4,16,768]{2,1,0:T(8,128)}) fusion(f32[12288,768]{1,0:T(8,128)} %param.25, bf16[2,4,4,16,12288]{4,3,2,1,0:T(8,128)(2,1)} %bitcast.662, s32[]{:T(128)S(6)} %select_n.835, s32[]{:T(128)S(6)} %select_n.836), kind=kOutput, calls=%fused_computation.684 | convolution fusion | flops 1217445888 | bytes 39616520 | tf_op jit(solution)/shard_map/dot_general | solution.py:27
  413.5 21.6 %fusion.104 = f32[12288,768]{1,0:T(8,128)} fusion(bf16[512,12288]{1,0:T(8,128)(2,1)} %select_convert_fusion, bf16[256,768]{1,0:T(8,128)(2,1)} %get-tuple-element.286, bf16[256,768]{1,0:T(8,128)(2,1)} %get-tuple-element.285), kind=kOutput, calls=%fused_computation.251 | convolution fusion | flops 9665249280 | bytes 51118080 | tf_op jit(solution)/shard_map/dot_general | solution.py:31
  454.4 3.0 fusion.169
  457.5 7.7 pad_maximum_fusion.1
  465.1 4.7 fusion.273
  490.9 11.2 %collective-permute-done.59 = f32[256,128]{0,1:T(8,128)S(1)} collective-permute-done((f32[256,128]{0,1:T(8,128)S(1)}, f32[256,128]{0,1:T(8,128)S(1)}, u32[]{:S(2)}, u32[]{:S(2)}) %collective-permute-start.59) | collective-permute-done | bytes 131104 | tf_op jit(solution)/shard_map/ppermute | solution.py:66
  512.4 5.9 fusion.26
  522.9 2.6 fusion.276
  526.1 5.0 fusion.102
  531.1 8.4 pad_maximum_fusion
  539.5 4.9 fusion.274
  545.7 3.8 collective-permute-start.90
  565.5 6.4 fusion.48
  571.9 8.0 fusion.7
  579.9 10.7 %fusion.9 = bf16[12,256,768]{1,2,0:T(8,128)(2,1)} fusion(f32[768,256,12]{1,0,2:T(8,128)} %get-tuple-element.371, f32[768,256,12]{1,0,2:T(8,128)} %copy-done.3, f32[12,256]{1,0:T(8,128)} %get-tuple-element.370, f32[12,256]{1,0:T(8,128)} %log_add_fusion, pred[256,768]{0,1:T(8,128)(4,1)S(1)} %copy-done.34), kind=kLoop, calls=%fused_computation.24 | loop fusion | flops 11796480 | bytes 23814144 | tf_op jit(solution)/shard_map/convert_element_type | solution.py:19
  590.7 4.0 convolution_bitcast_fusion.2
  624.5 2.7 collective-permute-start.93
  628.7 18.4 %collective-permute-done.66 = bf16[256,768]{1,0:T(8,128)(2,1)S(1)} collective-permute-done((bf16[256,768]{1,0:T(8,128)(2,1)S(1)}, bf16[256,768]{1,0:T(8,128)(2,1)S(1)}, u32[]{:S(2)}, u32[]{:S(2)}) %collective-permute-start.66) | collective-permute-done | bytes 393248 | tf_op jit(solution)/shard_map/ppermute | solution.py:61
  652.0 11.0 %collective-permute-done.101 = bf16[192,768]{1,0:T(8,128)(2,1)S(1)} collective-permute-done((bf16[192,768]{1,0:T(8,128)(2,1)S(1)}, bf16[192,768]{1,0:T(8,128)(2,1)S(1)}, u32[]{:S(2)}, u32[]{:S(2)}) %collective-permute-start.101) | collective-permute-done | bytes 294944 | tf_op jit(solution)/shard_map/ppermute | solution.py:61
  665.2 25.0 %collective-permute-done.102 = bf16[192,768]{1,0:T(8,128)(2,1)S(1)} collective-permute-done((bf16[192,768]{1,0:T(8,128)(2,1)S(1)}, bf16[192,768]{1,0:T(8,128)(2,1)S(1)}, u32[]{:S(2)}, u32[]{:S(2)}) %collective-permute-start.102) | collective-permute-done | bytes 294944 | tf_op jit(solution)/shard_map/ppermute | solution.py:61
  691.2 3.4 collective-permute-start.68
  694.7 7.6 collective-permute-done.95
  706.2 3.4 collective-permute-start.82
  710.0 19.9 %collective-permute-done.68 = bf16[4,256,768]{2,1,0:T(8,128)(2,1)S(1)} collective-permute-done((bf16[4,256,768]{2,1,0:T(8,128)(2,1)S(1)}, bf16[4,256,768]{2,1,0:T(8,128)(2,1)S(1)}, u32[]{:S(2)}, u32[]{:S(2)}) %collective-permute-start.68) | collective-permute-done | bytes 1572896 | tf_op jit(solution)/shard_map/ppermute | solution.py:61
  732.2 5.1 collective-permute-done.82
  739.8 3.2 copy.499
  743.0 10.5 %collective-permute-done.71 = bf16[2,256,768]{2,1,0:T(8,128)(2,1)S(1)} collective-permute-done((bf16[2,256,768]{2,1,0:T(8,128)(2,1)S(1)}, bf16[2,256,768]{2,1,0:T(8,128)(2,1)S(1)}, u32[]{:S(2)}, u32[]{:S(2)}) %collective-permute-start.71) | collective-permute-done | bytes 786464 | tf_op jit(solution)/shard_map/ppermute | solution.py:61
  753.4 2.9 collective-permute-done.70
  769.7 7.6 collective-permute-start.86
  780.6 2.9 collective-permute-start.78
  796.4 10.3 %broadcast_select_fusion.1 = (bf16[4096,768]{1,0:T(8,128)(2,1)}, bf16[4096,768]{1,0:T(8,128)(2,1)}) fusion(bf16[4096,768]{1,0:T(8,128)(2,1)} %collective-permute-done.72, pred[]{:T(512)S(6)} %eq.36, bf16[4,4,256,768]{3,2,1,0:T(8,128)(2,1)} %fusion.30), kind=kLoop, calls=%fused_computation.35 | loop fusion | flops 6291456 | bytes 25165824 | tf_op jit(solution)/shard_map/jit(_where)/select_n | solution.py:77
  806.7 82.8 %scatter_custom_fusion = f32[12288,768]{1,0:T(8,128)} fusion(f32[12288,768]{1,0:T(8,128)} %fusion.104, s32[8192]{0:T(1024)} %bitcast.738, bf16[4096,768]{1,0:T(8,128)(2,1)} %get-tuple-element.242, bf16[]{:T(256)} %constant.501, bf16[4096,768]{1,0:T(8,128)(2,1)} %get-tuple-element.241), kind=kCustom, calls=%fused_computation.7 | custom fusion | flops 31457280 | bytes 50332160 | tf_op jit(solution)/shard_map/scatter-add | solution.py:447
  889.6 15.8 %add_reduce_fusion.1 = f32[12288]{0:T(1024)S(1)} fusion(f32[12288,768]{1,0:T(8,128)} %scatter_custom_fusion), kind=kLoop, calls=%fused_computation.6 | loop fusion | flops 28299264 | bytes 37797888 | tf_op jit(solution)/shard_map/reduce_sum | solution.py:239
  906.0 6.3 copy-done.2
  912.3 8.4 divide_reduce_fusion
  920.7 6.4 concatenate.131
  928.8 2.8 collective-permute-start.105
  942.2 38.0 %multiply_subtract_fusion = f32[12288,768]{1,0:T(8,128)} fusion(f32[12288,768]{1,0:T(8,128)} %param.25, f32[12288,768]{1,0:T(8,128)} %scatter_custom_fusion, f32[]{:T(128)S(6)} %max.93, f32[]{:T(128)} %bitcast.234, f32[768]{0:T(1024)S(1)} %get-tuple-element.203, f32[]{:T(128)} %bitcast.233, f32[12288]{0:T(1024)S(1)} %get-tuple-element.223), kind=kLoop, calls=%fused_computation.2 | loop fusion | flops 56623104 | bytes 113298448 | tf_op jit(solution)/shard_map/sub | solution.py:254
  (941 shorter events, 322.3 us)
Async XLA Ops:
  4.1 69.9 %collective-permute-start.3 = (bf16[48,896]{1,0:T(8,128)(2,1)}, bf16[48,896]{1,0:T(8,128)(2,1)S(1)}, u32[]{:S(2)}, u32[]{:S(2)}) collective-permute-start(bf16[48,896]{1,0:T(8,128)(2,1)} %broadcast_select_fusion.20), channel_id=1, source_target_pairs={{0,16},{16,0},{1,17},{17,1},{2,18},{18,2},{3,19},{19,3},{4,20},{20... | collective-permute-start | bytes 258056 | tf_op jit(solution)/shard_map/ppermute | solution.py:57
  12.3 94.8 %collective-permute-start.15 = (bf16[192,768]{1,0:T(8,128)(2,1)}, bf16[192,768]{1,0:T(8,128)(2,1)}, u32[]{:S(2)}, u32[]{:S(2)}) collective-permute-start(bf16[192,768]{1,0:T(8,128)(2,1)} %pad_maximum_fusion.34), channel_id=1, source_target_pairs={{0,16},{16,0},{1,17},{17,1},{2,18},{18,2},{3,19},{19,3},{4,20},{20... | collective-permute-start | bytes 884744 | tf_op jit(solution)/shard_map/ppermute | solution.py:57
  30.3 79.3 %collective-permute-start = (bf16[256,768]{1,0:T(8,128)(2,1)}, bf16[256,768]{1,0:T(8,128)(2,1)S(1)}, u32[]{:S(2)}, u32[]{:S(2)}) collective-permute-start(bf16[256,768]{1,0:T(8,128)(2,1)} %get-tuple-element.267), channel_id=1, source_target_pairs={{0,4},{4,0},{8,12},{12,8},{1,5},{5,1},{9,13},{13,9},{2,6},{6,2},{1... | collective-permute-start | bytes 1179656 | tf_op jit(solution)/shard_map/ppermute | solution.py:61
  85.5 18.6 %collective-permute-start.25 = (bf16[48,896]{1,0:T(8,128)(2,1)S(1)}, bf16[48,896]{1,0:T(8,128)(2,1)S(1)}, u32[]{:S(2)}, u32[]{:S(2)}) collective-permute-start(bf16[48,896]{1,0:T(8,128)(2,1)S(1)} %get-tuple-element.234), channel_id=1, source_target_pairs={{0,8},{4,12},{8,0},{12,4},{1,9},{5,13},{9,1},{13,5},{2,10},{6,14},... | collective-permute-start | bytes 258056 | tf_op jit(solution)/shard_map/ppermute | solution.py:61
  85.8 18.4 %collective-permute-start.24 = (bf16[48,896]{1,0:T(8,128)(2,1)S(1)}, bf16[48,896]{1,0:T(8,128)(2,1)S(1)}, u32[]{:S(2)}, u32[]{:S(2)}) collective-permute-start(bf16[48,896]{1,0:T(8,128)(2,1)S(1)} %get-tuple-element.234), channel_id=1, source_target_pairs={{0,4},{4,0},{8,12},{12,8},{1,5},{5,1},{9,13},{13,9},{2,6},{6,2},{1... | collective-permute-start | bytes 258056 | tf_op jit(solution)/shard_map/ppermute | solution.py:61
  89.2 21.1 %collective-permute-start.2 = (bf16[256,768]{1,0:T(8,128)(2,1)}, bf16[256,768]{1,0:T(8,128)(2,1)S(1)}, u32[]{:S(2)}, u32[]{:S(2)}) collective-permute-start(bf16[256,768]{1,0:T(8,128)(2,1)} %get-tuple-element.268), channel_id=1, source_target_pairs={{0,12},{4,8},{8,4},{12,0},{1,13},{5,9},{9,5},{13,1},{2,14},{6,10},... | collective-permute-start | bytes 1179656 | tf_op jit(solution)/shard_map/ppermute | solution.py:61
  104.1 27.2 %collective-permute-start.1 = (bf16[256,768]{1,0:T(8,128)(2,1)}, bf16[256,768]{1,0:T(8,128)(2,1)S(1)}, u32[]{:S(2)}, u32[]{:S(2)}) collective-permute-start(bf16[256,768]{1,0:T(8,128)(2,1)} %get-tuple-element.269), channel_id=1, source_target_pairs={{0,8},{4,12},{8,0},{12,4},{1,9},{5,13},{9,1},{13,5},{2,10},{6,14},... | collective-permute-start | bytes 1179656 | tf_op jit(solution)/shard_map/ppermute | solution.py:61
  104.3 32.8 %collective-permute-start.7 = (bf16[4,48,896]{2,1,0:T(8,128)(2,1)S(1)}, bf16[4,48,896]{2,1,0:T(8,128)(2,1)S(1)}, u32[]{:S(2)}, u32[]{:S(2)}) collective-permute-start(bf16[4,48,896]{2,1,0:T(8,128)(2,1)S(1)} %pad_maximum_fusion.29), channel_id=1, source_target_pairs={{0,1},{1,0},{2,3},{3,2},{4,5},{5,4},{6,7},{7,6},{8,9},{9,8},{10,11... | collective-permute-start | bytes 1032200 | tf_op jit(solution)/shard_map/ppermute | solution.py:61
  107.1 30.0 %collective-permute-start.8 = (bf16[4,48,896]{2,1,0:T(8,128)(2,1)S(1)}, bf16[4,48,896]{2,1,0:T(8,128)(2,1)S(1)}, u32[]{:S(2)}, u32[]{:S(2)}) collective-permute-start(bf16[4,48,896]{2,1,0:T(8,128)(2,1)S(1)} %pad_maximum_fusion.29), channel_id=1, source_target_pairs={{0,2},{1,3},{2,0},{3,1},{4,6},{5,7},{6,4},{7,5},{8,10},{9,11},{10,... | collective-permute-start | bytes 1032200 | tf_op jit(solution)/shard_map/ppermute | solution.py:61
  109.7 28.0 %collective-permute-start.27 = (bf16[4,48,896]{2,1,0:T(8,128)(2,1)S(1)}, bf16[4,48,896]{2,1,0:T(8,128)(2,1)S(1)}, u32[]{:S(2)}, u32[]{:S(2)}) collective-permute-start(bf16[4,48,896]{2,1,0:T(8,128)(2,1)S(1)} %pad_maximum_fusion.30), channel_id=1, source_target_pairs={{0,1},{1,0},{2,3},{3,2},{4,5},{5,4},{6,7},{7,6},{8,9},{9,8},{10,11... | collective-permute-start | bytes 1032200 | tf_op jit(solution)/shard_map/ppermute | solution.py:61
  110.3 31.4 %collective-permute-start.28 = (bf16[4,48,896]{2,1,0:T(8,128)(2,1)S(1)}, bf16[4,48,896]{2,1,0:T(8,128)(2,1)S(1)}, u32[]{:S(2)}, u32[]{:S(2)}) collective-permute-start(bf16[4,48,896]{2,1,0:T(8,128)(2,1)S(1)} %pad_maximum_fusion.30), channel_id=1, source_target_pairs={{0,2},{1,3},{2,0},{3,1},{4,6},{5,7},{6,4},{7,5},{8,10},{9,11},{10,... | collective-permute-start | bytes 1032200 | tf_op jit(solution)/shard_map/ppermute | solution.py:61
  137.1 28.3 %collective-permute-start.36 = (bf16[192,768]{1,0:T(8,128)(2,1)S(1)}, bf16[192,768]{1,0:T(8,128)(2,1)S(1)}, u32[]{:S(2)}, u32[]{:S(2)}) collective-permute-start(bf16[192,768]{1,0:T(8,128)(2,1)S(1)} %get-tuple-element.291), channel_id=1, source_target_pairs={{0,8},{4,12},{8,0},{12,4},{1,9},{5,13},{9,1},{13,5},{2,10},{6,14},... | collective-permute-start | bytes 884744 | tf_op jit(solution)/shard_map/ppermute | solution.py:61
  137.1 28.7 %collective-permute-start.35 = (bf16[192,768]{1,0:T(8,128)(2,1)S(1)}, bf16[192,768]{1,0:T(8,128)(2,1)S(1)}, u32[]{:S(2)}, u32[]{:S(2)}) collective-permute-start(bf16[192,768]{1,0:T(8,128)(2,1)S(1)} %get-tuple-element.291), channel_id=1, source_target_pairs={{0,4},{4,0},{8,12},{12,8},{1,5},{5,1},{9,13},{13,9},{2,6},{6,2},{1... | collective-permute-start | bytes 884744 | tf_op jit(solution)/shard_map/ppermute | solution.py:61
  137.8 30.0 %collective-permute-start.18 = (bf16[192,768]{1,0:T(8,128)(2,1)S(1)}, bf16[192,768]{1,0:T(8,128)(2,1)S(1)}, u32[]{:S(2)}, u32[]{:S(2)}) collective-permute-start(bf16[192,768]{1,0:T(8,128)(2,1)S(1)} %get-tuple-element.292), channel_id=1, source_target_pairs={{0,12},{4,8},{8,4},{12,0},{1,13},{5,9},{9,5},{13,1},{2,14},{6,10},... | collective-permute-start | bytes 884744 | tf_op jit(solution)/shard_map/ppermute | solution.py:61
  141.7 32.2 %collective-permute-start.17 = (bf16[192,768]{1,0:T(8,128)(2,1)S(1)}, bf16[192,768]{1,0:T(8,128)(2,1)S(1)}, u32[]{:S(2)}, u32[]{:S(2)}) collective-permute-start(bf16[192,768]{1,0:T(8,128)(2,1)S(1)} %get-tuple-element.292), channel_id=1, source_target_pairs={{0,8},{4,12},{8,0},{12,4},{1,9},{5,13},{9,1},{13,5},{2,10},{6,14},... | collective-permute-start | bytes 884744 | tf_op jit(solution)/shard_map/ppermute | solution.py:61
  143.4 30.5 %collective-permute-start.16 = (bf16[192,768]{1,0:T(8,128)(2,1)S(1)}, bf16[192,768]{1,0:T(8,128)(2,1)S(1)}, u32[]{:S(2)}, u32[]{:S(2)}) collective-permute-start(bf16[192,768]{1,0:T(8,128)(2,1)S(1)} %get-tuple-element.292), channel_id=1, source_target_pairs={{0,4},{4,0},{8,12},{12,8},{1,5},{5,1},{9,13},{13,9},{2,6},{6,2},{1... | collective-permute-start | bytes 884744 | tf_op jit(solution)/shard_map/ppermute | solution.py:61
  166.2 58.3 %collective-permute-start.38 = (bf16[4,192,768]{2,1,0:T(8,128)(2,1)S(1)}, bf16[4,192,768]{2,1,0:T(8,128)(2,1)S(1)}, u32[]{:S(2)}, u32[]{:S(2)}) collective-permute-start(bf16[4,192,768]{2,1,0:T(8,128)(2,1)S(1)} %pad_maximum_fusion.13), channel_id=1, source_target_pairs={{0,1},{1,0},{2,3},{3,2},{4,5},{5,4},{6,7},{7,6},{8,9},{9,8},{10,11... | collective-permute-start | bytes 3538952 | tf_op jit(solution)/shard_map/ppermute | solution.py:61
  167.7 58.1 %collective-permute-start.39 = (bf16[4,192,768]{2,1,0:T(8,128)(2,1)S(1)}, bf16[4,192,768]{2,1,0:T(8,128)(2,1)S(1)}, u32[]{:S(2)}, u32[]{:S(2)}) collective-permute-start(bf16[4,192,768]{2,1,0:T(8,128)(2,1)S(1)} %pad_maximum_fusion.13), channel_id=1, source_target_pairs={{0,2},{1,3},{2,0},{3,1},{4,6},{5,7},{6,4},{7,5},{8,10},{9,11},{10,... | collective-permute-start | bytes 3538952 | tf_op jit(solution)/shard_map/ppermute | solution.py:61
  174.2 54.5 %collective-permute-start.19 = (bf16[4,192,768]{2,1,0:T(8,128)(2,1)S(1)}, bf16[4,192,768]{2,1,0:T(8,128)(2,1)S(1)}, u32[]{:S(2)}, u32[]{:S(2)}) collective-permute-start(bf16[4,192,768]{2,1,0:T(8,128)(2,1)S(1)} %pad_maximum_fusion.12), channel_id=1, source_target_pairs={{0,1},{1,0},{2,3},{3,2},{4,5},{5,4},{6,7},{7,6},{8,9},{9,8},{10,11... | collective-permute-start | bytes 3538952 | tf_op jit(solution)/shard_map/ppermute | solution.py:61
  174.8 54.7 %collective-permute-start.20 = (bf16[4,192,768]{2,1,0:T(8,128)(2,1)S(1)}, bf16[4,192,768]{2,1,0:T(8,128)(2,1)S(1)}, u32[]{:S(2)}, u32[]{:S(2)}) collective-permute-start(bf16[4,192,768]{2,1,0:T(8,128)(2,1)S(1)} %pad_maximum_fusion.12), channel_id=1, source_target_pairs={{0,2},{1,3},{2,0},{3,1},{4,6},{5,7},{6,4},{7,5},{8,10},{9,11},{10,... | collective-permute-start | bytes 3538952 | tf_op jit(solution)/shard_map/ppermute | solution.py:61
  177.1 34.8 %collective-permute-start.9 = (bf16[2,48,896]{2,1,0:T(8,128)(2,1)S(1)}, bf16[2,48,896]{2,1,0:T(8,128)(2,1)S(1)}, u32[]{:S(2)}, u32[]{:S(2)}) collective-permute-start(bf16[2,48,896]{2,1,0:T(8,128)(2,1)S(1)} %slice.477), channel_id=1, source_target_pairs={{0,1},{1,0},{2,3},{3,2},{4,5},{5,4},{6,7},{7,6},{8,9},{9,8},{10,11... | collective-permute-start | bytes 516104 | tf_op jit(solution)/shard_map/ppermute | solution.py:61
  224.4 40.7 %collective-permute-start.31 = (bf16[768,896]{1,0:T(8,128)(2,1)}, bf16[768,896]{1,0:T(8,128)(2,1)}, u32[]{:S(2)}, u32[]{:S(2)}) collective-permute-start(bf16[768,896]{1,0:T(8,128)(2,1)} %bitcast.66), channel_id=1, source_target_pairs={{0,16},{16,0},{1,17},{17,1},{2,18},{18,2},{3,19},{19,3},{4,20},{20... | collective-permute-start | bytes 4128776 | tf_op jit(solution)/shard_map/ppermute | solution.py:57
  225.8 42.9 %collective-permute-start.41 = (bf16[2,192,768]{2,1,0:T(8,128)(2,1)}, bf16[2,192,768]{2,1,0:T(8,128)(2,1)}, u32[]{:S(2)}, u32[]{:S(2)}) collective-permute-start(bf16[2,192,768]{2,1,0:T(8,128)(2,1)} %slice.513), channel_id=1, source_target_pairs={{0,2},{1,3},{2,0},{3,1},{4,6},{5,7},{6,4},{7,5},{8,10},{9,11},{10,... | collective-permute-start | bytes 1769480 | tf_op jit(solution)/shard_map/ppermute | solution.py:61
  228.7 40.0 %collective-permute-start.40 = (bf16[2,192,768]{2,1,0:T(8,128)(2,1)}, bf16[2,192,768]{2,1,0:T(8,128)(2,1)}, u32[]{:S(2)}, u32[]{:S(2)}) collective-permute-start(bf16[2,192,768]{2,1,0:T(8,128)(2,1)} %slice.512), channel_id=1, source_target_pairs={{0,1},{1,0},{2,3},{3,2},{4,5},{5,4},{6,7},{7,6},{8,9},{9,8},{10,11... | collective-permute-start | bytes 1769480 | tf_op jit(solution)/shard_map/ppermute | solution.py:61
  243.1 15.9 %collective-permute-start.22 = (bf16[2,192,768]{2,1,0:T(8,128)(2,1)}, bf16[2,192,768]{2,1,0:T(8,128)(2,1)S(1)}, u32[]{:S(2)}, u32[]{:S(2)}) collective-permute-start(bf16[2,192,768]{2,1,0:T(8,128)(2,1)} %slice.494), channel_id=1, source_target_pairs={{0,2},{1,3},{2,0},{3,1},{4,6},{5,7},{6,4},{7,5},{8,10},{9,11},{10,... | collective-permute-start | bytes 1769480 | tf_op jit(solution)/shard_map/ppermute | solution.py:61
  410.1 36.0 %collective-permute-start.54 = (bf16[16,768]{1,0:T(8,128)(2,1)}, bf16[16,768]{1,0:T(8,128)(2,1)}, u32[]{:S(2)}, u32[]{:S(2)}) collective-permute-start(bf16[16,768]{1,0:T(8,128)(2,1)} %get-tuple-element.322), channel_id=1, source_target_pairs={{0,4},{4,0},{8,12},{12,8},{1,5},{5,1},{9,13},{13,9},{2,6},{6,2},{1... | collective-permute-start | bytes 73736 | tf_op jit(solution)/shard_map/ppermute | solution.py:61
  410.9 35.2 %collective-permute-start.56 = (bf16[16,768]{1,0:T(8,128)(2,1)}, bf16[16,768]{1,0:T(8,128)(2,1)}, u32[]{:S(2)}, u32[]{:S(2)}) collective-permute-start(bf16[16,768]{1,0:T(8,128)(2,1)} %get-tuple-element.323), channel_id=1, source_target_pairs={{0,12},{4,8},{8,4},{12,0},{1,13},{5,9},{9,5},{13,1},{2,14},{6,10},... | collective-permute-start | bytes 73736 | tf_op jit(solution)/shard_map/ppermute | solution.py:61
  412.2 33.9 %collective-permute-start.55 = (bf16[16,768]{1,0:T(8,128)(2,1)}, bf16[16,768]{1,0:T(8,128)(2,1)}, u32[]{:S(2)}, u32[]{:S(2)}) collective-permute-start(bf16[16,768]{1,0:T(8,128)(2,1)} %get-tuple-element.324), channel_id=1, source_target_pairs={{0,8},{4,12},{8,0},{12,4},{1,9},{5,13},{9,1},{13,5},{2,10},{6,14},... | collective-permute-start | bytes 73736 | tf_op jit(solution)/shard_map/ppermute | solution.py:61
  451.3 23.4 %collective-permute-start.58 = (f32[16,768]{1,0:T(8,128)S(1)}, f32[16,768]{1,0:T(8,128)S(1)}, u32[]{:S(2)}, u32[]{:S(2)}) collective-permute-start(f32[16,768]{1,0:T(8,128)S(1)} %slice.531), channel_id=1, source_target_pairs={{0,16},{16,0},{1,17},{17,1},{2,18},{18,2},{3,19},{19,3},{4,20},{20... | collective-permute-start | bytes 147464 | tf_op jit(solution)/shard_map/ppermute | solution.py:57
  471.1 79.5 %collective-permute-start.97 = (bf16[2,2,192,768]{3,2,0,1:T(8,128)(2,1)}, bf16[2,2,192,768]{3,2,0,1:T(8,128)(2,1)}, u32[]{:S(2)}, u32[]{:S(2)}) collective-permute-start(bf16[2,2,192,768]{3,2,0,1:T(8,128)(2,1)} %fusion.44), channel_id=1, source_target_pairs={{0,1},{1,0},{2,3},{3,2},{4,5},{5,4},{6,7},{7,6},{8,9},{9,8},{10,11... | collective-permute-start | bytes 3538952 | tf_op jit(solution)/shard_map/ppermute | solution.py:61
  473.0 83.0 %collective-permute-start.99 = (bf16[2,2,192,768]{3,2,0,1:T(8,128)(2,1)}, bf16[2,2,192,768]{3,2,0,1:T(8,128)(2,1)}, u32[]{:S(2)}, u32[]{:S(2)}) collective-permute-start(bf16[2,2,192,768]{3,2,0,1:T(8,128)(2,1)} %fusion.45), channel_id=1, source_target_pairs={{0,2},{1,3},{2,0},{3,1},{4,6},{5,7},{6,4},{7,5},{8,10},{9,11},{10,... | collective-permute-start | bytes 3538952 | tf_op jit(solution)/shard_map/ppermute | solution.py:61
  486.4 15.7 %collective-permute-start.59 = (f32[256,128]{0,1:T(8,128)S(1)}, f32[256,128]{0,1:T(8,128)S(1)}, u32[]{:S(2)}, u32[]{:S(2)}) collective-permute-start(f32[256,128]{0,1:T(8,128)S(1)} %get-tuple-element.296), channel_id=1, source_target_pairs={{1,0},{2,1},{3,2},{5,4},{6,5},{7,6},{9,8},{10,9},{11,10},{13,12},{... | collective-permute-start | bytes 393224 | tf_op jit(solution)/shard_map/ppermute | solution.py:66
  487.7 16.2 %collective-permute-start.60 = (f32[256,128]{0,1:T(8,128)S(1)}, f32[256,128]{0,1:T(8,128)S(1)}, u32[]{:S(2)}, u32[]{:S(2)}) collective-permute-start(f32[256,128]{0,1:T(8,128)S(1)} %get-tuple-element.297), channel_id=1, source_target_pairs={{2,0},{3,1},{6,4},{7,5},{10,8},{11,9},{14,12},{15,13},{18,16},{19,... | collective-permute-start | bytes 393224 | tf_op jit(solution)/shard_map/ppermute | solution.py:66
  520.9 37.7 %collective-permute-start.62 = (f32[256,768]{1,0:T(8,128)S(1)}, f32[256,768]{1,0:T(8,128)}, u32[]{:S(2)}, u32[]{:S(2)}) collective-permute-start(f32[256,768]{1,0:T(8,128)S(1)} %slice.539), channel_id=1, source_target_pairs={{0,16},{16,0},{1,17},{17,1},{2,18},{18,2},{3,19},{19,3},{4,20},{20... | collective-permute-start | bytes 2359304 | tf_op jit(solution)/shard_map/ppermute | solution.py:57
  545.7 70.3 %collective-permute-start.90 = (bf16[2,2,192,768]{3,2,0,1:T(8,128)(2,1)}, bf16[2,2,192,768]{3,2,0,1:T(8,128)(2,1)}, u32[]{:S(2)}, u32[]{:S(2)}) collective-permute-start(bf16[2,2,192,768]{3,2,0,1:T(8,128)(2,1)} %fusion.42), channel_id=1, source_target_pairs={{0,1},{1,0},{2,3},{3,2},{4,5},{5,4},{6,7},{7,6},{8,9},{9,8},{10,11... | collective-permute-start | bytes 3538952 | tf_op jit(solution)/shard_map/ppermute | solution.py:61
  550.6 68.1 %collective-permute-start.92 = (bf16[2,2,192,768]{3,2,0,1:T(8,128)(2,1)}, bf16[2,2,192,768]{3,2,0,1:T(8,128)(2,1)}, u32[]{:S(2)}, u32[]{:S(2)}) collective-permute-start(bf16[2,2,192,768]{3,2,0,1:T(8,128)(2,1)} %fusion.43), channel_id=1, source_target_pairs={{0,2},{1,3},{2,0},{3,1},{4,6},{5,7},{6,4},{7,5},{8,10},{9,11},{10,... | collective-permute-start | bytes 3538952 | tf_op jit(solution)/shard_map/ppermute | solution.py:61
  553.9 67.8 %collective-permute-start.98 = (bf16[2,192,768]{2,1,0:T(8,128)(2,1)}, bf16[2,192,768]{2,1,0:T(8,128)(2,1)}, u32[]{:S(2)}, u32[]{:S(2)}) collective-permute-start(bf16[2,192,768]{2,1,0:T(8,128)(2,1)} %fusion.86), channel_id=1, source_target_pairs={{0,2},{1,3},{2,0},{3,1},{4,6},{5,7},{6,4},{7,5},{8,10},{9,11},{10,... | collective-permute-start | bytes 1769480 | tf_op jit(solution)/shard_map/ppermute | solution.py:61
  602.9 21.5 %collective-permute-start.100 = (bf16[2,192,768]{2,1,0:T(8,128)(2,1)}, bf16[2,192,768]{2,1,0:T(8,128)(2,1)}, u32[]{:S(2)}, u32[]{:S(2)}) collective-permute-start(bf16[2,192,768]{2,1,0:T(8,128)(2,1)} %fusion.87), channel_id=1, source_target_pairs={{0,1},{1,0},{2,3},{3,2},{4,5},{5,4},{6,7},{7,6},{8,9},{9,8},{10,11... | collective-permute-start | bytes 1769480 | tf_op jit(solution)/shard_map/ppermute | solution.py:61
  611.2 17.5 %collective-permute-start.67 = (bf16[256,768]{1,0:T(8,128)(2,1)S(1)}, bf16[256,768]{1,0:T(8,128)(2,1)S(1)}, u32[]{:S(2)}, u32[]{:S(2)}) collective-permute-start(bf16[256,768]{1,0:T(8,128)(2,1)S(1)} %add_convert_fusion), channel_id=1, source_target_pairs={{0,12},{4,8},{8,4},{12,0},{1,13},{5,9},{9,5},{13,1},{2,14},{6,10},... | collective-permute-start | bytes 1179656 | tf_op jit(solution)/shard_map/ppermute | solution.py:61
  616.0 31.1 %collective-permute-start.66 = (bf16[256,768]{1,0:T(8,128)(2,1)S(1)}, bf16[256,768]{1,0:T(8,128)(2,1)S(1)}, u32[]{:S(2)}, u32[]{:S(2)}) collective-permute-start(bf16[256,768]{1,0:T(8,128)(2,1)S(1)} %add_convert_fusion), channel_id=1, source_target_pairs={{0,8},{4,12},{8,0},{12,4},{1,9},{5,13},{9,1},{13,5},{2,10},{6,14},... | collective-permute-start | bytes 1179656 | tf_op jit(solution)/shard_map/ppermute | solution.py:61
  618.8 28.3 %collective-permute-start.65 = (bf16[256,768]{1,0:T(8,128)(2,1)S(1)}, bf16[256,768]{1,0:T(8,128)(2,1)S(1)}, u32[]{:S(2)}, u32[]{:S(2)}) collective-permute-start(bf16[256,768]{1,0:T(8,128)(2,1)S(1)} %add_convert_fusion), channel_id=1, source_target_pairs={{0,4},{4,0},{8,12},{12,8},{1,5},{5,1},{9,13},{13,9},{2,6},{6,2},{1... | collective-permute-start | bytes 1179656 | tf_op jit(solution)/shard_map/ppermute | solution.py:61
  621.8 25.5 %collective-permute-start.91 = (bf16[2,192,768]{2,1,0:T(8,128)(2,1)S(1)}, bf16[2,192,768]{2,1,0:T(8,128)(2,1)S(1)}, u32[]{:S(2)}, u32[]{:S(2)}) collective-permute-start(bf16[2,192,768]{2,1,0:T(8,128)(2,1)S(1)} %fusion.84), channel_id=1, source_target_pairs={{0,2},{1,3},{2,0},{3,1},{4,6},{5,7},{6,4},{7,5},{8,10},{9,11},{10,... | collective-permute-start | bytes 1769480 | tf_op jit(solution)/shard_map/ppermute | solution.py:61
  624.5 24.2 %collective-permute-start.93 = (bf16[2,192,768]{2,1,0:T(8,128)(2,1)S(1)}, bf16[2,192,768]{2,1,0:T(8,128)(2,1)S(1)}, u32[]{:S(2)}, u32[]{:S(2)}) collective-permute-start(bf16[2,192,768]{2,1,0:T(8,128)(2,1)S(1)} %fusion.85), channel_id=1, source_target_pairs={{0,1},{1,0},{2,3},{3,2},{4,5},{5,4},{6,7},{7,6},{8,9},{9,8},{10,11... | collective-permute-start | bytes 1769480 | tf_op jit(solution)/shard_map/ppermute | solution.py:61
  628.6 76.1 %collective-permute-start.81 = (bf16[768,896]{1,0:T(8,128)(2,1)S(1)}, bf16[768,896]{1,0:T(8,128)(2,1)S(1)}, u32[]{:S(2)}, u32[]{:S(2)}) collective-permute-start(bf16[768,896]{1,0:T(8,128)(2,1)S(1)} %get-tuple-element.349), channel_id=1, source_target_pairs={{0,16},{16,0},{1,17},{17,1},{2,18},{18,2},{3,19},{19,3},{4,20},{20... | collective-permute-start | bytes 4128776 | tf_op jit(solution)/shard_map/ppermute | solution.py:57
  647.1 57.7 %collective-permute-start.73 = (bf16[768,896]{1,0:T(8,128)(2,1)S(1)}, bf16[768,896]{1,0:T(8,128)(2,1)S(1)}, u32[]{:S(2)}, u32[]{:S(2)}) collective-permute-start(bf16[768,896]{1,0:T(8,128)(2,1)S(1)} %get-tuple-element.350), channel_id=1, source_target_pairs={{0,16},{16,0},{1,17},{17,1},{2,18},{18,2},{3,19},{19,3},{4,20},{20... | collective-permute-start | bytes 4128776 | tf_op jit(solution)/shard_map/ppermute | solution.py:57
  647.1 16.0 %collective-permute-start.101 = (bf16[192,768]{1,0:T(8,128)(2,1)S(1)}, bf16[192,768]{1,0:T(8,128)(2,1)S(1)}, u32[]{:S(2)}, u32[]{:S(2)}) collective-permute-start(bf16[192,768]{1,0:T(8,128)(2,1)S(1)} %get-tuple-element.271), channel_id=1, source_target_pairs={{0,4},{4,0},{8,12},{12,8},{1,5},{5,1},{9,13},{13,9},{2,6},{6,2},{1... | collective-permute-start | bytes 884744 | tf_op jit(solution)/shard_map/ppermute | solution.py:61
  647.3 15.8 %collective-permute-start.103 = (bf16[192,768]{1,0:T(8,128)(2,1)S(1)}, bf16[192,768]{1,0:T(8,128)(2,1)S(1)}, u32[]{:S(2)}, u32[]{:S(2)}) collective-permute-start(bf16[192,768]{1,0:T(8,128)(2,1)S(1)} %get-tuple-element.272), channel_id=1, source_target_pairs={{0,12},{4,8},{8,4},{12,0},{1,13},{5,9},{9,5},{13,1},{2,14},{6,10},... | collective-permute-start | bytes 884744 | tf_op jit(solution)/shard_map/ppermute | solution.py:61
  648.7 41.5 %collective-permute-start.102 = (bf16[192,768]{1,0:T(8,128)(2,1)S(1)}, bf16[192,768]{1,0:T(8,128)(2,1)S(1)}, u32[]{:S(2)}, u32[]{:S(2)}) collective-permute-start(bf16[192,768]{1,0:T(8,128)(2,1)S(1)} %get-tuple-element.273), channel_id=1, source_target_pairs={{0,8},{4,12},{8,0},{12,4},{1,9},{5,13},{9,1},{13,5},{2,10},{6,14},... | collective-permute-start | bytes 884744 | tf_op jit(solution)/shard_map/ppermute | solution.py:61
  663.1 28.2 %collective-permute-start.94 = (bf16[192,768]{1,0:T(8,128)(2,1)S(1)}, bf16[192,768]{1,0:T(8,128)(2,1)S(1)}, u32[]{:S(2)}, u32[]{:S(2)}) collective-permute-start(bf16[192,768]{1,0:T(8,128)(2,1)S(1)} %get-tuple-element.274), channel_id=1, source_target_pairs={{0,4},{4,0},{8,12},{12,8},{1,5},{5,1},{9,13},{13,9},{2,6},{6,2},{1... | collective-permute-start | bytes 884744 | tf_op jit(solution)/shard_map/ppermute | solution.py:61
  663.1 31.6 %collective-permute-start.96 = (bf16[192,768]{1,0:T(8,128)(2,1)S(1)}, bf16[192,768]{1,0:T(8,128)(2,1)}, u32[]{:S(2)}, u32[]{:S(2)}) collective-permute-start(bf16[192,768]{1,0:T(8,128)(2,1)S(1)} %get-tuple-element.275), channel_id=1, source_target_pairs={{0,12},{4,8},{8,4},{12,0},{1,13},{5,9},{9,5},{13,1},{2,14},{6,10},... | collective-permute-start | bytes 884744 | tf_op jit(solution)/shard_map/ppermute | solution.py:61
  691.2 38.7 %collective-permute-start.68 = (bf16[4,256,768]{2,1,0:T(8,128)(2,1)S(1)}, bf16[4,256,768]{2,1,0:T(8,128)(2,1)S(1)}, u32[]{:S(2)}, u32[]{:S(2)}) collective-permute-start(bf16[4,256,768]{2,1,0:T(8,128)(2,1)S(1)} %pad_maximum_fusion.7), channel_id=1, source_target_pairs={{0,1},{1,0},{2,3},{3,2},{4,5},{5,4},{6,7},{7,6},{8,9},{9,8},{10,11... | collective-permute-start | bytes 4718600 | tf_op jit(solution)/shard_map/ppermute | solution.py:61
  694.7 37.4 %collective-permute-start.69 = (bf16[4,256,768]{2,1,0:T(8,128)(2,1)S(1)}, bf16[4,256,768]{2,1,0:T(8,128)(2,1)S(1)}, u32[]{:S(2)}, u32[]{:S(2)}) collective-permute-start(bf16[4,256,768]{2,1,0:T(8,128)(2,1)S(1)} %pad_maximum_fusion.7), channel_id=1, source_target_pairs={{0,2},{1,3},{2,0},{3,1},{4,6},{5,7},{6,4},{7,5},{8,10},{9,11},{10,... | collective-permute-start | bytes 4718600 | tf_op jit(solution)/shard_map/ppermute | solution.py:61
  704.7 59.3 %collective-permute-start.104 = (f32[192,768]{1,0:T(8,128)}, f32[192,768]{1,0:T(8,128)S(1)}, u32[]{:S(2)}, u32[]{:S(2)}) collective-permute-start(f32[192,768]{1,0:T(8,128)} %get-tuple-element.210), channel_id=1, source_target_pairs={{0,16},{16,0},{1,17},{17,1},{2,18},{18,2},{3,19},{19,3},{4,20},{20... | collective-permute-start | bytes 1769480 | tf_op jit(solution)/shard_map/ppermute | solution.py:57
  706.2 31.1 %collective-permute-start.82 = (bf16[2,2,48,896]{3,2,0,1:T(8,128)(2,1)S(1)}, bf16[2,2,48,896]{3,2,0,1:T(8,128)(2,1)S(1)}, u32[]{:S(2)}, u32[]{:S(2)}) collective-permute-start(bf16[2,2,48,896]{3,2,0,1:T(8,128)(2,1)S(1)} %fusion.111), channel_id=1, source_target_pairs={{0,1},{1,0},{2,3},{3,2},{4,5},{5,4},{6,7},{7,6},{8,9},{9,8},{10,11... | collective-permute-start | bytes 1032200 | tf_op jit(solution)/shard_map/ppermute | solution.py:61
  709.7 47.9 %collective-permute-start.84 = (bf16[2,2,48,896]{3,2,1,0:T(8,128)(2,1)S(1)}, bf16[2,2,48,896]{3,2,1,0:T(8,128)(2,1)S(1)}, u32[]{:S(2)}, u32[]{:S(2)}) collective-permute-start(bf16[2,2,48,896]{3,2,1,0:T(8,128)(2,1)S(1)} %fusion.109), channel_id=1, source_target_pairs={{0,2},{1,3},{2,0},{3,1},{4,6},{5,7},{6,4},{7,5},{8,10},{9,11},{10,... | collective-permute-start | bytes 1032200 | tf_op jit(solution)/shard_map/ppermute | solution.py:61
  730.0 28.4 %collective-permute-start.74 = (bf16[2,2,48,896]{3,2,0,1:T(8,128)(2,1)S(1)}, bf16[2,2,48,896]{3,2,0,1:T(8,128)(2,1)S(1)}, u32[]{:S(2)}, u32[]{:S(2)}) collective-permute-start(bf16[2,2,48,896]{3,2,0,1:T(8,128)(2,1)S(1)} %fusion.110), channel_id=1, source_target_pairs={{0,1},{1,0},{2,3},{3,2},{4,5},{5,4},{6,7},{7,6},{8,9},{9,8},{10,11... | collective-permute-start | bytes 1032200 | tf_op jit(solution)/shard_map/ppermute | solution.py:61
  732.0 21.4 %collective-permute-start.71 = (bf16[2,256,768]{2,1,0:T(8,128)(2,1)S(1)}, bf16[2,256,768]{2,1,0:T(8,128)(2,1)S(1)}, u32[]{:S(2)}, u32[]{:S(2)}) collective-permute-start(bf16[2,256,768]{2,1,0:T(8,128)(2,1)S(1)} %slice.545), channel_id=1, source_target_pairs={{0,2},{1,3},{2,0},{3,1},{4,6},{5,7},{6,4},{7,5},{8,10},{9,11},{10,... | collective-permute-start | bytes 2359304 | tf_op jit(solution)/shard_map/ppermute | solution.py:61
  737.3 19.0 %collective-permute-start.70 = (bf16[2,256,768]{2,1,0:T(8,128)(2,1)S(1)}, bf16[2,256,768]{2,1,0:T(8,128)(2,1)S(1)}, u32[]{:S(2)}, u32[]{:S(2)}) collective-permute-start(bf16[2,256,768]{2,1,0:T(8,128)(2,1)S(1)} %slice.544), channel_id=1, source_target_pairs={{0,1},{1,0},{2,3},{3,2},{4,5},{5,4},{6,7},{7,6},{8,9},{9,8},{10,11... | collective-permute-start | bytes 2359304 | tf_op jit(solution)/shard_map/ppermute | solution.py:61
  757.6 38.8 %collective-permute-start.72 = (bf16[4096,768]{1,0:T(8,128)(2,1)}, bf16[4096,768]{1,0:T(8,128)(2,1)}, u32[]{:S(2)}, u32[]{:S(2)}) collective-permute-start(bf16[4096,768]{1,0:T(8,128)(2,1)} %bitcast.146), channel_id=1, source_target_pairs={{0,16},{16,0},{1,17},{17,1},{2,18},{18,2},{3,19},{19,3},{4,20},{20... | collective-permute-start | bytes 18874376 | tf_op jit(solution)/shard_map/ppermute | solution.py:57
  761.2 16.2 %collective-permute-start.75 = (bf16[2,48,896]{2,1,0:T(8,128)(2,1)}, bf16[2,48,896]{2,1,0:T(8,128)(2,1)S(1)}, u32[]{:S(2)}, u32[]{:S(2)}) collective-permute-start(bf16[2,48,896]{2,1,0:T(8,128)(2,1)} %fusion.126), channel_id=1, source_target_pairs={{0,2},{1,3},{2,0},{3,1},{4,6},{5,7},{6,4},{7,5},{8,10},{9,11},{10,... | collective-permute-start | bytes 516104 | tf_op jit(solution)/shard_map/ppermute | solution.py:61
  764.0 14.8 %collective-permute-start.77 = (bf16[2,48,896]{2,1,0:T(8,128)(2,1)}, bf16[2,48,896]{2,1,0:T(8,128)(2,1)}, u32[]{:S(2)}, u32[]{:S(2)}) collective-permute-start(bf16[2,48,896]{2,1,0:T(8,128)(2,1)} %fusion.127), channel_id=1, source_target_pairs={{0,1},{1,0},{2,3},{3,2},{4,5},{5,4},{6,7},{7,6},{8,9},{9,8},{10,11... | collective-permute-start | bytes 516104 | tf_op jit(solution)/shard_map/ppermute | solution.py:61
  935.9 44.3 %collective-permute-start.109 = (f32[11024]{0:T(1024)S(1)}, f32[11024]{0:T(1024)S(1)}, u32[]{:S(2)}, u32[]{:S(2)}) collective-permute-start(f32[11024]{0:T(1024)S(1)} %slice.566), channel_id=1, source_target_pairs={{0,2},{1,3},{2,0},{3,1},{4,6},{5,7},{6,4},{7,5},{8,10},{9,11},{10,... | collective-permute-start | bytes 132296 | tf_op jit(solution)/shard_map/ppermute | solution.py:61
  937.7 42.5 %collective-permute-start.110 = (f32[11024]{0:T(1024)S(1)}, f32[11024]{0:T(1024)S(1)}, u32[]{:S(2)}, u32[]{:S(2)}) collective-permute-start(f32[11024]{0:T(1024)S(1)} %slice.566), channel_id=1, source_target_pairs={{0,3},{1,2},{2,1},{3,0},{4,7},{5,6},{6,5},{7,4},{8,11},{9,10},{10,... | collective-permute-start | bytes 132296 | tf_op jit(solution)/shard_map/ppermute | solution.py:61
  937.9 42.3 %collective-permute-start.108 = (f32[11024]{0:T(1024)S(1)}, f32[11024]{0:T(1024)S(1)}, u32[]{:S(2)}, u32[]{:S(2)}) collective-permute-start(f32[11024]{0:T(1024)S(1)} %slice.566), channel_id=1, source_target_pairs={{0,1},{1,0},{2,3},{3,2},{4,5},{5,4},{6,7},{7,6},{8,9},{9,8},{10,11... | collective-permute-start | bytes 132296 | tf_op jit(solution)/shard_map/ppermute | solution.py:61
  (247 other events, 3394.9 us)

commit v2 on v1

v2 whole, which is shorter than its diff:
```python
import functools

import jax
import jax.numpy as jnp
from jax import lax
from jax.experimental import pallas as pl
from jax.experimental.pallas import tpu as pltpu
from jax.sharding import PartitionSpec as P

HD = 64
WINDOW = 512
STEP = 10
NORM_EPS = 1e-05
SQUARE_EPS = 1e-30
SCALE_FLOOR = 0.001
RELATIVE_RATE = 0.5
MASKED = -1e30
DECAY = 1.0 - STEP ** (-0.8)
BLOCKS = ("dp", "ctx")
LANES = 128
DEAD = -(1 << 30)
MIB = 1 << 20


def bfloat(values):
    return values.astype(jnp.bfloat16)


def single(values):
    return values.astype(jnp.float32)


def matmul(left, right):
    return jnp.dot(left, right, preferred_element_type=jnp.float32)


def matmul_left(left, right):
    return lax.dot_general(
        left, right, (((0,), (0,)), ((), ())), preferred_element_type=jnp.float32
    )


def matmul_right(left, right):
    return lax.dot_general(
        left, right, (((1,), (1,)), ((), ())), preferred_element_type=jnp.float32
    )


def layer_norm(values, gain, shift):
    center = values - jnp.mean(values, -1, keepdims=True)
    spread = jnp.mean(center * center, -1, keepdims=True)
    return center * lax.rsqrt(spread + NORM_EPS) * gain + shift


def gelu_tanh(values):
    return jax.nn.gelu(values, approximate=True)


def at(values, index, axis):
    return lax.dynamic_index_in_dim(values, index, axis, keepdims=False)


def swap(values):
    return lax.ppermute(values, "section", [(0, 1), (1, 0)])


def cross(values, axis, bits):
    return lax.ppermute(values, axis, [(i, i ^ bits) for i in range(lax.axis_size(axis))])


def shifted(values, axis, distance):
    devices = range(lax.axis_size(axis))
    return lax.ppermute(
        values, axis, [(i, i + distance) for i in devices if i + distance in devices]
    )


def by_fours():
    return lax.axis_size("dp") == 4 and lax.axis_size("ctx") == 4


def mine_first(mine, theirs):
    first = lax.axis_index("section") == 0
    return jnp.where(first, mine, theirs), jnp.where(first, theirs, mine)


def after(values, *earlier):
    return lax.optimization_barrier((values, *earlier))[0]


def column_pieces(part):
    if not by_fours():
        return (lax.all_gather(part, "dp", axis=0),)
    return tuple(cross(part, "dp", k) for k in (1, 2, 3))


def column_join(part, pieces):
    if not by_fours():
        return pieces[0]
    return in_order((part, *pieces), "dp")


def plane_near(column):
    if not by_fours():
        return (lax.all_gather(column, "ctx", axis=1),)
    return cross(column, "ctx", 1), cross(column, "ctx", 2)


def plane_far(near):
    if not by_fours():
        return ()
    beside, above = near
    return cross(above[:2], "ctx", 1), cross(beside[2:], "ctx", 2)


def plane_list(column, near, far):
    if not by_fours():
        return near[0].reshape((-1,) + column.shape[1:])
    return (column, *near, jnp.concatenate(far))


def plane_near_half(column, side):
    if not by_fours():
        return plane_near(column) if side == 0 else ()
    return plane_near(column[2 * side : 2 * side + 2])


def plane_far_half(first, second):
    if not by_fours():
        return ()
    return cross(first[1], "ctx", 1), cross(second[0], "ctx", 2)


def plane_halves(column, near, far):
    if not by_fours():
        return plane_list(column, near[0], far)
    return (column, *zip(*near), tuple(far))


def in_order(pieces, axis, at_axis=0):
    i = lax.axis_index(axis)
    return jnp.stack(
        [lax.select_n(i, *[pieces[place ^ k] for k in range(4)]) for place in range(4)], at_axis
    )


def weights_kernel(place_ref, *refs):
    *pieces, in_ref, out_ref = refs
    c, first = place_ref[0], place_ref[1] == 0
    columns, part = pieces[0].shape[:2]

    def lay(ref, pieces):
        for k, piece in enumerate(pieces):
            for z in range(columns):
                rows = pl.ds(pl.multiple_of((4 * z + (c ^ k)) * part, 16), part)
                ref[rows, :] = piece[z]

    @pl.when(first)
    def _():
        lay(in_ref, pieces[:4])
        lay(out_ref, pieces[4:])

    @pl.when(~first)
    def _():
        lay(in_ref, pieces[4:])
        lay(out_ref, pieces[:4])


def attention_weights(mine, theirs, model, layer):
    if by_fours():
        columns, both, wide = mine[0].shape
        place = jnp.stack([lax.axis_index("ctx"), lax.axis_index("section")])
        weight_in, weight_out = pl.pallas_call(
            weights_kernel,
            grid_spec=pltpu.PrefetchScalarGridSpec(
                num_scalar_prefetch=1,
                grid=(1,),
                in_specs=[pl.BlockSpec((columns, both // 2, wide), lambda *_: (0, layer, 0))] * 8,
                out_specs=[whole_block((model, wide))] * 2,
            ),
            out_shape=[jax.ShapeDtypeStruct((model, wide), jnp.bfloat16)] * 2,
            compiler_params=vmem(24),
            cost_estimate=small_cost(
                flops=0, bytes_accessed=8 * model * wide, transcendentals=0
            ),
        )(place, *mine, *theirs)
    else:
        part = mine.shape[1] // 2
        weights = mine_first(mine, theirs)
        weight_in, weight_out = (
            w[:, layer * part : (layer + 1) * part].reshape(model, -1) for w in weights
        )
    return weight_in, weight_out[:, :model], single(weight_out[:, model : model + 4]).T


def gather_blocks(part):
    return gather_ctx(column_join(part, column_pieces(part))).swapaxes(0, 1).reshape(
        (-1,) + part.shape
    )


def gather_ctx(part):
    if not by_fours():
        return lax.all_gather(part, "ctx", axis=0)
    return in_order([part] + [cross(part, "ctx", k) for k in (1, 2, 3)], "ctx")


def scattered(parts):
    return single(lax.psum_scatter(parts, BLOCKS, scatter_dimension=0))


def corner(parts, rows, z, y=None, x=None):
    grid = parts.reshape((4, 2, 2) + parts.shape[1:])
    first, count = rows
    start = (z, 0 if y is None else y, 0 if x is None else x, first, 0)
    size = (2, 2 if y is None else 1, 2 if x is None else 1, count, parts.shape[2])
    return lax.dynamic_slice(grid, start, size)


def plane_bits():
    c = lax.axis_index("ctx")
    return c & 1, c >> 1


def half_first(parts, rows):
    x, y = plane_bits()
    return (
        cross(corner(parts, rows, 0, x=1 - x), "ctx", 1),
        cross(corner(parts, rows, 2, y=1 - y), "ctx", 2),
    )


def half_kept(parts, rows, got):
    x, y = plane_bits()
    near = bfloat(single(corner(parts, rows, 0, x=x)) + single(got[0]))
    far = bfloat(single(corner(parts, rows, 2, y=y)) + single(got[1]))
    near, far = near[:, :, 0], far[:, 0]
    return (at(near, y, 1), at(far, x, 1)), (at(near, 1 - y, 1), at(far, 1 - x, 1))


def half_send(halves):
    return cross(halves[0], "ctx", 2), cross(halves[1], "ctx", 1)


def half_column(kept, got):
    return jnp.concatenate([bfloat(single(one) + single(two)) for one, two in zip(kept, got)])


def row_pieces(parts):
    if not by_fours():
        return (lax.psum_scatter(bfloat(parts), "dp", scatter_dimension=0),)
    z = lax.axis_index("dp")
    low = bfloat(parts)
    return tuple(cross(at(low, z ^ k, 0), "dp", k) for k in (1, 2, 3))


def row_sum(parts, pieces):
    total = single(pieces[0])
    for piece in pieces[1:]:
        total = total + single(piece)
    return single(at(parts, lax.axis_index("dp"), 0)) + total if by_fours() else total


def scatter_rows(parts):
    return row_sum(parts, row_pieces(parts))


def summed(values, axes):
    if not by_fours():
        return lax.psum(values, axes)
    for axis in axes:
        one, two, three = (cross(values, axis, k) for k in (1, 2, 3))
        values = (values + one) + (two + three)
    return values


def doc_numbers(lengths, places):
    bounds = jnp.cumsum(lengths)
    return jnp.sum((places[:, None] >= bounds[None, :]).astype(jnp.int32), -1)


def pair_bias(lengths, query_places, key_places):
    query_docs = doc_numbers(lengths, query_places)
    key_docs = doc_numbers(lengths, key_places)
    allowed = (
        (key_places[None, :] <= query_places[:, None])
        & (key_places[None, :] > query_places[:, None] - WINDOW)
        & (key_places[None, :] >= 0)
        & (key_docs[None, :] == query_docs[:, None])
    )
    return jnp.where(allowed, 0.0, MASKED)


def earlier_count(local_len):
    return min(lax.axis_size("ctx") - 1, -(-(WINDOW - 1) // local_len))


def key_rows(keyval):
    reach = earlier_count(keyval.shape[0])
    return jnp.concatenate(
        [shifted(keyval, "ctx", k) for k in range(reach, 0, -1)] + [keyval]
    )


def key_rows_back(grads, local_len):
    reach = earlier_count(local_len)
    starts = [(reach - k) * local_len for k in range(1, reach + 1)]
    return tuple(
        shifted(grads[start : start + local_len], "ctx", -(k + 1))
        for k, start in enumerate(starts)
    )


def key_rows_sum(grads, pieces, local_len):
    total = grads[earlier_count(local_len) * local_len :]
    for piece in pieces:
        total = total + piece
    return bfloat(total)


def whole_block(shape):
    return pl.BlockSpec(shape, lambda *_: (0,) * len(shape))


def vmem(mebibytes):
    return pltpu.CompilerParams(vmem_limit_bytes=mebibytes * MIB)


def small_cost(flops, bytes_accessed, transcendentals):
    return pl.CostEstimate(
        flops=flops // 16, bytes_accessed=bytes_accessed // 16, transcendentals=0 * transcendentals
    )


def row_block(rows, most):
    block = most
    while rows % block:
        block //= 2
    return block


def turned(values):
    return pltpu.roll(values, HD, 1)


def softmax_rows(scores):
    exponents = jnp.exp(scores - jnp.max(scores, -1, keepdims=True))
    return exponents / jnp.sum(exponents, -1, keepdims=True)


def attend_kernel(query_ref, keyval_ref, bias_ref, out_ref):
    keyval = keyval_ref[...]
    bias = bias_ref[...]
    pair = single(query_ref[...])
    left = lax.broadcasted_iota(jnp.int32, pair.shape, 1) < HD
    outs = []
    for heads in (pair, turned(pair)):
        query = bfloat(jnp.where(left, heads, 0.0))
        probs = softmax_rows(matmul_right(query, keyval) + bias)
        outs.append(matmul(bfloat(probs), keyval))
    out_ref[...] = bfloat(jnp.where(left, turned(outs[0]), outs[1]))


def attend(query, keyval, bias):
    rows, columns = query.shape
    pair = 2 * HD
    return pl.pallas_call(
        attend_kernel,
        grid=(columns // pair,),
        in_specs=[
            pl.BlockSpec((rows, pair), lambda i: (0, i)),
            whole_block(keyval.shape),
            whole_block(bias.shape),
        ],
        out_specs=pl.BlockSpec((rows, pair), lambda i: (0, i)),
        out_shape=jax.ShapeDtypeStruct((rows, columns), jnp.bfloat16),
        compiler_params=vmem(40),
        cost_estimate=small_cost(
            flops=4 * rows * columns * keyval.shape[0],
            bytes_accessed=8 * rows * columns,
            transcendentals=rows * columns * keyval.shape[0] // HD,
        ),
    )(query, keyval, bias)


def attend_back_kernel(query_ref, keyval_ref, bias_ref, grad_ref, grad_query_ref, grad_keyval_ref):
    keyval = keyval_ref[...]
    bias = bias_ref[...]
    pair = single(query_ref[...])
    grads = single(grad_ref[...])
    left = lax.broadcasted_iota(jnp.int32, pair.shape, 1) < HD
    total = jnp.where(pl.program_id(0) == 0, 0.0, grad_keyval_ref[...])
    outs = []
    for heads, grad_heads in ((pair, turned(grads)), (turned(pair), grads)):
        query = bfloat(jnp.where(left, heads, 0.0))
        grad = bfloat(jnp.where(left, 0.0, grad_heads))
        probs = softmax_rows(matmul_right(query, keyval) + bias)
        grad_probs = matmul_right(grad, keyval)
        inner = jnp.sum(probs * grad_probs, -1, keepdims=True)
        grad_scores = bfloat(probs * (grad_probs - inner))
        outs.append(matmul(grad_scores, keyval))
        total = total + matmul_left(grad_scores, query) + matmul_left(bfloat(probs), grad)
    grad_keyval_ref[...] = total
    grad_query = single(bfloat(jnp.where(left, outs[0], turned(outs[1])))) * HD ** (-0.5)
    grad_query_ref[...] = bfloat(grad_query)


def attend_back(query, keyval, bias, grad_out):
    rows, columns = query.shape
    pair = 2 * HD
    pairs = pl.BlockSpec((rows, pair), lambda i: (0, i))
    return pl.pallas_call(
        attend_back_kernel,
        grid=(columns // pair,),
        in_specs=[pairs, whole_block(keyval.shape), whole_block(bias.shape), pairs],
        out_specs=[pairs, whole_block(keyval.shape)],
        out_shape=[
            jax.ShapeDtypeStruct((rows, columns), jnp.bfloat16),
            jax.ShapeDtypeStruct(keyval.shape, jnp.float32),
        ],
        compiler_params=vmem(48),
        cost_estimate=small_cost(
            flops=10 * rows * columns * keyval.shape[0],
            bytes_accessed=8 * rows * columns,
            transcendentals=rows * columns * keyval.shape[0] // HD,
        ),
    )(query, keyval, bias, grad_out)


def lower_kernel(table_ref, *refs):
    low_ref, square_ref = refs[-2:]
    weights = table_ref[...]
    low_ref[...] = bfloat(weights)
    squares = jnp.sum((weights * weights).reshape(-1, 8, weights.shape[1]), 0)
    square_ref[...] = jnp.where(pl.program_id(0) == 0, 0.0, square_ref[...]) + squares


def lowered(table, low, index, count):
    vocab_here, model = table.shape
    block = row_block(vocab_here, 1024)
    steps = vocab_here // block
    first, last = index * steps // count, (index + 1) * steps // count
    rows = pl.BlockSpec((block, model), lambda i: (i + first, 0))
    return pl.pallas_call(
        lower_kernel,
        grid=(last - first,),
        in_specs=[rows] + ([] if low is None else [pl.BlockSpec(memory_space=pl.ANY)]),
        out_specs=[rows, whole_block((8, model))],
        out_shape=[
            jax.ShapeDtypeStruct(table.shape, jnp.bfloat16),
            jax.ShapeDtypeStruct((8, model), jnp.float32),
        ],
        input_output_aliases={} if low is None else {1: 0},
        compiler_params=vmem(40),
        cost_estimate=small_cost(
            flops=2 * vocab_here * model // count,
            bytes_accessed=6 * vocab_here * model // count,
            transcendentals=0,
        ),
    )(*((table,) if low is None else (table, low)))


def head_stats_kernel(chosen_ref, target_ref, low_ref, stats_ref):
    step = pl.program_id(0)
    rows = low_ref.shape[0]

    @pl.when(step == 0)
    def _():
        stats_ref[...] = jnp.zeros_like(stats_ref)
        stats_ref[0:1, :] = jnp.full((1, stats_ref.shape[1]), MASKED, jnp.float32)

    logits = matmul(low_ref[...], chosen_ref[...])
    places = lax.broadcasted_iota(jnp.int32, logits.shape, 0)
    matches = places == target_ref[...] - step * rows
    before, totals = stats_ref[0:1, :], stats_ref[1:2, :]
    highest = jnp.maximum(before, jnp.max(logits, 0, keepdims=True))
    stats_ref[1:2, :] = totals * jnp.exp(before - highest) + jnp.sum(
        jnp.exp(logits - highest), 0, keepdims=True
    )
    stats_ref[0:1, :] = highest
    stats_ref[2:3, :] = stats_ref[2:3, :] + jnp.sum(
        jnp.where(matches, logits, 0.0), 0, keepdims=True
    )


def head_stats(chosen_across, target_row, low):
    vocab_here, model = low.shape
    slots = chosen_across.shape[1]
    block = row_block(vocab_here, 1024)
    return pl.pallas_call(
        head_stats_kernel,
        grid=(vocab_here // block,),
        in_specs=[
            whole_block(chosen_across.shape),
            whole_block((1, slots)),
            pl.BlockSpec((block, model), lambda i: (i, 0)),
        ],
        out_specs=whole_block((8, slots)),
        out_shape=jax.ShapeDtypeStruct((8, slots), jnp.float32),
        compiler_params=vmem(40),
        cost_estimate=small_cost(
            flops=2 * slots * vocab_here * model,
            bytes_accessed=2 * vocab_here * model,
            transcendentals=slots * vocab_here,
        ),
    )(chosen_across, target_row, low)


def head_rows_kernel(chosen_ref, target_ref, logsum_ref, low_ref, grad_ref):
    step = pl.program_id(0)
    rows = low_ref.shape[0]
    low = low_ref[...]
    logits = matmul_right(chosen_ref[...], low)
    places = lax.broadcasted_iota(jnp.int32, logits.shape, 1) + step * rows
    target = target_ref[...]
    matches = jnp.where(places == target, 1.0, 0.0)
    grads = jnp.where(target != DEAD, jnp.exp(logits - logsum_ref[...]) - matches, 0.0)
    before = jnp.where(step == 0, 0.0, grad_ref[...])
    grad_ref[...] = before + matmul(bfloat(grads), low)


def head_rows(chosen, target_column, logsum_column, low):
    vocab_here, model = low.shape
    slots = chosen.shape[0]
    block = row_block(vocab_here, 1024)
    return pl.pallas_call(
        head_rows_kernel,
        grid=(vocab_here // block,),
        in_specs=[
            whole_block(chosen.shape),
            whole_block((slots, 1)),
            whole_block((slots, 1)),
            pl.BlockSpec((block, model), lambda i: (i, 0)),
        ],
        out_specs=whole_block((slots, model)),
        out_shape=jax.ShapeDtypeStruct((slots, model), jnp.float32),
        compiler_params=vmem(40),
        cost_estimate=small_cost(
            flops=4 * slots * vocab_here * model,
            bytes_accessed=2 * vocab_here * model,
            transcendentals=slots * vocab_here,
        ),
    )(chosen, target_column, logsum_column, low)


def head_table_kernel(first, chosen_ref, across_ref, target_ref, logsum_ref, low_ref, *refs):
    step = pl.program_id(0) + first
    grad_ref = refs[-1]
    rows = low_ref.shape[0]
    logits = matmul(low_ref[...], across_ref[...])
    places = lax.broadcasted_iota(jnp.int32, logits.shape, 0) + step * rows
    target = target_ref[...]
    matches = jnp.where(places == target, 1.0, 0.0)
    grads = jnp.where(target != DEAD, jnp.exp(logits - logsum_ref[...]) - matches, 0.0)
    grad_ref[...] = matmul(bfloat(grads), chosen_ref[...])


def head_table(chosen, chosen_across, target_row, logsum_row, low, grads, index, count):
    vocab_here, model = low.shape
    slots = chosen.shape[0]
    block = row_block(vocab_here, 1024)
    steps = vocab_here // block
    first, last = index * steps // count, (index + 1) * steps // count
    rows = pl.BlockSpec((block, model), lambda i: (i + first, 0))
    return pl.pallas_call(
        functools.partial(head_table_kernel, first),
        grid=(last - first,),
        in_specs=[
            whole_block(chosen.shape),
            whole_block(chosen_across.shape),
            whole_block((1, slots)),
            whole_block((1, slots)),
            rows,
        ]
        + ([] if grads is None else [pl.BlockSpec(memory_space=pl.ANY)]),
        out_specs=rows,
        out_shape=jax.ShapeDtypeStruct(low.shape, jnp.float32),
        input_output_aliases={} if grads is None else {5: 0},
        compiler_params=vmem(48),
        cost_estimate=small_cost(
            flops=4 * slots * vocab_here * model // count,
            bytes_accessed=6 * vocab_here * model // count,
            transcendentals=slots * vocab_here // count,
        ),
    )(*((chosen, chosen_across, target_row, logsum_row, low) + (() if grads is None else (grads,))))


def table_sums_kernel(first, place_ref, starts_ref, ids_ref, order_ref, head_ref, stat_ref, *refs):
    pieces = refs[:8]
    grad_ref, rows_ref, sums_ref, wide_ref = refs[-4:]
    step = pl.program_id(0) + first
    rows, model = head_ref.shape
    room = pieces[0].shape[1]

    @pl.when(pl.program_id(0) == 0)
    def _():
        for side in range(2):
            section = place_ref[1] if side == 0 else 1 - place_ref[1]
            for k in range(4):
                for z in range(4):
                    block = (4 * section + z) * 4 + (place_ref[0] ^ k)
                    row = pl.multiple_of(block * room, 16)
                    wide_ref[pl.ds(row, room), :] = single(pieces[4 * side + k][z])
        sums_ref[...] = jnp.zeros_like(sums_ref)

    grad_ref[...] = head_ref[...]
    start, end = starts_ref[step], starts_ref[step + 1]

    @pl.loop(0, (end - start + 3) // 4)
    def _(i):
        places, values = [], []
        for k in range(4):
            j = jnp.minimum(start + 4 * i + k, end - 1)
            row = wide_ref[pl.ds(order_ref[j], 1), :]
            values.append(jnp.where(start + 4 * i + k < end, row, 0.0))
            places.append(pl.ds(ids_ref[j] - step * rows, 1))
        for place, row in zip(places, values):
            grad_ref[place, :] = grad_ref[place, :] + row

    stats = stat_ref[...]
    columns = jnp.zeros((8, model), jnp.float32)
    scaled = jnp.zeros((8, model), jnp.float32)
    for k in range(rows // LANES):
        part = grad_ref[k * LANES : (k + 1) * LANES, :]
        square = part * part
        mean = jnp.sum(square + SQUARE_EPS, -1, keepdims=True) * (1.0 / model)
        stat = jnp.transpose(jnp.broadcast_to(stats[k : k + 1, :], (LANES, LANES)))
        new = DECAY * stat + (1.0 - DECAY) * mean
        rows_ref[k : k + 1, :] = jnp.transpose(new)[0:1, :]
        columns = columns + jnp.sum((square + SQUARE_EPS).reshape(LANES // 8, 8, model), 0)
        ratio = square * (1.0 / new[:, 0:1])
        scaled = scaled + jnp.sum(ratio.reshape(LANES // 8, 8, model), 0)
    sums_ref[0:8, :] = sums_ref[0:8, :] + columns
    sums_ref[8:16, :] = sums_ref[8:16, :] + scaled


def table_sums(starts, ids, order, pieces, head, row_stat, block, earlier, index, count):
    vocab_here, model = head.shape
    steps = vocab_here // block
    first, last = index * steps // count, (index + 1) * steps // count
    rows = pl.BlockSpec((block, model), lambda i, *_: (i + first, 0))
    stats = pl.BlockSpec((block // LANES, LANES), lambda i, *_: (i + first, 0))
    kept = [] if earlier is None else [pl.BlockSpec(memory_space=pl.ANY)] * 2
    return pl.pallas_call(
        functools.partial(table_sums_kernel, first),
        grid_spec=pltpu.PrefetchScalarGridSpec(
            num_scalar_prefetch=4,
            grid=(last - first,),
            in_specs=[rows, stats]
            + [
                pl.BlockSpec(piece.shape, lambda *_: (0, 0, 0), pipeline_mode=pl.Buffered(1))
                for piece in pieces
            ]
            + kept,
            out_specs=[rows, stats, pl.BlockSpec((16, model), lambda *_: (0, 0))],
            scratch_shapes=[pltpu.VMEM((32 * pieces[0].shape[1], model), jnp.float32)],
        ),
        out_shape=[
            jax.ShapeDtypeStruct(head.shape, jnp.float32),
            jax.ShapeDtypeStruct((vocab_here // LANES, LANES), jnp.float32),
            jax.ShapeDtypeStruct((16, model), jnp.float32),
        ],
        input_output_aliases={} if earlier is None else {14: 0, 15: 1},
        compiler_params=vmem(56),
        cost_estimate=small_cost(
            flops=8 * vocab_here * model // count,
            bytes_accessed=8 * vocab_here * model // count,
            transcendentals=0,
        ),
    )(
        jnp.stack([lax.axis_index("ctx"), lax.axis_index("section")]),
        starts,
        ids,
        order,
        head,
        row_stat.reshape(-1, LANES),
        *pieces,
        *(earlier or ()),
    )


def gelu_slope(values):
    factor = (2.0 / jnp.pi) ** 0.5
    inner = jnp.tanh(factor * (values + 0.044715 * values * values * values))
    slope = factor * (1.0 + 3.0 * 0.044715 * values * values)
    return 0.5 * (1.0 + inner) + 0.5 * values * (1.0 - inner * inner) * slope


def put_together(c, step, pieces, up_ref, down_ref):
    model = up_ref.shape[0]
    columns, packed = pieces[0].shape[:2]
    part, half = model // (8 * columns), packed // 2
    for k in range(4):
        for z in range(2 * columns):
            piece = pieces[2 * k + z // columns]
            rows = pl.ds(pl.multiple_of((4 * z + (c ^ k)) * part, 16), part)
            place = pl.ds(pl.multiple_of(step * part, 16), part)
            up_ref[rows, :] = piece[z % columns, place, :]
    for side in range(2):

        @pl.when(step == side)
        def _():
            for k in range(4):
                for z in range(columns):
                    rows = pl.ds(pl.multiple_of((4 * z + (c ^ k)) * half, 16), half)
                    down_ref[rows, :] = pieces[2 * k + side][z, half : 2 * half, :]


def half_specs(hidden):
    if not isinstance(hidden, tuple):
        grid = hidden.reshape((4, 4) + hidden.shape[1:])
        shape = (2, None) + hidden.shape[1:]
        specs = [
            pl.BlockSpec(shape, lambda *_, k=k, side=side: (side, k, 0, 0))
            for k in range(4)
            for side in range(2)
        ]
        return jnp.zeros(1, jnp.int32), [grid] * 8, specs
    arrays, specs = [], []
    for piece in hidden:
        for side in range(2):
            array = piece[side] if isinstance(piece, tuple) else piece
            shape = (2,) + array.shape[1:]
            place = 0 if isinstance(piece, tuple) else side
            arrays.append(array)
            specs.append(pl.BlockSpec(shape, lambda *_, place=place: (place, 0, 0)))
    return lax.axis_index("ctx").reshape(1), arrays, specs


def hidden_kernel(place_ref, both_ref, *refs):
    *pieces, upper_ref, partial_ref, up_ref, down_ref = refs
    step = pl.program_id(0)
    put_together(place_ref[0], step, pieces, up_ref, down_ref)
    upper = matmul(both_ref[...], up_ref[...])
    upper_ref[...] = upper
    before = jnp.where(step == 0, 0.0, partial_ref[...])
    partial_ref[...] = before + matmul(bfloat(gelu_tanh(upper)), down_ref[...])


def hidden_forward(both, hidden):
    rows, model = both.shape
    blocks = lax.axis_size("dp") * lax.axis_size("ctx")
    if not by_fours():
        up, down = hidden_weights(hidden)
        upper = matmul(both, up)
        return upper, matmul(bfloat(gelu_tanh(upper)), down)
    packed = (hidden[0] if isinstance(hidden, tuple) else hidden).shape[1]
    size = blocks * packed * model
    steps = size // (2 * model * model)
    square = pltpu.VMEM((model, model), jnp.bfloat16)
    place, arrays, specs = half_specs(hidden)
    return pl.pallas_call(
        hidden_kernel,
        grid_spec=pltpu.PrefetchScalarGridSpec(
            num_scalar_prefetch=1,
            grid=(steps,),
            in_specs=[whole_block(both.shape)] + specs,
            out_specs=[pl.BlockSpec((rows, model), lambda j, _: (0, j)), whole_block(both.shape)],
            scratch_shapes=[square, square],
        ),
        out_shape=[
            jax.ShapeDtypeStruct((rows, steps * model), jnp.float32),
            jax.ShapeDtypeStruct((rows, model), jnp.float32),
        ],
        compiler_params=vmem(48),
        cost_estimate=small_cost(
            flops=2 * rows * size,
            bytes_accessed=2 * size + 8 * rows * steps * model,
            transcendentals=rows * steps * model,
        ),
    )(place, both, *arrays)


def hidden_back_kernel(place_ref, both_ref, upper_ref, grad_ref, *refs):
    *pieces, partial_ref, grads_ref, up_ref, down_ref = refs
    step = pl.program_id(0)
    model = both_ref.shape[1]
    blocks, half = grads_ref.shape[0], grads_ref.shape[1] // 2
    rows, per_step = model // blocks, model // half
    put_together(place_ref[0], step, pieces, up_ref, down_ref)
    both, upper, grad = both_ref[...], upper_ref[...], grad_ref[...]
    active = bfloat(gelu_tanh(upper))
    grad_upper = bfloat(matmul_right(grad, down_ref[...]) * gelu_slope(upper))
    before = jnp.where(step == 0, 0.0, partial_ref[...])
    partial_ref[...] = before + matmul_right(grad_upper, up_ref[...])
    grad_up = bfloat(matmul_left(both, grad_upper)).reshape(blocks, rows, model)
    grads_ref[:, pl.ds(pl.multiple_of(step * rows, 16), rows), :] = grad_up
    grad_down = bfloat(matmul_left(active, grad)).reshape(per_step, half, model)
    grads_ref[pl.ds(step * per_step, per_step), half : 2 * half, :] = grad_down


def hidden_backward(both, upper, grad_both, hidden):
    rows, model = both.shape
    blocks = lax.axis_size("dp") * lax.axis_size("ctx")
    if not by_fours():
        up, down = hidden_weights(hidden)
        active = bfloat(gelu_tanh(upper))
        grad_upper = bfloat(matmul_right(grad_both, down) * gelu_slope(upper))
        grad_up, grad_down = matmul_left(both, grad_upper), matmul_left(active, grad_both)
        parts = [
            grad_up[:, k : k + model].reshape(blocks, -1, model)
            for k in range(0, grad_up.shape[1], model)
        ]
        packed = jnp.concatenate(parts + [grad_down.reshape(blocks, -1, model)], 1)
        return matmul_right(grad_upper, up), bfloat(packed)
    packed = (hidden[0] if isinstance(hidden, tuple) else hidden).shape[1]
    size = blocks * packed * model
    steps = size // (2 * model * model)
    square = pltpu.VMEM((model, model), jnp.bfloat16)
    grads = (blocks, packed, model)
    place, arrays, specs = half_specs(hidden)
    return pl.pallas_call(
        hidden_back_kernel,
        grid_spec=pltpu.PrefetchScalarGridSpec(
            num_scalar_prefetch=1,
            grid=(steps,),
            in_specs=[
                whole_block(both.shape),
                pl.BlockSpec((rows, model), lambda j, _: (0, j)),
                whole_block(both.shape),
            ]
            + specs,
            out_specs=[whole_block(both.shape), whole_block(grads)],
            scratch_shapes=[square, square],
        ),
        out_shape=[
            jax.ShapeDtypeStruct((rows, model), jnp.float32),
            jax.ShapeDtypeStruct(grads, jnp.bfloat16),
        ],
        compiler_params=vmem(56),
        cost_estimate=small_cost(
            flops=4 * rows * size,
            bytes_accessed=4 * size + 4 * rows * steps * model,
            transcendentals=2 * rows * steps * model,
        ),
    )(place, both, upper, grad_both, *arrays)


def hidden_weights(hidden):
    blocks, packed, model = hidden.shape
    part = model // blocks
    parts = [hidden[:, k : k + part].reshape(model, model) for k in range(0, packed // 2, part)]
    return jnp.concatenate(parts, 1), hidden[:, packed // 2 :].reshape(-1, model)


def both_rows(values):
    return jnp.concatenate([values, swap(values)])


def own_rows(partial, pieces=1):
    rows = partial.shape[0] // 2
    return partial[:rows] + swap(partial[rows:])


def factored_sums(weight, gradient, row_stat):
    square = gradient * gradient + SQUARE_EPS
    rows_new = DECAY * row_stat + (1.0 - DECAY) * jnp.mean(square, -1)
    columns = jnp.sum(square, 0)
    scaled = jnp.sum(gradient * gradient / rows_new[:, None], 0)
    return rows_new, columns, scaled, jnp.sum(rows_new), jnp.sum(weight * weight)


def factored_new(weight, gradient, rows_new, col_stat, sums, row_count):
    columns, scaled, rows_sum, weight_sum = sums
    entries = row_count * weight.shape[1]
    cols_new = DECAY * col_stat + (1.0 - DECAY) * columns / row_count
    mean_rows = rows_sum / row_count
    update_sum = mean_rows * jnp.sum(scaled / cols_new)
    clipping = jnp.maximum(1.0, jnp.sqrt(update_sum / entries))
    size = jnp.maximum(SCALE_FLOOR, jnp.sqrt(weight_sum / entries))
    update = gradient * lax.rsqrt(rows_new[:, None] * cols_new[None, :] / mean_rows)
    return cols_new, weight - RELATIVE_RATE * size * (update / clipping)


def distinct_slots(ids, vocab_here):
    count = ids.shape[1]
    shard = ids // vocab_here
    earlier = jnp.arange(count)[None, :] < jnp.arange(count)[:, None]
    same = ids[:, :, None] == ids[:, None, :]
    first = ~jnp.any(same & earlier, -1)
    mates = (shard[:, :, None] == shard[:, None, :]) & first[:, None, :] & earlier
    rank = jnp.sum(mates.astype(jnp.int32), -1)
    slot = jnp.sum(jnp.where(same & first[:, None, :], rank[:, None, :], 0), -1)
    return slot, shard


def asked_ids(local, slot, here, room):
    places = jnp.arange(room, dtype=jnp.int32)[None, :, None]
    matches = (slot[:, None, :] == places) & here[:, None, :]
    return jnp.min(jnp.where(matches, local[:, None, :], 1 << 30), -1)


def picked_kernel(ids_ref, table_ref, out_ref, rows_ref, sem):
    count = rows_ref.shape[0]

    @pl.loop(0, count // 8)
    def _(i):
        for k in range(8):
            row = table_ref.at[pl.ds(ids_ref[8 * i + k], 1), :]
            pltpu.make_async_copy(row, rows_ref.at[pl.ds(8 * i + k, 1), :], sem).start()

    pltpu.make_async_copy(table_ref.at[pl.ds(0, count), :], rows_ref, sem).wait()
    out_ref[...] = bfloat(rows_ref[...])


def picked_rows(ids, table):
    shape = (ids.shape[0], table.shape[1])
    return pl.pallas_call(
        picked_kernel,
        grid_spec=pltpu.PrefetchScalarGridSpec(
            num_scalar_prefetch=1,
            grid=(1,),
            in_specs=[pl.BlockSpec(memory_space=pl.ANY)],
            out_specs=whole_block(shape),
            scratch_shapes=[pltpu.VMEM(shape, jnp.float32), pltpu.SemaphoreType.DMA],
        ),
        out_shape=jax.ShapeDtypeStruct(shape, jnp.bfloat16),
        compiler_params=vmem(24),
        cost_estimate=small_cost(
            flops=0, bytes_accessed=4 * shape[0] * shape[1], transcendentals=0
        ),
    )(ids, table)


def spilled_inside(ids, slot, room, vocab_here):
    local = ids - lax.axis_index("dp") * vocab_here
    return local, (local >= 0) & (local < vocab_here) & (slot >= room)


def spilled_rows(token_ids, slot, room, table):
    ids = at(token_ids, lax.axis_index("section"), 0)
    local, inside = spilled_inside(ids, slot, room, table.shape[0])
    rows = jnp.take(table, jnp.clip(local, 0, table.shape[0] - 1), axis=0)
    rows = jnp.where(inside[..., None], bfloat(rows), 0)
    return single(lax.psum_scatter(rows, "dp", scatter_dimension=0))


def spilled_grads(token_ids, slot, room, grad_start, vocab_here):
    ids = at(token_ids, lax.axis_index("section"), 0)
    local, inside = spilled_inside(ids, slot, room, vocab_here)
    column = lax.all_gather(grad_start, "dp")
    total = jax.ops.segment_sum(
        single(column.reshape(-1, column.shape[-1])),
        jnp.where(inside, local, vocab_here).reshape(-1),
        num_segments=vocab_here,
    )
    return single(lax.psum(bfloat(total), ("section", "ctx")))


def put_rows(ref, row, vector):
    for k in range(vector.shape[1] // LANES):
        ref[row + k : row + k + 1, :] = vector[:, k * LANES : (k + 1) * LANES]


def got_rows(ref, row, width):
    count = width // LANES
    return jnp.concatenate([ref[row + k : row + k + 1, :] for k in range(count)], 1)


def total(values):
    return jnp.sum(jnp.sum(values, 0, keepdims=True), 1, keepdims=True)


def pair(first, second):
    lanes = lax.broadcasted_iota(jnp.int32, (first.shape[0], LANES), 1)
    return jnp.where(lanes == 0, first, jnp.where(lanes == 1, second, 0.0))


def sum_rows(widths):
    starts = [0]
    for width in widths:
        starts.append(starts[-1] + 2 * width // LANES)
    scalars = -(-starts[-1] // 8) * 8
    return starts, scalars, scalars + 8


def layer_sums_kernel(*refs):
    grads, weights, stats = refs[:5], refs[5:10], refs[10:15]
    first_ref, second_ref, table_rows_ref, square_ref = refs[15:19]
    packed_ref, *new_refs = refs[19:]
    model = first_ref.shape[1]
    starts, scalars, table = sum_rows([ref.shape[1] for ref in grads[:4]])
    packed_ref[...] = jnp.zeros_like(packed_ref)
    for k in range(4):
        grad, weight = grads[k][...], weights[k][...]
        square = grad * grad
        full = square + SQUARE_EPS
        mean = jnp.sum(full, -1, keepdims=True) * (1.0 / grad.shape[1])
        new = DECAY * stats[k][...] + (1.0 - DECAY) * mean
        new_refs[k][...] = new
        count = grad.shape[1] // LANES
        put_rows(packed_ref, starts[k], jnp.sum(full, 0, keepdims=True))
        scaled = jnp.sum(square * (1.0 / new), 0, keepdims=True)
        put_rows(packed_ref, starts[k] + count, scaled)
        packed_ref[scalars + k : scalars + k + 1, :] = pair(total(new), total(weight * weight))
    grad, weight = grads[4][...], weights[4][...]
    new = DECAY * stats[4][...] + (1.0 - DECAY) * (grad * grad + SQUARE_EPS)
    new_refs[4][...] = new
    update = grad * lax.rsqrt(new)
    packed_ref[scalars + 4 : scalars + 8, :] = pair(
        jnp.sum(weight * weight, 1, keepdims=True), jnp.sum(update * update, 1, keepdims=True)
    )
    sums = first_ref[...] + second_ref[...]
    put_rows(packed_ref, table, jnp.sum(sums[0:8], 0, keepdims=True))
    put_rows(packed_ref, table + model // LANES, jnp.sum(sums[8:16], 0, keepdims=True))
    place = table + 2 * model // LANES
    packed_ref[place : place + 1, :] = pair(total(table_rows_ref[...]), total(square_ref[...]))


def layer_sums(grads, weights, stats, sums_first, sums_second, table_rows_new, squares):
    shapes = [stat.shape for stat in stats]
    _, _, table = sum_rows([grad.shape[1] for grad in grads[:4]])
    height = table + -(-(2 * sums_first.shape[1] // LANES + 1) // 8) * 8
    return pl.pallas_call(
        layer_sums_kernel,
        out_shape=[jax.ShapeDtypeStruct((height, LANES), jnp.float32)]
        + [jax.ShapeDtypeStruct(shape, jnp.float32) for shape in shapes],
        compiler_params=vmem(40),
        cost_estimate=small_cost(flops=0, bytes_accessed=1 << 22, transcendentals=0),
    )(*grads, *weights, *stats, sums_first, sums_second, table_rows_new, squares)


def factored_sizes(ref, start, scalar, col_stat, row_count):
    width = col_stat.shape[1]
    columns = got_rows(ref, start, width)
    scaled = got_rows(ref, start + width // LANES, width)
    rows_sum, weight_sum = ref[scalar : scalar + 1, 0:1], ref[scalar : scalar + 1, 1:2]
    new = DECAY * col_stat + (1.0 - DECAY) * columns * (1.0 / row_count)
    mean_rows = rows_sum * (1.0 / row_count)
    entries = row_count * width
    update_sum = mean_rows * jnp.sum(scaled / new, 1, keepdims=True)
    clipping = jnp.maximum(1.0, jnp.sqrt(update_sum * (1.0 / entries)))
    size = jnp.maximum(SCALE_FLOOR, jnp.sqrt(weight_sum * (1.0 / entries)))
    return new, mean_rows, RELATIVE_RATE * size / clipping


def layer_new_kernel(counts, totals_ref, *refs):
    grads, weights, rows, cols = refs[:5], refs[5:10], refs[10:15], refs[15:19]
    new_refs, col_refs = refs[19:24], refs[24:28]
    starts, scalars, _ = sum_rows([ref.shape[1] for ref in grads[:4]])
    for k in range(4):
        cols_new, mean_rows, rate = factored_sizes(
            totals_ref, starts[k], scalars + k, cols[k][...], counts[k]
        )
        col_refs[k][...] = cols_new
        scale = lax.rsqrt(rows[k][...] * cols_new / mean_rows)
        new_refs[k][...] = weights[k][...] - rate * (grads[k][...] * scale)
    model = counts[4]
    squares = totals_ref[scalars + 4 : scalars + 8, 0:1]
    updates = totals_ref[scalars + 4 : scalars + 8, 1:2]
    clipping = jnp.maximum(1.0, jnp.sqrt(updates * (1.0 / model)))
    size = jnp.maximum(SCALE_FLOOR, jnp.sqrt(squares * (1.0 / model)))
    update = grads[4][...] * lax.rsqrt(rows[4][...])
    new_refs[4][...] = weights[4][...] - RELATIVE_RATE * size / clipping * update


def layer_new(totals, grads, weights, rows, cols, counts):
    outs = [grad.shape for grad in grads] + [col.shape for col in cols]
    return pl.pallas_call(
        functools.partial(layer_new_kernel, counts),
        out_shape=[jax.ShapeDtypeStruct(shape, jnp.float32) for shape in outs],
        compiler_params=vmem(40),
        cost_estimate=small_cost(flops=0, bytes_accessed=1 << 22, transcendentals=0),
    )(totals, *grads, *weights, *rows, *cols)


def table_new_kernel(start, row_count, totals_ref, table_ref, grad_ref, rows_ref, cols_ref, *refs):
    new_ref, col_ref = refs
    scalar = start + 2 * cols_ref.shape[1] // LANES
    cols_new, mean_rows, rate = factored_sizes(totals_ref, start, scalar, cols_ref[...], row_count)
    col_ref[...] = cols_new
    across = rate * lax.rsqrt(cols_new)
    down = lax.rsqrt(rows_ref[...] / mean_rows)
    for k in range(rows_ref.shape[0]):
        place = slice(k * LANES, (k + 1) * LANES)
        scale = jnp.transpose(jnp.broadcast_to(down[k : k + 1, :], (LANES, LANES)))[:, 0:1]
        new_ref[place, :] = table_ref[place, :] - grad_ref[place, :] * scale * across


def table_new(totals, start, table, grad, rows_new, cols, row_count):
    vocab_here, model = table.shape
    block = row_block(vocab_here, 1024)
    rows = pl.BlockSpec((block, model), lambda i: (i, 0))
    return pl.pallas_call(
        functools.partial(table_new_kernel, start, row_count),
        grid=(vocab_here // block,),
        in_specs=[
            whole_block(totals.shape),
            rows,
            rows,
            pl.BlockSpec((block // LANES, LANES), lambda i: (i, 0)),
            whole_block(cols.shape),
        ],
        out_specs=[rows, whole_block(cols.shape)],
        out_shape=[
            jax.ShapeDtypeStruct(table.shape, jnp.float32),
            jax.ShapeDtypeStruct(cols.shape, jnp.float32),
        ],
        compiler_params=vmem(48),
        cost_estimate=small_cost(
            flops=4 * vocab_here * model,
            bytes_accessed=12 * vocab_here * model,
            transcendentals=0,
        ),
    )(totals, table, grad, rows_new, cols)


def body(
    token_ids,
    doc_lengths,
    picks,
    targets,
    table,
    table_rows,
    table_cols,
    attention_in,
    attention_in_rows,
    attention_in_cols,
    attention_out,
    attention_out_rows,
    attention_out_cols,
    hidden_in,
    hidden_in_rows,
    hidden_in_cols,
    hidden_out,
    hidden_out_rows,
    hidden_out_cols,
    gains,
    gains_stat,
):
    section = lax.axis_index("section")
    first = section == 0
    z, c = lax.axis_index("dp"), lax.axis_index("ctx")
    z_count, c_count = lax.axis_size("dp"), lax.axis_size("ctx")
    blocks = z_count * c_count
    model = table.shape[1]
    part = attention_in.shape[1]
    units = hidden_in.shape[2]
    half = units // (2 * blocks)
    wide = attention_in.shape[2]
    local_len = token_ids.shape[2]
    slots = picks.shape[2]
    vocab_here = table.shape[0]
    vocab_base = z * vocab_here

    low_in = bfloat(attention_in[0])
    low_out = jnp.concatenate(
        [bfloat(attention_out[0]), bfloat(gains[0]).T, jnp.zeros((part, wide - model - 4), jnp.bfloat16)], 1
    )
    barrier = lax.optimization_barrier
    at_p = jnp.concatenate(
        mine_first(
            jnp.where(first, low_in, low_out), swap(jnp.where(first, low_out, low_in))
        )
    )
    at_p, hidden_in_now, hidden_out_now = barrier((at_p, hidden_in, hidden_out))
    at_z = column_pieces(at_p)
    low_up = bfloat(hidden_in_now[0]).reshape(part, blocks, 2, half)
    low_down = bfloat(hidden_out_now[0])

    def unit_half(index):
        up = at(low_up, index, 2).reshape(part, -1, model)
        down = lax.dynamic_slice_in_dim(low_down, index * half, half, 0)
        return jnp.concatenate([up[:, k] for k in range(up.shape[1])] + [down])

    hid_p0, hid_p1 = mine_first(unit_half(section), swap(unit_half(1 - section)))

    room = local_len * 3 // 128 * 16

    hidden_w0 = lax.all_gather(hid_p0, BLOCKS, axis=0)

    if by_fours():
        slot, shard = distinct_slots(at(token_ids, section, 0), vocab_here)
        asked = asked_ids(at(token_ids, section, 0) - vocab_base, slot, shard == z, room)
        spilled = jnp.max(slot) >= room
        wanted = jnp.minimum(asked, vocab_here - 1).reshape(-1)
        place = at(jnp.where(slot < room, shard * room + slot, -1), z, 0)
        placed = bfloat(
            single(place[:, None] == jnp.arange(z_count * room, dtype=jnp.int32)[None, :])
        )
        notes = [asked.reshape(-1), spilled.astype(jnp.int32)[None], targets.reshape(-1)]
        notes = jnp.concatenate(notes)
        notes = jnp.stack(mine_first(notes, swap(notes)))
        x, y = plane_bits()
        beside = cross(notes, "ctx", 1)
        notes = jnp.stack([jnp.where(x == 0, notes, beside), jnp.where(x == 0, beside, notes)])
        above = cross(notes, "ctx", 2)
        notes = jnp.concatenate([jnp.where(y == 0, notes, above), jnp.where(y == 0, above, notes)])
        looked = picked_rows(after(wanted, at_p), table).reshape(z_count, room, model)
    else:
        my_ids = at(token_ids, section, 0) - vocab_base
        inside = (my_ids >= 0) & (my_ids < vocab_here)
        looked = jnp.take(table, jnp.clip(my_ids, 0, vocab_here - 1), axis=0)
        looked = jnp.where(inside[..., None], bfloat(looked), 0)
        notes = []

    at_z, hid_p1, looked, notes, table_now = barrier((at_z, hid_p1, looked, notes, table))
    at_c = column_join(at_p, at_z)
    at_n = plane_near(at_c)
    start_pieces = row_pieces(looked)
    low_first, square_first = lowered(table_now, None, 0, 3)
    at_n, start_pieces, low_first, hid_p1 = barrier((at_n, start_pieces, low_first, hid_p1))
    at_f = plane_far(at_n)
    table_low, square_second = lowered(table, low_first, 1, 3)
    at_f, table_low, at_c = barrier((at_f, table_low, at_c))
    at_w = plane_list(at_c, at_n, at_f)
    at_o = swap(at_w)
    table_low, square_third = lowered(table, table_low, 2, 3)
    at_o, table_low, hid_p1 = barrier((at_o, table_low, hid_p1))
    hid_z1 = column_pieces(hid_p1)
    if by_fours():
        target_notes = notes[:, 0, asked.size + 1 :]
        asked_all = notes[..., : asked.size].reshape(c_count, 2, z_count, room)
        local = jnp.minimum(asked_all.transpose(1, 2, 0, 3).reshape(-1), vocab_here)
        order = jnp.arange(local.shape[0], dtype=jnp.int32)
        local, order = lax.sort((local, order), num_keys=1)
        block = row_block(vocab_here, 1024)
        edges = jnp.arange(vocab_here // block + 1, dtype=jnp.int32) * block
        starts = jnp.sum((local[None, :] < edges[:, None]).astype(jnp.int32), 1)
    else:
        local = order = starts = notes
    in0, out0, gains0 = attention_weights(at_w, at_o, model, 0)
    if by_fours():
        spilled = jnp.max(notes[..., asked.size]) > 0
        found = column_join(at(looked, z, 0), start_pieces)
        start = matmul(placed, found.reshape(-1, model))
        start = start + lax.cond(
            spilled,
            lambda: spilled_rows(token_ids, slot, room, table),
            lambda: jnp.zeros_like(start),
        )
    else:
        target_notes = lax.all_gather(targets, "ctx")
        start = row_sum(looked, start_pieces)
    lengths = at(doc_lengths, section, 0)[0]
    my_picks = at(picks, section, 0)[0]

    places = c * local_len + jnp.arange(local_len, dtype=jnp.int32)
    reach = earlier_count(local_len)
    key_places = (c - reach) * local_len + jnp.arange((reach + 1) * local_len, dtype=jnp.int32)
    bias = pair_bias(lengths, places, key_places)
    pick_bias = pair_bias(lengths, c * local_len + jnp.maximum(my_picks, 0), key_places)
    onehot = (my_picks[:, None] == jnp.arange(local_len, dtype=jnp.int32)[None, :]).astype(
        jnp.bfloat16
    )

    normed0 = bfloat(layer_norm(start, gains0[0], gains0[1]))
    mixed_in = matmul(normed0, in0)
    query0 = bfloat(mixed_in[:, :model] * HD ** (-0.5))
    keyval0, query0, local, order, starts = barrier(
        (bfloat(mixed_in[:, model:]), query0, local, order, starts)
    )
    keyval0, query0 = barrier((key_rows(keyval0), query0))
    attended0 = attend(query0, keyval0, bias)
    mixed0 = start + matmul(attended0, out0)
    normed_two0 = bfloat(layer_norm(mixed0, gains0[2], gains0[3]))
    hid_z1, mixed0, normed_two0 = barrier((hid_z1, mixed0, normed_two0))
    hid_c1 = column_join(hid_p1, hid_z1)
    both0, hid_c1 = barrier((both_rows(normed_two0), hid_c1))
    hid_n1 = plane_near_half(hid_c1, 0)
    upper0, partial = hidden_forward(both0, hidden_w0)
    in1, out1, gains1 = attention_weights(at_w, at_o, model, 1)
    hid_n1, partial, in1, out1, hid_c1 = barrier((hid_n1, partial, in1, out1, hid_c1))
    hid_m1 = plane_near_half(hid_c1, 1)
    result0 = mixed0 + own_rows(partial)

    inputs1_low = bfloat(result0)
    inputs1 = single(inputs1_low)
    normed1 = bfloat(layer_norm(inputs1, gains1[0], gains1[1]))
    keyval1 = bfloat(matmul(normed1, in1[:, model:]))
    picked_normed = bfloat(matmul(onehot, normed1))
    picked = matmul(onehot, inputs1_low)
    query1 = bfloat(matmul(picked_normed, in1[:, :model]) * HD ** (-0.5))
    keyval1, query1 = barrier((keyval1, query1))
    keyval1, hid_n1, hid_m1 = barrier((key_rows(keyval1), hid_n1, hid_m1))
    hid_f1 = plane_far_half(hid_n1, hid_m1)
    hidden_w1 = plane_halves(hid_c1, (hid_n1, hid_m1), hid_f1)
    all_targets = target_notes.reshape((c_count,) + targets.shape).transpose(1, 2, 0, 3).reshape(-1)
    heads1 = query1.reshape(slots, -1, HD).transpose(1, 0, 2).reshape(-1, HD)
    heads1 = jnp.concatenate([heads1, jnp.zeros_like(heads1)], 1)
    pick_bias = jnp.tile(pick_bias, (model // HD, 1))

    def side_by_side(heads):
        return heads.reshape(-1, slots, HD).transpose(1, 0, 2).reshape(slots, model)

    attended1 = side_by_side(attend(heads1, keyval1, pick_bias)[:, :HD])
    mixed1 = picked + matmul(attended1, out1)
    normed_two1 = bfloat(layer_norm(mixed1, gains1[2], gains1[3]))
    both1 = both_rows(normed_two1)
    upper1, partial = hidden_forward(both1, hidden_w1)
    result1 = mixed1 + own_rows(partial)

    chosen_mine = gather_blocks(bfloat(result1)).reshape(-1, model)
    chosen = jnp.concatenate(mine_first(chosen_mine, swap(chosen_mine)))
    live = all_targets >= 0
    local_target = jnp.where(live, all_targets - vocab_base, DEAD)
    across = chosen.T
    stats = head_stats(across, local_target[None], table_low)

    def combine(one, two):
        top = jnp.maximum(one[0], two[0])
        both = one[1] * jnp.exp(one[0] - top) + two[1] * jnp.exp(two[0] - top)
        return jnp.stack([top, both, one[2] + two[2]])

    if by_fours():
        stats = stats[:3]
        one, two, three = (cross(stats, "dp", k) for k in (1, 2, 3))
        stats = combine(combine(stats, one), combine(two, three))
    else:
        stats = lax.scan(
            lambda total, share: (combine(total, share), None),
            jnp.stack([jnp.full_like(stats[0], MASKED), 0 * stats[0], 0 * stats[0]]),
            lax.all_gather(stats, "dp"),
        )[0]
    logsum = stats[0] + jnp.log(stats[1])
    loss_sum = jnp.sum(jnp.where(live, logsum - stats[2], 0.0))
    loss_count = jnp.sum(single(live))

    def own_slots(values):
        shape = (2, z_count, c_count, slots) + values.shape[1:]
        return at(at(values.reshape(shape), section, 0), c, 1).reshape((-1,) + values.shape[1:])

    grad_chosen = head_rows(
        own_slots(chosen), own_slots(local_target)[:, None], own_slots(logsum)[:, None], table_low
    )
    grad_result1 = scatter_rows(grad_chosen.reshape(z_count, slots, model))

    def attention_grads(grad_in, grad_out, grad_gains):
        grad_out = jnp.concatenate(
            [
                bfloat(grad_out),
                bfloat(grad_gains).T,
                jnp.zeros((model, wide - model - 4), jnp.bfloat16),
            ],
            1,
        )
        grad_in = bfloat(grad_in)
        return jnp.where(first, grad_in, grad_out), jnp.where(first, grad_out, grad_in)

    def attention_sum(kept, sent):
        return bfloat(single(kept) + single(sent)).reshape(blocks, part, wide)

    low = bfloat(grad_result1)
    partial, hidden_grads1 = hidden_backward(both1, upper1, both_rows(low), hidden_w1)
    hidden1 = scattered(hidden_grads1)
    _, pull = jax.vjp(layer_norm, mixed1, gains1[2], gains1[3])
    grad_mixed1, grad_gain2, grad_shift2 = pull(own_rows(partial))
    grad_mixed1 = grad_mixed1 + grad_result1
    grad_low = bfloat(grad_mixed1)
    grad_out1 = matmul_left(attended1, grad_low)
    grad_heads = bfloat(matmul_right(grad_low, out1)).reshape(slots, -1, HD)
    grad_heads = grad_heads.transpose(1, 0, 2).reshape(-1, HD)
    grad_heads = jnp.concatenate([grad_heads, jnp.zeros_like(grad_heads)], 1)
    grad_query, grad_keyval = attend_back(heads1, keyval1, pick_bias, grad_heads)
    grad_query = side_by_side(grad_query[:, :HD])
    grad_keyval = key_rows_sum(grad_keyval, key_rows_back(grad_keyval, local_len), local_len)
    grad_in1 = jnp.concatenate(
        [matmul_left(picked_normed, grad_query), matmul_left(normed1, grad_keyval)], 1
    )
    spread = jnp.dot(
        single(onehot).T,
        jnp.concatenate([matmul_right(grad_query, in1[:, :model]), grad_mixed1], 1),
        precision=lax.Precision.HIGHEST,
    )
    grad_normed = matmul_right(grad_keyval, in1[:, model:]) + spread[:, :model]
    _, pull = jax.vjp(layer_norm, inputs1, gains1[0], gains1[1])
    grad_inputs1, grad_gain1, grad_shift1 = pull(grad_normed)
    grad_result0 = single(bfloat(grad_inputs1 + spread[:, model:]))
    grad_gains1 = jnp.stack([grad_gain1, grad_shift1, grad_gain2, grad_shift2])
    kept1, sent1 = attention_grads(grad_in1, grad_out1, grad_gains1)

    low = bfloat(grad_result0)
    partial, hidden_grads0 = hidden_backward(both0, upper0, both_rows(low), hidden_w0)
    ups, downs = (0, 2 * part), (2 * part, half)
    partial, hidden_grads0, sent1 = barrier((own_rows(partial), hidden_grads0, swap(sent1)))
    up_s = half_first(hidden_grads0, ups) if by_fours() else ()
    _, pull = jax.vjp(layer_norm, mixed0, gains0[2], gains0[3])
    grad_mixed0, grad_gain2, grad_shift2 = pull(partial)
    grad_mixed0 = grad_mixed0 + grad_result0
    grad_low = bfloat(grad_mixed0)
    grad_out0 = matmul_left(attended0, grad_low)
    grad_query, grad_keyval = attend_back(
        query0, keyval0, bias, bfloat(matmul_right(grad_low, out0))
    )
    up_s, grad_query, grad_keyval = barrier((up_s, grad_query, grad_keyval))
    returned, hidden_grads0 = barrier((key_rows_back(grad_keyval, local_len), hidden_grads0))
    if by_fours():
        down_s = half_first(hidden_grads0, downs)
        up_k, up_h = half_kept(hidden_grads0, ups, up_s)
    grad_keyval = key_rows_sum(grad_keyval, returned, local_len)
    grad_mixed_in = jnp.concatenate([grad_query, grad_keyval], 1)
    grad_in0 = matmul_left(normed0, grad_mixed_in)
    _, pull = jax.vjp(layer_norm, start, gains0[0], gains0[1])
    grad_start, grad_gain1, grad_shift1 = pull(matmul_right(grad_mixed_in, in0))
    grad_start = bfloat(grad_start + grad_mixed0)
    grad_gains0 = jnp.stack([grad_gain1, grad_shift1, grad_gain2, grad_shift2])
    kept0, sent0 = attention_grads(grad_in0, grad_out0, grad_gains0)
    def head_part(grads, index, count):
        return head_table(
            chosen, across, local_target[None], logsum[None], table_low, grads, index, count
        )

    table_square = square_first + square_second + square_third
    if by_fours():
        sent = bfloat(matmul_left(placed, grad_start)).reshape(z_count, room, model)
        row_z = row_pieces(sent)
        chosen = after(chosen, sent)
        grad_head = head_part(None, 0, 3)
        row_z, grad_head, down_s, up_h = barrier((row_z, grad_head, down_s, up_h))
        column = column_join(at(sent, z, 0), row_z)
        other = swap(column)
        near = plane_near(column)
        up_t = half_send(up_h)
        down_k, down_h = half_kept(hidden_grads0, downs, down_s)
        grad_head = head_part(grad_head, 1, 3)
        near, grad_head, up_t, other, down_h, hidden1 = barrier(
            (near, grad_head, up_t, other, down_h, hidden1)
        )
        far = plane_far(near)
        up_v = half_column(up_k, up_t)
        up_q = row_pieces(up_v)
        grad_head = head_part(grad_head, 2, 3)
        grad_head = lax.while_loop(
            lambda carry: carry[0] < spilled.astype(jnp.int32),
            lambda carry: (
                carry[0] + 1,
                carry[1] + spilled_grads(token_ids, slot, room, grad_start, vocab_here),
            ),
            (jnp.zeros((), jnp.int32), grad_head),
        )[1]
        far, grad_head, down_h = barrier((far, grad_head, down_h))
        far = jnp.concatenate(far)
        others = swap((*near, far))
        down_t = half_send(down_h)
        attention_both = jnp.concatenate(
            [attention_sum(kept0, swap(sent0)), attention_sum(kept1, sent1)], 1
        )
        others, down_t, up_q, attention_both = barrier((others, down_t, up_q, attention_both))
        down_v = half_column(down_k, down_t)
        down_q = row_pieces(down_v)
        every = (0, 2 * part)
        at_s = half_first(attention_both, every)
        hidden0 = row_sum(up_v, up_q)
        pieces = (column, *near, far, other, *others)
        parts = (starts, local, order, pieces, grad_head, table_rows, block)
        grad_table, rows_new, sums_first = table_sums(*parts, None, 0, 2)
        down_q, at_s, grad_table, rows_new = barrier((down_q, at_s, grad_table, rows_new))
        at_k, at_h = half_kept(attention_both, every, at_s)
        at_t = half_send(at_h)
        grad_table, rows_new, sums_second = table_sums(*parts, (grad_table, rows_new), 1, 2)
        at_t, grad_table, rows_new = barrier((at_t, grad_table, rows_new))
        at_v = half_column(at_k, at_t)
        attention = row_sum(at_v, row_pieces(at_v))
        hidden0 = jnp.concatenate([hidden0, row_sum(down_v, down_q)])
    else:
        hidden0 = scattered(hidden_grads0)
        attention_both = jnp.concatenate(
            [attention_sum(kept0, swap(sent0)), attention_sum(kept1, sent1)], 1
        )
        attention = scattered(attention_both)
        column = lax.all_gather(grad_start, "dp").reshape(-1, model)
        local = jnp.where(inside, my_ids, vocab_here).reshape(-1)
        lookup_grad = jax.ops.segment_sum(single(column), local, num_segments=vocab_here)
        lookup_grad = single(lax.psum(bfloat(lookup_grad), ("section", "ctx")))
        grad_table = head_part(None, 0, 1) + lookup_grad
        table_sum = (
            *factored_sums(table, grad_table, table_rows)[:4],
            jnp.sum(table_square),
        )

    grads0, grads1 = (attention[:part], hidden0), (attention[part:], hidden1)
    owned, other = [], []
    for one, two in zip(grads0, grads1):
        owned.append(jnp.where(first, one, two))
        other.append(swap(jnp.where(first, two, one)))
    shard_in, shard_out = mine_first(owned[0], other[0])
    shard_gains = shard_out[:, model : model + 4].T
    shard_out = shard_out[:, :model]
    halves = jnp.stack(mine_first(owned[1], other[1]))
    ups = units // 2 // model
    shard_up = halves[:, : ups * part].reshape(2, ups, part, model).transpose(2, 0, 1, 3)
    shard_up = shard_up.reshape(part, 2, blocks, half).transpose(0, 2, 1, 3).reshape(part, units)
    shard_down = halves[:, ups * part :].reshape(2 * half, model)

    if by_fours():
        grads = (shard_in, shard_out, shard_up, shard_down, shard_gains)
        weights = (attention_in[0], attention_out[0], hidden_in[0], hidden_out[0], gains[0])
        rows = (attention_in_rows, attention_out_rows, hidden_in_rows, hidden_out_rows)
        rows = [stat.reshape(-1, 1) for stat in rows] + [gains_stat[0]]
        sums, *rows_news = layer_sums(
            grads, weights, rows, sums_first, sums_second, rows_new, table_square
        )
        sums = summed(sums, ("dp",))
        _, _, table_start = sum_rows([grad.shape[1] for grad in grads[:4]])
        layer_totals = summed(sums[:table_start], ("ctx",))
        table_news, table_cols_new = table_new(
            sums, table_start, table, grad_table, rows_new, table_cols[None], vocab_here * z_count
        )
        cols = (attention_in_cols, attention_out_cols, hidden_in_cols, hidden_out_cols)
        *news, in_cols, out_cols, up_cols, down_cols = layer_new(
            layer_totals, grads, weights, rows_news, cols, (model, model, model, units, model)
        )
        layered = []
        for k, cols_new in enumerate((in_cols, out_cols, up_cols, down_cols)):
            layered += [grads[k][None], rows_news[k].reshape(1, -1), cols_new, news[k][None]]
        return (
            loss_sum,
            loss_count,
            grad_table,
            rows_new.reshape(-1),
            table_cols_new[0],
            table_news,
            *layered,
            shard_gains[None],
            rows_news[4][None],
            news[4][None],
        )
    entries = [
        (table, grad_table, table_rows, table_cols, vocab_here * z_count),
        (attention_in[0], shard_in, attention_in_rows[0], attention_in_cols[0], model),
        (attention_out[0], shard_out, attention_out_rows[0], attention_out_cols[0], model),
        (hidden_in[0], shard_up, hidden_in_rows[0], hidden_in_cols[0], model),
        (hidden_out[0], shard_down, hidden_out_rows[0], hidden_out_cols[0], units),
    ]
    sums = [table_sum] + [factored_sums(*entry[:3]) for entry in entries[1:]]
    gain_weight = gains[0]
    gain_stat_new = DECAY * gains_stat[0] + (1.0 - DECAY) * (shard_gains * shard_gains + SQUARE_EPS)
    gain_update = shard_gains * lax.rsqrt(gain_stat_new)

    def packed(group):
        rows = []
        for item in group:
            flat = item.reshape(-1)
            if flat.shape[0] % LANES:
                flat = jnp.pad(flat, (0, LANES - flat.shape[0]))
            rows.append(flat.reshape(-1, LANES))
        return jnp.concatenate(rows), [item.shape for item in group]

    def unpacked(rows, shapes):
        items, start = [], 0
        for shape in shapes:
            size = 1
            for length in shape:
                size *= length
            count = -(-size // LANES)
            items.append(rows[start : start + count].reshape(-1)[:size].reshape(shape))
            start += count
        return items

    table_group, table_shapes = packed(sums[0][1:])
    layer_group, layer_shapes = packed(
        [item for entry in sums[1:] for item in entry[1:]]
        + [jnp.sum(gain_weight * gain_weight, -1), jnp.sum(gain_update * gain_update, -1)]
    )
    everything = summed(jnp.concatenate([table_group, layer_group]), ("dp",))
    table_totals = unpacked(everything[: table_group.shape[0]], table_shapes)
    layer_parts = unpacked(summed(everything[table_group.shape[0] :], ("ctx",)), layer_shapes)
    groups = [table_totals] + [layer_parts[4 * k : 4 * k + 4] for k in range(4)]
    gain_squares, gain_update_sums = layer_parts[16:]
    outs = []
    for (weight, gradient, _, col_stat, row_count), own, group in zip(entries, sums, groups):
        cols_new, new = factored_new(weight, gradient, own[0], col_stat, group, row_count)
        outs.append((gradient, own[0], cols_new, new))
    gain_clipping = jnp.maximum(1.0, jnp.sqrt(gain_update_sums / model))
    gain_size = jnp.maximum(SCALE_FLOOR, jnp.sqrt(gain_squares / model))
    gain_new = gain_weight - RELATIVE_RATE * gain_size[:, None] * (
        gain_update / gain_clipping[:, None]
    )
    layered = [item[None] for out in outs[1:] for item in out]
    return (
        loss_sum,
        loss_count,
        *outs[0],
        *layered,
        shard_gains[None],
        gain_stat_new[None],
        gain_new[None],
    )


def solution(mesh):
    rows = P("section", BLOCKS, None)
    row = P("section", BLOCKS)
    shared = P("section", None)
    side = P("section", None, BLOCKS)
    matrix_in = (rows, row, shared)
    matrix_out = (rows, row, shared, rows)
    placed = (
        P(None, None, "ctx"),
        P(None, "dp", None),
        P(None, "dp", "ctx"),
        P(None, None, "ctx"),
        P("dp", None),
        P("dp"),
        P(),
        *(matrix_in * 4),
        side,
        side,
    )
    return jax.shard_map(
        body,
        mesh=mesh,
        in_specs=placed,
        out_specs=(
            P(),
            P(),
            P("dp", None),
            P("dp"),
            P(),
            P("dp", None),
            *(matrix_out * 4),
            side,
            side,
            side,
        ),
        check_vma=False,
    )
```

time: 1010 us -> 667 us (0.66)
  other arithmetic: 311 us -> 66.4 us
  Pallas kernels: 0 us -> 240 us
  matrix products: 135 us -> 16.6 us
  waiting for transfers between devices: 225 us -> 123 us
  local copies, waits for them, and re-layouts: 135 us -> 66.5 us
  starting transfers between devices: 161 us -> 117 us
  blocking collectives: 17 us -> 0 us
    pallas_call x0 -> x24, Pallas kernels: none -> 240 us  [the longest x2 42.9 us: table_sums(): pl.pallas_call(functools.partial(table_sums_kernel, first), grid_spec=plt...]
    ppermute x85 -> x67, waiting for transfers between devices: 208 us -> 86.7 us  [cross(): lax.ppermute(values, axis, [(i, i ^ bits) for i in range(lax.axis_size(ax...]
    scatter-add x1 -> x0, other arithmetic: 82.8 us -> none  [body(): jax.ops.segment_sum(single(looked_grads), local, num_segments=vocab_here)]
    reduce_sum x28 -> x3, other arithmetic: 67.6 us -> 1.66 us  [the longest x1 0.8 us: body(): starts = jnp.sum((local[None, :] < edges[:, None]).astype(jnp.int32), 1)]
    ppermute x85 -> x67, starting transfers between devices: 140 us -> 94.7 us  [cross(): lax.ppermute(values, axis, [(i, i ^ bits) for i in range(lax.axis_size(ax...]
    sub x7 -> x2, other arithmetic: 41.2 us -> 0.52 us  [the longest x1 0.52 us: pair_bias(): query_places[:, None] - WINDOW]
    dot_general x10 -> x5, matrix products: 41.9 us -> 3.79 us  [matmul_right(): lax.dot_general(left, right, (((1,), (1,)), ((), ())), preferred_element_...]
    dot_general x10 -> x6, matrix products: 41.3 us -> 6.59 us  [matmul_left(): lax.dot_general(left, right, (((0,), (0,)), ((), ())), preferred_element_...]
  transfers between devices with their start and end apart: 111 -> 101, of which waited for: 38 -> 39; matrix products, arithmetic and copies ran while one was open for 34% -> 17% of each run, Pallas kernels for 0% -> 29%
where the time goes in v2:
time: 667 us; the launch traced here: 657 us
  Pallas kernels  240 us (36%)
  waiting for transfers between devices  123 us (18%)
  starting transfers between devices  117 us (18%)
  local copies, waits for them, and re-layouts  66.5 us (10%)
  other arithmetic  66.4 us (10%)
  between operations  20.6 us (3%)
  matrix products  16.6 us (2%)
  loops' own time  7.46 us (1%)
    ppermute x67, starting transfers between devices, cross(): lax.ppermute(values, axis, [(i, i ^ bits) for i in range(lax.axis_size(ax...  94.7 us
    ppermute x67, waiting for transfers between devices, cross(): lax.ppermute(values, axis, [(i, i ^ bits) for i in range(lax.axis_size(ax...  86.7 us
    pallas_call x2, Pallas kernels, table_sums(): pl.pallas_call(functools.partial(table_sums_kernel, first), grid_spec=plt...  42.9 us
    pallas_call x1, Pallas kernels, table_new(): pl.pallas_call(functools.partial(table_new_kernel, start, row_count), gri...  37.8 us
    pallas_call x3, Pallas kernels, head_table(): pl.pallas_call(functools.partial(head_table_kernel, first), grid=(last -...  34.7 us
    pallas_call x3, Pallas kernels, lowered(): pl.pallas_call(lower_kernel, grid=(last - first,), in_specs=[rows] + ([]...  22.7 us
    pallas_call x2, Pallas kernels, hidden_backward(): pl.pallas_call(hidden_back_kernel, grid_spec=pltpu.PrefetchScalarGridSpec...  20.7 us
    ppermute x8, starting transfers between devices, shifted(): lax.ppermute(values, axis, [(i, i + distance) for i in devices if i + dis...  18.6 us
  transfers between devices with their start and end apart: 101, of which 39 were waited for; matrix products, arithmetic and copies ran while one was open for 17% of the time, Pallas kernels for 29%

profile of v2, /device:TPU:0, one launch (start us, length us, event | category | flops | bytes accessed | tf_op | source)
XLA Modules:
  0.0 656.9 jit_solution(8667453840143786725)
XLA Ops:
  14.9 2.6 collective-permute-start.6
  19.1 2.1 collective-permute-start.7
  24.0 4.2 collective-permute-start.3
  29.3 2.6 dynamic-slice_reduce_fusion
  33.2 8.9 %shard_map.396 = bf16[384,768]{1,0:T(8,128)(2,1)S(1)} custom-call(s32[384]{0:T(512)S(1)} %broadcast_minimum_fusion.ids_ref, f32[12288,768]{1,0:T(8,128)} %table_ref.8), custom_call_target="tpu_custom_call" | custom-call | bytes 73728 | tf_op jit(solution)/shard_map/pallas_call | solution.py:908
  51.0 4.4 collective-permute-start.12
  55.9 7.6 %shard_map.397 = (bf16[12288,768]{1,0:T(8,128)(2,1)}, f32[8,768]{1,0:T(8,128)S(1)}) custom-call(f32[12288,768]{1,0:T(8,128)} %table_ref.8), custom_call_target="tpu_custom_call" | custom-call | flops 393216 | bytes 1179648 | tf_op jit(solution)/shard_map/pallas_call | solution.py:444
  63.7 5.8 sort.15
  70.3 4.2 collective-permute-done.11
  75.2 7.6 %shard_map.398 = (bf16[12288,768]{1,0:T(8,128)(2,1)}, f32[8,768]{1,0:T(8,128)S(1)}) custom-call(f32[12288,768]{1,0:T(8,128)} %table_ref.8, bf16[12288,768]{1,0:T(8,128)(2,1)} %get-tuple-element.239.refs_0_), custom_call_target="tpu_custom_call", output_to_operand_aliasing={{0}: (1, {})} | custom-call | flops 393216 | bytes 1179648 | tf_op jit(solution)/shard_map/pallas_call | solution.py:444
  86.1 7.3 %collective-permute-done.14 = bf16[2,96,896]{2,1,0:T(8,128)(2,1)S(1)} collective-permute-done((bf16[2,96,896]{2,1,0:T(8,128)(2,1)S(1)}, bf16[2,96,896]{2,1,0:T(8,128)(2,1)S(1)}, u32[]{:S(2)}, u32[]{:S(2)}) %collective-permute-start.14) | collective-permute-done | bytes 344096 | tf_op jit(solution)/shard_map/ppermute | solution.py:68
  93.5 3.1 collective-permute-done.13
  98.0 7.5 %shard_map.399 = (bf16[12288,768]{1,0:T(8,128)(2,1)}, f32[8,768]{1,0:T(8,128)S(1)}) custom-call(f32[12288,768]{1,0:T(8,128)} %table_ref.8, bf16[12288,768]{1,0:T(8,128)(2,1)} %get-tuple-element.244.refs_0_), custom_call_target="tpu_custom_call", output_to_operand_aliasing={{0}: (1, {})} | custom-call | flops 393216 | bytes 1179648 | tf_op jit(solution)/shard_map/pallas_call | solution.py:444
  108.3 2.2 collective-permute-start.23
  110.5 3.6 collective-permute-start.22
  114.5 3.4 collective-permute-start.21
  119.0 7.7 %shard_map.401 = bf16[256,768]{1,0:T(8,128)(2,1)S(1)} custom-call(bf16[256,768]{1,0:T(8,128)(2,1)S(1)} %fusion.24.query_ref, bf16[768,128]{1,0:T(8,128)(2,1)S(1)} %pad_maximum_fusion.16.keyval_ref, f32[256,768]{1,0:T(8,128)S(1)} %and_select_fusion.1.bias_ref), custom_call_target="tpu_custom_call" | custom-call | flops 37748736 | bytes 98304 | tf_op jit(solution)/shard_map/pallas_call | solution.py:367
  128.0 4.5 collective-permute-done.21
  132.5 26.2 %collective-permute-done.20 = bf16[192,768]{1,0:T(8,128)(2,1)S(1)} collective-permute-done((bf16[192,768]{1,0:T(8,128)(2,1)S(1)}, bf16[192,768]{1,0:T(8,128)(2,1)S(1)}, u32[]{:S(2)}, u32[]{:S(2)}) %collective-permute-start.20) | collective-permute-done | bytes 294944 | tf_op jit(solution)/shard_map/ppermute | solution.py:68
  168.7 6.1 shard_map.402
  188.2 2.2 convert_reduce_fusion.1
  192.5 3.1 collective-permute-start.29
  195.6 3.8 collective-permute-start.28
  200.3 2.5 collective-permute-done.29
  211.7 2.9 collective-permute-start.34
  217.9 9.3 %collective-permute-done.34.refs_7_ = bf16[2,192,768]{2,1,0:T(8,128)(2,1)S(1)} collective-permute-done((bf16[2,192,768]{2,1,0:T(8,128)(2,1)}, bf16[2,192,768]{2,1,0:T(8,128)(2,1)S(1)}, u32[]{:S(2)}, u32[]{:S(2)}) %collective-permute-start.34) | collective-permute-done | bytes 589856 | tf_op jit(solution)/shard_map/ppermute | solution.py:68
  228.6 3.4 shard_map.405
  235.4 3.0 collective-permute-start.36
  241.1 2.7 collective-permute-start.41
  251.5 18.0 %shard_map.406 = f32[8,512]{1,0:T(8,128)S(1)} custom-call(bf16[768,512]{1,0:T(8,128)(2,1)S(1)} %get-tuple-element.577.chosen_ref.across_ref, s32[1,512]{1,0:T(1,128)S(1)} %select_n.875.target_ref, bf16[12288,768]{1,0:T(8,128)(2,1)} %get-tuple-element.287.low_ref), custom_call_target="tpu_custom_call" | custom-call | flops 603979776 | bytes 1179648 | tf_op jit(solution)/shard_map/pallas_call | solution.py:490
  269.6 2.2 collective-permute-start.45
  274.0 2.3 copy.242
  279.4 15.6 %shard_map.407 = f32[64,768]{1,0:T(8,128)S(1)} custom-call(bf16[64,768]{1,0:T(8,128)(2,1)S(1)} %bitcast.393, s32[64,1]{1,0:T(8,128)S(1)} %broadcast_in_dim_reshape.16.target_ref, f32[64,1]{1,0:T(8,128)S(1)} %broadcast_in_dim_reshape.17.logsum_ref, bf16[12288,768]{1,0:T(8,128)(2,1)} %get-tuple-element.287.low_ref), custom_call_target="tpu_custom_call" | custom-call | flops 150994944 | bytes 1179648 | tf_op jit(solution)/shard_map/pallas_call | solution.py:526
  299.0 2.7 collective-permute-done.48
  304.3 7.9 %shard_map.408 = (f32[32,768]{1,0:T(8,128)}, bf16[16,192,768]{2,1,0:T(8,128)(2,1)}) custom-call(s32[1]{0:T(128)} %bitcast.36.place_ref, bf16[32,768]{1,0:T(8,128)(2,1)} %copy-done.36, f32[32,1536]{1,0:T(8,128)} %copy-done.42, bf16[32,768]{1,0:T(8,128)(2,1)} %pad_maximum_fusion.21.grad_ref, bf16[4,192,768]{2,1,0:T(8,128)(2,1)} %copy-done.2, ...), custom_call_target="tpu_custom_call" | custom-call | flops 18874368 | bytes 602112 | tf_op jit(solution)/shard_map/pallas_call | solution.py:812
  331.8 4.5 collective-permute-done.51
  343.2 12.8 %shard_map.410 = (f32[512,768]{1,0:T(8,128)}, bf16[16,192,768]{2,1,0:T(8,128)(2,1)}) custom-call(s32[1]{0:T(128)} %constant.388.clone.1.place_ref, bf16[512,768]{1,0:T(8,128)(2,1)} %copy-done.3, f32[512,1536]{1,0:T(8,128)} %copy-done.21, bf16[512,768]{1,0:T(8,128)(2,1)} %pad_maximum_fusion.5.grad_ref, bf16[4,4,192,768]{3,2,1,0:T(8,128)(2,1)} %bitcast.408, ...), custom_call_target="tpu_custom_call" | custom-call | flops 301989888 | bytes 786432 | tf_op jit(solution)/shard_map/pallas_call | solution.py:812
  363.8 3.4 collective-permute-start.56
  370.4 13.6 %shard_map.411 = (bf16[256,768]{1,0:T(8,128)(2,1)S(1)}, f32[768,128]{1,0:T(8,128)S(1)}) custom-call(bf16[256,768]{1,0:T(8,128)(2,1)S(1)} %copy-done.18, bf16[768,128]{1,0:T(8,128)(2,1)S(1)} %copy-done.26, f32[256,768]{1,0:T(8,128)S(1)} %and_select_fusion.1.bias_ref, bf16[256,768]{1,0:T(8,128)(2,1)S(1)} %convolution_convert_fusion.5.grad_ref), custom_call_target="tpu_custom_call" | custom-call | flops 94371840 | bytes 98304 | tf_op jit(solution)/shard_map/pallas_call | solution.py:412
  389.3 3.2 collective-permute-done.59
  392.6 2.4 collective-permute-done.58
  398.0 2.2 collective-permute-start.62
  400.3 2.2 collective-permute-start.60
  411.8 2.3 broadcast_select_fusion
  414.1 11.5 %shard_map.412.refs_0_ = f32[12288,768]{1,0:T(8,128)} custom-call(bf16[512,768]{1,0:T(8,128)(2,1)S(1)} %copy.249.chosen_ref, bf16[768,512]{1,0:T(8,128)(2,1)S(1)} %get-tuple-element.577.chosen_ref.across_ref, s32[1,512]{1,0:T(1,128)S(1)} %copy-done.44, f32[1,512]{1,0:T(1,128)S(1)} %log_add_fusion.logsum_ref, bf16[12288,768]{1,0:T(8,128)(2,1)} %get-tuple-element.287.low_ref), custom_call_target="tpu_custom_call" | custom-call | flops 402653184 | bytes 1179648 | tf_op jit(solution)/shard_map/pallas_call | solution.py:565
  433.7 11.6 %shard_map.413.refs_0_ = f32[12288,768]{1,0:T(8,128)} custom-call(bf16[512,768]{1,0:T(8,128)(2,1)S(1)} %copy.249.chosen_ref, bf16[768,512]{1,0:T(8,128)(2,1)S(1)} %get-tuple-element.577.chosen_ref.across_ref, s32[1,512]{1,0:T(1,128)S(1)} %copy-done.44, f32[1,512]{1,0:T(1,128)S(1)} %log_add_fusion.logsum_ref, ...), custom_call_target="tpu_custom_call", output_to_operand_aliasing={{}: (5, {})} | custom-call | flops 402653184 | bytes 1179648 | tf_op jit(solution)/shard_map/pallas_call | solution.py:565
  445.3 12.6 %reduce-scatter.5.cloned.1.call-done = bf16[1,192,768]{2,1,0:T(8,128)(2,1)} async-done(((bf16[16,192,768]{2,1,0:T(8,128)(2,1)}), bf16[1,192,768]{2,1,0:T(8,128)(2,1)}) %reduce-scatter.5.cloned.1.call-update) | async-done | bytes 294928 | tf_op jit(solution)/shard_map/reduce_scatter | solution.py:209
  469.9 11.5 %shard_map.414 = f32[12288,768]{1,0:T(8,128)} custom-call(bf16[512,768]{1,0:T(8,128)(2,1)S(1)} %copy.249.chosen_ref, bf16[768,512]{1,0:T(8,128)(2,1)S(1)} %get-tuple-element.577.chosen_ref.across_ref, s32[1,512]{1,0:T(1,128)S(1)} %copy-done.44, f32[1,512]{1,0:T(1,128)S(1)} %log_add_fusion.logsum_ref, ...), custom_call_target="tpu_custom_call", output_to_operand_aliasing={{}: (5, {})} | custom-call | flops 402653184 | bytes 1179648 | tf_op jit(solution)/shard_map/pallas_call | solution.py:565
  481.6 2.3 collective-permute-start.78
  483.9 7.4 %while.10 = (s32[]{:T(128)}, f32[12288,768]{1,0:T(8,128)}, pred[]{:T(512)}, s32[2,4,256]{2,1,0:T(4,128)S(1)}, s32[4,256]{1,0:T(4,128)S(1)}, /*index=5*/bf16[256,...) while((s32[]{:T(128)}, f32[12288,768]{1,0:T(8,128)}, ...), condition=%wide.region_43.44_spmd, body=%wide.region_40.43_spmd.sunk | while | flops 39328784 | bytes 309494080 | solution.py:1423
  496.0 5.7 add_convert_fusion.1
  511.3 2.2 collective-permute-start.83
  513.4 2.3 collective-permute-start.82
  515.7 21.4 %shard_map.415 = (f32[12288,768]{1,0:T(8,128)}, f32[96,128]{1,0:T(8,128)}, f32[16,768]{1,0:T(8,128)}) custom-call(s32[2]{0:T(128)} %copy-done.55, s32[13]{0:T(128)} %convert_reduce_fusion.2.starts_ref, s32[3072]{0:T(1024)} %copy-done.130, s32[3072]{0:T(1024)} %get-tuple-element.334.order_ref, f32[12288,768]{1,0:T(8,128)} %get-tuple-element.335.head_ref, ...), custom_call_target="tpu_custom_call" | custom-call | flops 2359296 | bytes 2359296 | tf_op jit(solution)/shard_map/pallas_call | solution.py:644
  541.1 21.6 %shard_map.416 = (f32[12288,768]{1,0:T(8,128)}, f32[96,128]{1,0:T(8,128)}, f32[16,768]{1,0:T(8,128)}) custom-call(s32[2]{0:T(128)} %copy-done.55, s32[13]{0:T(128)} %convert_reduce_fusion.2.starts_ref, s32[3072]{0:T(1024)} %copy-done.130, s32[3072]{0:T(1024)} %get-tuple-element.334.order_ref, ...), custom_call_target="tpu_custom_call", output_to_operand_aliasing={{0}: (14, {}), {1}: (15, {})} | custom-call | flops 2359296 | bytes 2359296 | tf_op jit(solution)/shard_map/pallas_call | solution.py:644
  563.3 3.1 collective-permute-start.89
  567.7 5.7 collective-permute-done.88
  573.4 5.6 collective-permute-done.89
  582.6 2.3 reshape.818.refs_2_
  588.6 2.4 collective-permute-start.95
  591.0 2.9 collective-permute-start.94
  594.7 3.5 collective-permute-done.94
  602.1 3.0 broadcast_in_dim_reshape.14
  608.4 37.8 %shard_map.418 = (f32[12288,768]{1,0:T(8,128)}, f32[1,768]{1,0:T(1,128)S(1)}) custom-call(f32[112,128]{1,0:T(8,128)S(1)} %add_add_fusion.4.totals_ref, f32[12288,768]{1,0:T(8,128)} %table_ref.8, f32[12288,768]{1,0:T(8,128)} %get-tuple-element.458.grad_ref, f32[96,128]{1,0:T(8,128)S(1)} %copy-done.37, f32[1,768]{1,0:T(1,128)S(1)} %broadcast_in_dim.227.cols_ref), custom_call_target="tpu_custom_call" | custom-call | flops 2359296 | bytes 7077888 | tf_op jit(solution)/shard_map/pallas_call | solution.py:1084
  (865 shorter events, 210.2 us)
Async XLA Ops:
  24.0 19.1 %collective-permute-start.3 = (bf16[96,896]{1,0:T(8,128)(2,1)S(1)}, bf16[96,896]{1,0:T(8,128)(2,1)S(1)}, u32[]{:S(2)}, u32[]{:S(2)}) collective-permute-start(bf16[96,896]{1,0:T(8,128)(2,1)S(1)} %pad_maximum_fusion.18), channel_id=1, source_target_pairs={{0,12},{4,8},{8,4},{12,0},{1,13},{5,9},{9,5},{13,1},{2,14},{6,10},... | collective-permute-start | bytes 516104 | tf_op jit(solution)/shard_map/ppermute | solution.py:68
  28.2 14.9 %collective-permute-start.2 = (bf16[96,896]{1,0:T(8,128)(2,1)S(1)}, bf16[96,896]{1,0:T(8,128)(2,1)S(1)}, u32[]{:S(2)}, u32[]{:S(2)}) collective-permute-start(bf16[96,896]{1,0:T(8,128)(2,1)S(1)} %pad_maximum_fusion.18), channel_id=1, source_target_pairs={{0,8},{4,12},{8,0},{12,4},{1,9},{5,13},{9,1},{13,5},{2,10},{6,14},... | collective-permute-start | bytes 516104 | tf_op jit(solution)/shard_map/ppermute | solution.py:68
  28.2 14.9 %collective-permute-start.1 = (bf16[96,896]{1,0:T(8,128)(2,1)S(1)}, bf16[96,896]{1,0:T(8,128)(2,1)S(1)}, u32[]{:S(2)}, u32[]{:S(2)}) collective-permute-start(bf16[96,896]{1,0:T(8,128)(2,1)S(1)} %pad_maximum_fusion.18), channel_id=1, source_target_pairs={{0,4},{4,0},{8,12},{12,8},{1,5},{5,1},{9,13},{13,9},{2,6},{6,2},{1... | collective-permute-start | bytes 516104 | tf_op jit(solution)/shard_map/ppermute | solution.py:68
  44.6 124.2 %all-gather.7.cloned.1.call-start = ((), (), s32[]{:S(2)}) async-start(), calls=%async_computation.4 | async-start | bytes 5013504 | tf_op jit(solution)/shard_map/all_gather | solution.py:1170
  45.1 412.7 %reduce-scatter.5.cloned.1.call-start = ((), (), s32[]{:S(2)}) async-start(), calls=%async_computation.3 | async-start | bytes 5013504 | tf_op jit(solution)/shard_map/reduce_scatter | solution.py:209
  47.6 26.8 %collective-permute-start.9 = (bf16[4,96,896]{2,1,0:T(8,128)(2,1)S(1)}, bf16[4,96,896]{2,1,0:T(8,128)(2,1)S(1)}, u32[]{:S(2)}, u32[]{:S(2)}) collective-permute-start(bf16[4,96,896]{2,1,0:T(8,128)(2,1)S(1)} %pad_maximum_fusion.6.refs_0_), channel_id=1, source_target_pairs={{0,2},{1,3},{2,0},{3,1},{4,6},{5,7},{6,4},{7,5},{8,10},{9,11},{10,... | collective-permute-start | bytes 2064392 | tf_op jit(solution)/shard_map/ppermute | solution.py:68
  49.0 25.5 %collective-permute-start.8 = (bf16[4,96,896]{2,1,0:T(8,128)(2,1)S(1)}, bf16[4,96,896]{2,1,0:T(8,128)(2,1)S(1)}, u32[]{:S(2)}, u32[]{:S(2)}) collective-permute-start(bf16[4,96,896]{2,1,0:T(8,128)(2,1)S(1)} %pad_maximum_fusion.6.refs_0_), channel_id=1, source_target_pairs={{0,1},{1,0},{2,3},{3,2},{4,5},{5,4},{6,7},{7,6},{8,9},{9,8},{10,11... | collective-permute-start | bytes 2064392 | tf_op jit(solution)/shard_map/ppermute | solution.py:68
  51.0 19.3 %collective-permute-start.12 = (bf16[96,768]{1,0:T(8,128)(2,1)}, bf16[96,768]{1,0:T(8,128)(2,1)S(1)}, u32[]{:S(2)}, u32[]{:S(2)}) collective-permute-start(bf16[96,768]{1,0:T(8,128)(2,1)} %get-tuple-element.598), channel_id=1, source_target_pairs={{0,12},{4,8},{8,4},{12,0},{1,13},{5,9},{9,5},{13,1},{2,14},{6,10},... | collective-permute-start | bytes 442376 | tf_op jit(solution)/shard_map/ppermute | solution.py:68
  55.4 19.1 %collective-permute-start.11 = (bf16[96,768]{1,0:T(8,128)(2,1)S(1)}, bf16[96,768]{1,0:T(8,128)(2,1)S(1)}, u32[]{:S(2)}, u32[]{:S(2)}) collective-permute-start(bf16[96,768]{1,0:T(8,128)(2,1)S(1)} %get-tuple-element.599), channel_id=1, source_target_pairs={{0,8},{4,12},{8,0},{12,4},{1,9},{5,13},{9,1},{13,5},{2,10},{6,14},... | collective-permute-start | bytes 442376 | tf_op jit(solution)/shard_map/ppermute | solution.py:68
  55.7 18.7 %collective-permute-start.10 = (bf16[96,768]{1,0:T(8,128)(2,1)S(1)}, bf16[96,768]{1,0:T(8,128)(2,1)S(1)}, u32[]{:S(2)}, u32[]{:S(2)}) collective-permute-start(bf16[96,768]{1,0:T(8,128)(2,1)S(1)} %get-tuple-element.600), channel_id=1, source_target_pairs={{0,4},{4,0},{8,12},{12,8},{1,5},{5,1},{9,13},{13,9},{2,6},{6,2},{1... | collective-permute-start | bytes 442376 | tf_op jit(solution)/shard_map/ppermute | solution.py:68
  75.1 30.4 %collective-permute-start.17 = (bf16[4,96,896]{2,1,0:T(8,128)(2,1)S(1)}, bf16[4,96,896]{2,1,0:T(8,128)(2,1)S(1)}, u32[]{:S(2)}, u32[]{:S(2)}) collective-permute-start(bf16[4,96,896]{2,1,0:T(8,128)(2,1)S(1)} %collective-permute-done.9.refs_2_), channel_id=1, source_target_pairs={{0,16},{16,0},{1,17},{17,1},{2,18},{18,2},{3,19},{19,3},{4,20},{20... | collective-permute-start | bytes 2064392 | tf_op jit(solution)/shard_map/ppermute | solution.py:64
  82.8 22.7 %collective-permute-start.16 = (bf16[4,96,896]{2,1,0:T(8,128)(2,1)S(1)}, bf16[4,96,896]{2,1,0:T(8,128)(2,1)S(1)}, u32[]{:S(2)}, u32[]{:S(2)}) collective-permute-start(bf16[4,96,896]{2,1,0:T(8,128)(2,1)S(1)} %collective-permute-done.8.refs_1_), channel_id=1, source_target_pairs={{0,16},{16,0},{1,17},{17,1},{2,18},{18,2},{3,19},{19,3},{4,20},{20... | collective-permute-start | bytes 2064392 | tf_op jit(solution)/shard_map/ppermute | solution.py:64
  83.3 10.1 %collective-permute-start.14 = (bf16[2,96,896]{2,1,0:T(8,128)(2,1)S(1)}, bf16[2,96,896]{2,1,0:T(8,128)(2,1)S(1)}, u32[]{:S(2)}, u32[]{:S(2)}) collective-permute-start(bf16[2,96,896]{2,1,0:T(8,128)(2,1)S(1)} %slice.221), channel_id=1, source_target_pairs={{0,2},{1,3},{2,0},{3,1},{4,6},{5,7},{6,4},{7,5},{8,10},{9,11},{10,... | collective-permute-start | bytes 1032200 | tf_op jit(solution)/shard_map/ppermute | solution.py:68
  84.5 12.1 %collective-permute-start.13 = (bf16[2,96,896]{2,1,0:T(8,128)(2,1)S(1)}, bf16[2,96,896]{2,1,0:T(8,128)(2,1)S(1)}, u32[]{:S(2)}, u32[]{:S(2)}) collective-permute-start(bf16[2,96,896]{2,1,0:T(8,128)(2,1)S(1)} %slice.220), channel_id=1, source_target_pairs={{0,1},{1,0},{2,3},{3,2},{4,5},{5,4},{6,7},{7,6},{8,9},{9,8},{10,11... | collective-permute-start | bytes 1032200 | tf_op jit(solution)/shard_map/ppermute | solution.py:68
  108.3 10.7 %collective-permute-start.23 = (bf16[256,128]{1,0:T(8,128)(2,1)S(1)}, bf16[256,128]{1,0:T(8,128)(2,1)S(1)}, u32[]{:S(2)}, u32[]{:S(2)}) collective-permute-start(bf16[256,128]{1,0:T(8,128)(2,1)S(1)} %slice.415), channel_id=1, source_target_pairs={{0,1},{1,2},{2,3},{4,5},{5,6},{6,7},{8,9},{9,10},{10,11},{12,13},{... | collective-permute-start | bytes 196616 | tf_op jit(solution)/shard_map/ppermute | solution.py:73
  114.5 18.0 %collective-permute-start.21 = (bf16[192,768]{1,0:T(8,128)(2,1)S(1)}, bf16[192,768]{1,0:T(8,128)(2,1)S(1)}, u32[]{:S(2)}, u32[]{:S(2)}) collective-permute-start(bf16[192,768]{1,0:T(8,128)(2,1)S(1)} %copy-done.104), channel_id=1, source_target_pairs={{0,12},{4,8},{8,4},{12,0},{1,13},{5,9},{9,5},{13,1},{2,14},{6,10},... | collective-permute-start | bytes 884744 | tf_op jit(solution)/shard_map/ppermute | solution.py:68
  117.9 40.9 %collective-permute-start.20 = (bf16[192,768]{1,0:T(8,128)(2,1)S(1)}, bf16[192,768]{1,0:T(8,128)(2,1)S(1)}, u32[]{:S(2)}, u32[]{:S(2)}) collective-permute-start(bf16[192,768]{1,0:T(8,128)(2,1)S(1)} %copy-done.104), channel_id=1, source_target_pairs={{0,8},{4,12},{8,0},{12,4},{1,9},{5,13},{9,1},{13,5},{2,10},{6,14},... | collective-permute-start | bytes 884744 | tf_op jit(solution)/shard_map/ppermute | solution.py:68
  117.9 40.9 %collective-permute-start.19 = (bf16[192,768]{1,0:T(8,128)(2,1)S(1)}, bf16[192,768]{1,0:T(8,128)(2,1)S(1)}, u32[]{:S(2)}, u32[]{:S(2)}) collective-permute-start(bf16[192,768]{1,0:T(8,128)(2,1)S(1)} %copy-done.104), channel_id=1, source_target_pairs={{0,4},{4,0},{8,12},{12,8},{1,5},{5,1},{9,13},{13,9},{2,6},{6,2},{1... | collective-permute-start | bytes 884744 | tf_op jit(solution)/shard_map/ppermute | solution.py:68
  161.5 15.7 %collective-permute-start.26 = (bf16[2,192,768]{2,1,0:T(8,128)(2,1)}, bf16[2,192,768]{2,1,0:T(8,128)(2,1)}, u32[]{:S(2)}, u32[]{:S(2)}) collective-permute-start(bf16[2,192,768]{2,1,0:T(8,128)(2,1)} %slice.232), channel_id=1, source_target_pairs={{0,2},{1,3},{2,0},{3,1},{4,6},{5,7},{6,4},{7,5},{8,10},{9,11},{10,... | collective-permute-start | bytes 1769480 | tf_op jit(solution)/shard_map/ppermute | solution.py:68
  162.9 15.4 %collective-permute-start.25 = (bf16[2,192,768]{2,1,0:T(8,128)(2,1)}, bf16[2,192,768]{2,1,0:T(8,128)(2,1)}, u32[]{:S(2)}, u32[]{:S(2)}) collective-permute-start(bf16[2,192,768]{2,1,0:T(8,128)(2,1)} %slice.232), channel_id=1, source_target_pairs={{0,1},{1,0},{2,3},{3,2},{4,5},{5,4},{6,7},{7,6},{8,9},{9,8},{10,11... | collective-permute-start | bytes 1769480 | tf_op jit(solution)/shard_map/ppermute | solution.py:68
  186.2 17.6 %collective-permute-start.31 = (bf16[2,192,768]{2,1,0:T(8,128)(2,1)}, bf16[2,192,768]{2,1,0:T(8,128)(2,1)}, u32[]{:S(2)}, u32[]{:S(2)}) collective-permute-start(bf16[2,192,768]{2,1,0:T(8,128)(2,1)} %slice.241), channel_id=1, source_target_pairs={{0,2},{1,3},{2,0},{3,1},{4,6},{5,7},{6,4},{7,5},{8,10},{9,11},{10,... | collective-permute-start | bytes 1769480 | tf_op jit(solution)/shard_map/ppermute | solution.py:68
  186.7 17.0 %collective-permute-start.30 = (bf16[2,192,768]{2,1,0:T(8,128)(2,1)}, bf16[2,192,768]{2,1,0:T(8,128)(2,1)}, u32[]{:S(2)}, u32[]{:S(2)}) collective-permute-start(bf16[2,192,768]{2,1,0:T(8,128)(2,1)} %slice.241), channel_id=1, source_target_pairs={{0,1},{1,0},{2,3},{3,2},{4,5},{5,4},{6,7},{7,6},{8,9},{9,8},{10,11... | collective-permute-start | bytes 1769480 | tf_op jit(solution)/shard_map/ppermute | solution.py:68
  192.5 10.3 %collective-permute-start.29 = (bf16[256,128]{1,0:T(8,128)(2,1)S(1)}, bf16[256,128]{1,0:T(8,128)(2,1)}, u32[]{:S(2)}, u32[]{:S(2)}) collective-permute-start(bf16[256,128]{1,0:T(8,128)(2,1)S(1)} %convolution_convert_fusion.7), channel_id=1, source_target_pairs={{0,1},{1,2},{2,3},{4,5},{5,6},{6,7},{8,9},{9,10},{10,11},{12,13},{... | collective-permute-start | bytes 196616 | tf_op jit(solution)/shard_map/ppermute | solution.py:73
  211.7 15.5 %collective-permute-start.34 = (bf16[2,192,768]{2,1,0:T(8,128)(2,1)}, bf16[2,192,768]{2,1,0:T(8,128)(2,1)S(1)}, u32[]{:S(2)}, u32[]{:S(2)}) collective-permute-start(bf16[2,192,768]{2,1,0:T(8,128)(2,1)} %collective-permute-done.30.refs_3_), channel_id=1, source_target_pairs={{0,2},{1,3},{2,0},{3,1},{4,6},{5,7},{6,4},{7,5},{8,10},{9,11},{10,... | collective-permute-start | bytes 1769480 | tf_op jit(solution)/shard_map/ppermute | solution.py:68
  214.5 14.1 %collective-permute-start.33 = (bf16[2,192,768]{2,1,0:T(8,128)(2,1)}, bf16[2,192,768]{2,1,0:T(8,128)(2,1)S(1)}, u32[]{:S(2)}, u32[]{:S(2)}) collective-permute-start(bf16[2,192,768]{2,1,0:T(8,128)(2,1)} %collective-permute-done.26.refs_4_), channel_id=1, source_target_pairs={{0,1},{1,0},{2,3},{3,2},{4,5},{5,4},{6,7},{7,6},{8,9},{9,8},{10,11... | collective-permute-start | bytes 1769480 | tf_op jit(solution)/shard_map/ppermute | solution.py:68
  328.7 9.4 %collective-permute-start.52 = (f32[256,128]{1,0:T(8,128)S(1)}, f32[256,128]{1,0:T(8,128)S(1)}, u32[]{:S(2)}, u32[]{:S(2)}) collective-permute-start(f32[256,128]{1,0:T(8,128)S(1)} %get-tuple-element.606), channel_id=1, source_target_pairs={{2,0},{3,1},{6,4},{7,5},{10,8},{11,9},{14,12},{15,13},{18,16},{19,... | collective-permute-start | bytes 393224 | tf_op jit(solution)/shard_map/ppermute | solution.py:73
  342.3 19.0 %collective-permute-start.55 = (bf16[768,896]{0,1:T(8,128)(2,1)}, bf16[768,896]{0,1:T(8,128)(2,1)}, u32[]{:S(2)}, u32[]{:S(2)}) collective-permute-start(bf16[768,896]{0,1:T(8,128)(2,1)} %broadcast_select_fusion.1), channel_id=1, source_target_pairs={{0,16},{16,0},{1,17},{17,1},{2,18},{18,2},{3,19},{19,3},{4,20},{20... | collective-permute-start | bytes 4128776 | tf_op jit(solution)/shard_map/ppermute | solution.py:64
  363.7 20.3 %collective-permute-start.57 = (bf16[2,1,2,96,768]{4,3,0,2,1:T(8,128)(2,1)S(1)}, bf16[2,1,2,96,768]{4,3,0,2,1:T(8,128)(2,1)S(1)}, u32[]{:S(2)}, u32[]{:S(2)}) collective-permute-start(bf16[2,1,2,96,768]{4,3,0,2,1:T(8,128)(2,1)S(1)} %copy.283), channel_id=1, source_target_pairs={{0,2},{1,3},{2,0},{3,1},{4,6},{5,7},{6,4},{7,5},{8,10},{9,11},{10,... | collective-permute-start | bytes 1769480 | tf_op jit(solution)/shard_map/ppermute | solution.py:68
  363.8 20.8 %collective-permute-start.56 = (bf16[2,2,1,96,768]{4,3,0,2,1:T(8,128)(2,1)S(1)}, bf16[2,2,1,96,768]{4,3,0,2,1:T(8,128)(2,1)S(1)}, u32[]{:S(2)}, u32[]{:S(2)}) collective-permute-start(bf16[2,2,1,96,768]{4,3,0,2,1:T(8,128)(2,1)S(1)} %copy.282), channel_id=1, source_target_pairs={{0,1},{1,0},{2,3},{3,2},{4,5},{5,4},{6,7},{7,6},{8,9},{9,8},{10,11... | collective-permute-start | bytes 1769480 | tf_op jit(solution)/shard_map/ppermute | solution.py:68
  398.0 28.4 %collective-permute-start.62 = (bf16[96,768]{1,0:T(8,128)(2,1)S(1)}, bf16[96,768]{1,0:T(8,128)(2,1)S(1)}, u32[]{:S(2)}, u32[]{:S(2)}) collective-permute-start(bf16[96,768]{1,0:T(8,128)(2,1)S(1)} %get-tuple-element.593), channel_id=1, source_target_pairs={{0,12},{4,8},{8,4},{12,0},{1,13},{5,9},{9,5},{13,1},{2,14},{6,10},... | collective-permute-start | bytes 442376 | tf_op jit(solution)/shard_map/ppermute | solution.py:68
  400.2 26.2 %collective-permute-start.61 = (bf16[96,768]{1,0:T(8,128)(2,1)S(1)}, bf16[96,768]{1,0:T(8,128)(2,1)S(1)}, u32[]{:S(2)}, u32[]{:S(2)}) collective-permute-start(bf16[96,768]{1,0:T(8,128)(2,1)S(1)} %get-tuple-element.594), channel_id=1, source_target_pairs={{0,8},{4,12},{8,0},{12,4},{1,9},{5,13},{9,1},{13,5},{2,10},{6,14},... | collective-permute-start | bytes 442376 | tf_op jit(solution)/shard_map/ppermute | solution.py:68
  400.3 26.2 %collective-permute-start.60 = (bf16[96,768]{1,0:T(8,128)(2,1)S(1)}, bf16[96,768]{1,0:T(8,128)(2,1)S(1)}, u32[]{:S(2)}, u32[]{:S(2)}) collective-permute-start(bf16[96,768]{1,0:T(8,128)(2,1)S(1)} %get-tuple-element.595), channel_id=1, source_target_pairs={{0,4},{4,0},{8,12},{12,8},{1,5},{5,1},{9,13},{13,9},{2,6},{6,2},{1... | collective-permute-start | bytes 442376 | tf_op jit(solution)/shard_map/ppermute | solution.py:68
  405.7 20.7 %collective-permute-start.64 = (bf16[2,1,2,96,768]{4,3,0,2,1:T(8,128)(2,1)S(1)}, bf16[2,1,2,96,768]{4,3,0,2,1:T(8,128)(2,1)S(1)}, u32[]{:S(2)}, u32[]{:S(2)}) collective-permute-start(bf16[2,1,2,96,768]{4,3,0,2,1:T(8,128)(2,1)S(1)} %copy.285), channel_id=1, source_target_pairs={{0,2},{1,3},{2,0},{3,1},{4,6},{5,7},{6,4},{7,5},{8,10},{9,11},{10,... | collective-permute-start | bytes 1769480 | tf_op jit(solution)/shard_map/ppermute | solution.py:68
  407.4 19.1 %collective-permute-start.63 = (bf16[2,2,1,96,768]{4,3,0,2,1:T(8,128)(2,1)S(1)}, bf16[2,2,1,96,768]{4,3,0,2,1:T(8,128)(2,1)S(1)}, u32[]{:S(2)}, u32[]{:S(2)}) collective-permute-start(bf16[2,2,1,96,768]{4,3,0,2,1:T(8,128)(2,1)S(1)} %copy.284), channel_id=1, source_target_pairs={{0,1},{1,0},{2,3},{3,2},{4,5},{5,4},{6,7},{7,6},{8,9},{9,8},{10,11... | collective-permute-start | bytes 1769480 | tf_op jit(solution)/shard_map/ppermute | solution.py:68
  427.5 32.3 %collective-permute-start.69 = (bf16[4,96,768]{2,1,0:T(8,128)(2,1)S(1)}, bf16[4,96,768]{2,1,0:T(8,128)(2,1)S(1)}, u32[]{:S(2)}, u32[]{:S(2)}) collective-permute-start(bf16[4,96,768]{2,1,0:T(8,128)(2,1)S(1)} %pad_maximum_fusion.9.refs_0_), channel_id=1, source_target_pairs={{0,16},{16,0},{1,17},{17,1},{2,18},{18,2},{3,19},{19,3},{4,20},{20... | collective-permute-start | bytes 1769480 | tf_op jit(solution)/shard_map/ppermute | solution.py:64
  427.6 32.2 %collective-permute-start.66 = (bf16[4,96,768]{2,1,0:T(8,128)(2,1)S(1)}, bf16[4,96,768]{2,1,0:T(8,128)(2,1)}, u32[]{:S(2)}, u32[]{:S(2)}) collective-permute-start(bf16[4,96,768]{2,1,0:T(8,128)(2,1)S(1)} %pad_maximum_fusion.9.refs_0_), channel_id=1, source_target_pairs={{0,2},{1,3},{2,0},{3,1},{4,6},{5,7},{6,4},{7,5},{8,10},{9,11},{10,... | collective-permute-start | bytes 1769480 | tf_op jit(solution)/shard_map/ppermute | solution.py:68
  429.6 30.2 %collective-permute-start.65 = (bf16[4,96,768]{2,1,0:T(8,128)(2,1)S(1)}, bf16[4,96,768]{2,1,0:T(8,128)(2,1)}, u32[]{:S(2)}, u32[]{:S(2)}) collective-permute-start(bf16[4,96,768]{2,1,0:T(8,128)(2,1)S(1)} %pad_maximum_fusion.9.refs_0_), channel_id=1, source_target_pairs={{0,1},{1,0},{2,3},{3,2},{4,5},{5,4},{6,7},{7,6},{8,9},{9,8},{10,11... | collective-permute-start | bytes 1769480 | tf_op jit(solution)/shard_map/ppermute | solution.py:68
  429.6 30.2 %collective-permute-start.67 = (bf16[2,96,768]{2,1,0:T(8,128)(2,1)}, bf16[2,96,768]{2,1,0:T(8,128)(2,1)}, u32[]{:S(2)}, u32[]{:S(2)}) collective-permute-start(bf16[2,96,768]{2,1,0:T(8,128)(2,1)} %dynamic-slice_bitcast_fusion.5), channel_id=1, source_target_pairs={{0,2},{1,3},{2,0},{3,1},{4,6},{5,7},{6,4},{7,5},{8,10},{9,11},{10,... | collective-permute-start | bytes 884744 | tf_op jit(solution)/shard_map/ppermute | solution.py:68
  431.2 28.6 %collective-permute-start.68 = (bf16[2,96,768]{2,1,0:T(8,128)(2,1)}, bf16[2,96,768]{2,1,0:T(8,128)(2,1)}, u32[]{:S(2)}, u32[]{:S(2)}) collective-permute-start(bf16[2,96,768]{2,1,0:T(8,128)(2,1)} %dynamic-slice_bitcast_fusion.4), channel_id=1, source_target_pairs={{0,1},{1,0},{2,3},{3,2},{4,5},{5,4},{6,7},{7,6},{8,9},{9,8},{10,11... | collective-permute-start | bytes 884744 | tf_op jit(solution)/shard_map/ppermute | solution.py:68
  459.8 34.0 %collective-permute-start.80 = (bf16[768,896]{0,1:T(8,128)(2,1)}, bf16[768,896]{0,1:T(8,128)(2,1)}, u32[]{:S(2)}, u32[]{:S(2)}) collective-permute-start(bf16[768,896]{0,1:T(8,128)(2,1)} %get-tuple-element.644), channel_id=1, source_target_pairs={{0,16},{16,0},{1,17},{17,1},{2,18},{18,2},{3,19},{19,3},{4,20},{20... | collective-permute-start | bytes 4128776 | tf_op jit(solution)/shard_map/ppermute | solution.py:64
  461.0 45.4 %collective-permute-start.70 = (bf16[4,96,768]{2,1,0:T(8,128)(2,1)}, bf16[4,96,768]{2,1,0:T(8,128)(2,1)}, u32[]{:S(2)}, u32[]{:S(2)}) collective-permute-start(bf16[4,96,768]{2,1,0:T(8,128)(2,1)} %collective-permute-done.65.refs_1_), channel_id=1, source_target_pairs={{0,16},{16,0},{1,17},{17,1},{2,18},{18,2},{3,19},{19,3},{4,20},{20... | collective-permute-start | bytes 1769480 | tf_op jit(solution)/shard_map/ppermute | solution.py:64
  463.7 17.7 %collective-permute-start.72 = (bf16[2,96,768]{2,1,0:T(8,128)(2,1)S(1)}, bf16[2,96,768]{2,1,0:T(8,128)(2,1)S(1)}, u32[]{:S(2)}, u32[]{:S(2)}) collective-permute-start(bf16[2,96,768]{2,1,0:T(8,128)(2,1)S(1)} %slice.273), channel_id=1, source_target_pairs={{0,1},{1,0},{2,3},{3,2},{4,5},{5,4},{6,7},{7,6},{8,9},{9,8},{10,11... | collective-permute-start | bytes 884744 | tf_op jit(solution)/shard_map/ppermute | solution.py:68
  465.2 16.4 %collective-permute-start.73 = (bf16[2,96,768]{2,1,0:T(8,128)(2,1)S(1)}, bf16[2,96,768]{2,1,0:T(8,128)(2,1)S(1)}, u32[]{:S(2)}, u32[]{:S(2)}) collective-permute-start(bf16[2,96,768]{2,1,0:T(8,128)(2,1)S(1)} %slice.274), channel_id=1, source_target_pairs={{0,2},{1,3},{2,0},{3,1},{4,6},{5,7},{6,4},{7,5},{8,10},{9,11},{10,... | collective-permute-start | bytes 884744 | tf_op jit(solution)/shard_map/ppermute | solution.py:68
  467.8 26.0 %collective-permute-start.79 = (bf16[96,768]{1,0:T(8,128)(2,1)}, bf16[96,768]{1,0:T(8,128)(2,1)}, u32[]{:S(2)}, u32[]{:S(2)}) collective-permute-start(bf16[96,768]{1,0:T(8,128)(2,1)} %get-tuple-element.590), channel_id=1, source_target_pairs={{0,12},{4,8},{8,4},{12,0},{1,13},{5,9},{9,5},{13,1},{2,14},{6,10},... | collective-permute-start | bytes 442376 | tf_op jit(solution)/shard_map/ppermute | solution.py:68
  481.5 13.8 %collective-permute-start.77 = (bf16[96,768]{1,0:T(8,128)(2,1)}, bf16[96,768]{1,0:T(8,128)(2,1)}, u32[]{:S(2)}, u32[]{:S(2)}) collective-permute-start(bf16[96,768]{1,0:T(8,128)(2,1)} %get-tuple-element.591), channel_id=1, source_target_pairs={{0,4},{4,0},{8,12},{12,8},{1,5},{5,1},{9,13},{13,9},{2,6},{6,2},{1... | collective-permute-start | bytes 442376 | tf_op jit(solution)/shard_map/ppermute | solution.py:68
  481.6 14.3 %collective-permute-start.78 = (bf16[96,768]{1,0:T(8,128)(2,1)}, bf16[96,768]{1,0:T(8,128)(2,1)}, u32[]{:S(2)}, u32[]{:S(2)}) collective-permute-start(bf16[96,768]{1,0:T(8,128)(2,1)} %get-tuple-element.592), channel_id=1, source_target_pairs={{0,8},{4,12},{8,0},{12,4},{1,9},{5,13},{9,1},{13,5},{2,10},{6,14},... | collective-permute-start | bytes 442376 | tf_op jit(solution)/shard_map/ppermute | solution.py:68
  493.8 12.6 %collective-permute-start.71 = (bf16[4,96,768]{2,1,0:T(8,128)(2,1)}, bf16[4,96,768]{2,1,0:T(8,128)(2,1)}, u32[]{:S(2)}, u32[]{:S(2)}) collective-permute-start(bf16[4,96,768]{2,1,0:T(8,128)(2,1)} %collective-permute-done.66.refs_2_), channel_id=1, source_target_pairs={{0,16},{16,0},{1,17},{17,1},{2,18},{18,2},{3,19},{19,3},{4,20},{20... | collective-permute-start | bytes 1769480 | tf_op jit(solution)/shard_map/ppermute | solution.py:64
  493.8 12.6 %collective-permute-start.75 = (bf16[2,96,768]{2,1,0:T(8,128)(2,1)}, bf16[2,96,768]{2,1,0:T(8,128)(2,1)}, u32[]{:S(2)}, u32[]{:S(2)}) collective-permute-start(bf16[2,96,768]{2,1,0:T(8,128)(2,1)} %dynamic-slice_bitcast_fusion.3), channel_id=1, source_target_pairs={{0,2},{1,3},{2,0},{3,1},{4,6},{5,7},{6,4},{7,5},{8,10},{9,11},{10,... | collective-permute-start | bytes 884744 | tf_op jit(solution)/shard_map/ppermute | solution.py:68
  495.3 11.1 %collective-permute-start.76 = (bf16[2,96,768]{2,1,0:T(8,128)(2,1)}, bf16[2,96,768]{2,1,0:T(8,128)(2,1)}, u32[]{:S(2)}, u32[]{:S(2)}) collective-permute-start(bf16[2,96,768]{2,1,0:T(8,128)(2,1)} %dynamic-slice_bitcast_fusion.2), channel_id=1, source_target_pairs={{0,1},{1,0},{2,3},{3,2},{4,5},{5,4},{6,7},{7,6},{8,9},{9,8},{10,11... | collective-permute-start | bytes 884744 | tf_op jit(solution)/shard_map/ppermute | solution.py:68
  495.9 10.5 %collective-permute-start.74 = (bf16[4,96,768]{2,1,0:T(8,128)(2,1)}, bf16[4,96,768]{2,1,0:T(8,128)(2,1)}, u32[]{:S(2)}, u32[]{:S(2)}) collective-permute-start(bf16[4,96,768]{2,1,0:T(8,128)(2,1)} %constant_dynamic-update-slice_fusion.2.refs_3_), channel_id=1, source_target_pairs={{0,16},{16,0},{1,17},{17,1},{2,18},{18,2},{3,19},{19,3},{4,20},{20... | collective-permute-start | bytes 1769480 | tf_op jit(solution)/shard_map/ppermute | solution.py:64
  506.9 31.4 %collective-permute-start.85 = (bf16[2,1,2,96,896]{4,3,0,2,1:T(8,128)(2,1)S(1)}, bf16[2,1,2,96,896]{4,3,0,2,1:T(8,128)(2,1)S(1)}, u32[]{:S(2)}, u32[]{:S(2)}) collective-permute-start(bf16[2,1,2,96,896]{4,3,0,2,1:T(8,128)(2,1)S(1)} %copy.292), channel_id=1, source_target_pairs={{0,2},{1,3},{2,0},{3,1},{4,6},{5,7},{6,4},{7,5},{8,10},{9,11},{10,... | collective-permute-start | bytes 2064392 | tf_op jit(solution)/shard_map/ppermute | solution.py:68
  508.4 29.9 %collective-permute-start.84 = (bf16[2,2,1,96,896]{4,3,0,2,1:T(8,128)(2,1)S(1)}, bf16[2,2,1,96,896]{4,3,0,2,1:T(8,128)(2,1)S(1)}, u32[]{:S(2)}, u32[]{:S(2)}) collective-permute-start(bf16[2,2,1,96,896]{4,3,0,2,1:T(8,128)(2,1)S(1)} %copy.291), channel_id=1, source_target_pairs={{0,1},{1,0},{2,3},{3,2},{4,5},{5,4},{6,7},{7,6},{8,9},{9,8},{10,11... | collective-permute-start | bytes 2064392 | tf_op jit(solution)/shard_map/ppermute | solution.py:68
  511.3 27.0 %collective-permute-start.83 = (bf16[96,768]{1,0:T(8,128)(2,1)S(1)}, bf16[96,768]{1,0:T(8,128)(2,1)S(1)}, u32[]{:S(2)}, u32[]{:S(2)}) collective-permute-start(bf16[96,768]{1,0:T(8,128)(2,1)S(1)} %get-tuple-element.587), channel_id=1, source_target_pairs={{0,12},{4,8},{8,4},{12,0},{1,13},{5,9},{9,5},{13,1},{2,14},{6,10},... | collective-permute-start | bytes 442376 | tf_op jit(solution)/shard_map/ppermute | solution.py:68
  513.4 24.9 %collective-permute-start.81 = (bf16[96,768]{1,0:T(8,128)(2,1)S(1)}, bf16[96,768]{1,0:T(8,128)(2,1)S(1)}, u32[]{:S(2)}, u32[]{:S(2)}) collective-permute-start(bf16[96,768]{1,0:T(8,128)(2,1)S(1)} %get-tuple-element.588), channel_id=1, source_target_pairs={{0,4},{4,0},{8,12},{12,8},{1,5},{5,1},{9,13},{13,9},{2,6},{6,2},{1... | collective-permute-start | bytes 442376 | tf_op jit(solution)/shard_map/ppermute | solution.py:68
  513.4 24.9 %collective-permute-start.82 = (bf16[96,768]{1,0:T(8,128)(2,1)S(1)}, bf16[96,768]{1,0:T(8,128)(2,1)S(1)}, u32[]{:S(2)}, u32[]{:S(2)}) collective-permute-start(bf16[96,768]{1,0:T(8,128)(2,1)S(1)} %get-tuple-element.589), channel_id=1, source_target_pairs={{0,8},{4,12},{8,0},{12,4},{1,9},{5,13},{9,1},{13,5},{2,10},{6,14},... | collective-permute-start | bytes 442376 | tf_op jit(solution)/shard_map/ppermute | solution.py:68
  538.8 24.0 %collective-permute-start.86 = (bf16[2,96,896]{2,1,0:T(8,128)(2,1)S(1)}, bf16[2,96,896]{2,1,0:T(8,128)(2,1)S(1)}, u32[]{:S(2)}, u32[]{:S(2)}) collective-permute-start(bf16[2,96,896]{2,1,0:T(8,128)(2,1)S(1)} %dynamic-slice_bitcast_fusion.1), channel_id=1, source_target_pairs={{0,2},{1,3},{2,0},{3,1},{4,6},{5,7},{6,4},{7,5},{8,10},{9,11},{10,... | collective-permute-start | bytes 1032200 | tf_op jit(solution)/shard_map/ppermute | solution.py:68
  540.3 22.5 %collective-permute-start.87 = (bf16[2,96,896]{2,1,0:T(8,128)(2,1)S(1)}, bf16[2,96,896]{2,1,0:T(8,128)(2,1)S(1)}, u32[]{:S(2)}, u32[]{:S(2)}) collective-permute-start(bf16[2,96,896]{2,1,0:T(8,128)(2,1)S(1)} %dynamic-slice_bitcast_fusion), channel_id=1, source_target_pairs={{0,1},{1,0},{2,3},{3,2},{4,5},{5,4},{6,7},{7,6},{8,9},{9,8},{10,11... | collective-permute-start | bytes 1032200 | tf_op jit(solution)/shard_map/ppermute | solution.py:68
  541.1 38.9 %collective-permute-start.92 = (f32[192,768]{1,0:T(8,128)S(1)}, f32[192,768]{1,0:T(8,128)S(1)}, u32[]{:S(2)}, u32[]{:S(2)}) collective-permute-start(f32[192,768]{1,0:T(8,128)S(1)} %fusion.33), channel_id=1, source_target_pairs={{0,16},{16,0},{1,17},{17,1},{2,18},{18,2},{3,19},{19,3},{4,20},{20... | collective-permute-start | bytes 1769480 | tf_op jit(solution)/shard_map/ppermute | solution.py:64
  563.2 10.2 %collective-permute-start.88 = (bf16[96,896]{1,0:T(8,128)(2,1)S(1)}, bf16[96,896]{1,0:T(8,128)(2,1)S(1)}, u32[]{:S(2)}, u32[]{:S(2)}) collective-permute-start(bf16[96,896]{1,0:T(8,128)(2,1)S(1)} %get-tuple-element.580), channel_id=1, source_target_pairs={{0,4},{4,0},{8,12},{12,8},{1,5},{5,1},{9,13},{13,9},{2,6},{6,2},{1... | collective-permute-start | bytes 516104 | tf_op jit(solution)/shard_map/ppermute | solution.py:68
  563.3 15.7 %collective-permute-start.89 = (bf16[96,896]{1,0:T(8,128)(2,1)S(1)}, bf16[96,896]{1,0:T(8,128)(2,1)S(1)}, u32[]{:S(2)}, u32[]{:S(2)}) collective-permute-start(bf16[96,896]{1,0:T(8,128)(2,1)S(1)} %get-tuple-element.581), channel_id=1, source_target_pairs={{0,8},{4,12},{8,0},{12,4},{1,9},{5,13},{9,1},{13,5},{2,10},{6,14},... | collective-permute-start | bytes 516104 | tf_op jit(solution)/shard_map/ppermute | solution.py:68
  566.5 12.6 %collective-permute-start.90 = (bf16[96,896]{1,0:T(8,128)(2,1)S(1)}, bf16[96,896]{1,0:T(8,128)(2,1)S(1)}, u32[]{:S(2)}, u32[]{:S(2)}) collective-permute-start(bf16[96,896]{1,0:T(8,128)(2,1)S(1)} %get-tuple-element.582), channel_id=1, source_target_pairs={{0,12},{4,8},{8,4},{12,0},{1,13},{5,9},{9,5},{13,1},{2,14},{6,10},... | collective-permute-start | bytes 516104 | tf_op jit(solution)/shard_map/ppermute | solution.py:68
  598.6 48.2 %collective-permute-start.97 = (f32[96,128]{1,0:T(8,128)S(1)}, f32[96,128]{1,0:T(8,128)S(1)}, u32[]{:S(2)}, u32[]{:S(2)}) collective-permute-start(f32[96,128]{1,0:T(8,128)S(1)} %slice.320), channel_id=1, source_target_pairs={{0,2},{1,3},{2,0},{3,1},{4,6},{5,7},{6,4},{7,5},{8,10},{9,11},{10,... | collective-permute-start | bytes 147464 | tf_op jit(solution)/shard_map/ppermute | solution.py:68
  600.1 46.7 %collective-permute-start.98 = (f32[96,128]{1,0:T(8,128)S(1)}, f32[96,128]{1,0:T(8,128)S(1)}, u32[]{:S(2)}, u32[]{:S(2)}) collective-permute-start(f32[96,128]{1,0:T(8,128)S(1)} %slice.320), channel_id=1, source_target_pairs={{0,3},{1,2},{2,1},{3,0},{4,7},{5,6},{6,5},{7,4},{8,11},{9,10},{10,... | collective-permute-start | bytes 147464 | tf_op jit(solution)/shard_map/ppermute | solution.py:68
  601.6 45.3 %collective-permute-start.96 = (f32[96,128]{1,0:T(8,128)S(1)}, f32[96,128]{1,0:T(8,128)}, u32[]{:S(2)}, u32[]{:S(2)}) collective-permute-start(f32[96,128]{1,0:T(8,128)S(1)} %slice.320), channel_id=1, source_target_pairs={{0,1},{1,0},{2,3},{3,2},{4,5},{5,4},{6,7},{7,6},{8,9},{9,8},{10,11... | collective-permute-start | bytes 147464 | tf_op jit(solution)/shard_map/ppermute | solution.py:68
  (238 other events, 2053.8 us)
Sparse Core Ops, SparseCore 1:
  48.4 106.1 all-gather.6
  313.3 144.5 reduce-scatter.4

commit v3 on v2

--- a/solution.py
+++ b/solution.py
@@ -145,37 +145,37 @@
 
 
 def weights_kernel(place_ref, *refs):
-    *pieces, in_ref, out_ref = refs
+    mine, theirs, in_ref, out_ref = refs
     c, first = place_ref[0], place_ref[1] == 0
-    columns, part = pieces[0].shape[:2]
+    part = mine.shape[1]
 
     def lay(ref, pieces):
-        for k, piece in enumerate(pieces):
-            for z in range(columns):
+        for k in range(4):
+            for z in range(4):
                 rows = pl.ds(pl.multiple_of((4 * z + (c ^ k)) * part, 16), part)
-                ref[rows, :] = piece[z]
+                ref[rows, :] = pieces[4 * k + z]
 
     @pl.when(first)
     def _():
-        lay(in_ref, pieces[:4])
-        lay(out_ref, pieces[4:])
+        lay(in_ref, mine)
+        lay(out_ref, theirs)
 
     @pl.when(~first)
     def _():
-        lay(in_ref, pieces[4:])
-        lay(out_ref, pieces[:4])
+        lay(in_ref, theirs)
+        lay(out_ref, mine)
 
 
 def attention_weights(mine, theirs, model, layer):
     if by_fours():
-        columns, both, wide = mine[0].shape
+        blocks, both, wide = mine.shape
         place = jnp.stack([lax.axis_index("ctx"), lax.axis_index("section")])
         weight_in, weight_out = pl.pallas_call(
             weights_kernel,
             grid_spec=pltpu.PrefetchScalarGridSpec(
                 num_scalar_prefetch=1,
                 grid=(1,),
-                in_specs=[pl.BlockSpec((columns, both // 2, wide), lambda *_: (0, layer, 0))] * 8,
+                in_specs=[pl.BlockSpec((blocks, both // 2, wide), lambda *_: (0, layer, 0))] * 2,
                 out_specs=[whole_block((model, wide))] * 2,
             ),
             out_shape=[jax.ShapeDtypeStruct((model, wide), jnp.bfloat16)] * 2,
@@ -183,7 +183,7 @@
             cost_estimate=small_cost(
                 flops=0, bytes_accessed=8 * model * wide, transcendentals=0
             ),
-        )(place, *mine, *theirs)
+        )(place, mine, theirs)
     else:
         part = mine.shape[1] // 2
         weights = mine_first(mine, theirs)
@@ -345,7 +345,7 @@
 
 def softmax_rows(scores):
     exponents = jnp.exp(scores - jnp.max(scores, -1, keepdims=True))
-    return exponents / jnp.sum(exponents, -1, keepdims=True)
+    return exponents * (1.0 / jnp.sum(exponents, -1, keepdims=True))
 
 
 def attend_kernel(query_ref, keyval_ref, bias_ref, out_ref):
@@ -890,6 +890,33 @@
     return jnp.min(jnp.where(matches, local[:, None, :], 1 << 30), -1)
 
 
+def attention_sum_kernel(kept0_ref, sent0_ref, kept1_ref, sent1_ref, out_ref):
+    part = kept0_ref.shape[1]
+    out_ref[:, :part] = bfloat(single(kept0_ref[...]) + single(sent0_ref[...]))
+    out_ref[:, part:] = bfloat(single(kept1_ref[...]) + single(sent1_ref[...]))
+
+
+def attention_sums(grads, blocks):
+    wide = grads[0].shape[1]
+    grads = [grad.reshape(blocks, -1, wide) for grad in grads]
+    part = grads[0].shape[1]
+    if part % 16:
+        total = [bfloat(single(grads[k]) + single(grads[k + 1])) for k in (0, 2)]
+        return jnp.concatenate(total, 1)
+    step = row_block(blocks, 4)
+    return pl.pallas_call(
+        attention_sum_kernel,
+        grid=(blocks // step,),
+        in_specs=[pl.BlockSpec((step, part, wide), lambda i: (i, 0, 0))] * 4,
+        out_specs=pl.BlockSpec((step, 2 * part, wide), lambda i: (i, 0, 0)),
+        out_shape=jax.ShapeDtypeStruct((blocks, 2 * part, wide), jnp.bfloat16),
+        compiler_params=vmem(24),
+        cost_estimate=small_cost(
+            flops=0, bytes_accessed=8 * grads[0].size, transcendentals=0
+        ),
+    )(*grads)
+
+
 def picked_kernel(ids_ref, table_ref, out_ref, rows_ref, sem):
     count = rows_ref.shape[0]
 
@@ -1201,13 +1228,15 @@
     low_first, square_first = lowered(table_now, None, 0, 3)
     at_n, start_pieces, low_first, hid_p1 = barrier((at_n, start_pieces, low_first, hid_p1))
     at_f = plane_far(at_n)
+    hid_z1 = column_pieces(hid_p1)
     table_low, square_second = lowered(table, low_first, 1, 3)
     at_f, table_low, at_c = barrier((at_f, table_low, at_c))
     at_w = plane_list(at_c, at_n, at_f)
+    if by_fours():
+        at_w = jnp.concatenate(at_w)
     at_o = swap(at_w)
     table_low, square_third = lowered(table, table_low, 2, 3)
-    at_o, table_low, hid_p1 = barrier((at_o, table_low, hid_p1))
-    hid_z1 = column_pieces(hid_p1)
+    at_o, table_low = barrier((at_o, table_low))
     if by_fours():
         target_notes = notes[:, 0, asked.size + 1 :]
         asked_all = notes[..., : asked.size].reshape(c_count, 2, z_count, room)
@@ -1250,18 +1279,19 @@
     keyval0, query0, local, order, starts = barrier(
         (bfloat(mixed_in[:, model:]), query0, local, order, starts)
     )
-    keyval0, query0 = barrier((key_rows(keyval0), query0))
+    keyval0, query0, hid_z1 = barrier((key_rows(keyval0), query0, hid_z1))
+    hid_c1 = column_join(hid_p1, hid_z1)
+    hid_n1 = plane_near_half(hid_c1, 0)
     attended0 = attend(query0, keyval0, bias)
     mixed0 = start + matmul(attended0, out0)
     normed_two0 = bfloat(layer_norm(mixed0, gains0[2], gains0[3]))
-    hid_z1, mixed0, normed_two0 = barrier((hid_z1, mixed0, normed_two0))
-    hid_c1 = column_join(hid_p1, hid_z1)
+    hid_n1, mixed0, normed_two0 = barrier((hid_n1, mixed0, normed_two0))
     both0, hid_c1 = barrier((both_rows(normed_two0), hid_c1))
-    hid_n1 = plane_near_half(hid_c1, 0)
+    hid_m1 = plane_near_half(hid_c1, 1)
     upper0, partial = hidden_forward(both0, hidden_w0)
     in1, out1, gains1 = attention_weights(at_w, at_o, model, 1)
-    hid_n1, partial, in1, out1, hid_c1 = barrier((hid_n1, partial, in1, out1, hid_c1))
-    hid_m1 = plane_near_half(hid_c1, 1)
+    hid_m1, partial, in1, out1 = barrier((hid_m1, partial, in1, out1))
+    hid_f1 = plane_far_half(hid_n1, hid_m1)
     result0 = mixed0 + own_rows(partial)
 
     inputs1_low = bfloat(result0)
@@ -1271,9 +1301,8 @@
     picked_normed = bfloat(matmul(onehot, normed1))
     picked = matmul(onehot, inputs1_low)
     query1 = bfloat(matmul(picked_normed, in1[:, :model]) * HD ** (-0.5))
-    keyval1, query1 = barrier((keyval1, query1))
-    keyval1, hid_n1, hid_m1 = barrier((key_rows(keyval1), hid_n1, hid_m1))
-    hid_f1 = plane_far_half(hid_n1, hid_m1)
+    keyval1, query1, hid_f1 = barrier((keyval1, query1, hid_f1))
+    keyval1 = key_rows(keyval1)
     hidden_w1 = plane_halves(hid_c1, (hid_n1, hid_m1), hid_f1)
     all_targets = target_notes.reshape((c_count,) + targets.shape).transpose(1, 2, 0, 3).reshape(-1)
     heads1 = query1.reshape(slots, -1, HD).transpose(1, 0, 2).reshape(-1, HD)
@@ -1336,9 +1365,6 @@
         )
         grad_in = bfloat(grad_in)
         return jnp.where(first, grad_in, grad_out), jnp.where(first, grad_out, grad_in)
-
-    def attention_sum(kept, sent):
-        return bfloat(single(kept) + single(sent)).reshape(blocks, part, wide)
 
     low = bfloat(grad_result1)
     partial, hidden_grads1 = hidden_backward(both1, upper1, both_rows(low), hidden_w1)
@@ -1371,9 +1397,9 @@
 
     low = bfloat(grad_result0)
     partial, hidden_grads0 = hidden_backward(both0, upper0, both_rows(low), hidden_w0)
-    ups, downs = (0, 2 * part), (2 * part, half)
+    every, wide_rows = (0, 2 * part + half), (0, 2 * part)
     partial, hidden_grads0, sent1 = barrier((own_rows(partial), hidden_grads0, swap(sent1)))
-    up_s = half_first(hidden_grads0, ups) if by_fours() else ()
+    hid_s = half_first(hidden_grads0, every) if by_fours() else ()
     _, pull = jax.vjp(layer_norm, mixed0, gains0[2], gains0[3])
     grad_mixed0, grad_gain2, grad_shift2 = pull(partial)
     grad_mixed0 = grad_mixed0 + grad_result0
@@ -1382,11 +1408,10 @@
     grad_query, grad_keyval = attend_back(
         query0, keyval0, bias, bfloat(matmul_right(grad_low, out0))
     )
-    up_s, grad_query, grad_keyval = barrier((up_s, grad_query, grad_keyval))
-    returned, hidden_grads0 = barrier((key_rows_back(grad_keyval, local_len), hidden_grads0))
+    grad_query, grad_keyval = barrier((grad_query, grad_keyval))
+    returned, hid_s = barrier((key_rows_back(grad_keyval, local_len), hid_s))
     if by_fours():
-        down_s = half_first(hidden_grads0, downs)
-        up_k, up_h = half_kept(hidden_grads0, ups, up_s)
+        hid_k, hid_h = half_kept(hidden_grads0, every, hid_s)
     grad_keyval = key_rows_sum(grad_keyval, returned, local_len)
     grad_mixed_in = jnp.concatenate([grad_query, grad_keyval], 1)
     grad_in0 = matmul_left(normed0, grad_mixed_in)
@@ -1395,6 +1420,16 @@
     grad_start = bfloat(grad_start + grad_mixed0)
     grad_gains0 = jnp.stack([grad_gain1, grad_shift1, grad_gain2, grad_shift2])
     kept0, sent0 = attention_grads(grad_in0, grad_out0, grad_gains0)
+    def owned(one, two):
+        return mine_first(jnp.where(first, one, two), swap(jnp.where(first, two, one)))
+
+    def hidden_shards(one, two):
+        halves = jnp.stack(owned(one, two))
+        ups = units // 2 // model
+        up = halves[:, : ups * part].reshape(2, ups, part, model).transpose(2, 0, 1, 3)
+        up = up.reshape(part, 2, blocks, half).transpose(0, 2, 1, 3).reshape(part, units)
+        return up, halves[:, ups * part :].reshape(2 * half, model)
+
     def head_part(grads, index, count):
         return head_table(
             chosen, across, local_target[None], logsum[None], table_low, grads, index, count
@@ -1403,22 +1438,21 @@
     table_square = square_first + square_second + square_third
     if by_fours():
         sent = bfloat(matmul_left(placed, grad_start)).reshape(z_count, room, model)
+        sent, hid_h = barrier((sent, hid_h))
         row_z = row_pieces(sent)
+        hid_t = half_send(hid_h)
         chosen = after(chosen, sent)
         grad_head = head_part(None, 0, 3)
-        row_z, grad_head, down_s, up_h = barrier((row_z, grad_head, down_s, up_h))
+        row_z, grad_head, hid_t, kept0, sent0 = barrier((row_z, grad_head, hid_t, kept0, sent0))
         column = column_join(at(sent, z, 0), row_z)
-        other = swap(column)
         near = plane_near(column)
-        up_t = half_send(up_h)
-        down_k, down_h = half_kept(hidden_grads0, downs, down_s)
+        other, sent0 = swap((column, sent0))
+        hid_v = half_column(hid_k, hid_t)
         grad_head = head_part(grad_head, 1, 3)
-        near, grad_head, up_t, other, down_h, hidden1 = barrier(
-            (near, grad_head, up_t, other, down_h, hidden1)
-        )
+        near, grad_head, other, sent0, hid_v = barrier((near, grad_head, other, sent0, hid_v))
         far = plane_far(near)
-        up_v = half_column(up_k, up_t)
-        up_q = row_pieces(up_v)
+        attention_both = attention_sums((kept0, sent0, kept1, sent1), blocks)
+        at_s = half_first(attention_both, wide_rows)
         grad_head = head_part(grad_head, 2, 3)
         grad_head = lax.while_loop(
             lambda carry: carry[0] < spilled.astype(jnp.int32),
@@ -1428,35 +1462,30 @@
             ),
             (jnp.zeros((), jnp.int32), grad_head),
         )[1]
-        far, grad_head, down_h = barrier((far, grad_head, down_h))
+        far, grad_head, hidden1 = barrier((far, grad_head, hidden1))
         far = jnp.concatenate(far)
-        others = swap((*near, far))
-        down_t = half_send(down_h)
-        attention_both = jnp.concatenate(
-            [attention_sum(kept0, swap(sent0)), attention_sum(kept1, sent1)], 1
-        )
-        others, down_t, up_q, attention_both = barrier((others, down_t, up_q, attention_both))
-        down_v = half_column(down_k, down_t)
-        down_q = row_pieces(down_v)
-        every = (0, 2 * part)
-        at_s = half_first(attention_both, every)
-        hidden0 = row_sum(up_v, up_q)
+        others, hid_v = barrier((swap((*near, far)), hid_v))
+        hid_q = row_pieces(hid_v)
         pieces = (column, *near, far, other, *others)
         parts = (starts, local, order, pieces, grad_head, table_rows, block)
-        grad_table, rows_new, sums_first = table_sums(*parts, None, 0, 2)
-        down_q, at_s, grad_table, rows_new = barrier((down_q, at_s, grad_table, rows_new))
-        at_k, at_h = half_kept(attention_both, every, at_s)
+        grad_table, rows_new, sums_first = table_sums(*parts, None, 0, 3)
+        at_s, hid_q, grad_table, rows_new = barrier((at_s, hid_q, grad_table, rows_new))
+        at_k, at_h = half_kept(attention_both, wide_rows, at_s)
         at_t = half_send(at_h)
-        grad_table, rows_new, sums_second = table_sums(*parts, (grad_table, rows_new), 1, 2)
+        grad_table, rows_new, sums_second = table_sums(*parts, (grad_table, rows_new), 1, 3)
         at_t, grad_table, rows_new = barrier((at_t, grad_table, rows_new))
         at_v = half_column(at_k, at_t)
-        attention = row_sum(at_v, row_pieces(at_v))
-        hidden0 = jnp.concatenate([hidden0, row_sum(down_v, down_q)])
+        at_q = row_pieces(at_v)
+        shard_up, shard_down = hidden_shards(row_sum(hid_v, hid_q), hidden1)
+        grad_table, rows_new, sums_third = table_sums(*parts, (grad_table, rows_new), 2, 3)
+        sums_second = sums_second + sums_third
+        at_q, grad_table, rows_new, shard_up, shard_down = barrier(
+            (at_q, grad_table, rows_new, shard_up, shard_down)
+        )
+        attention = row_sum(at_v, at_q)
     else:
         hidden0 = scattered(hidden_grads0)
-        attention_both = jnp.concatenate(
-            [attention_sum(kept0, swap(sent0)), attention_sum(kept1, sent1)], 1
-        )
+        attention_both = attention_sums((kept0, swap(sent0), kept1, sent1), blocks)
         attention = scattered(attention_both)
         column = lax.all_gather(grad_start, "dp").reshape(-1, model)
         local = jnp.where(inside, my_ids, vocab_here).reshape(-1)
@@ -1468,19 +1497,11 @@
             jnp.sum(table_square),
         )
 
-    grads0, grads1 = (attention[:part], hidden0), (attention[part:], hidden1)
-    owned, other = [], []
-    for one, two in zip(grads0, grads1):
-        owned.append(jnp.where(first, one, two))
-        other.append(swap(jnp.where(first, two, one)))
-    shard_in, shard_out = mine_first(owned[0], other[0])
+    if not by_fours():
+        shard_up, shard_down = hidden_shards(hidden0, hidden1)
+    shard_in, shard_out = owned(attention[:part], attention[part:])
     shard_gains = shard_out[:, model : model + 4].T
     shard_out = shard_out[:, :model]
-    halves = jnp.stack(mine_first(owned[1], other[1]))
-    ups = units // 2 // model
-    shard_up = halves[:, : ups * part].reshape(2, ups, part, model).transpose(2, 0, 1, 3)
-    shard_up = shard_up.reshape(part, 2, blocks, half).transpose(0, 2, 1, 3).reshape(part, units)
-    shard_down = halves[:, ups * part :].reshape(2 * half, model)
 
     if by_fours():
         grads = (shard_in, shard_out, shard_up, shard_down, shard_gains)

time: 667 us -> 648 us (0.972)
  waiting for transfers between devices: 123 us -> 100 us
  Pallas kernels: 240 us -> 251 us
  other arithmetic: 66.4 us -> 59.1 us
    ppermute x67 -> x60, waiting for transfers between devices: 86.7 us -> 70.4 us  [cross(): lax.ppermute(values, axis, [(i, i ^ bits) for i in range(lax.axis_size(ax...]
    reduce_scatter x1, waiting for transfers between devices: 12.6 us -> 0.01 us  [scattered(): return single(lax.psum_scatter(parts, BLOCKS, scatter_dimension=0))]
    ppermute x67 -> x60, starting transfers between devices: 94.7 us -> 89.2 us  [cross(): lax.ppermute(values, axis, [(i, i ^ bits) for i in range(lax.axis_size(ax...]
    pallas_call x2 -> x3, Pallas kernels: 42.9 us -> 47.4 us  [table_sums(): pl.pallas_call(functools.partial(table_sums_kernel, first), grid_spec=plt...]
    unnamed x411 -> x420, local copies, waits for them, and re-layouts: 17.2 us -> 21.2 us
  transfers between devices with their start and end apart: 101 -> 91, of which waited for: 39 -> 36; matrix products, arithmetic and copies ran while one was open for 17% -> 17% of each run, Pallas kernels for 29% -> 31%
where the time goes in v3:
time: 648 us; the launch traced here: 644 us
  Pallas kernels  251 us (39%)
  starting transfers between devices  111 us (17%)
  waiting for transfers between devices  100 us (15%)
  local copies, waits for them, and re-layouts  72.5 us (11%)
  other arithmetic  59.1 us (9%)
  matrix products  21.8 us (3%)
  between operations  20.5 us (3%)
  loops' own time  7.37 us (1%)
    ppermute x60, starting transfers between devices, cross(): lax.ppermute(values, axis, [(i, i ^ bits) for i in range(lax.axis_size(ax...  89.2 us
    ppermute x60, waiting for transfers between devices, cross(): lax.ppermute(values, axis, [(i, i ^ bits) for i in range(lax.axis_size(ax...  70.4 us
    pallas_call x3, Pallas kernels, table_sums(): pl.pallas_call(functools.partial(table_sums_kernel, first), grid_spec=plt...  47.4 us
    pallas_call x1, Pallas kernels, table_new(): pl.pallas_call(functools.partial(table_new_kernel, start, row_count), gri...  37.8 us
    pallas_call x3, Pallas kernels, head_table(): pl.pallas_call(functools.partial(head_table_kernel, first), grid=(last -...  34.6 us
    pallas_call x3, Pallas kernels, lowered(): pl.pallas_call(lower_kernel, grid=(last - first,), in_specs=[rows] + ([]...  23.3 us
    unnamed x420, local copies, waits for them, and re-layouts  21.2 us
    pallas_call x2, Pallas kernels, hidden_backward(): pl.pallas_call(hidden_back_kernel, grid_spec=pltpu.PrefetchScalarGridSpec...  20.5 us
  transfers between devices with their start and end apart: 91, of which 36 were waited for; matrix products, arithmetic and copies ran while one was open for 17% of the time, Pallas kernels for 31%

profile of v3, /device:TPU:0, one launch (start us, length us, event | category | flops | bytes accessed | tf_op | source)
XLA Modules:
  0.0 643.6 jit_solution(4011598494335831300)
XLA Ops:
  14.9 2.6 collective-permute-start.6
  19.1 2.1 collective-permute-start.7
  24.0 4.2 collective-permute-start.3
  29.2 2.6 dynamic-slice_reduce_fusion
  33.2 9.4 %shard_map.396 = bf16[384,768]{1,0:T(8,128)(2,1)S(1)} custom-call(s32[384]{0:T(512)S(1)} %broadcast_minimum_fusion.ids_ref, f32[12288,768]{1,0:T(8,128)} %table_ref.8), custom_call_target="tpu_custom_call" | custom-call | bytes 73728 | tf_op jit(solution)/shard_map/pallas_call | solution.py:935
  47.1 2.3 collective-permute-start.9
  53.2 2.2 collective-permute-start.10
  55.3 7.5 %shard_map.397 = (bf16[12288,768]{1,0:T(8,128)(2,1)}, f32[8,768]{1,0:T(8,128)S(1)}) custom-call(f32[12288,768]{1,0:T(8,128)} %table_ref.8), custom_call_target="tpu_custom_call" | custom-call | flops 393216 | bytes 1179648 | tf_op jit(solution)/shard_map/pallas_call | solution.py:444
  62.9 10.0 %collective-permute-done.11 = bf16[96,768]{1,0:T(8,128)(2,1)S(1)} collective-permute-done((bf16[96,768]{1,0:T(8,128)(2,1)S(1)}, bf16[96,768]{1,0:T(8,128)(2,1)S(1)}, u32[]{:S(2)}, u32[]{:S(2)}) %collective-permute-start.11) | collective-permute-done | bytes 147488 | tf_op jit(solution)/shard_map/ppermute | solution.py:68
  73.8 7.6 %shard_map.398 = (bf16[12288,768]{1,0:T(8,128)(2,1)}, f32[8,768]{1,0:T(8,128)S(1)}) custom-call(f32[12288,768]{1,0:T(8,128)} %table_ref.8, bf16[12288,768]{1,0:T(8,128)(2,1)} %get-tuple-element.238.refs_0_), custom_call_target="tpu_custom_call", output_to_operand_aliasing={{0}: (1, {})} | custom-call | flops 393216 | bytes 1179648 | tf_op jit(solution)/shard_map/pallas_call | solution.py:444
  82.0 5.1 collective-permute-done.14
  89.7 5.8 sort.15
  96.2 4.4 collective-permute-start.18
  102.6 8.1 %shard_map.399 = (bf16[12288,768]{1,0:T(8,128)(2,1)}, f32[8,768]{1,0:T(8,128)S(1)}) custom-call(f32[12288,768]{1,0:T(8,128)} %table_ref.8, bf16[12288,768]{1,0:T(8,128)(2,1)} %get-tuple-element.243.refs_0_), custom_call_target="tpu_custom_call", output_to_operand_aliasing={{0}: (1, {})} | custom-call | flops 393216 | bytes 1179648 | tf_op jit(solution)/shard_map/pallas_call | solution.py:444
  110.7 2.2 shard_map.400
  116.0 4.5 collective-permute-start.16
  120.9 2.1 collective-permute-done.16
  123.0 15.9 %collective-permute-done.19 = bf16[192,768]{1,0:T(8,128)(2,1)S(1)} collective-permute-done((bf16[192,768]{1,0:T(8,128)(2,1)}, bf16[192,768]{1,0:T(8,128)(2,1)S(1)}, u32[]{:S(2)}, u32[]{:S(2)}) %collective-permute-start.19) | collective-permute-done | bytes 294944 | tf_op jit(solution)/shard_map/ppermute | solution.py:68
  139.2 4.1 collective-permute-start.21
  143.2 7.7 %shard_map.401 = bf16[256,768]{1,0:T(8,128)(2,1)S(1)} custom-call(bf16[256,768]{1,0:T(8,128)(2,1)S(1)} %fusion.26.query_ref, bf16[768,128]{1,0:T(8,128)(2,1)S(1)} %pad_maximum_fusion.15.keyval_ref, f32[256,768]{1,0:T(8,128)S(1)} %and_select_fusion.1.bias_ref), custom_call_target="tpu_custom_call" | custom-call | flops 37748736 | bytes 98304 | tf_op jit(solution)/shard_map/pallas_call | solution.py:367
  152.2 2.1 collective-permute-done.22.refs_4_
  154.3 2.7 collective-permute-done.21.refs_2_
  163.1 2.2 shard_map.403
  168.7 7.2 %shard_map.402 = (f32[512,1536]{1,0:T(8,128)S(1)}, f32[512,768]{1,0:T(8,128)}) custom-call(s32[1]{0:T(128)} %constant.370.clone.1.place_ref, bf16[512,768]{1,0:T(8,128)(2,1)S(1)} %pad_maximum_fusion.2.both_ref, bf16[4,4,192,768]{3,2,1,0:T(8,128)(2,1)} %bitcast.387, bf16[4,4,192,768]{3,2,1,0:T(8,128)(2,1)} %bitcast.388, bf16[4,4,192,768]{3,2,1,0:T(8,128)(2,1)} %bitcast.389, ...), custom_call_target="tpu_custom_call" | custom-call | flops 150994944 | bytes 688128 | tf_op jit(solution)/shard_map/pallas_call | solution.py:752
  176.8 2.5 slice.234
  184.7 2.2 convert_reduce_fusion.1
  190.2 8.6 %collective-permute-done.27.refs_6_ = bf16[2,192,768]{2,1,0:T(8,128)(2,1)} collective-permute-done((bf16[2,192,768]{2,1,0:T(8,128)(2,1)}, bf16[2,192,768]{2,1,0:T(8,128)(2,1)}, u32[]{:S(2)}, u32[]{:S(2)}) %collective-permute-start.27) | collective-permute-done | bytes 589856 | tf_op jit(solution)/shard_map/ppermute | solution.py:68
  200.8 2.9 collective-permute-start.29
  204.4 3.6 collective-permute-start.30
  223.2 3.0 shard_map.405
  228.2 5.3 collective-permute-start.35
  235.3 2.9 collective-permute-done.34
  248.6 18.0 %shard_map.406 = f32[8,512]{1,0:T(8,128)S(1)} custom-call(bf16[768,512]{1,0:T(8,128)(2,1)S(1)} %get-tuple-element.572.chosen_ref.across_ref, s32[1,512]{1,0:T(1,128)S(1)} %select_n.867.target_ref, bf16[12288,768]{1,0:T(8,128)(2,1)} %get-tuple-element.276.low_ref), custom_call_target="tpu_custom_call" | custom-call | flops 603979776 | bytes 1179648 | tf_op jit(solution)/shard_map/pallas_call | solution.py:490
  268.8 2.3 collective-permute-start.40
  271.1 2.3 copy.237
  276.5 15.6 %shard_map.407 = f32[64,768]{1,0:T(8,128)S(1)} custom-call(bf16[64,768]{1,0:T(8,128)(2,1)S(1)} %bitcast.380, s32[64,1]{1,0:T(8,128)S(1)} %broadcast_in_dim_reshape.8.target_ref, f32[64,1]{1,0:T(8,128)S(1)} %broadcast_in_dim_reshape.9.logsum_ref, bf16[12288,768]{1,0:T(8,128)(2,1)} %get-tuple-element.276.low_ref), custom_call_target="tpu_custom_call" | custom-call | flops 150994944 | bytes 1179648 | tf_op jit(solution)/shard_map/pallas_call | solution.py:526
  292.6 2.2 collective-permute-start.45
  296.1 2.1 collective-permute-done.45
  301.5 7.9 %shard_map.408 = (f32[32,768]{1,0:T(8,128)}, bf16[16,192,768]{2,1,0:T(8,128)(2,1)}) custom-call(s32[1]{0:T(128)} %bitcast.36.place_ref, bf16[32,768]{1,0:T(8,128)(2,1)} %copy-done.40, f32[32,1536]{1,0:T(8,128)} %copy-done.45, bf16[32,768]{1,0:T(8,128)(2,1)} %pad_maximum_fusion.19.grad_ref, bf16[4,192,768]{2,1,0:T(8,128)(2,1)} %copy-done.2, ...), custom_call_target="tpu_custom_call" | custom-call | flops 18874368 | bytes 602112 | tf_op jit(solution)/shard_map/pallas_call | solution.py:812
  331.8 3.0 collective-permute-done.48
  344.0 12.6 %shard_map.410 = (f32[512,768]{1,0:T(8,128)}, bf16[16,192,768]{2,1,0:T(8,128)(2,1)}) custom-call(s32[1]{0:T(128)} %constant.370.clone.1.place_ref, bf16[512,768]{1,0:T(8,128)(2,1)} %copy-done.5, f32[512,1536]{1,0:T(8,128)} %copy-done.20, bf16[512,768]{1,0:T(8,128)(2,1)} %pad_maximum_fusion.4.grad_ref, bf16[4,4,192,768]{3,2,1,0:T(8,128)(2,1)} %bitcast.395, ...), custom_call_target="tpu_custom_call" | custom-call | flops 301989888 | bytes 786432 | tf_op jit(solution)/shard_map/pallas_call | solution.py:812
  356.7 2.1 slice.267
  362.9 2.4 constant_dynamic-slice_fusion.7
  366.9 3.4 collective-permute-start.55
  373.4 13.6 %shard_map.411 = (bf16[256,768]{1,0:T(8,128)(2,1)S(1)}, f32[768,128]{1,0:T(8,128)S(1)}) custom-call(bf16[256,768]{1,0:T(8,128)(2,1)S(1)} %copy-done.17, bf16[768,128]{1,0:T(8,128)(2,1)S(1)} %pad_maximum_fusion.15.keyval_ref, f32[256,768]{1,0:T(8,128)S(1)} %and_select_fusion.1.bias_ref, bf16[256,768]{1,0:T(8,128)(2,1)S(1)} %convolution_convert_fusion.5.grad_ref), custom_call_target="tpu_custom_call" | custom-call | flops 94371840 | bytes 98304 | tf_op jit(solution)/shard_map/pallas_call | solution.py:412
  391.6 12.2 %collective-permute-done.54 = f32[256,128]{1,0:T(8,128)S(1)} collective-permute-done((f32[256,128]{1,0:T(8,128)S(1)}, f32[256,128]{1,0:T(8,128)S(1)}, u32[]{:S(2)}, u32[]{:S(2)}) %collective-permute-start.54) | collective-permute-done | bytes 131104 | tf_op jit(solution)/shard_map/ppermute | solution.py:73
  411.4 2.9 collective-permute-start.61
  417.5 2.2 collective-permute-start.57
  419.7 3.2 broadcast_select_fusion
  424.4 11.6 %shard_map.412.refs_0_ = f32[12288,768]{1,0:T(8,128)} custom-call(bf16[512,768]{1,0:T(8,128)(2,1)S(1)} %copy.247.chosen_ref, bf16[768,512]{1,0:T(8,128)(2,1)S(1)} %get-tuple-element.572.chosen_ref.across_ref, s32[1,512]{1,0:T(1,128)S(1)} %copy-done.47, f32[1,512]{1,0:T(1,128)S(1)} %copy-done.49, bf16[12288,768]{1,0:T(8,128)(2,1)} %get-tuple-element.276.low_ref), custom_call_target="tpu_custom_call" | custom-call | flops 402653184 | bytes 1179648 | tf_op jit(solution)/shard_map/pallas_call | solution.py:565
  438.0 3.7 collective-permute-start.63
  443.3 11.5 %shard_map.413.refs_0_ = f32[12288,768]{1,0:T(8,128)} custom-call(bf16[512,768]{1,0:T(8,128)(2,1)S(1)} %copy.247.chosen_ref, bf16[768,512]{1,0:T(8,128)(2,1)S(1)} %get-tuple-element.572.chosen_ref.across_ref, s32[1,512]{1,0:T(1,128)S(1)} %copy-done.47, f32[1,512]{1,0:T(1,128)S(1)} %copy-done.49, ...), custom_call_target="tpu_custom_call", output_to_operand_aliasing={{}: (5, {})} | custom-call | flops 402653184 | bytes 1179648 | tf_op jit(solution)/shard_map/pallas_call | solution.py:565
  464.8 11.6 %shard_map.415 = f32[12288,768]{1,0:T(8,128)} custom-call(bf16[512,768]{1,0:T(8,128)(2,1)S(1)} %copy.247.chosen_ref, bf16[768,512]{1,0:T(8,128)(2,1)S(1)} %get-tuple-element.572.chosen_ref.across_ref, s32[1,512]{1,0:T(1,128)S(1)} %copy-done.47, f32[1,512]{1,0:T(1,128)S(1)} %copy-done.49, ...), custom_call_target="tpu_custom_call", output_to_operand_aliasing={{}: (5, {})} | custom-call | flops 402653184 | bytes 1179648 | tf_op jit(solution)/shard_map/pallas_call | solution.py:565
  478.2 7.4 %while.10 = (s32[]{:T(128)}, f32[12288,768]{1,0:T(8,128)}, pred[]{:T(512)}, s32[2,4,256]{2,1,0:T(4,128)S(1)}, s32[4,256]{1,0:T(4,128)S(1)}, /*index=5*/bf16[256,...) while((s32[]{:T(128)}, f32[12288,768]{1,0:T(8,128)}, ...), condition=%wide.region_46.47_spmd, body=%wide.region_43.46_spmd.sunk | while | flops 39328784 | bytes 309494080 | solution.py:1457
  489.6 2.5 shard_map.414
  495.3 2.6 collective-permute-start.75
  499.8 16.0 %shard_map.416 = (f32[12288,768]{1,0:T(8,128)}, f32[96,128]{1,0:T(8,128)}, f32[16,768]{1,0:T(8,128)}) custom-call(s32[2]{0:T(128)} %copy-done.57, s32[13]{0:T(128)} %convert_reduce_fusion.2.starts_ref, s32[3072]{0:T(1024)} %copy-done.124, s32[3072]{0:T(1024)} %get-tuple-element.317.order_ref, f32[12288,768]{1,0:T(8,128)} %get-tuple-element.318.head_ref, ...), custom_call_target="tpu_custom_call" | custom-call | flops 1572864 | bytes 1572864 | tf_op jit(solution)/shard_map/pallas_call | solution.py:644
  515.8 5.9 collective-permute-done.74
  527.3 15.9 %shard_map.417 = (f32[12288,768]{1,0:T(8,128)}, f32[96,128]{1,0:T(8,128)}, f32[16,768]{1,0:T(8,128)}) custom-call(s32[2]{0:T(128)} %copy-done.57, s32[13]{0:T(128)} %convert_reduce_fusion.2.starts_ref, s32[3072]{0:T(1024)} %copy-done.124, s32[3072]{0:T(1024)} %get-tuple-element.317.order_ref, ...), custom_call_target="tpu_custom_call", output_to_operand_aliasing={{0}: (14, {}), {1}: (15, {})} | custom-call | flops 1572864 | bytes 1572864 | tf_op jit(solution)/shard_map/pallas_call | solution.py:644
  548.8 2.7 collective-permute-start.79
  551.4 15.5 %shard_map.418 = (f32[12288,768]{1,0:T(8,128)}, f32[96,128]{1,0:T(8,128)}, f32[16,768]{1,0:T(8,128)}) custom-call(s32[2]{0:T(128)} %copy-done.57, s32[13]{0:T(128)} %convert_reduce_fusion.2.starts_ref, s32[3072]{0:T(1024)} %copy-done.124, s32[3072]{0:T(1024)} %get-tuple-element.317.order_ref, ...), custom_call_target="tpu_custom_call", output_to_operand_aliasing={{0}: (14, {}), {1}: (15, {})} | custom-call | flops 1572864 | bytes 1572864 | tf_op jit(solution)/shard_map/pallas_call | solution.py:644
  571.4 2.2 reshape.809.refs_2_
  579.3 2.6 collective-permute-start.85
  595.1 37.8 %shard_map.420 = (f32[12288,768]{1,0:T(8,128)}, f32[1,768]{1,0:T(1,128)S(1)}) custom-call(f32[112,128]{1,0:T(8,128)S(1)} %add_add_fusion.4.totals_ref, f32[12288,768]{1,0:T(8,128)} %table_ref.8, f32[12288,768]{1,0:T(8,128)} %get-tuple-element.448.grad_ref, f32[96,128]{1,0:T(8,128)S(1)} %copy-done.39, f32[1,768]{1,0:T(1,128)S(1)} %broadcast_in_dim.233.cols_ref), custom_call_target="tpu_custom_call" | custom-call | flops 2359296 | bytes 7077888 | tf_op jit(solution)/shard_map/pallas_call | solution.py:1111
  (845 shorter events, 210.2 us)
Async XLA Ops:
  24.0 19.5 %collective-permute-start.3 = (bf16[96,896]{1,0:T(8,128)(2,1)S(1)}, bf16[96,896]{1,0:T(8,128)(2,1)S(1)}, u32[]{:S(2)}, u32[]{:S(2)}) collective-permute-start(bf16[96,896]{1,0:T(8,128)(2,1)S(1)} %pad_maximum_fusion.16), channel_id=1, source_target_pairs={{0,12},{4,8},{8,4},{12,0},{1,13},{5,9},{9,5},{13,1},{2,14},{6,10},... | collective-permute-start | bytes 516104 | tf_op jit(solution)/shard_map/ppermute | solution.py:68
  28.2 15.4 %collective-permute-start.2 = (bf16[96,896]{1,0:T(8,128)(2,1)S(1)}, bf16[96,896]{1,0:T(8,128)(2,1)S(1)}, u32[]{:S(2)}, u32[]{:S(2)}) collective-permute-start(bf16[96,896]{1,0:T(8,128)(2,1)S(1)} %pad_maximum_fusion.16), channel_id=1, source_target_pairs={{0,8},{4,12},{8,0},{12,4},{1,9},{5,13},{9,1},{13,5},{2,10},{6,14},... | collective-permute-start | bytes 516104 | tf_op jit(solution)/shard_map/ppermute | solution.py:68
  28.2 15.4 %collective-permute-start.1 = (bf16[96,896]{1,0:T(8,128)(2,1)S(1)}, bf16[96,896]{1,0:T(8,128)(2,1)S(1)}, u32[]{:S(2)}, u32[]{:S(2)}) collective-permute-start(bf16[96,896]{1,0:T(8,128)(2,1)S(1)} %pad_maximum_fusion.16), channel_id=1, source_target_pairs={{0,4},{4,0},{8,12},{12,8},{1,5},{5,1},{9,13},{13,9},{2,6},{6,2},{1... | collective-permute-start | bytes 516104 | tf_op jit(solution)/shard_map/ppermute | solution.py:68
  32.9 9.7 %collective-permute-start.4 = (bf16[192,768]{1,0:T(8,128)(2,1)S(1)}, bf16[192,768]{1,0:T(8,128)(2,1)S(1)}, u32[]{:S(2)}, u32[]{:S(2)}) collective-permute-start(bf16[192,768]{1,0:T(8,128)(2,1)S(1)} %pad_maximum_fusion.13), channel_id=1, source_target_pairs={{0,16},{16,0},{1,17},{17,1},{2,18},{18,2},{3,19},{19,3},{4,20},{20... | collective-permute-start | bytes 884744 | tf_op jit(solution)/shard_map/ppermute | solution.py:64
  45.0 123.7 %all-gather.7.cloned.1.call-start = ((), (), s32[]{:S(2)}) async-start(), calls=%async_computation.4 | async-start | bytes 5013504 | tf_op jit(solution)/shard_map/all_gather | solution.py:1197
  45.6 430.8 %reduce-scatter.5.cloned.1.call-start = ((), (), s32[]{:S(2)}) async-start(), calls=%async_computation.3 | async-start | bytes 5013504 | tf_op jit(solution)/shard_map/reduce_scatter | solution.py:209
  47.1 25.8 %collective-permute-start.9 = (bf16[4,96,896]{2,1,0:T(8,128)(2,1)S(1)}, bf16[4,96,896]{2,1,0:T(8,128)(2,1)S(1)}, u32[]{:S(2)}, u32[]{:S(2)}) collective-permute-start(bf16[4,96,896]{2,1,0:T(8,128)(2,1)S(1)} %pad_maximum_fusion.5), channel_id=1, source_target_pairs={{0,2},{1,3},{2,0},{3,1},{4,6},{5,7},{6,4},{7,5},{8,10},{9,11},{10,... | collective-permute-start | bytes 2064392 | tf_op jit(solution)/shard_map/ppermute | solution.py:68
  49.3 23.6 %collective-permute-start.8 = (bf16[4,96,896]{2,1,0:T(8,128)(2,1)S(1)}, bf16[4,96,896]{2,1,0:T(8,128)(2,1)S(1)}, u32[]{:S(2)}, u32[]{:S(2)}) collective-permute-start(bf16[4,96,896]{2,1,0:T(8,128)(2,1)S(1)} %pad_maximum_fusion.5), channel_id=1, source_target_pairs={{0,1},{1,0},{2,3},{3,2},{4,5},{5,4},{6,7},{7,6},{8,9},{9,8},{10,11... | collective-permute-start | bytes 2064392 | tf_op jit(solution)/shard_map/ppermute | solution.py:68
  50.9 12.0 %collective-permute-start.12 = (bf16[96,768]{1,0:T(8,128)(2,1)S(1)}, bf16[96,768]{1,0:T(8,128)(2,1)S(1)}, u32[]{:S(2)}, u32[]{:S(2)}) collective-permute-start(bf16[96,768]{1,0:T(8,128)(2,1)S(1)} %get-tuple-element.587), channel_id=1, source_target_pairs={{0,12},{4,8},{8,4},{12,0},{1,13},{5,9},{9,5},{13,1},{2,14},{6,10},... | collective-permute-start | bytes 442376 | tf_op jit(solution)/shard_map/ppermute | solution.py:68
  52.9 19.9 %collective-permute-start.11 = (bf16[96,768]{1,0:T(8,128)(2,1)S(1)}, bf16[96,768]{1,0:T(8,128)(2,1)S(1)}, u32[]{:S(2)}, u32[]{:S(2)}) collective-permute-start(bf16[96,768]{1,0:T(8,128)(2,1)S(1)} %get-tuple-element.588), channel_id=1, source_target_pairs={{0,8},{4,12},{8,0},{12,4},{1,9},{5,13},{9,1},{13,5},{2,10},{6,14},... | collective-permute-start | bytes 442376 | tf_op jit(solution)/shard_map/ppermute | solution.py:68
  53.2 19.7 %collective-permute-start.10 = (bf16[96,768]{1,0:T(8,128)(2,1)S(1)}, bf16[96,768]{1,0:T(8,128)(2,1)S(1)}, u32[]{:S(2)}, u32[]{:S(2)}) collective-permute-start(bf16[96,768]{1,0:T(8,128)(2,1)S(1)} %get-tuple-element.589), channel_id=1, source_target_pairs={{0,4},{4,0},{8,12},{12,8},{1,5},{5,1},{9,13},{13,9},{2,6},{6,2},{1... | collective-permute-start | bytes 442376 | tf_op jit(solution)/shard_map/ppermute | solution.py:68
  73.7 13.4 %collective-permute-start.14 = (bf16[2,96,896]{2,1,0:T(8,128)(2,1)S(1)}, bf16[2,96,896]{2,1,0:T(8,128)(2,1)S(1)}, u32[]{:S(2)}, u32[]{:S(2)}) collective-permute-start(bf16[2,96,896]{2,1,0:T(8,128)(2,1)S(1)} %slice.221), channel_id=1, source_target_pairs={{0,2},{1,3},{2,0},{3,1},{4,6},{5,7},{6,4},{7,5},{8,10},{9,11},{10,... | collective-permute-start | bytes 1032200 | tf_op jit(solution)/shard_map/ppermute | solution.py:68
  73.7 13.8 %collective-permute-start.13 = (bf16[2,96,896]{2,1,0:T(8,128)(2,1)S(1)}, bf16[2,96,896]{2,1,0:T(8,128)(2,1)S(1)}, u32[]{:S(2)}, u32[]{:S(2)}) collective-permute-start(bf16[2,96,896]{2,1,0:T(8,128)(2,1)S(1)} %slice.220), channel_id=1, source_target_pairs={{0,1},{1,0},{2,3},{3,2},{4,5},{5,4},{6,7},{7,6},{8,9},{9,8},{10,11... | collective-permute-start | bytes 1032200 | tf_op jit(solution)/shard_map/ppermute | solution.py:68
  88.9 21.8 %collective-permute-start.15 = (bf16[16,96,896]{2,1,0:T(8,128)(2,1)S(1)}, bf16[16,96,896]{2,1,0:T(8,128)(2,1)}, u32[]{:S(2)}, u32[]{:S(2)}) collective-permute-start(bf16[16,96,896]{2,1,0:T(8,128)(2,1)S(1)} %constant_dynamic-update-slice_fusion.refs_0_), channel_id=1, source_target_pairs={{0,16},{16,0},{1,17},{17,1},{2,18},{18,2},{3,19},{19,3},{4,20},{20... | collective-permute-start | bytes 8257544 | tf_op jit(solution)/shard_map/ppermute | solution.py:64
  96.2 26.8 %collective-permute-start.20 = (bf16[192,768]{1,0:T(8,128)(2,1)}, bf16[192,768]{1,0:T(8,128)(2,1)S(1)}, u32[]{:S(2)}, u32[]{:S(2)}) collective-permute-start(bf16[192,768]{1,0:T(8,128)(2,1)} %get-tuple-element.232), channel_id=1, source_target_pairs={{0,12},{4,8},{8,4},{12,0},{1,13},{5,9},{9,5},{13,1},{2,14},{6,10},... | collective-permute-start | bytes 884744 | tf_op jit(solution)/shard_map/ppermute | solution.py:68
  96.2 42.7 %collective-permute-start.19 = (bf16[192,768]{1,0:T(8,128)(2,1)}, bf16[192,768]{1,0:T(8,128)(2,1)S(1)}, u32[]{:S(2)}, u32[]{:S(2)}) collective-permute-start(bf16[192,768]{1,0:T(8,128)(2,1)} %get-tuple-element.232), channel_id=1, source_target_pairs={{0,8},{4,12},{8,0},{12,4},{1,9},{5,13},{9,1},{13,5},{2,10},{6,14},... | collective-permute-start | bytes 884744 | tf_op jit(solution)/shard_map/ppermute | solution.py:68
  96.2 42.7 %collective-permute-start.18 = (bf16[192,768]{1,0:T(8,128)(2,1)}, bf16[192,768]{1,0:T(8,128)(2,1)S(1)}, u32[]{:S(2)}, u32[]{:S(2)}) collective-permute-start(bf16[192,768]{1,0:T(8,128)(2,1)} %get-tuple-element.232), channel_id=1, source_target_pairs={{0,4},{4,0},{8,12},{12,8},{1,5},{5,1},{9,13},{13,9},{2,6},{6,2},{1... | collective-permute-start | bytes 884744 | tf_op jit(solution)/shard_map/ppermute | solution.py:68
  116.0 7.0 %collective-permute-start.16 = (bf16[256,128]{1,0:T(8,128)(2,1)S(1)}, bf16[256,128]{1,0:T(8,128)(2,1)S(1)}, u32[]{:S(2)}, u32[]{:S(2)}) collective-permute-start(bf16[256,128]{1,0:T(8,128)(2,1)S(1)} %slice.413), channel_id=1, source_target_pairs={{0,2},{1,3},{4,6},{5,7},{8,10},{9,11},{12,14},{13,15},{16,18},{17,... | collective-permute-start | bytes 196616 | tf_op jit(solution)/shard_map/ppermute | solution.py:73
  139.1 15.2 %collective-permute-start.22 = (bf16[2,192,768]{2,1,0:T(8,128)(2,1)S(1)}, bf16[2,192,768]{2,1,0:T(8,128)(2,1)}, u32[]{:S(2)}, u32[]{:S(2)}) collective-permute-start(bf16[2,192,768]{2,1,0:T(8,128)(2,1)S(1)} %pad_maximum_fusion.8), channel_id=1, source_target_pairs={{0,2},{1,3},{2,0},{3,1},{4,6},{5,7},{6,4},{7,5},{8,10},{9,11},{10,... | collective-permute-start | bytes 1769480 | tf_op jit(solution)/shard_map/ppermute | solution.py:68
  139.2 17.8 %collective-permute-start.21 = (bf16[2,192,768]{2,1,0:T(8,128)(2,1)S(1)}, bf16[2,192,768]{2,1,0:T(8,128)(2,1)S(1)}, u32[]{:S(2)}, u32[]{:S(2)}) collective-permute-start(bf16[2,192,768]{2,1,0:T(8,128)(2,1)S(1)} %pad_maximum_fusion.8), channel_id=1, source_target_pairs={{0,1},{1,0},{2,3},{3,2},{4,5},{5,4},{6,7},{7,6},{8,9},{9,8},{10,11... | collective-permute-start | bytes 1769480 | tf_op jit(solution)/shard_map/ppermute | solution.py:68
  159.7 16.2 %collective-permute-start.25 = (bf16[2,192,768]{2,1,0:T(8,128)(2,1)}, bf16[2,192,768]{2,1,0:T(8,128)(2,1)S(1)}, u32[]{:S(2)}, u32[]{:S(2)}) collective-permute-start(bf16[2,192,768]{2,1,0:T(8,128)(2,1)} %slice.231), channel_id=1, source_target_pairs={{0,2},{1,3},{2,0},{3,1},{4,6},{5,7},{6,4},{7,5},{8,10},{9,11},{10,... | collective-permute-start | bytes 1769480 | tf_op jit(solution)/shard_map/ppermute | solution.py:68
  161.3 15.4 %collective-permute-start.24 = (bf16[2,192,768]{2,1,0:T(8,128)(2,1)}, bf16[2,192,768]{2,1,0:T(8,128)(2,1)}, u32[]{:S(2)}, u32[]{:S(2)}) collective-permute-start(bf16[2,192,768]{2,1,0:T(8,128)(2,1)} %slice.231), channel_id=1, source_target_pairs={{0,1},{1,0},{2,3},{3,2},{4,5},{5,4},{6,7},{7,6},{8,9},{9,8},{10,11... | collective-permute-start | bytes 1769480 | tf_op jit(solution)/shard_map/ppermute | solution.py:68
  182.7 16.1 %collective-permute-start.27 = (bf16[2,192,768]{2,1,0:T(8,128)(2,1)}, bf16[2,192,768]{2,1,0:T(8,128)(2,1)}, u32[]{:S(2)}, u32[]{:S(2)}) collective-permute-start(bf16[2,192,768]{2,1,0:T(8,128)(2,1)} %collective-permute-done.22.refs_4_), channel_id=1, source_target_pairs={{0,1},{1,0},{2,3},{3,2},{4,5},{5,4},{6,7},{7,6},{8,9},{9,8},{10,11... | collective-permute-start | bytes 1769480 | tf_op jit(solution)/shard_map/ppermute | solution.py:68
  184.2 15.7 %collective-permute-start.28 = (bf16[2,192,768]{2,1,0:T(8,128)(2,1)}, bf16[2,192,768]{2,1,0:T(8,128)(2,1)S(1)}, u32[]{:S(2)}, u32[]{:S(2)}) collective-permute-start(bf16[2,192,768]{2,1,0:T(8,128)(2,1)} %collective-permute-done.24.refs_3_), channel_id=1, source_target_pairs={{0,2},{1,3},{2,0},{3,1},{4,6},{5,7},{6,4},{7,5},{8,10},{9,11},{10,... | collective-permute-start | bytes 1769480 | tf_op jit(solution)/shard_map/ppermute | solution.py:68
  200.8 9.6 %collective-permute-start.29 = (bf16[256,128]{1,0:T(8,128)(2,1)}, bf16[256,128]{1,0:T(8,128)(2,1)}, u32[]{:S(2)}, u32[]{:S(2)}) collective-permute-start(bf16[256,128]{1,0:T(8,128)(2,1)} %convolution_convert_fusion.7), channel_id=1, source_target_pairs={{0,2},{1,3},{4,6},{5,7},{8,10},{9,11},{12,14},{13,15},{16,18},{17,... | collective-permute-start | bytes 196616 | tf_op jit(solution)/shard_map/ppermute | solution.py:73
  204.4 6.9 %collective-permute-start.30 = (bf16[256,128]{1,0:T(8,128)(2,1)}, bf16[256,128]{1,0:T(8,128)(2,1)}, u32[]{:S(2)}, u32[]{:S(2)}) collective-permute-start(bf16[256,128]{1,0:T(8,128)(2,1)} %convolution_convert_fusion.7), channel_id=1, source_target_pairs={{0,1},{1,2},{2,3},{4,5},{5,6},{6,7},{8,9},{9,10},{10,11},{12,13},{... | collective-permute-start | bytes 196616 | tf_op jit(solution)/shard_map/ppermute | solution.py:73
  228.2 7.1 %collective-permute-start.35 = (bf16[16,768]{1,0:T(8,128)(2,1)S(1)}, bf16[16,768]{1,0:T(8,128)(2,1)S(1)}, u32[]{:S(2)}, u32[]{:S(2)}) collective-permute-start(bf16[16,768]{1,0:T(8,128)(2,1)S(1)} %add_convert_fusion.10), channel_id=1, source_target_pairs={{0,12},{4,8},{8,4},{12,0},{1,13},{5,9},{9,5},{13,1},{2,14},{6,10},... | collective-permute-start | bytes 73736 | tf_op jit(solution)/shard_map/ppermute | solution.py:68
  266.7 7.6 %collective-permute-start.42 = (f32[3,512]{1,0:T(4,128)S(1)}, f32[3,512]{1,0:T(4,128)S(1)}, u32[]{:S(2)}, u32[]{:S(2)}) collective-permute-start(f32[3,512]{1,0:T(4,128)S(1)} %slice.298), channel_id=1, source_target_pairs={{0,12},{4,8},{8,4},{12,0},{1,13},{5,9},{9,5},{13,1},{2,14},{6,10},... | collective-permute-start | bytes 18440 | tf_op jit(solution)/shard_map/ppermute | solution.py:68
  326.4 8.5 %collective-permute-start.48 = (f32[256,128]{1,0:T(8,128)S(1)}, f32[256,128]{1,0:T(8,128)S(1)}, u32[]{:S(2)}, u32[]{:S(2)}) collective-permute-start(f32[256,128]{1,0:T(8,128)S(1)} %get-tuple-element.594), channel_id=1, source_target_pairs={{1,0},{2,1},{3,2},{5,4},{6,5},{7,6},{9,8},{10,9},{11,10},{13,12},{... | collective-permute-start | bytes 393224 | tf_op jit(solution)/shard_map/ppermute | solution.py:73
  327.7 8.3 %collective-permute-start.49 = (f32[256,128]{1,0:T(8,128)S(1)}, f32[256,128]{1,0:T(8,128)S(1)}, u32[]{:S(2)}, u32[]{:S(2)}) collective-permute-start(f32[256,128]{1,0:T(8,128)S(1)} %get-tuple-element.595), channel_id=1, source_target_pairs={{2,0},{3,1},{6,4},{7,5},{10,8},{11,9},{14,12},{15,13},{18,16},{19,... | collective-permute-start | bytes 393224 | tf_op jit(solution)/shard_map/ppermute | solution.py:73
  342.7 20.2 %collective-permute-start.52 = (bf16[768,896]{1,0:T(8,128)(2,1)}, bf16[768,896]{1,0:T(8,128)(2,1)S(1)}, u32[]{:S(2)}, u32[]{:S(2)}) collective-permute-start(bf16[768,896]{1,0:T(8,128)(2,1)} %maximum_select_fusion), channel_id=1, source_target_pairs={{0,16},{16,0},{1,17},{17,1},{2,18},{18,2},{3,19},{19,3},{4,20},{20... | collective-permute-start | bytes 4128776 | tf_op jit(solution)/shard_map/ppermute | solution.py:64
  366.9 38.2 %collective-permute-start.56 = (bf16[2,1,2,192,768]{4,3,0,2,1:T(8,128)(2,1)S(1)}, bf16[2,1,2,192,768]{4,3,0,2,1:T(8,128)(2,1)S(1)}, u32[]{:S(2)}, u32[]{:S(2)}) collective-permute-start(bf16[2,1,2,192,768]{4,3,0,2,1:T(8,128)(2,1)S(1)} %copy.273), channel_id=1, source_target_pairs={{0,2},{1,3},{2,0},{3,1},{4,6},{5,7},{6,4},{7,5},{8,10},{9,11},{10,... | collective-permute-start | bytes 3538952 | tf_op jit(solution)/shard_map/ppermute | solution.py:68
  366.9 38.1 %collective-permute-start.55 = (bf16[2,2,1,192,768]{4,3,0,2,1:T(8,128)(2,1)S(1)}, bf16[2,2,1,192,768]{4,3,0,2,1:T(8,128)(2,1)S(1)}, u32[]{:S(2)}, u32[]{:S(2)}) collective-permute-start(bf16[2,2,1,192,768]{4,3,0,2,1:T(8,128)(2,1)S(1)} %copy.272), channel_id=1, source_target_pairs={{0,1},{1,0},{2,3},{3,2},{4,5},{5,4},{6,7},{7,6},{8,9},{9,8},{10,11... | collective-permute-start | bytes 3538952 | tf_op jit(solution)/shard_map/ppermute | solution.py:68
  387.1 16.7 %collective-permute-start.54 = (f32[256,128]{1,0:T(8,128)S(1)}, f32[256,128]{1,0:T(8,128)S(1)}, u32[]{:S(2)}, u32[]{:S(2)}) collective-permute-start(f32[256,128]{1,0:T(8,128)S(1)} %get-tuple-element.592), channel_id=1, source_target_pairs={{2,0},{3,1},{6,4},{7,5},{10,8},{11,9},{14,12},{15,13},{18,16},{19,... | collective-permute-start | bytes 393224 | tf_op jit(solution)/shard_map/ppermute | solution.py:73
  388.5 16.5 %collective-permute-start.53 = (f32[256,128]{1,0:T(8,128)S(1)}, f32[256,128]{1,0:T(8,128)S(1)}, u32[]{:S(2)}, u32[]{:S(2)}) collective-permute-start(f32[256,128]{1,0:T(8,128)S(1)} %get-tuple-element.593), channel_id=1, source_target_pairs={{1,0},{2,1},{3,2},{5,4},{6,5},{7,6},{9,8},{10,9},{11,10},{13,12},{... | collective-permute-start | bytes 393224 | tf_op jit(solution)/shard_map/ppermute | solution.py:73
  409.9 26.0 %collective-permute-start.60 = (bf16[2,192,768]{2,1,0:T(8,128)(2,1)}, bf16[2,192,768]{2,1,0:T(8,128)(2,1)}, u32[]{:S(2)}, u32[]{:S(2)}) collective-permute-start(bf16[2,192,768]{2,1,0:T(8,128)(2,1)} %dynamic-slice_bitcast_fusion.1), channel_id=1, source_target_pairs={{0,2},{1,3},{2,0},{3,1},{4,6},{5,7},{6,4},{7,5},{8,10},{9,11},{10,... | collective-permute-start | bytes 1769480 | tf_op jit(solution)/shard_map/ppermute | solution.py:68
  411.4 24.6 %collective-permute-start.61 = (bf16[2,192,768]{2,1,0:T(8,128)(2,1)}, bf16[2,192,768]{2,1,0:T(8,128)(2,1)}, u32[]{:S(2)}, u32[]{:S(2)}) collective-permute-start(bf16[2,192,768]{2,1,0:T(8,128)(2,1)} %dynamic-slice_bitcast_fusion), channel_id=1, source_target_pairs={{0,1},{1,0},{2,3},{3,2},{4,5},{5,4},{6,7},{7,6},{8,9},{9,8},{10,11... | collective-permute-start | bytes 1769480 | tf_op jit(solution)/shard_map/ppermute | solution.py:68
  415.3 20.7 %collective-permute-start.59 = (bf16[96,768]{1,0:T(8,128)(2,1)}, bf16[96,768]{1,0:T(8,128)(2,1)}, u32[]{:S(2)}, u32[]{:S(2)}) collective-permute-start(bf16[96,768]{1,0:T(8,128)(2,1)} %get-tuple-element.582), channel_id=1, source_target_pairs={{0,12},{4,8},{8,4},{12,0},{1,13},{5,9},{9,5},{13,1},{2,14},{6,10},... | collective-permute-start | bytes 442376 | tf_op jit(solution)/shard_map/ppermute | solution.py:68
  417.2 18.8 %collective-permute-start.58 = (bf16[96,768]{1,0:T(8,128)(2,1)}, bf16[96,768]{1,0:T(8,128)(2,1)}, u32[]{:S(2)}, u32[]{:S(2)}) collective-permute-start(bf16[96,768]{1,0:T(8,128)(2,1)} %get-tuple-element.583), channel_id=1, source_target_pairs={{0,8},{4,12},{8,0},{12,4},{1,9},{5,13},{9,1},{13,5},{2,10},{6,14},... | collective-permute-start | bytes 442376 | tf_op jit(solution)/shard_map/ppermute | solution.py:68
  417.5 18.5 %collective-permute-start.57 = (bf16[96,768]{1,0:T(8,128)(2,1)}, bf16[96,768]{1,0:T(8,128)(2,1)}, u32[]{:S(2)}, u32[]{:S(2)}) collective-permute-start(bf16[96,768]{1,0:T(8,128)(2,1)} %get-tuple-element.584), channel_id=1, source_target_pairs={{0,4},{4,0},{8,12},{12,8},{1,5},{5,1},{9,13},{13,9},{2,6},{6,2},{1... | collective-permute-start | bytes 442376 | tf_op jit(solution)/shard_map/ppermute | solution.py:68
  436.0 23.5 %collective-permute-start.65 = (bf16[768,896]{1,0:T(8,128)(2,1)}, bf16[768,896]{1,0:T(8,128)(2,1)}, u32[]{:S(2)}, u32[]{:S(2)}) collective-permute-start(bf16[768,896]{1,0:T(8,128)(2,1)} %get-tuple-element.301), channel_id=1, source_target_pairs={{0,16},{16,0},{1,17},{17,1},{2,18},{18,2},{3,19},{19,3},{4,20},{20... | collective-permute-start | bytes 4128776 | tf_op jit(solution)/shard_map/ppermute | solution.py:64
  437.4 21.3 %collective-permute-start.64 = (bf16[4,96,768]{2,1,0:T(8,128)(2,1)S(1)}, bf16[4,96,768]{2,1,0:T(8,128)(2,1)S(1)}, u32[]{:S(2)}, u32[]{:S(2)}) collective-permute-start(bf16[4,96,768]{2,1,0:T(8,128)(2,1)S(1)} %pad_maximum_fusion.9.refs_0_), channel_id=1, source_target_pairs={{0,16},{16,0},{1,17},{17,1},{2,18},{18,2},{3,19},{19,3},{4,20},{20... | collective-permute-start | bytes 1769480 | tf_op jit(solution)/shard_map/ppermute | solution.py:64
  438.0 20.7 %collective-permute-start.63 = (bf16[4,96,768]{2,1,0:T(8,128)(2,1)S(1)}, bf16[4,96,768]{2,1,0:T(8,128)(2,1)}, u32[]{:S(2)}, u32[]{:S(2)}) collective-permute-start(bf16[4,96,768]{2,1,0:T(8,128)(2,1)S(1)} %pad_maximum_fusion.9.refs_0_), channel_id=1, source_target_pairs={{0,2},{1,3},{2,0},{3,1},{4,6},{5,7},{6,4},{7,5},{8,10},{9,11},{10,... | collective-permute-start | bytes 1769480 | tf_op jit(solution)/shard_map/ppermute | solution.py:68
  441.7 17.2 %collective-permute-start.62 = (bf16[4,96,768]{2,1,0:T(8,128)(2,1)S(1)}, bf16[4,96,768]{2,1,0:T(8,128)(2,1)}, u32[]{:S(2)}, u32[]{:S(2)}) collective-permute-start(bf16[4,96,768]{2,1,0:T(8,128)(2,1)S(1)} %pad_maximum_fusion.9.refs_0_), channel_id=1, source_target_pairs={{0,1},{1,0},{2,3},{3,2},{4,5},{5,4},{6,7},{7,6},{8,9},{9,8},{10,11... | collective-permute-start | bytes 1769480 | tf_op jit(solution)/shard_map/ppermute | solution.py:68
  461.1 34.1 %collective-permute-start.68 = (bf16[4,96,768]{2,1,0:T(8,128)(2,1)}, bf16[4,96,768]{2,1,0:T(8,128)(2,1)}, u32[]{:S(2)}, u32[]{:S(2)}) collective-permute-start(bf16[4,96,768]{2,1,0:T(8,128)(2,1)} %collective-permute-done.62.refs_1_), channel_id=1, source_target_pairs={{0,16},{16,0},{1,17},{17,1},{2,18},{18,2},{3,19},{19,3},{4,20},{20... | collective-permute-start | bytes 1769480 | tf_op jit(solution)/shard_map/ppermute | solution.py:64
  462.8 32.4 %collective-permute-start.69 = (bf16[4,96,768]{2,1,0:T(8,128)(2,1)}, bf16[4,96,768]{2,1,0:T(8,128)(2,1)}, u32[]{:S(2)}, u32[]{:S(2)}) collective-permute-start(bf16[4,96,768]{2,1,0:T(8,128)(2,1)} %collective-permute-done.63.refs_2_), channel_id=1, source_target_pairs={{0,16},{16,0},{1,17},{17,1},{2,18},{18,2},{3,19},{19,3},{4,20},{20... | collective-permute-start | bytes 1769480 | tf_op jit(solution)/shard_map/ppermute | solution.py:64
  463.4 22.2 %collective-permute-start.70 = (bf16[2,96,768]{2,1,0:T(8,128)(2,1)}, bf16[2,96,768]{2,1,0:T(8,128)(2,1)}, u32[]{:S(2)}, u32[]{:S(2)}) collective-permute-start(bf16[2,96,768]{2,1,0:T(8,128)(2,1)} %slice.271), channel_id=1, source_target_pairs={{0,1},{1,0},{2,3},{3,2},{4,5},{5,4},{6,7},{7,6},{8,9},{9,8},{10,11... | collective-permute-start | bytes 884744 | tf_op jit(solution)/shard_map/ppermute | solution.py:68
  464.4 21.1 %collective-permute-start.71 = (bf16[2,96,768]{2,1,0:T(8,128)(2,1)}, bf16[2,96,768]{2,1,0:T(8,128)(2,1)}, u32[]{:S(2)}, u32[]{:S(2)}) collective-permute-start(bf16[2,96,768]{2,1,0:T(8,128)(2,1)} %slice.272), channel_id=1, source_target_pairs={{0,2},{1,3},{2,0},{3,1},{4,6},{5,7},{6,4},{7,5},{8,10},{9,11},{10,... | collective-permute-start | bytes 884744 | tf_op jit(solution)/shard_map/ppermute | solution.py:68
  487.7 7.6 %collective-permute-start.72 = (bf16[4,96,768]{2,1,0:T(8,128)(2,1)S(1)}, bf16[4,96,768]{2,1,0:T(8,128)(2,1)S(1)}, u32[]{:S(2)}, u32[]{:S(2)}) collective-permute-start(bf16[4,96,768]{2,1,0:T(8,128)(2,1)S(1)} %constant_dynamic-update-slice_fusion.8.refs_3_), channel_id=1, source_target_pairs={{0,16},{16,0},{1,17},{17,1},{2,18},{18,2},{3,19},{19,3},{4,20},{20... | collective-permute-start | bytes 1769480 | tf_op jit(solution)/shard_map/ppermute | solution.py:64
  492.6 23.2 %collective-permute-start.67 = (bf16[2,1,2,96,896]{4,3,0,2,1:T(8,128)(2,1)S(1)}, bf16[2,1,2,96,896]{4,3,0,2,1:T(8,128)(2,1)S(1)}, u32[]{:S(2)}, u32[]{:S(2)}) collective-permute-start(bf16[2,1,2,96,896]{4,3,0,2,1:T(8,128)(2,1)S(1)} %copy.278), channel_id=1, source_target_pairs={{0,2},{1,3},{2,0},{3,1},{4,6},{5,7},{6,4},{7,5},{8,10},{9,11},{10,... | collective-permute-start | bytes 2064392 | tf_op jit(solution)/shard_map/ppermute | solution.py:68
  494.3 21.5 %collective-permute-start.66 = (bf16[2,2,1,96,896]{4,3,0,2,1:T(8,128)(2,1)S(1)}, bf16[2,2,1,96,896]{4,3,0,2,1:T(8,128)(2,1)S(1)}, u32[]{:S(2)}, u32[]{:S(2)}) collective-permute-start(bf16[2,2,1,96,896]{4,3,0,2,1:T(8,128)(2,1)S(1)} %copy.277), channel_id=1, source_target_pairs={{0,1},{1,0},{2,3},{3,2},{4,5},{5,4},{6,7},{7,6},{8,9},{9,8},{10,11... | collective-permute-start | bytes 2064392 | tf_op jit(solution)/shard_map/ppermute | solution.py:68
  495.3 20.5 %collective-permute-start.75 = (bf16[192,768]{1,0:T(8,128)(2,1)S(1)}, bf16[192,768]{1,0:T(8,128)(2,1)S(1)}, u32[]{:S(2)}, u32[]{:S(2)}) collective-permute-start(bf16[192,768]{1,0:T(8,128)(2,1)S(1)} %get-tuple-element.555), channel_id=1, source_target_pairs={{0,12},{4,8},{8,4},{12,0},{1,13},{5,9},{9,5},{13,1},{2,14},{6,10},... | collective-permute-start | bytes 884744 | tf_op jit(solution)/shard_map/ppermute | solution.py:68
  497.9 23.8 %collective-permute-start.74 = (bf16[192,768]{1,0:T(8,128)(2,1)S(1)}, bf16[192,768]{1,0:T(8,128)(2,1)S(1)}, u32[]{:S(2)}, u32[]{:S(2)}) collective-permute-start(bf16[192,768]{1,0:T(8,128)(2,1)S(1)} %get-tuple-element.556), channel_id=1, source_target_pairs={{0,8},{4,12},{8,0},{12,4},{1,9},{5,13},{9,1},{13,5},{2,10},{6,14},... | collective-permute-start | bytes 884744 | tf_op jit(solution)/shard_map/ppermute | solution.py:68
  498.0 23.8 %collective-permute-start.73 = (bf16[192,768]{1,0:T(8,128)(2,1)S(1)}, bf16[192,768]{1,0:T(8,128)(2,1)S(1)}, u32[]{:S(2)}, u32[]{:S(2)}) collective-permute-start(bf16[192,768]{1,0:T(8,128)(2,1)S(1)} %get-tuple-element.557), channel_id=1, source_target_pairs={{0,4},{4,0},{8,12},{12,8},{1,5},{5,1},{9,13},{13,9},{2,6},{6,2},{1... | collective-permute-start | bytes 884744 | tf_op jit(solution)/shard_map/ppermute | solution.py:68
  523.8 19.4 %collective-permute-start.76 = (bf16[2,96,896]{2,1,0:T(8,128)(2,1)}, bf16[2,96,896]{2,1,0:T(8,128)(2,1)S(1)}, u32[]{:S(2)}, u32[]{:S(2)}) collective-permute-start(bf16[2,96,896]{2,1,0:T(8,128)(2,1)} %dynamic-slice_bitcast_fusion.3), channel_id=1, source_target_pairs={{0,2},{1,3},{2,0},{3,1},{4,6},{5,7},{6,4},{7,5},{8,10},{9,11},{10,... | collective-permute-start | bytes 1032200 | tf_op jit(solution)/shard_map/ppermute | solution.py:68
  524.5 18.7 %collective-permute-start.77 = (bf16[2,96,896]{2,1,0:T(8,128)(2,1)}, bf16[2,96,896]{2,1,0:T(8,128)(2,1)}, u32[]{:S(2)}, u32[]{:S(2)}) collective-permute-start(bf16[2,96,896]{2,1,0:T(8,128)(2,1)} %dynamic-slice_bitcast_fusion.2), channel_id=1, source_target_pairs={{0,1},{1,0},{2,3},{3,2},{4,5},{5,4},{6,7},{7,6},{8,9},{9,8},{10,11... | collective-permute-start | bytes 1032200 | tf_op jit(solution)/shard_map/ppermute | solution.py:68
  527.2 39.8 %collective-permute-start.81 = (f32[192,768]{1,0:T(8,128)S(1)}, f32[192,768]{1,0:T(8,128)S(1)}, u32[]{:S(2)}, u32[]{:S(2)}) collective-permute-start(f32[192,768]{1,0:T(8,128)S(1)} %get-tuple-element.516), channel_id=1, source_target_pairs={{0,16},{16,0},{1,17},{17,1},{2,18},{18,2},{3,19},{19,3},{4,20},{20... | collective-permute-start | bytes 1769480 | tf_op jit(solution)/shard_map/ppermute | solution.py:64
  547.1 26.6 %collective-permute-start.80 = (bf16[96,896]{1,0:T(8,128)(2,1)}, bf16[96,896]{1,0:T(8,128)(2,1)}, u32[]{:S(2)}, u32[]{:S(2)}) collective-permute-start(bf16[96,896]{1,0:T(8,128)(2,1)} %get-tuple-element.575), channel_id=1, source_target_pairs={{0,12},{4,8},{8,4},{12,0},{1,13},{5,9},{9,5},{13,1},{2,14},{6,10},... | collective-permute-start | bytes 516104 | tf_op jit(solution)/shard_map/ppermute | solution.py:68
  548.8 24.9 %collective-permute-start.78 = (bf16[96,896]{1,0:T(8,128)(2,1)}, bf16[96,896]{1,0:T(8,128)(2,1)}, u32[]{:S(2)}, u32[]{:S(2)}) collective-permute-start(bf16[96,896]{1,0:T(8,128)(2,1)} %get-tuple-element.576), channel_id=1, source_target_pairs={{0,4},{4,0},{8,12},{12,8},{1,5},{5,1},{9,13},{13,9},{2,6},{6,2},{1... | collective-permute-start | bytes 516104 | tf_op jit(solution)/shard_map/ppermute | solution.py:68
  548.8 24.9 %collective-permute-start.79 = (bf16[96,896]{1,0:T(8,128)(2,1)S(1)}, bf16[96,896]{1,0:T(8,128)(2,1)}, u32[]{:S(2)}, u32[]{:S(2)}) collective-permute-start(bf16[96,896]{1,0:T(8,128)(2,1)S(1)} %get-tuple-element.577), channel_id=1, source_target_pairs={{0,8},{4,12},{8,0},{12,4},{1,9},{5,13},{9,1},{13,5},{2,10},{6,14},... | collective-permute-start | bytes 516104 | tf_op jit(solution)/shard_map/ppermute | solution.py:68
  579.3 6.4 %collective-permute-start.85 = (f32[112,128]{1,0:T(8,128)S(1)}, f32[112,128]{1,0:T(8,128)S(1)}, u32[]{:S(2)}, u32[]{:S(2)}) collective-permute-start(f32[112,128]{1,0:T(8,128)S(1)} %get-tuple-element.354), channel_id=1, source_target_pairs={{0,12},{4,8},{8,4},{12,0},{1,13},{5,9},{9,5},{13,1},{2,14},{6,10},... | collective-permute-start | bytes 172040 | tf_op jit(solution)/shard_map/ppermute | solution.py:68
  587.5 45.9 %collective-permute-start.87 = (f32[96,128]{1,0:T(8,128)S(1)}, f32[96,128]{1,0:T(8,128)S(1)}, u32[]{:S(2)}, u32[]{:S(2)}) collective-permute-start(f32[96,128]{1,0:T(8,128)S(1)} %slice.318), channel_id=1, source_target_pairs={{0,2},{1,3},{2,0},{3,1},{4,6},{5,7},{6,4},{7,5},{8,10},{9,11},{10,... | collective-permute-start | bytes 147464 | tf_op jit(solution)/shard_map/ppermute | solution.py:68
  589.0 44.4 %collective-permute-start.88 = (f32[96,128]{1,0:T(8,128)S(1)}, f32[96,128]{1,0:T(8,128)S(1)}, u32[]{:S(2)}, u32[]{:S(2)}) collective-permute-start(f32[96,128]{1,0:T(8,128)S(1)} %slice.318), channel_id=1, source_target_pairs={{0,3},{1,2},{2,1},{3,0},{4,7},{5,6},{6,5},{7,4},{8,11},{9,10},{10,... | collective-permute-start | bytes 147464 | tf_op jit(solution)/shard_map/ppermute | solution.py:68
  590.1 43.4 %collective-permute-start.86 = (f32[96,128]{1,0:T(8,128)S(1)}, f32[96,128]{1,0:T(8,128)}, u32[]{:S(2)}, u32[]{:S(2)}) collective-permute-start(f32[96,128]{1,0:T(8,128)S(1)} %slice.318), channel_id=1, source_target_pairs={{0,1},{1,0},{2,3},{3,2},{4,5},{5,4},{6,7},{7,6},{8,9},{9,8},{10,11... | collective-permute-start | bytes 147464 | tf_op jit(solution)/shard_map/ppermute | solution.py:68
  (231 other events, 2030.5 us)
Sparse Core Ops, SparseCore 1:
  48.8 98.9 all-gather.6
  310.5 152.1 reduce-scatter.4

commit v4 on v3

--- a/solution.py
+++ b/solution.py
@@ -1513,10 +1513,13 @@
         )
         sums = summed(sums, ("dp",))
         _, _, table_start = sum_rows([grad.shape[1] for grad in grads[:4]])
-        layer_totals = summed(sums[:table_start], ("ctx",))
+        layer_part = sums[:table_start]
+        layer_pieces = [cross(layer_part, "ctx", k) for k in (1, 2, 3)]
         table_news, table_cols_new = table_new(
             sums, table_start, table, grad_table, rows_new, table_cols[None], vocab_here * z_count
         )
+        (one, two, three), table_cols_new = barrier((layer_pieces, table_cols_new))
+        layer_totals = (layer_part + one) + (two + three)
         cols = (attention_in_cols, attention_out_cols, hidden_in_cols, hidden_out_cols)
         *news, in_cols, out_cols, up_cols, down_cols = layer_new(
             layer_totals, grads, weights, rows_news, cols, (model, model, model, units, model)

time: 648 us -> 643 us (level)
  waiting for transfers between devices: 100 us -> 92.9 us
    ppermute x60, waiting for transfers between devices: 70.4 us -> 63.8 us  [cross(): lax.ppermute(values, axis, [(i, i ^ bits) for i in range(lax.axis_size(ax...]
  transfers between devices with their start and end apart: 91 -> 91, of which waited for: 36 -> 37; matrix products, arithmetic and copies ran while one was open for 17% -> 17% of each run, Pallas kernels for 31% -> 32%
where the time goes in v4:
time: 643 us; the launch traced here: 633 us
  Pallas kernels  250 us (39%)
  starting transfers between devices  109 us (17%)
  waiting for transfers between devices  92.9 us (14%)
  local copies, waits for them, and re-layouts  71.8 us (11%)
  other arithmetic  59.1 us (9%)
  matrix products  21.8 us (3%)
  between operations  20.5 us (3%)
  loops' own time  7.37 us (1%)
    ppermute x60, starting transfers between devices, cross(): lax.ppermute(values, axis, [(i, i ^ bits) for i in range(lax.axis_size(ax...  85.1 us
    ppermute x60, waiting for transfers between devices, cross(): lax.ppermute(values, axis, [(i, i ^ bits) for i in range(lax.axis_size(ax...  63.8 us
    pallas_call x3, Pallas kernels, table_sums(): pl.pallas_call(functools.partial(table_sums_kernel, first), grid_spec=plt...  47.6 us
    pallas_call x1, Pallas kernels, table_new(): pl.pallas_call(functools.partial(table_new_kernel, start, row_count), gri...  37.8 us
    pallas_call x3, Pallas kernels, head_table(): pl.pallas_call(functools.partial(head_table_kernel, first), grid=(last -...  34.6 us
    pallas_call x3, Pallas kernels, lowered(): pl.pallas_call(lower_kernel, grid=(last - first,), in_specs=[rows] + ([]...  22.6 us
    unnamed x420, local copies, waits for them, and re-layouts  20.9 us
    pallas_call x2, Pallas kernels, hidden_backward(): pl.pallas_call(hidden_back_kernel, grid_spec=pltpu.PrefetchScalarGridSpec...  20.5 us
  transfers between devices with their start and end apart: 91, of which 37 were waited for; matrix products, arithmetic and copies ran while one was open for 17% of the time, Pallas kernels for 32%

profile of v4, /device:TPU:0, one launch (start us, length us, event | category | flops | bytes accessed | tf_op | source)
XLA Modules:
  0.0 632.9 jit_solution(14591600732708720628)
XLA Ops:
  14.9 2.6 collective-permute-start.6
  19.1 2.1 collective-permute-start.7
  24.0 4.2 collective-permute-start.3
  29.2 2.6 dynamic-slice_reduce_fusion
  33.2 9.4 %shard_map.396 = bf16[384,768]{1,0:T(8,128)(2,1)S(1)} custom-call(s32[384]{0:T(512)S(1)} %broadcast_minimum_fusion.ids_ref, f32[12288,768]{1,0:T(8,128)} %table_ref.8), custom_call_target="tpu_custom_call" | custom-call | bytes 73728 | tf_op jit(solution)/shard_map/pallas_call | solution.py:935
  48.5 2.0 collective-permute-start.8
  50.5 3.7 collective-permute-start.12
  55.0 7.6 %shard_map.397 = (bf16[12288,768]{1,0:T(8,128)(2,1)}, f32[8,768]{1,0:T(8,128)S(1)}) custom-call(f32[12288,768]{1,0:T(8,128)} %table_ref.8), custom_call_target="tpu_custom_call" | custom-call | flops 393216 | bytes 1179648 | tf_op jit(solution)/shard_map/pallas_call | solution.py:444
  62.7 6.6 %collective-permute-done.11 = bf16[96,768]{1,0:T(8,128)(2,1)S(1)} collective-permute-done((bf16[96,768]{1,0:T(8,128)(2,1)S(1)}, bf16[96,768]{1,0:T(8,128)(2,1)S(1)}, u32[]{:S(2)}, u32[]{:S(2)}) %collective-permute-start.11) | collective-permute-done | bytes 147488 | tf_op jit(solution)/shard_map/ppermute | solution.py:68
  70.7 7.5 %shard_map.398 = (bf16[12288,768]{1,0:T(8,128)(2,1)}, f32[8,768]{1,0:T(8,128)S(1)}) custom-call(f32[12288,768]{1,0:T(8,128)} %table_ref.8, bf16[12288,768]{1,0:T(8,128)(2,1)} %get-tuple-element.242.refs_0_), custom_call_target="tpu_custom_call", output_to_operand_aliasing={{0}: (1, {})} | custom-call | flops 393216 | bytes 1179648 | tf_op jit(solution)/shard_map/pallas_call | solution.py:444
  82.0 5.8 sort.15
  88.5 3.9 collective-permute-start.20
  94.9 7.5 %shard_map.399 = (bf16[12288,768]{1,0:T(8,128)(2,1)}, f32[8,768]{1,0:T(8,128)S(1)}) custom-call(f32[12288,768]{1,0:T(8,128)} %table_ref.8, bf16[12288,768]{1,0:T(8,128)(2,1)} %get-tuple-element.247.refs_0_), custom_call_target="tpu_custom_call", output_to_operand_aliasing={{0}: (1, {})} | custom-call | flops 393216 | bytes 1179648 | tf_op jit(solution)/shard_map/pallas_call | solution.py:444
  102.5 2.2 shard_map.400
  106.4 3.2 collective-permute-start.17
  109.6 3.6 collective-permute-start.16
  115.1 16.1 %collective-permute-done.19 = bf16[192,768]{1,0:T(8,128)(2,1)S(1)} collective-permute-done((bf16[192,768]{1,0:T(8,128)(2,1)}, bf16[192,768]{1,0:T(8,128)(2,1)S(1)}, u32[]{:S(2)}, u32[]{:S(2)}) %collective-permute-start.19) | collective-permute-done | bytes 294944 | tf_op jit(solution)/shard_map/ppermute | solution.py:68
  133.4 7.7 %shard_map.401 = bf16[256,768]{1,0:T(8,128)(2,1)S(1)} custom-call(bf16[256,768]{1,0:T(8,128)(2,1)S(1)} %fusion.26.query_ref, bf16[768,128]{1,0:T(8,128)(2,1)S(1)} %pad_maximum_fusion.15.keyval_ref, f32[256,768]{1,0:T(8,128)S(1)} %and_select_fusion.1.bias_ref), custom_call_target="tpu_custom_call" | custom-call | flops 37748736 | bytes 98304 | tf_op jit(solution)/shard_map/pallas_call | solution.py:367
  142.3 5.3 collective-permute-done.22.refs_4_
  152.4 2.2 shard_map.403
  158.0 7.2 %shard_map.402 = (f32[512,1536]{1,0:T(8,128)S(1)}, f32[512,768]{1,0:T(8,128)}) custom-call(s32[1]{0:T(128)} %constant.370.clone.1.place_ref, bf16[512,768]{1,0:T(8,128)(2,1)S(1)} %pad_maximum_fusion.2.both_ref, bf16[4,4,192,768]{3,2,1,0:T(8,128)(2,1)} %bitcast.387, bf16[4,4,192,768]{3,2,1,0:T(8,128)(2,1)} %bitcast.388, bf16[4,4,192,768]{3,2,1,0:T(8,128)(2,1)} %bitcast.389, ...), custom_call_target="tpu_custom_call" | custom-call | flops 150994944 | bytes 688128 | tf_op jit(solution)/shard_map/pallas_call | solution.py:752
  167.1 2.1 slice.234
  175.1 2.2 convert_reduce_fusion.1
  180.5 8.2 %collective-permute-done.27.refs_6_ = bf16[2,192,768]{2,1,0:T(8,128)(2,1)} collective-permute-done((bf16[2,192,768]{2,1,0:T(8,128)(2,1)}, bf16[2,192,768]{2,1,0:T(8,128)(2,1)}, u32[]{:S(2)}, u32[]{:S(2)}) %collective-permute-start.27) | collective-permute-done | bytes 589856 | tf_op jit(solution)/shard_map/ppermute | solution.py:68
  190.1 4.0 collective-permute-start.29
  194.8 3.6 collective-permute-start.30
  213.6 3.0 shard_map.405
  218.5 3.4 collective-permute-start.35
  224.2 2.4 collective-permute-done.34
  237.1 18.0 %shard_map.406 = f32[8,512]{1,0:T(8,128)S(1)} custom-call(bf16[768,512]{1,0:T(8,128)(2,1)S(1)} %get-tuple-element.580.chosen_ref.across_ref, s32[1,512]{1,0:T(1,128)S(1)} %select_n.867.target_ref, bf16[12288,768]{1,0:T(8,128)(2,1)} %get-tuple-element.280.low_ref), custom_call_target="tpu_custom_call" | custom-call | flops 603979776 | bytes 1179648 | tf_op jit(solution)/shard_map/pallas_call | solution.py:490
  257.3 2.3 collective-permute-start.40
  259.6 2.3 copy.237
  265.0 15.6 %shard_map.407 = f32[64,768]{1,0:T(8,128)S(1)} custom-call(bf16[64,768]{1,0:T(8,128)(2,1)S(1)} %bitcast.380, s32[64,1]{1,0:T(8,128)S(1)} %broadcast_in_dim_reshape.8.target_ref, f32[64,1]{1,0:T(8,128)S(1)} %broadcast_in_dim_reshape.9.logsum_ref, bf16[12288,768]{1,0:T(8,128)(2,1)} %get-tuple-element.280.low_ref), custom_call_target="tpu_custom_call" | custom-call | flops 150994944 | bytes 1179648 | tf_op jit(solution)/shard_map/pallas_call | solution.py:526
  281.1 2.2 collective-permute-start.45
  284.6 2.1 collective-permute-done.45
  289.9 7.9 %shard_map.408 = (f32[32,768]{1,0:T(8,128)}, bf16[16,192,768]{2,1,0:T(8,128)(2,1)}) custom-call(s32[1]{0:T(128)} %bitcast.36.place_ref, bf16[32,768]{1,0:T(8,128)(2,1)} %copy-done.40, f32[32,1536]{1,0:T(8,128)} %copy-done.45, bf16[32,768]{1,0:T(8,128)(2,1)} %pad_maximum_fusion.19.grad_ref, bf16[4,192,768]{2,1,0:T(8,128)(2,1)} %copy-done.2, ...), custom_call_target="tpu_custom_call" | custom-call | flops 18874368 | bytes 602112 | tf_op jit(solution)/shard_map/pallas_call | solution.py:812
  308.6 2.0 shard_map.409
  320.2 3.1 collective-permute-done.48
  332.5 12.6 %shard_map.410 = (f32[512,768]{1,0:T(8,128)}, bf16[16,192,768]{2,1,0:T(8,128)(2,1)}) custom-call(s32[1]{0:T(128)} %constant.370.clone.1.place_ref, bf16[512,768]{1,0:T(8,128)(2,1)} %copy-done.5, f32[512,1536]{1,0:T(8,128)} %copy-done.20, bf16[512,768]{1,0:T(8,128)(2,1)} %pad_maximum_fusion.4.grad_ref, bf16[4,4,192,768]{3,2,1,0:T(8,128)(2,1)} %bitcast.395, ...), custom_call_target="tpu_custom_call" | custom-call | flops 301989888 | bytes 786432 | tf_op jit(solution)/shard_map/pallas_call | solution.py:812
  345.1 2.1 slice.267
  351.4 2.3 constant_dynamic-slice_fusion.7
  355.4 3.4 collective-permute-start.55
  361.9 13.6 %shard_map.411 = (bf16[256,768]{1,0:T(8,128)(2,1)S(1)}, f32[768,128]{1,0:T(8,128)S(1)}) custom-call(bf16[256,768]{1,0:T(8,128)(2,1)S(1)} %copy-done.17, bf16[768,128]{1,0:T(8,128)(2,1)S(1)} %pad_maximum_fusion.15.keyval_ref, f32[256,768]{1,0:T(8,128)S(1)} %and_select_fusion.1.bias_ref, bf16[256,768]{1,0:T(8,128)(2,1)S(1)} %convolution_convert_fusion.5.grad_ref), custom_call_target="tpu_custom_call" | custom-call | flops 94371840 | bytes 98304 | tf_op jit(solution)/shard_map/pallas_call | solution.py:412
  380.1 12.2 %collective-permute-done.54 = f32[256,128]{1,0:T(8,128)S(1)} collective-permute-done((f32[256,128]{1,0:T(8,128)S(1)}, f32[256,128]{1,0:T(8,128)S(1)}, u32[]{:S(2)}, u32[]{:S(2)}) %collective-permute-start.54) | collective-permute-done | bytes 131104 | tf_op jit(solution)/shard_map/ppermute | solution.py:73
  399.9 2.9 collective-permute-start.61
  406.0 2.2 collective-permute-start.57
  408.2 3.2 broadcast_select_fusion
  412.9 11.6 %shard_map.412.refs_0_ = f32[12288,768]{1,0:T(8,128)} custom-call(bf16[512,768]{1,0:T(8,128)(2,1)S(1)} %copy.247.chosen_ref, bf16[768,512]{1,0:T(8,128)(2,1)S(1)} %get-tuple-element.580.chosen_ref.across_ref, s32[1,512]{1,0:T(1,128)S(1)} %copy-done.47, f32[1,512]{1,0:T(1,128)S(1)} %copy-done.49, bf16[12288,768]{1,0:T(8,128)(2,1)} %get-tuple-element.280.low_ref), custom_call_target="tpu_custom_call" | custom-call | flops 402653184 | bytes 1179648 | tf_op jit(solution)/shard_map/pallas_call | solution.py:565
  426.5 4.0 collective-permute-start.63
  431.8 11.5 %shard_map.413.refs_0_ = f32[12288,768]{1,0:T(8,128)} custom-call(bf16[512,768]{1,0:T(8,128)(2,1)S(1)} %copy.247.chosen_ref, bf16[768,512]{1,0:T(8,128)(2,1)S(1)} %get-tuple-element.580.chosen_ref.across_ref, s32[1,512]{1,0:T(1,128)S(1)} %copy-done.47, f32[1,512]{1,0:T(1,128)S(1)} %copy-done.49, ...), custom_call_target="tpu_custom_call", output_to_operand_aliasing={{}: (5, {})} | custom-call | flops 402653184 | bytes 1179648 | tf_op jit(solution)/shard_map/pallas_call | solution.py:565
  453.3 11.5 %shard_map.415 = f32[12288,768]{1,0:T(8,128)} custom-call(bf16[512,768]{1,0:T(8,128)(2,1)S(1)} %copy.247.chosen_ref, bf16[768,512]{1,0:T(8,128)(2,1)S(1)} %get-tuple-element.580.chosen_ref.across_ref, s32[1,512]{1,0:T(1,128)S(1)} %copy-done.47, f32[1,512]{1,0:T(1,128)S(1)} %copy-done.49, ...), custom_call_target="tpu_custom_call", output_to_operand_aliasing={{}: (5, {})} | custom-call | flops 402653184 | bytes 1179648 | tf_op jit(solution)/shard_map/pallas_call | solution.py:565
  466.7 7.4 %while.10 = (s32[]{:T(128)}, f32[12288,768]{1,0:T(8,128)}, pred[]{:T(512)}, s32[2,4,256]{2,1,0:T(4,128)S(1)}, s32[4,256]{1,0:T(4,128)S(1)}, /*index=5*/bf16[256,...) while((s32[]{:T(128)}, f32[12288,768]{1,0:T(8,128)}, ...), condition=%wide.region_46.47_spmd, body=%wide.region_43.46_spmd.sunk | while | flops 39328784 | bytes 309494080 | solution.py:1457
  478.1 2.5 shard_map.414
  483.8 2.5 collective-permute-start.75
  488.3 16.2 %shard_map.416 = (f32[12288,768]{1,0:T(8,128)}, f32[96,128]{1,0:T(8,128)}, f32[16,768]{1,0:T(8,128)}) custom-call(s32[2]{0:T(128)} %copy-done.57, s32[13]{0:T(128)} %convert_reduce_fusion.2.starts_ref, s32[3072]{0:T(1024)} %copy-done.124, s32[3072]{0:T(1024)} %get-tuple-element.321.order_ref, f32[12288,768]{1,0:T(8,128)} %get-tuple-element.322.head_ref, ...), custom_call_target="tpu_custom_call" | custom-call | flops 1572864 | bytes 1572864 | tf_op jit(solution)/shard_map/pallas_call | solution.py:644
  504.5 6.3 collective-permute-done.74
  516.3 16.2 %shard_map.417 = (f32[12288,768]{1,0:T(8,128)}, f32[96,128]{1,0:T(8,128)}, f32[16,768]{1,0:T(8,128)}) custom-call(s32[2]{0:T(128)} %copy-done.57, s32[13]{0:T(128)} %convert_reduce_fusion.2.starts_ref, s32[3072]{0:T(1024)} %copy-done.124, s32[3072]{0:T(1024)} %get-tuple-element.321.order_ref, ...), custom_call_target="tpu_custom_call", output_to_operand_aliasing={{0}: (14, {}), {1}: (15, {})} | custom-call | flops 1572864 | bytes 1572864 | tf_op jit(solution)/shard_map/pallas_call | solution.py:644
  536.4 2.1 collective-permute-start.80
  538.4 2.3 collective-permute-start.79
  540.8 15.2 %shard_map.418 = (f32[12288,768]{1,0:T(8,128)}, f32[96,128]{1,0:T(8,128)}, f32[16,768]{1,0:T(8,128)}) custom-call(s32[2]{0:T(128)} %copy-done.57, s32[13]{0:T(128)} %convert_reduce_fusion.2.starts_ref, s32[3072]{0:T(1024)} %copy-done.124, s32[3072]{0:T(1024)} %get-tuple-element.321.order_ref, ...), custom_call_target="tpu_custom_call", output_to_operand_aliasing={{0}: (14, {}), {1}: (15, {})} | custom-call | flops 1572864 | bytes 1572864 | tf_op jit(solution)/shard_map/pallas_call | solution.py:644
  560.5 2.2 reshape.809.refs_2_
  568.3 3.0 collective-permute-start.85
  572.7 2.1 collective-permute-done.85
  584.4 37.8 %shard_map.420 = (f32[12288,768]{1,0:T(8,128)}, f32[1,768]{1,0:T(1,128)S(1)}) custom-call(f32[112,128]{1,0:T(8,128)S(1)} %add_add_fusion.4.totals_ref, f32[12288,768]{1,0:T(8,128)} %table_ref.8, f32[12288,768]{1,0:T(8,128)} %get-tuple-element.456.grad_ref, f32[96,128]{1,0:T(8,128)S(1)} %copy-done.39, f32[1,768]{1,0:T(1,128)S(1)} %broadcast_in_dim.233.cols_ref), custom_call_target="tpu_custom_call" | custom-call | flops 2359296 | bytes 7077888 | tf_op jit(solution)/shard_map/pallas_call | solution.py:1111
  (845 shorter events, 206.1 us)
Async XLA Ops:
  24.0 19.6 %collective-permute-start.3 = (bf16[96,896]{1,0:T(8,128)(2,1)S(1)}, bf16[96,896]{1,0:T(8,128)(2,1)S(1)}, u32[]{:S(2)}, u32[]{:S(2)}) collective-permute-start(bf16[96,896]{1,0:T(8,128)(2,1)S(1)} %pad_maximum_fusion.16), channel_id=1, source_target_pairs={{0,12},{4,8},{8,4},{12,0},{1,13},{5,9},{9,5},{13,1},{2,14},{6,10},... | collective-permute-start | bytes 516104 | tf_op jit(solution)/shard_map/ppermute | solution.py:68
  28.2 15.4 %collective-permute-start.2 = (bf16[96,896]{1,0:T(8,128)(2,1)S(1)}, bf16[96,896]{1,0:T(8,128)(2,1)S(1)}, u32[]{:S(2)}, u32[]{:S(2)}) collective-permute-start(bf16[96,896]{1,0:T(8,128)(2,1)S(1)} %pad_maximum_fusion.16), channel_id=1, source_target_pairs={{0,8},{4,12},{8,0},{12,4},{1,9},{5,13},{9,1},{13,5},{2,10},{6,14},... | collective-permute-start | bytes 516104 | tf_op jit(solution)/shard_map/ppermute | solution.py:68
  28.2 15.4 %collective-permute-start.1 = (bf16[96,896]{1,0:T(8,128)(2,1)S(1)}, bf16[96,896]{1,0:T(8,128)(2,1)S(1)}, u32[]{:S(2)}, u32[]{:S(2)}) collective-permute-start(bf16[96,896]{1,0:T(8,128)(2,1)S(1)} %pad_maximum_fusion.16), channel_id=1, source_target_pairs={{0,4},{4,0},{8,12},{12,8},{1,5},{5,1},{9,13},{13,9},{2,6},{6,2},{1... | collective-permute-start | bytes 516104 | tf_op jit(solution)/shard_map/ppermute | solution.py:68
  32.9 9.8 %collective-permute-start.4 = (bf16[192,768]{1,0:T(8,128)(2,1)S(1)}, bf16[192,768]{1,0:T(8,128)(2,1)S(1)}, u32[]{:S(2)}, u32[]{:S(2)}) collective-permute-start(bf16[192,768]{1,0:T(8,128)(2,1)S(1)} %pad_maximum_fusion.13), channel_id=1, source_target_pairs={{0,16},{16,0},{1,17},{17,1},{2,18},{18,2},{3,19},{19,3},{4,20},{20... | collective-permute-start | bytes 884744 | tf_op jit(solution)/shard_map/ppermute | solution.py:64
  45.0 113.0 %all-gather.7.cloned.1.call-start = ((), (), s32[]{:S(2)}) async-start(), calls=%async_computation.4 | async-start | bytes 5013504 | tf_op jit(solution)/shard_map/all_gather | solution.py:1197
  45.6 419.2 %reduce-scatter.5.cloned.1.call-start = ((), (), s32[]{:S(2)}) async-start(), calls=%async_computation.3 | async-start | bytes 5013504 | tf_op jit(solution)/shard_map/reduce_scatter | solution.py:209
  47.1 22.2 %collective-permute-start.9 = (bf16[4,96,896]{2,1,0:T(8,128)(2,1)S(1)}, bf16[4,96,896]{2,1,0:T(8,128)(2,1)S(1)}, u32[]{:S(2)}, u32[]{:S(2)}) collective-permute-start(bf16[4,96,896]{2,1,0:T(8,128)(2,1)S(1)} %pad_maximum_fusion.5), channel_id=1, source_target_pairs={{0,2},{1,3},{2,0},{3,1},{4,6},{5,7},{6,4},{7,5},{8,10},{9,11},{10,... | collective-permute-start | bytes 2064392 | tf_op jit(solution)/shard_map/ppermute | solution.py:68
  48.5 20.8 %collective-permute-start.8 = (bf16[4,96,896]{2,1,0:T(8,128)(2,1)S(1)}, bf16[4,96,896]{2,1,0:T(8,128)(2,1)S(1)}, u32[]{:S(2)}, u32[]{:S(2)}) collective-permute-start(bf16[4,96,896]{2,1,0:T(8,128)(2,1)S(1)} %pad_maximum_fusion.5), channel_id=1, source_target_pairs={{0,1},{1,0},{2,3},{3,2},{4,5},{5,4},{6,7},{7,6},{8,9},{9,8},{10,11... | collective-permute-start | bytes 2064392 | tf_op jit(solution)/shard_map/ppermute | solution.py:68
  50.5 12.1 %collective-permute-start.12 = (bf16[96,768]{1,0:T(8,128)(2,1)S(1)}, bf16[96,768]{1,0:T(8,128)(2,1)S(1)}, u32[]{:S(2)}, u32[]{:S(2)}) collective-permute-start(bf16[96,768]{1,0:T(8,128)(2,1)S(1)} %get-tuple-element.595), channel_id=1, source_target_pairs={{0,12},{4,8},{8,4},{12,0},{1,13},{5,9},{9,5},{13,1},{2,14},{6,10},... | collective-permute-start | bytes 442376 | tf_op jit(solution)/shard_map/ppermute | solution.py:68
  54.3 15.0 %collective-permute-start.11 = (bf16[96,768]{1,0:T(8,128)(2,1)S(1)}, bf16[96,768]{1,0:T(8,128)(2,1)S(1)}, u32[]{:S(2)}, u32[]{:S(2)}) collective-permute-start(bf16[96,768]{1,0:T(8,128)(2,1)S(1)} %get-tuple-element.596), channel_id=1, source_target_pairs={{0,8},{4,12},{8,0},{12,4},{1,9},{5,13},{9,1},{13,5},{2,10},{6,14},... | collective-permute-start | bytes 442376 | tf_op jit(solution)/shard_map/ppermute | solution.py:68
  54.3 15.0 %collective-permute-start.10 = (bf16[96,768]{1,0:T(8,128)(2,1)S(1)}, bf16[96,768]{1,0:T(8,128)(2,1)S(1)}, u32[]{:S(2)}, u32[]{:S(2)}) collective-permute-start(bf16[96,768]{1,0:T(8,128)(2,1)S(1)} %get-tuple-element.597), channel_id=1, source_target_pairs={{0,4},{4,0},{8,12},{12,8},{1,5},{5,1},{9,13},{13,9},{2,6},{6,2},{1... | collective-permute-start | bytes 442376 | tf_op jit(solution)/shard_map/ppermute | solution.py:68
  70.1 9.6 %collective-permute-start.14 = (bf16[2,96,896]{2,1,0:T(8,128)(2,1)S(1)}, bf16[2,96,896]{2,1,0:T(8,128)(2,1)S(1)}, u32[]{:S(2)}, u32[]{:S(2)}) collective-permute-start(bf16[2,96,896]{2,1,0:T(8,128)(2,1)S(1)} %slice.221), channel_id=1, source_target_pairs={{0,2},{1,3},{2,0},{3,1},{4,6},{5,7},{6,4},{7,5},{8,10},{9,11},{10,... | collective-permute-start | bytes 1032200 | tf_op jit(solution)/shard_map/ppermute | solution.py:68
  70.3 9.4 %collective-permute-start.13 = (bf16[2,96,896]{2,1,0:T(8,128)(2,1)S(1)}, bf16[2,96,896]{2,1,0:T(8,128)(2,1)S(1)}, u32[]{:S(2)}, u32[]{:S(2)}) collective-permute-start(bf16[2,96,896]{2,1,0:T(8,128)(2,1)S(1)} %slice.220), channel_id=1, source_target_pairs={{0,1},{1,0},{2,3},{3,2},{4,5},{5,4},{6,7},{7,6},{8,9},{9,8},{10,11... | collective-permute-start | bytes 1032200 | tf_op jit(solution)/shard_map/ppermute | solution.py:68
  81.2 21.3 %collective-permute-start.15 = (bf16[16,96,896]{2,1,0:T(8,128)(2,1)S(1)}, bf16[16,96,896]{2,1,0:T(8,128)(2,1)}, u32[]{:S(2)}, u32[]{:S(2)}) collective-permute-start(bf16[16,96,896]{2,1,0:T(8,128)(2,1)S(1)} %constant_dynamic-update-slice_fusion.refs_0_), channel_id=1, source_target_pairs={{0,16},{16,0},{1,17},{17,1},{2,18},{18,2},{3,19},{19,3},{4,20},{20... | collective-permute-start | bytes 8257544 | tf_op jit(solution)/shard_map/ppermute | solution.py:64
  88.5 26.6 %collective-permute-start.20 = (bf16[192,768]{1,0:T(8,128)(2,1)}, bf16[192,768]{1,0:T(8,128)(2,1)S(1)}, u32[]{:S(2)}, u32[]{:S(2)}) collective-permute-start(bf16[192,768]{1,0:T(8,128)(2,1)} %get-tuple-element.236), channel_id=1, source_target_pairs={{0,12},{4,8},{8,4},{12,0},{1,13},{5,9},{9,5},{13,1},{2,14},{6,10},... | collective-permute-start | bytes 884744 | tf_op jit(solution)/shard_map/ppermute | solution.py:68
  92.4 38.8 %collective-permute-start.19 = (bf16[192,768]{1,0:T(8,128)(2,1)}, bf16[192,768]{1,0:T(8,128)(2,1)S(1)}, u32[]{:S(2)}, u32[]{:S(2)}) collective-permute-start(bf16[192,768]{1,0:T(8,128)(2,1)} %get-tuple-element.236), channel_id=1, source_target_pairs={{0,8},{4,12},{8,0},{12,4},{1,9},{5,13},{9,1},{13,5},{2,10},{6,14},... | collective-permute-start | bytes 884744 | tf_op jit(solution)/shard_map/ppermute | solution.py:68
  92.4 38.8 %collective-permute-start.18 = (bf16[192,768]{1,0:T(8,128)(2,1)}, bf16[192,768]{1,0:T(8,128)(2,1)S(1)}, u32[]{:S(2)}, u32[]{:S(2)}) collective-permute-start(bf16[192,768]{1,0:T(8,128)(2,1)} %get-tuple-element.236), channel_id=1, source_target_pairs={{0,4},{4,0},{8,12},{12,8},{1,5},{5,1},{9,13},{13,9},{2,6},{6,2},{1... | collective-permute-start | bytes 884744 | tf_op jit(solution)/shard_map/ppermute | solution.py:68
  106.4 7.1 %collective-permute-start.17 = (bf16[256,128]{1,0:T(8,128)(2,1)S(1)}, bf16[256,128]{1,0:T(8,128)(2,1)S(1)}, u32[]{:S(2)}, u32[]{:S(2)}) collective-permute-start(bf16[256,128]{1,0:T(8,128)(2,1)S(1)} %slice.413), channel_id=1, source_target_pairs={{0,1},{1,2},{2,3},{4,5},{5,6},{6,7},{8,9},{9,10},{10,11},{12,13},{... | collective-permute-start | bytes 196616 | tf_op jit(solution)/shard_map/ppermute | solution.py:73
  131.4 16.2 %collective-permute-start.22 = (bf16[2,192,768]{2,1,0:T(8,128)(2,1)S(1)}, bf16[2,192,768]{2,1,0:T(8,128)(2,1)}, u32[]{:S(2)}, u32[]{:S(2)}) collective-permute-start(bf16[2,192,768]{2,1,0:T(8,128)(2,1)S(1)} %pad_maximum_fusion.8), channel_id=1, source_target_pairs={{0,2},{1,3},{2,0},{3,1},{4,6},{5,7},{6,4},{7,5},{8,10},{9,11},{10,... | collective-permute-start | bytes 1769480 | tf_op jit(solution)/shard_map/ppermute | solution.py:68
  133.4 14.2 %collective-permute-start.21 = (bf16[2,192,768]{2,1,0:T(8,128)(2,1)S(1)}, bf16[2,192,768]{2,1,0:T(8,128)(2,1)S(1)}, u32[]{:S(2)}, u32[]{:S(2)}) collective-permute-start(bf16[2,192,768]{2,1,0:T(8,128)(2,1)S(1)} %pad_maximum_fusion.8), channel_id=1, source_target_pairs={{0,1},{1,0},{2,3},{3,2},{4,5},{5,4},{6,7},{7,6},{8,9},{9,8},{10,11... | collective-permute-start | bytes 1769480 | tf_op jit(solution)/shard_map/ppermute | solution.py:68
  150.4 15.6 %collective-permute-start.25 = (bf16[2,192,768]{2,1,0:T(8,128)(2,1)}, bf16[2,192,768]{2,1,0:T(8,128)(2,1)S(1)}, u32[]{:S(2)}, u32[]{:S(2)}) collective-permute-start(bf16[2,192,768]{2,1,0:T(8,128)(2,1)} %slice.231), channel_id=1, source_target_pairs={{0,2},{1,3},{2,0},{3,1},{4,6},{5,7},{6,4},{7,5},{8,10},{9,11},{10,... | collective-permute-start | bytes 1769480 | tf_op jit(solution)/shard_map/ppermute | solution.py:68
  151.7 15.4 %collective-permute-start.24 = (bf16[2,192,768]{2,1,0:T(8,128)(2,1)}, bf16[2,192,768]{2,1,0:T(8,128)(2,1)}, u32[]{:S(2)}, u32[]{:S(2)}) collective-permute-start(bf16[2,192,768]{2,1,0:T(8,128)(2,1)} %slice.231), channel_id=1, source_target_pairs={{0,1},{1,0},{2,3},{3,2},{4,5},{5,4},{6,7},{7,6},{8,9},{9,8},{10,11... | collective-permute-start | bytes 1769480 | tf_op jit(solution)/shard_map/ppermute | solution.py:68
  172.6 16.1 %collective-permute-start.27 = (bf16[2,192,768]{2,1,0:T(8,128)(2,1)}, bf16[2,192,768]{2,1,0:T(8,128)(2,1)}, u32[]{:S(2)}, u32[]{:S(2)}) collective-permute-start(bf16[2,192,768]{2,1,0:T(8,128)(2,1)} %collective-permute-done.22.refs_4_), channel_id=1, source_target_pairs={{0,1},{1,0},{2,3},{3,2},{4,5},{5,4},{6,7},{7,6},{8,9},{9,8},{10,11... | collective-permute-start | bytes 1769480 | tf_op jit(solution)/shard_map/ppermute | solution.py:68
  173.5 15.7 %collective-permute-start.28 = (bf16[2,192,768]{2,1,0:T(8,128)(2,1)}, bf16[2,192,768]{2,1,0:T(8,128)(2,1)S(1)}, u32[]{:S(2)}, u32[]{:S(2)}) collective-permute-start(bf16[2,192,768]{2,1,0:T(8,128)(2,1)} %collective-permute-done.24.refs_3_), channel_id=1, source_target_pairs={{0,2},{1,3},{2,0},{3,1},{4,6},{5,7},{6,4},{7,5},{8,10},{9,11},{10,... | collective-permute-start | bytes 1769480 | tf_op jit(solution)/shard_map/ppermute | solution.py:68
  190.1 10.7 %collective-permute-start.29 = (bf16[256,128]{1,0:T(8,128)(2,1)}, bf16[256,128]{1,0:T(8,128)(2,1)}, u32[]{:S(2)}, u32[]{:S(2)}) collective-permute-start(bf16[256,128]{1,0:T(8,128)(2,1)} %convolution_convert_fusion.7), channel_id=1, source_target_pairs={{0,2},{1,3},{4,6},{5,7},{8,10},{9,11},{12,14},{13,15},{16,18},{17,... | collective-permute-start | bytes 196616 | tf_op jit(solution)/shard_map/ppermute | solution.py:73
  194.8 6.8 %collective-permute-start.30 = (bf16[256,128]{1,0:T(8,128)(2,1)}, bf16[256,128]{1,0:T(8,128)(2,1)}, u32[]{:S(2)}, u32[]{:S(2)}) collective-permute-start(bf16[256,128]{1,0:T(8,128)(2,1)} %convolution_convert_fusion.7), channel_id=1, source_target_pairs={{0,1},{1,2},{2,3},{4,5},{5,6},{6,7},{8,9},{9,10},{10,11},{12,13},{... | collective-permute-start | bytes 196616 | tf_op jit(solution)/shard_map/ppermute | solution.py:73
  255.1 7.6 %collective-permute-start.42 = (f32[3,512]{1,0:T(4,128)S(1)}, f32[3,512]{1,0:T(4,128)S(1)}, u32[]{:S(2)}, u32[]{:S(2)}) collective-permute-start(f32[3,512]{1,0:T(4,128)S(1)} %slice.298), channel_id=1, source_target_pairs={{0,12},{4,8},{8,4},{12,0},{1,13},{5,9},{9,5},{13,1},{2,14},{6,10},... | collective-permute-start | bytes 18440 | tf_op jit(solution)/shard_map/ppermute | solution.py:68
  256.7 6.1 collective-permute-start.41
  314.8 8.5 %collective-permute-start.48 = (f32[256,128]{1,0:T(8,128)S(1)}, f32[256,128]{1,0:T(8,128)S(1)}, u32[]{:S(2)}, u32[]{:S(2)}) collective-permute-start(f32[256,128]{1,0:T(8,128)S(1)} %get-tuple-element.602), channel_id=1, source_target_pairs={{1,0},{2,1},{3,2},{5,4},{6,5},{7,6},{9,8},{10,9},{11,10},{13,12},{... | collective-permute-start | bytes 393224 | tf_op jit(solution)/shard_map/ppermute | solution.py:73
  316.2 8.3 %collective-permute-start.49 = (f32[256,128]{1,0:T(8,128)S(1)}, f32[256,128]{1,0:T(8,128)S(1)}, u32[]{:S(2)}, u32[]{:S(2)}) collective-permute-start(f32[256,128]{1,0:T(8,128)S(1)} %get-tuple-element.603), channel_id=1, source_target_pairs={{2,0},{3,1},{6,4},{7,5},{10,8},{11,9},{14,12},{15,13},{18,16},{19,... | collective-permute-start | bytes 393224 | tf_op jit(solution)/shard_map/ppermute | solution.py:73
  331.1 20.2 %collective-permute-start.52 = (bf16[768,896]{1,0:T(8,128)(2,1)}, bf16[768,896]{1,0:T(8,128)(2,1)S(1)}, u32[]{:S(2)}, u32[]{:S(2)}) collective-permute-start(bf16[768,896]{1,0:T(8,128)(2,1)} %maximum_select_fusion), channel_id=1, source_target_pairs={{0,16},{16,0},{1,17},{17,1},{2,18},{18,2},{3,19},{19,3},{4,20},{20... | collective-permute-start | bytes 4128776 | tf_op jit(solution)/shard_map/ppermute | solution.py:64
  355.3 38.0 %collective-permute-start.56 = (bf16[2,1,2,192,768]{4,3,0,2,1:T(8,128)(2,1)S(1)}, bf16[2,1,2,192,768]{4,3,0,2,1:T(8,128)(2,1)S(1)}, u32[]{:S(2)}, u32[]{:S(2)}) collective-permute-start(bf16[2,1,2,192,768]{4,3,0,2,1:T(8,128)(2,1)S(1)} %copy.273), channel_id=1, source_target_pairs={{0,2},{1,3},{2,0},{3,1},{4,6},{5,7},{6,4},{7,5},{8,10},{9,11},{10,... | collective-permute-start | bytes 3538952 | tf_op jit(solution)/shard_map/ppermute | solution.py:68
  355.4 37.9 %collective-permute-start.55 = (bf16[2,2,1,192,768]{4,3,0,2,1:T(8,128)(2,1)S(1)}, bf16[2,2,1,192,768]{4,3,0,2,1:T(8,128)(2,1)S(1)}, u32[]{:S(2)}, u32[]{:S(2)}) collective-permute-start(bf16[2,2,1,192,768]{4,3,0,2,1:T(8,128)(2,1)S(1)} %copy.272), channel_id=1, source_target_pairs={{0,1},{1,0},{2,3},{3,2},{4,5},{5,4},{6,7},{7,6},{8,9},{9,8},{10,11... | collective-permute-start | bytes 3538952 | tf_op jit(solution)/shard_map/ppermute | solution.py:68
  375.6 16.7 %collective-permute-start.54 = (f32[256,128]{1,0:T(8,128)S(1)}, f32[256,128]{1,0:T(8,128)S(1)}, u32[]{:S(2)}, u32[]{:S(2)}) collective-permute-start(f32[256,128]{1,0:T(8,128)S(1)} %get-tuple-element.600), channel_id=1, source_target_pairs={{2,0},{3,1},{6,4},{7,5},{10,8},{11,9},{14,12},{15,13},{18,16},{19,... | collective-permute-start | bytes 393224 | tf_op jit(solution)/shard_map/ppermute | solution.py:73
  377.0 16.3 %collective-permute-start.53 = (f32[256,128]{1,0:T(8,128)S(1)}, f32[256,128]{1,0:T(8,128)S(1)}, u32[]{:S(2)}, u32[]{:S(2)}) collective-permute-start(f32[256,128]{1,0:T(8,128)S(1)} %get-tuple-element.601), channel_id=1, source_target_pairs={{1,0},{2,1},{3,2},{5,4},{6,5},{7,6},{9,8},{10,9},{11,10},{13,12},{... | collective-permute-start | bytes 393224 | tf_op jit(solution)/shard_map/ppermute | solution.py:73
  398.2 26.3 %collective-permute-start.60 = (bf16[2,192,768]{2,1,0:T(8,128)(2,1)}, bf16[2,192,768]{2,1,0:T(8,128)(2,1)}, u32[]{:S(2)}, u32[]{:S(2)}) collective-permute-start(bf16[2,192,768]{2,1,0:T(8,128)(2,1)} %dynamic-slice_bitcast_fusion.1), channel_id=1, source_target_pairs={{0,2},{1,3},{2,0},{3,1},{4,6},{5,7},{6,4},{7,5},{8,10},{9,11},{10,... | collective-permute-start | bytes 1769480 | tf_op jit(solution)/shard_map/ppermute | solution.py:68
  399.9 24.5 %collective-permute-start.61 = (bf16[2,192,768]{2,1,0:T(8,128)(2,1)}, bf16[2,192,768]{2,1,0:T(8,128)(2,1)}, u32[]{:S(2)}, u32[]{:S(2)}) collective-permute-start(bf16[2,192,768]{2,1,0:T(8,128)(2,1)} %dynamic-slice_bitcast_fusion), channel_id=1, source_target_pairs={{0,1},{1,0},{2,3},{3,2},{4,5},{5,4},{6,7},{7,6},{8,9},{9,8},{10,11... | collective-permute-start | bytes 1769480 | tf_op jit(solution)/shard_map/ppermute | solution.py:68
  403.8 20.6 %collective-permute-start.59 = (bf16[96,768]{1,0:T(8,128)(2,1)}, bf16[96,768]{1,0:T(8,128)(2,1)}, u32[]{:S(2)}, u32[]{:S(2)}) collective-permute-start(bf16[96,768]{1,0:T(8,128)(2,1)} %get-tuple-element.590), channel_id=1, source_target_pairs={{0,12},{4,8},{8,4},{12,0},{1,13},{5,9},{9,5},{13,1},{2,14},{6,10},... | collective-permute-start | bytes 442376 | tf_op jit(solution)/shard_map/ppermute | solution.py:68
  405.7 18.8 %collective-permute-start.58 = (bf16[96,768]{1,0:T(8,128)(2,1)}, bf16[96,768]{1,0:T(8,128)(2,1)}, u32[]{:S(2)}, u32[]{:S(2)}) collective-permute-start(bf16[96,768]{1,0:T(8,128)(2,1)} %get-tuple-element.591), channel_id=1, source_target_pairs={{0,8},{4,12},{8,0},{12,4},{1,9},{5,13},{9,1},{13,5},{2,10},{6,14},... | collective-permute-start | bytes 442376 | tf_op jit(solution)/shard_map/ppermute | solution.py:68
  406.0 18.5 %collective-permute-start.57 = (bf16[96,768]{1,0:T(8,128)(2,1)}, bf16[96,768]{1,0:T(8,128)(2,1)}, u32[]{:S(2)}, u32[]{:S(2)}) collective-permute-start(bf16[96,768]{1,0:T(8,128)(2,1)} %get-tuple-element.592), channel_id=1, source_target_pairs={{0,4},{4,0},{8,12},{12,8},{1,5},{5,1},{9,13},{13,9},{2,6},{6,2},{1... | collective-permute-start | bytes 442376 | tf_op jit(solution)/shard_map/ppermute | solution.py:68
  424.5 23.4 %collective-permute-start.65 = (bf16[768,896]{1,0:T(8,128)(2,1)}, bf16[768,896]{1,0:T(8,128)(2,1)}, u32[]{:S(2)}, u32[]{:S(2)}) collective-permute-start(bf16[768,896]{1,0:T(8,128)(2,1)} %get-tuple-element.305), channel_id=1, source_target_pairs={{0,16},{16,0},{1,17},{17,1},{2,18},{18,2},{3,19},{19,3},{4,20},{20... | collective-permute-start | bytes 4128776 | tf_op jit(solution)/shard_map/ppermute | solution.py:64
  425.9 21.2 %collective-permute-start.64 = (bf16[4,96,768]{2,1,0:T(8,128)(2,1)S(1)}, bf16[4,96,768]{2,1,0:T(8,128)(2,1)S(1)}, u32[]{:S(2)}, u32[]{:S(2)}) collective-permute-start(bf16[4,96,768]{2,1,0:T(8,128)(2,1)S(1)} %pad_maximum_fusion.9.refs_0_), channel_id=1, source_target_pairs={{0,16},{16,0},{1,17},{17,1},{2,18},{18,2},{3,19},{19,3},{4,20},{20... | collective-permute-start | bytes 1769480 | tf_op jit(solution)/shard_map/ppermute | solution.py:64
  426.5 20.7 %collective-permute-start.63 = (bf16[4,96,768]{2,1,0:T(8,128)(2,1)S(1)}, bf16[4,96,768]{2,1,0:T(8,128)(2,1)}, u32[]{:S(2)}, u32[]{:S(2)}) collective-permute-start(bf16[4,96,768]{2,1,0:T(8,128)(2,1)S(1)} %pad_maximum_fusion.9.refs_0_), channel_id=1, source_target_pairs={{0,2},{1,3},{2,0},{3,1},{4,6},{5,7},{6,4},{7,5},{8,10},{9,11},{10,... | collective-permute-start | bytes 1769480 | tf_op jit(solution)/shard_map/ppermute | solution.py:68
  430.4 17.2 %collective-permute-start.62 = (bf16[4,96,768]{2,1,0:T(8,128)(2,1)S(1)}, bf16[4,96,768]{2,1,0:T(8,128)(2,1)}, u32[]{:S(2)}, u32[]{:S(2)}) collective-permute-start(bf16[4,96,768]{2,1,0:T(8,128)(2,1)S(1)} %pad_maximum_fusion.9.refs_0_), channel_id=1, source_target_pairs={{0,1},{1,0},{2,3},{3,2},{4,5},{5,4},{6,7},{7,6},{8,9},{9,8},{10,11... | collective-permute-start | bytes 1769480 | tf_op jit(solution)/shard_map/ppermute | solution.py:68
  449.6 34.1 %collective-permute-start.68 = (bf16[4,96,768]{2,1,0:T(8,128)(2,1)}, bf16[4,96,768]{2,1,0:T(8,128)(2,1)}, u32[]{:S(2)}, u32[]{:S(2)}) collective-permute-start(bf16[4,96,768]{2,1,0:T(8,128)(2,1)} %collective-permute-done.62.refs_1_), channel_id=1, source_target_pairs={{0,16},{16,0},{1,17},{17,1},{2,18},{18,2},{3,19},{19,3},{4,20},{20... | collective-permute-start | bytes 1769480 | tf_op jit(solution)/shard_map/ppermute | solution.py:64
  451.3 32.4 %collective-permute-start.69 = (bf16[4,96,768]{2,1,0:T(8,128)(2,1)}, bf16[4,96,768]{2,1,0:T(8,128)(2,1)}, u32[]{:S(2)}, u32[]{:S(2)}) collective-permute-start(bf16[4,96,768]{2,1,0:T(8,128)(2,1)} %collective-permute-done.63.refs_2_), channel_id=1, source_target_pairs={{0,16},{16,0},{1,17},{17,1},{2,18},{18,2},{3,19},{19,3},{4,20},{20... | collective-permute-start | bytes 1769480 | tf_op jit(solution)/shard_map/ppermute | solution.py:64
  451.8 22.2 %collective-permute-start.70 = (bf16[2,96,768]{2,1,0:T(8,128)(2,1)}, bf16[2,96,768]{2,1,0:T(8,128)(2,1)}, u32[]{:S(2)}, u32[]{:S(2)}) collective-permute-start(bf16[2,96,768]{2,1,0:T(8,128)(2,1)} %slice.271), channel_id=1, source_target_pairs={{0,1},{1,0},{2,3},{3,2},{4,5},{5,4},{6,7},{7,6},{8,9},{9,8},{10,11... | collective-permute-start | bytes 884744 | tf_op jit(solution)/shard_map/ppermute | solution.py:68
  452.9 21.1 %collective-permute-start.71 = (bf16[2,96,768]{2,1,0:T(8,128)(2,1)}, bf16[2,96,768]{2,1,0:T(8,128)(2,1)}, u32[]{:S(2)}, u32[]{:S(2)}) collective-permute-start(bf16[2,96,768]{2,1,0:T(8,128)(2,1)} %slice.272), channel_id=1, source_target_pairs={{0,2},{1,3},{2,0},{3,1},{4,6},{5,7},{6,4},{7,5},{8,10},{9,11},{10,... | collective-permute-start | bytes 884744 | tf_op jit(solution)/shard_map/ppermute | solution.py:68
  476.1 7.6 %collective-permute-start.72 = (bf16[4,96,768]{2,1,0:T(8,128)(2,1)S(1)}, bf16[4,96,768]{2,1,0:T(8,128)(2,1)S(1)}, u32[]{:S(2)}, u32[]{:S(2)}) collective-permute-start(bf16[4,96,768]{2,1,0:T(8,128)(2,1)S(1)} %constant_dynamic-update-slice_fusion.8.refs_3_), channel_id=1, source_target_pairs={{0,16},{16,0},{1,17},{17,1},{2,18},{18,2},{3,19},{19,3},{4,20},{20... | collective-permute-start | bytes 1769480 | tf_op jit(solution)/shard_map/ppermute | solution.py:64
  481.0 23.5 %collective-permute-start.67 = (bf16[2,1,2,96,896]{4,3,0,2,1:T(8,128)(2,1)S(1)}, bf16[2,1,2,96,896]{4,3,0,2,1:T(8,128)(2,1)S(1)}, u32[]{:S(2)}, u32[]{:S(2)}) collective-permute-start(bf16[2,1,2,96,896]{4,3,0,2,1:T(8,128)(2,1)S(1)} %copy.278), channel_id=1, source_target_pairs={{0,2},{1,3},{2,0},{3,1},{4,6},{5,7},{6,4},{7,5},{8,10},{9,11},{10,... | collective-permute-start | bytes 2064392 | tf_op jit(solution)/shard_map/ppermute | solution.py:68
  482.8 21.7 %collective-permute-start.66 = (bf16[2,2,1,96,896]{4,3,0,2,1:T(8,128)(2,1)S(1)}, bf16[2,2,1,96,896]{4,3,0,2,1:T(8,128)(2,1)S(1)}, u32[]{:S(2)}, u32[]{:S(2)}) collective-permute-start(bf16[2,2,1,96,896]{4,3,0,2,1:T(8,128)(2,1)S(1)} %copy.277), channel_id=1, source_target_pairs={{0,1},{1,0},{2,3},{3,2},{4,5},{5,4},{6,7},{7,6},{8,9},{9,8},{10,11... | collective-permute-start | bytes 2064392 | tf_op jit(solution)/shard_map/ppermute | solution.py:68
  483.8 20.7 %collective-permute-start.75 = (bf16[192,768]{1,0:T(8,128)(2,1)S(1)}, bf16[192,768]{1,0:T(8,128)(2,1)S(1)}, u32[]{:S(2)}, u32[]{:S(2)}) collective-permute-start(bf16[192,768]{1,0:T(8,128)(2,1)S(1)} %get-tuple-element.563), channel_id=1, source_target_pairs={{0,12},{4,8},{8,4},{12,0},{1,13},{5,9},{9,5},{13,1},{2,14},{6,10},... | collective-permute-start | bytes 884744 | tf_op jit(solution)/shard_map/ppermute | solution.py:68
  486.3 24.5 %collective-permute-start.74 = (bf16[192,768]{1,0:T(8,128)(2,1)S(1)}, bf16[192,768]{1,0:T(8,128)(2,1)S(1)}, u32[]{:S(2)}, u32[]{:S(2)}) collective-permute-start(bf16[192,768]{1,0:T(8,128)(2,1)S(1)} %get-tuple-element.564), channel_id=1, source_target_pairs={{0,8},{4,12},{8,0},{12,4},{1,9},{5,13},{9,1},{13,5},{2,10},{6,14},... | collective-permute-start | bytes 884744 | tf_op jit(solution)/shard_map/ppermute | solution.py:68
  486.3 24.5 %collective-permute-start.73 = (bf16[192,768]{1,0:T(8,128)(2,1)S(1)}, bf16[192,768]{1,0:T(8,128)(2,1)S(1)}, u32[]{:S(2)}, u32[]{:S(2)}) collective-permute-start(bf16[192,768]{1,0:T(8,128)(2,1)S(1)} %get-tuple-element.565), channel_id=1, source_target_pairs={{0,4},{4,0},{8,12},{12,8},{1,5},{5,1},{9,13},{13,9},{2,6},{6,2},{1... | collective-permute-start | bytes 884744 | tf_op jit(solution)/shard_map/ppermute | solution.py:68
  512.9 19.7 %collective-permute-start.76 = (bf16[2,96,896]{2,1,0:T(8,128)(2,1)}, bf16[2,96,896]{2,1,0:T(8,128)(2,1)S(1)}, u32[]{:S(2)}, u32[]{:S(2)}) collective-permute-start(bf16[2,96,896]{2,1,0:T(8,128)(2,1)} %dynamic-slice_bitcast_fusion.3), channel_id=1, source_target_pairs={{0,2},{1,3},{2,0},{3,1},{4,6},{5,7},{6,4},{7,5},{8,10},{9,11},{10,... | collective-permute-start | bytes 1032200 | tf_op jit(solution)/shard_map/ppermute | solution.py:68
  513.5 19.0 %collective-permute-start.77 = (bf16[2,96,896]{2,1,0:T(8,128)(2,1)}, bf16[2,96,896]{2,1,0:T(8,128)(2,1)}, u32[]{:S(2)}, u32[]{:S(2)}) collective-permute-start(bf16[2,96,896]{2,1,0:T(8,128)(2,1)} %dynamic-slice_bitcast_fusion.2), channel_id=1, source_target_pairs={{0,1},{1,0},{2,3},{3,2},{4,5},{5,4},{6,7},{7,6},{8,9},{9,8},{10,11... | collective-permute-start | bytes 1032200 | tf_op jit(solution)/shard_map/ppermute | solution.py:68
  516.3 39.7 %collective-permute-start.81 = (f32[192,768]{1,0:T(8,128)S(1)}, f32[192,768]{1,0:T(8,128)S(1)}, u32[]{:S(2)}, u32[]{:S(2)}) collective-permute-start(f32[192,768]{1,0:T(8,128)S(1)} %get-tuple-element.524), channel_id=1, source_target_pairs={{0,16},{16,0},{1,17},{17,1},{2,18},{18,2},{3,19},{19,3},{4,20},{20... | collective-permute-start | bytes 1769480 | tf_op jit(solution)/shard_map/ppermute | solution.py:64
  536.4 26.3 %collective-permute-start.80 = (bf16[96,896]{1,0:T(8,128)(2,1)}, bf16[96,896]{1,0:T(8,128)(2,1)}, u32[]{:S(2)}, u32[]{:S(2)}) collective-permute-start(bf16[96,896]{1,0:T(8,128)(2,1)} %get-tuple-element.583), channel_id=1, source_target_pairs={{0,12},{4,8},{8,4},{12,0},{1,13},{5,9},{9,5},{13,1},{2,14},{6,10},... | collective-permute-start | bytes 516104 | tf_op jit(solution)/shard_map/ppermute | solution.py:68
  538.4 24.3 %collective-permute-start.78 = (bf16[96,896]{1,0:T(8,128)(2,1)}, bf16[96,896]{1,0:T(8,128)(2,1)}, u32[]{:S(2)}, u32[]{:S(2)}) collective-permute-start(bf16[96,896]{1,0:T(8,128)(2,1)} %get-tuple-element.584), channel_id=1, source_target_pairs={{0,4},{4,0},{8,12},{12,8},{1,5},{5,1},{9,13},{13,9},{2,6},{6,2},{1... | collective-permute-start | bytes 516104 | tf_op jit(solution)/shard_map/ppermute | solution.py:68
  538.4 24.3 %collective-permute-start.79 = (bf16[96,896]{1,0:T(8,128)(2,1)S(1)}, bf16[96,896]{1,0:T(8,128)(2,1)}, u32[]{:S(2)}, u32[]{:S(2)}) collective-permute-start(bf16[96,896]{1,0:T(8,128)(2,1)S(1)} %get-tuple-element.585), channel_id=1, source_target_pairs={{0,8},{4,12},{8,0},{12,4},{1,9},{5,13},{9,1},{13,5},{2,10},{6,14},... | collective-permute-start | bytes 516104 | tf_op jit(solution)/shard_map/ppermute | solution.py:68
  568.3 6.5 %collective-permute-start.85 = (f32[112,128]{1,0:T(8,128)S(1)}, f32[112,128]{1,0:T(8,128)S(1)}, u32[]{:S(2)}, u32[]{:S(2)}) collective-permute-start(f32[112,128]{1,0:T(8,128)S(1)} %get-tuple-element.358), channel_id=1, source_target_pairs={{0,12},{4,8},{8,4},{12,0},{1,13},{5,9},{9,5},{13,1},{2,14},{6,10},... | collective-permute-start | bytes 172040 | tf_op jit(solution)/shard_map/ppermute | solution.py:68
  576.9 45.3 %collective-permute-start.88 = (f32[96,128]{1,0:T(8,128)S(1)}, f32[96,128]{1,0:T(8,128)S(1)}, u32[]{:S(2)}, u32[]{:S(2)}) collective-permute-start(f32[96,128]{1,0:T(8,128)S(1)} %slice.318), channel_id=1, source_target_pairs={{0,3},{1,2},{2,1},{3,0},{4,7},{5,6},{6,5},{7,4},{8,11},{9,10},{10,... | collective-permute-start | bytes 147464 | tf_op jit(solution)/shard_map/ppermute | solution.py:68
  578.8 43.4 %collective-permute-start.87 = (f32[96,128]{1,0:T(8,128)S(1)}, f32[96,128]{1,0:T(8,128)S(1)}, u32[]{:S(2)}, u32[]{:S(2)}) collective-permute-start(f32[96,128]{1,0:T(8,128)S(1)} %slice.318), channel_id=1, source_target_pairs={{0,2},{1,3},{2,0},{3,1},{4,6},{5,7},{6,4},{7,5},{8,10},{9,11},{10,... | collective-permute-start | bytes 147464 | tf_op jit(solution)/shard_map/ppermute | solution.py:68
  579.4 42.8 %collective-permute-start.86 = (f32[96,128]{1,0:T(8,128)S(1)}, f32[96,128]{1,0:T(8,128)}, u32[]{:S(2)}, u32[]{:S(2)}) collective-permute-start(f32[96,128]{1,0:T(8,128)S(1)} %slice.318), channel_id=1, source_target_pairs={{0,1},{1,0},{2,3},{3,2},{4,5},{5,4},{6,7},{7,6},{8,9},{9,8},{10,11... | collective-permute-start | bytes 147464 | tf_op jit(solution)/shard_map/ppermute | solution.py:68
  (231 other events, 1999.9 us)
Sparse Core Ops, SparseCore 1:
  48.9 101.1 all-gather.6
  299.0 152.5 reduce-scatter.4
